TPU v7x, 32 devices: a whole 2x2x4 slice. The times are simulated.
32 devices in a mesh: ctx: 8 (over z, y), fsdp: 4 (over x, core).
Axes of the slice: x: 2, y: 2, z: 4, core: 2. Of those that a mesh axis runs over, the one named last changes fastest.
Arguments:
- tokens: bfloat16 [2, 4096, 1024], P(None, ('fsdp', 'ctx')), may hold values from -6 to 6
- encoder: bfloat16 [2, 12288, 1024], P(None, ('fsdp', 'ctx')), may hold values from -6 to 6
- seq_lengths: int32 [4, 2, 3], P('fsdp'), may hold values from 1 to 768, 1024 in all within a row
- slot_ids: int32 [4, 2, 1024], P('fsdp', None, 'ctx'), may hold values from 0 to 1023, each once within a row
- enc_lengths: int32 [4, 2, 3], P('fsdp'), may hold values from 1 to 1024, 2048 in all within a row
- cotangent: bfloat16 [2, 4096, 1024], P(None, ('fsdp', 'ctx')), may hold values from -6 to 6
- self_in: bfloat16 [1024, 3072], P('fsdp'), may hold values from -0.1875 to 0.1875
- self_out: bfloat16 [1024, 1024], P('fsdp'), may hold values from -4 to 4
- cross_query: bfloat16 [1024, 1024], P('fsdp'), may hold values from -0.1875 to 0.1875
- cross_pair: bfloat16 [1024, 2048], P('fsdp'), may hold values from -0.1875 to 0.1875
- cross_out: bfloat16 [1024, 1024], P('fsdp'), may hold values from -3 to 3
- feed_up: bfloat16 [1024, 4096], P('fsdp'), may hold values from -0.1875 to 0.1875
- feed_down: bfloat16 [4096, 1024], P('fsdp'), may hold values from -0.09375 to 0.09375
- vectors: bfloat16 [1024, 12], P('fsdp'), as said below
- feed_bias: bfloat16 [4096], P('fsdp'), may hold values from -1.5 to 1.5
- self_bias: bfloat16 [1024], P('fsdp'), may hold values from -2.5 to 2.5
Outputs:
- layer_out: bfloat16 [2, 4096, 1024], P(None, ('fsdp', 'ctx'))
- grad_tokens: float32 [2, 4096, 1024], P(None, ('fsdp', 'ctx'))
- grad_encoder: float32 [2, 12288, 1024], P(None, ('fsdp', 'ctx'))
- grad_self_in: float32 [1024, 3072], P(('ctx', 'fsdp'))
- grad_self_out: float32 [1024, 1024], P(('ctx', 'fsdp'))
- grad_cross_query: float32 [1024, 1024], P(('ctx', 'fsdp'))
- grad_cross_pair: float32 [1024, 2048], P(('ctx', 'fsdp'))
- grad_cross_out: float32 [1024, 1024], P(('ctx', 'fsdp'))
- grad_feed_up: float32 [1024, 4096], P(('ctx', 'fsdp'))
- grad_feed_down: float32 [4096, 1024], P(('ctx', 'fsdp'))
- grad_vectors: float32 [1024, 12], P(('ctx', 'fsdp'))
- grad_feed_bias: float32 [4096], P(('ctx', 'fsdp'))
- grad_self_bias: float32 [1024], P(('ctx', 'fsdp'))
Inputs may be any that keep to these rules, and one draw needn't show every extreme that they name: `seq_lengths`: each row sums to 1024; its longest sequence has exactly 768 tokens. `slot_ids`: each row is a permutation of the packed positions. `enc_lengths`: each row sums to 2048; its largest entry is exactly 1024. `vectors`: columns 0 to 2 are gains near one, the rest of order 0.3.
All inputs are finite; a program needn't handle non-finite values.
Results may differ from a plain program's by a relative error of at most 0.02.
The roundings to bfloat16 on the way count: a program that leaves them out, or rounds other values in their place, can miss the bound.
Values may be sent and summed in bfloat16 or wider, within the bound.
No kernel may reach another device: no remote copies, remote signals or barrier semaphores. Data moves between devices by JAX's collectives and lax.ppermute only.
A program may use at most 576 MiB of HBM per device.

v0:
```python
import jax
import jax.numpy as jnp
from jax import lax
from jax.sharding import PartitionSpec as P

D = 1024
HD = 64
ENC = 1024
NSEQ = 3
MICRO = 2
DEPTH = 6


EPSILON = 1e-05
GROUP_HEADS = 2
MASKED = -1e30


def norm_forward(resid, gain, offset):
    average = jnp.mean(resid, -1, keepdims=True)
    centered = resid - average
    inverse = lax.rsqrt(jnp.mean(centered * centered, -1, keepdims=True) + EPSILON)
    normed = centered * inverse
    return (normed * gain + offset, normed, inverse)


def norm_backward(grad_out, normed, inverse, gain):
    grad_normed = grad_out * gain
    first_mean = jnp.mean(grad_normed, -1, keepdims=True)
    second_mean = jnp.mean(grad_normed * normed, -1, keepdims=True)
    grad_resid = inverse * (grad_normed - first_mean - normed * second_mean)
    return (grad_resid, jnp.sum(grad_out * normed, 0), jnp.sum(grad_out, 0))


def gelu_slope(values):
    cumulative = 0.5 * (1.0 + jax.scipy.special.erf(values * 0.7071067811865476))
    density = jnp.exp(-0.5 * values * values) * 0.3989422804014327
    return cumulative + values * density


def column_sum(left, right):
    return lax.dot_general(
        left, right, (((0,), (0,)), ((), ())), preferred_element_type=jnp.float32
    )


def input_grad(grad_rows, weight):
    return lax.dot_general(
        grad_rows, weight, (((1,), (1,)), ((), ())), preferred_element_type=jnp.float32
    )


def linear(inputs, weight):
    return jnp.dot(inputs, weight, preferred_element_type=jnp.float32)


def head_slice(matrix, offset, group_width):
    return lax.dynamic_slice_in_dim(matrix, offset * group_width, group_width, 1).reshape(
        matrix.shape[0], GROUP_HEADS, HD
    )


def join_groups(parts):
    return jnp.transpose(parts, (1, 0, 2)).reshape(parts.shape[1], parts.shape[0] * parts.shape[2])


def attend_forward(queries, keys, values, allow):
    group_width = GROUP_HEADS * HD
    score_scale = HD ** (-0.5)

    def one_group(offset):
        query_part = head_slice(queries, offset, group_width)
        key_part = head_slice(keys, offset, group_width)
        value_part = head_slice(values, offset, group_width)
        scores = (
            jnp.einsum("qhd,khd->hqk", query_part, key_part, preferred_element_type=jnp.float32)
            * score_scale
        )
        scores = jnp.where(allow[None], scores, MASKED)
        maxima = jnp.max(scores, -1, keepdims=True)
        exponent = jnp.exp(scores - maxima)
        totals = jnp.sum(exponent, -1, keepdims=True)
        probabilities = (exponent / totals).astype(jnp.bfloat16)
        result = jnp.einsum(
            "hqk,khd->qhd", probabilities, value_part, preferred_element_type=jnp.float32
        )
        return (result.reshape(result.shape[0], group_width), (maxima + jnp.log(totals))[..., 0])

    results, log_totals = lax.map(
        one_group, jnp.arange(queries.shape[1] // group_width, dtype=jnp.int32)
    )
    return (join_groups(results), log_totals)


def attend_backward(queries, keys, values, allow, log_totals, grad_out):
    group_width = GROUP_HEADS * HD
    score_scale = HD ** (-0.5)

    def one_group(offset):
        query_part = head_slice(queries, offset, group_width)
        key_part = head_slice(keys, offset, group_width)
        value_part = head_slice(values, offset, group_width)
        grad_part = head_slice(grad_out, offset, group_width)
        scores = (
            jnp.einsum("qhd,khd->hqk", query_part, key_part, preferred_element_type=jnp.float32)
            * score_scale
        )
        scores = jnp.where(allow[None], scores, MASKED)
        probabilities = jnp.exp(scores - log_totals[offset][..., None])
        grad_probs = jnp.einsum(
            "qhd,khd->hqk", grad_part, value_part, preferred_element_type=jnp.float32
        )
        delta_rows = jnp.sum(probabilities * grad_probs, -1, keepdims=True)
        grad_scores = (probabilities * (grad_probs - delta_rows)).astype(jnp.bfloat16)
        grad_query = (
            jnp.einsum("hqk,khd->qhd", grad_scores, key_part, preferred_element_type=jnp.float32)
            * score_scale
        )
        grad_key = (
            jnp.einsum("hqk,qhd->khd", grad_scores, query_part, preferred_element_type=jnp.float32)
            * score_scale
        )
        grad_value = jnp.einsum(
            "hqk,qhd->khd",
            probabilities.astype(jnp.bfloat16),
            grad_part,
            preferred_element_type=jnp.float32,
        )
        return (
            grad_query.reshape(grad_query.shape[0], group_width),
            grad_key.reshape(grad_key.shape[0], group_width),
            grad_value.reshape(grad_value.shape[0], group_width),
        )

    grad_query, grad_key, grad_value = lax.map(
        one_group, jnp.arange(queries.shape[1] // group_width, dtype=jnp.int32)
    )
    return (
        join_groups(grad_query),
        jnp.concatenate([join_groups(grad_key), join_groups(grad_value)], 1),
    )


def on_device(
    tokens,
    encoder,
    seq_lengths,
    slot_ids,
    enc_lengths,
    cotangent,
    self_in,
    self_out,
    cross_query,
    cross_pair,
    cross_out,
    feed_up,
    feed_down,
    vectors,
    feed_bias,
    self_bias,
):
    residual_scale = (3.0 * DEPTH) ** 0.25
    every_slot = lax.all_gather(slot_ids, "ctx", axis=2, tiled=True)

    def fetch_weights():
        return (
            lax.all_gather(self_in, "fsdp", axis=0, tiled=True),
            lax.all_gather(self_out, "fsdp", axis=0, tiled=True),
            lax.all_gather(cross_query, "fsdp", axis=0, tiled=True),
            lax.all_gather(cross_pair, "fsdp", axis=0, tiled=True),
            lax.all_gather(cross_out, "fsdp", axis=0, tiled=True),
            lax.all_gather(feed_up, "fsdp", axis=0, tiled=True),
            lax.all_gather(feed_down, "fsdp", axis=0, tiled=True),
            lax.all_gather(vectors, "fsdp", axis=0, tiled=True),
            lax.all_gather(feed_bias, "fsdp", axis=0, tiled=True),
            lax.all_gather(self_bias, "fsdp", axis=0, tiled=True),
        )

    own_enc_rows = encoder.shape[1]
    kept_state = []
    layer_rows = []
    for micro_step in range(MICRO):
        (
            full_self_in,
            full_self_out,
            full_cross_q,
            full_cross_pair,
            full_cross_out,
            full_up,
            full_down,
            full_vectors,
            full_bias,
            full_self_bias,
        ) = fetch_weights()
        vec_table = full_vectors.astype(jnp.float32)
        zero_row = jnp.zeros((D,), jnp.float32)
        seq_ends = jnp.cumsum(seq_lengths[0, micro_step])
        own_ids = slot_ids[0, micro_step]
        key_ids = every_slot[0, micro_step]
        own_seq = jnp.sum((own_ids[:, None] >= seq_ends[None, :]).astype(jnp.int32), 1)
        key_seq = jnp.sum((key_ids[:, None] >= seq_ends[None, :]).astype(jnp.int32), 1)
        allow_self = (own_seq[:, None] == key_seq[None, :]) & (key_ids[None, :] <= own_ids[:, None])
        allow_self_keys = (key_seq[:, None] == own_seq[None, :]) & (
            own_ids[None, :] <= key_ids[:, None]
        )
        enc_index = jnp.arange(NSEQ * ENC, dtype=jnp.int32)
        enc_seq = enc_index // ENC
        seq_index = jnp.arange(NSEQ, dtype=jnp.int32)
        enc_limit = jnp.sum(
            jnp.where(
                enc_seq[:, None] == seq_index[None, :], enc_lengths[0, micro_step][None, :], 0
            ),
            1,
        )
        enc_live = enc_index % ENC < enc_limit
        allow_cross = (own_seq[:, None] == enc_seq[None, :]) & enc_live[None, :]
        enc_start = lax.axis_index("ctx") * own_enc_rows
        own_enc_seq = lax.dynamic_slice_in_dim(enc_seq, enc_start, own_enc_rows, 0)
        own_enc_live = lax.dynamic_slice_in_dim(enc_live, enc_start, own_enc_rows, 0)
        allow_cross_keys = (key_seq[:, None] == own_enc_seq[None, :]) & own_enc_live[None, :]
        tokens_in = tokens[micro_step]
        qkv = (
            linear(tokens_in, full_self_in)
            + jnp.concatenate([vec_table[:, 6], zero_row, vec_table[:, 7]])
        ).astype(jnp.bfloat16)
        own_queries = qkv[:, :D]
        own_pairs = qkv[:, D:]
        pair_table = lax.all_gather(own_pairs, "ctx", axis=0, tiled=True)
        attended, log_self = attend_forward(
            own_queries, pair_table[:, :D], pair_table[:, D:], allow_self
        )
        attended = attended.astype(jnp.bfloat16)
        resid_one = (
            residual_scale * tokens_in.astype(jnp.float32)
            + linear(attended, full_self_out)
            + full_self_bias.astype(jnp.float32)
        )
        normed_one, unit_one, inverse_one = norm_forward(
            resid_one, vec_table[:, 0], vec_table[:, 3]
        )
        normed_one_low = normed_one.astype(jnp.bfloat16)
        cross_queries = (linear(normed_one_low, full_cross_q) + vec_table[:, 8]).astype(
            jnp.bfloat16
        )
        enc_pairs = (
            linear(encoder[micro_step], full_cross_pair)
            + jnp.concatenate([zero_row, vec_table[:, 9]])
        ).astype(jnp.bfloat16)
        enc_table = lax.all_gather(enc_pairs, "ctx", axis=0, tiled=True)
        crossed, log_cross = attend_forward(
            cross_queries, enc_table[:, :D], enc_table[:, D:], allow_cross
        )
        crossed = crossed.astype(jnp.bfloat16)
        resid_two = residual_scale * normed_one + linear(crossed, full_cross_out) + vec_table[:, 10]
        normed_two, unit_two, inverse_two = norm_forward(
            resid_two, vec_table[:, 1], vec_table[:, 4]
        )
        normed_two_low = normed_two.astype(jnp.bfloat16)
        pre_active = linear(normed_two_low, full_up) + full_bias.astype(jnp.float32)
        hidden = jax.nn.gelu(pre_active, approximate=False).astype(jnp.bfloat16)
        resid_three = residual_scale * normed_two + linear(hidden, full_down) + vec_table[:, 11]
        layer_value, unit_three, inverse_three = norm_forward(
            resid_three, vec_table[:, 2], vec_table[:, 5]
        )
        layer_rows.append(layer_value.astype(jnp.bfloat16))
        kept_state.append(
            (
                own_queries,
                own_pairs,
                pair_table,
                allow_self,
                log_self,
                attended,
                unit_one,
                inverse_one,
                normed_one_low,
                cross_queries,
                enc_table,
                allow_cross,
                log_cross,
                crossed,
                unit_two,
                inverse_two,
                normed_two_low,
                pre_active,
                hidden,
                unit_three,
                inverse_three,
                allow_self_keys,
                allow_cross_keys,
                enc_pairs,
            )
        )
    grad_rows = [None] * MICRO
    grad_enc_rows = [None] * MICRO
    summed_grads = None
    for micro_step in reversed(range(MICRO)):
        (
            full_self_in,
            full_self_out,
            full_cross_q,
            full_cross_pair,
            full_cross_out,
            full_up,
            full_down,
            full_vectors,
            full_bias,
            full_self_bias,
        ) = fetch_weights()
        vec_table = full_vectors.astype(jnp.float32)
        (
            own_queries,
            own_pairs,
            pair_table,
            allow_self,
            log_self,
            attended,
            unit_one,
            inverse_one,
            normed_one_low,
            cross_queries,
            enc_table,
            allow_cross,
            log_cross,
            crossed,
            unit_two,
            inverse_two,
            normed_two_low,
            pre_active,
            hidden,
            unit_three,
            inverse_three,
            allow_self_keys,
            allow_cross_keys,
            enc_pairs,
        ) = kept_state[micro_step]
        grad_three, gain_three, offset_three = norm_backward(
            cotangent[micro_step].astype(jnp.float32), unit_three, inverse_three, vec_table[:, 2]
        )
        grad_branch = grad_three.astype(jnp.bfloat16)
        grad_down = column_sum(hidden, grad_branch)
        bias_down = jnp.sum(grad_branch.astype(jnp.float32), 0)
        grad_hidden = input_grad(grad_branch, full_down)
        grad_pre = (grad_hidden * gelu_slope(pre_active)).astype(jnp.bfloat16)
        grad_up = column_sum(normed_two_low, grad_pre)
        bias_up = jnp.sum(grad_pre.astype(jnp.float32), 0)
        grad_two_in = residual_scale * grad_three + input_grad(grad_pre, full_up)
        grad_two, gain_two, offset_two = norm_backward(
            grad_two_in, unit_two, inverse_two, vec_table[:, 1]
        )
        grad_crossed_out = grad_two.astype(jnp.bfloat16)
        grad_cross_out = column_sum(crossed, grad_crossed_out)
        bias_cross_out = jnp.sum(grad_crossed_out.astype(jnp.float32), 0)
        grad_crossed = input_grad(grad_crossed_out, full_cross_out).astype(jnp.bfloat16)
        grad_cross_queries, enc_pair_terms = attend_backward(
            cross_queries, enc_table[:, :D], enc_table[:, D:], allow_cross, log_cross, grad_crossed
        )
        grad_enc_pairs = lax.psum_scatter(
            enc_pair_terms, "ctx", scatter_dimension=0, tiled=True
        ).astype(jnp.bfloat16)
        grad_cross_queries = grad_cross_queries.astype(jnp.bfloat16)
        grad_cross_q = column_sum(normed_one_low, grad_cross_queries)
        bias_cross_q = jnp.sum(grad_cross_queries.astype(jnp.float32), 0)
        grad_cross_pair = column_sum(encoder[micro_step], grad_enc_pairs)
        bias_cross_value = jnp.sum(grad_enc_pairs[:, D:].astype(jnp.float32), 0)
        grad_enc_rows[micro_step] = input_grad(grad_enc_pairs, full_cross_pair)
        grad_one_in = residual_scale * grad_two + input_grad(grad_cross_queries, full_cross_q)
        grad_one, gain_one, offset_one = norm_backward(
            grad_one_in, unit_one, inverse_one, vec_table[:, 0]
        )
        grad_attended_out = grad_one.astype(jnp.bfloat16)
        grad_self_out = column_sum(attended, grad_attended_out)
        bias_self_out = jnp.sum(grad_attended_out.astype(jnp.float32), 0)
        grad_attended = input_grad(grad_attended_out, full_self_out).astype(jnp.bfloat16)
        key_table = lax.all_gather(own_pairs, "ctx", axis=0, tiled=True)
        grad_queries, pair_terms = attend_backward(
            own_queries, key_table[:, :D], key_table[:, D:], allow_self, log_self, grad_attended
        )
        grad_pairs = lax.psum_scatter(pair_terms, "ctx", scatter_dimension=0, tiled=True).astype(
            jnp.bfloat16
        )
        grad_qkv = jnp.concatenate([grad_queries.astype(jnp.bfloat16), grad_pairs], 1)
        tokens_in = tokens[micro_step]
        grad_self_in = column_sum(tokens_in, grad_qkv)
        bias_self_q = jnp.sum(grad_qkv[:, :D].astype(jnp.float32), 0)
        bias_self_value = jnp.sum(grad_pairs[:, D:].astype(jnp.float32), 0)
        grad_rows[micro_step] = residual_scale * grad_one + input_grad(grad_qkv, full_self_in)
        grad_vec = jnp.stack(
            [
                gain_one,
                gain_two,
                gain_three,
                offset_one,
                offset_two,
                offset_three,
                bias_self_q,
                bias_self_value,
                bias_cross_q,
                bias_cross_value,
                bias_cross_out,
                bias_down,
            ],
            1,
        )
        micro_grads = (
            grad_self_in,
            grad_self_out,
            grad_cross_q,
            grad_cross_pair,
            grad_cross_out,
            grad_up,
            grad_down,
            grad_vec,
            bias_up,
            bias_self_out,
        )
        if summed_grads is None:
            summed_grads = micro_grads
        else:
            summed_grads = jax.tree.map(
                lambda first_term, second_term: first_term + second_term, summed_grads, micro_grads
            )
    (
        total_self_in,
        total_self_out,
        total_cross_q,
        total_cross_pair,
        total_cross_out,
        total_up,
        total_down,
        total_vec,
        total_bias,
        total_self_bias,
    ) = summed_grads
    shard_grads = (
        lax.psum_scatter(total_self_in, ("ctx", "fsdp"), scatter_dimension=0, tiled=True),
        lax.psum_scatter(total_self_out, ("ctx", "fsdp"), scatter_dimension=0, tiled=True),
        lax.psum_scatter(total_cross_q, ("ctx", "fsdp"), scatter_dimension=0, tiled=True),
        lax.psum_scatter(total_cross_pair, ("ctx", "fsdp"), scatter_dimension=0, tiled=True),
        lax.psum_scatter(total_cross_out, ("ctx", "fsdp"), scatter_dimension=0, tiled=True),
        lax.psum_scatter(total_up, ("ctx", "fsdp"), scatter_dimension=0, tiled=True),
        lax.psum_scatter(total_down, ("ctx", "fsdp"), scatter_dimension=0, tiled=True),
        lax.psum_scatter(total_vec, ("ctx", "fsdp"), scatter_dimension=0, tiled=True),
        lax.psum_scatter(total_bias, ("ctx", "fsdp"), scatter_dimension=0, tiled=True),
        lax.psum_scatter(total_self_bias, ("ctx", "fsdp"), scatter_dimension=0, tiled=True),
    )
    return (
        jnp.stack(layer_rows, 0),
        jnp.stack(grad_rows, 0),
        jnp.stack(grad_enc_rows, 0),
        shard_grads[0],
        shard_grads[1],
        shard_grads[2],
        shard_grads[3],
        shard_grads[4],
        shard_grads[5],
        shard_grads[6],
        shard_grads[7],
        shard_grads[8],
        shard_grads[9],
    )


def solution(mesh):
    in_specs = (
        P(None, ("fsdp", "ctx"), None),
        P(None, ("fsdp", "ctx"), None),
        P("fsdp", None, None),
        P("fsdp", None, "ctx"),
        P("fsdp", None, None),
        P(None, ("fsdp", "ctx"), None),
        P("fsdp", None),
        P("fsdp", None),
        P("fsdp", None),
        P("fsdp", None),
        P("fsdp", None),
        P("fsdp", None),
        P("fsdp", None),
        P("fsdp", None),
        P("fsdp"),
        P("fsdp"),
    )
    out_specs = (
        P(None, ("fsdp", "ctx"), None),
        P(None, ("fsdp", "ctx"), None),
        P(None, ("fsdp", "ctx"), None),
        P(("ctx", "fsdp"), None),
        P(("ctx", "fsdp"), None),
        P(("ctx", "fsdp"), None),
        P(("ctx", "fsdp"), None),
        P(("ctx", "fsdp"), None),
        P(("ctx", "fsdp"), None),
        P(("ctx", "fsdp"), None),
        P(("ctx", "fsdp"), None),
        P(("ctx", "fsdp")),
        P(("ctx", "fsdp")),
    )
    return jax.shard_map(
        on_device, mesh=mesh, in_specs=in_specs, out_specs=out_specs, check_vma=False
    )
```

profile of v0, /device:TPU:0, one launch (start us, length us, event | category | flops | bytes accessed | tf_op | source)
XLA Modules:
  0.0 3649.3 jit_solution(17627081874102832554)
XLA Ops:
  8.7 6.2 all_gather.31
  15.6 43.1 %all-gather.13.cloned.1.call-done = bf16[1024,3072]{1,0:T(8,128)(2,1)} async-done(((bf16[256,3072]{1,0:T(8,128)(2,1)}), bf16[1024,3072]{1,0:T(8,128)(2,1)}) %all-gather.13.cloned.1.call-update) | async-done | bytes 6291472 | tf_op jit(solution)/shard_map/all_gather | solution.py:167
  69.7 25.1 all-gather.19.cloned.1.call-done
  94.8 5.4 add_convert_fusion
  102.4 5.2 all_gather.41
  107.5 5.1 all-gather
  113.0 20.6 all_gather.33
  134.0 5.4 add_convert_fusion.1
  140.7 30.3 all-gather.31.cloned.1.call-done
  171.0 4.7 fusion.187
  182.7 29.6 while.114
  220.4 73.0 %all-gather.15.cloned.1.call-done = bf16[1024,2048]{1,0:T(8,128)(2,1)} async-done(((bf16[128,2048]{1,0:T(8,128)(2,1)}), bf16[1024,2048]{1,0:T(8,128)(2,1)}) %all-gather.15.cloned.1.call-update) | async-done | bytes 4194320 | tf_op jit(solution)/shard_map/all_gather | solution.py:228
  303.9 36.6 %while.112 = (s32[]{:T(128)}, bf16[8,128,128]{1,2,0:T(8,128)(2,1)S(1)}, f32[8,2,128]{2,1,0:T(2,128)S(1)}, s32[8]{0:T(128)S(1)}, bf16[1024,1024]{0,1:T(8,128)(2,1...) while((s32[]{:T(128)}, ...), condition=%wide.region_6.7_spmd.clone, body=%wide.region_3.6_spmd.clone.sunk | while | flops 69598976 | bytes 5194975 | solution.py:89
  344.5 125.8 %all-gather.33.cloned.1.call-done = bf16[3072,2048]{1,0:T(8,128)(2,1)} async-done(((bf16[384,2048]{1,0:T(8,128)(2,1)}), bf16[3072,2048]{1,0:T(8,128)(2,1)}) %all-gather.33.cloned.1.call-update) | async-done | bytes 12582928 | tf_op jit(solution)/shard_map/all_gather | solution.py:249
  470.3 10.5 fusion.185
  480.8 8.6 copy.98
  489.4 8.8 copy.100
  498.2 50.3 %while.115 = (s32[]{:T(128)}, bf16[8,128,128]{1,2,0:T(8,128)(2,1)S(1)}, f32[8,2,128]{2,1,0:T(2,128)S(1)}, s32[8]{0:T(128)S(1)}, bf16[3072,1024]{0,1:T(8,128)(2,1...) while((s32[]{:T(128)}, ...), condition=%wide.region_31.32_spmd.clone, body=%wide.region_28.31_spmd.clone.sunk | while | flops 208404224 | bytes 15163095 | solution.py:89
  552.5 6.0 convolution_add_fusion.2
  558.6 53.7 %all-gather.29.cloned.1.call-done = bf16[4096,1024]{1,0:T(8,128)(2,1)} async-done(((bf16[1024,1024]{1,0:T(8,128)(2,1)}), bf16[4096,1024]{1,0:T(8,128)(2,1)}) %all-gather.29.cloned.1.call-update) | async-done | bytes 8388624 | tf_op jit(solution)/shard_map/all_gather | solution.py:173
  612.3 9.6 fusion.192
  622.0 168.9 %all-gather.21.cloned.1.call-done = bf16[3072,2048]{1,0:T(8,128)(2,1)} async-done(((bf16[384,2048]{1,0:T(8,128)(2,1)}), bf16[3072,2048]{1,0:T(8,128)(2,1)}) %all-gather.21.cloned.1.call-update) | async-done | bytes 12582928 | tf_op jit(solution)/shard_map/all_gather | solution.py:249
  791.0 10.5 fusion.184
  801.4 8.6 copy.92
  810.1 8.7 copy.94
  818.8 49.9 %while.113 = (s32[]{:T(128)}, bf16[8,128,128]{1,2,0:T(8,128)(2,1)S(1)}, f32[8,2,128]{2,1,0:T(2,128)S(1)}, s32[8]{0:T(128)S(1)}, bf16[3072,1024]{0,1:T(8,128)(2,1...) while((s32[]{:T(128)}, ...), condition=%wide.region_13.14_spmd.clone, body=%wide.region_10.13_spmd.clone.sunk | while | flops 208404224 | bytes 15163095 | solution.py:89
  869.6 5.4 convolution_add_fusion.3
  875.1 5.5 fusion.195
  895.2 4.4 convert_reduce_fusion.9
  900.5 6.0 broadcast.513.clone
  906.5 6.1 broadcast.513.clone.1
  912.6 122.2 %while.116 = (s32[]{:T(128)}, bf16[8,128,128]{1,2,0:T(8,128)(2,1)S(1)}, f32[8,3072,128]{1,2,0:T(8,128)}, f32[8,3072,128]{1,2,0:T(8,128)}, s32[8]{0:T(128)S(1)}, ...) while((s32[]{:T(128)}, ...), condition=%wide.region_42.43_spmd.clone, body=%wide.region_40.42_spmd.clone.sunk | while | flops 511606528 | bytes 45011832 | solution.py:135
  1034.8 4.4 multiply_reduce_fusion.5
  1040.9 6.2 broadcast.513.clone.2
  1047.1 6.0 broadcast.513.clone.3
  1053.2 128.7 %while.118 = (s32[]{:T(128)}, bf16[8,128,128]{1,2,0:T(8,128)(2,1)S(1)}, f32[8,3072,128]{1,2,0:T(8,128)}, f32[8,3072,128]{1,2,0:T(8,128)}, s32[8]{0:T(128)S(1)}, ...) while((s32[]{:T(128)}, ...), condition=%wide.region_55.56_spmd.clone, body=%wide.region_53.55_spmd.clone.sunk | while | flops 511606528 | bytes 45011832 | solution.py:135
  1182.6 4.6 convert_reduce_fusion.6
  1195.5 84.6 %while.119 = (s32[]{:T(128)}, bf16[8,128,128]{1,2,0:T(8,128)(2,1)}, f32[8,1024,128]{1,2,0:T(8,128)}, f32[8,1024,128]{1,2,0:T(8,128)}, s32[8]{0:T(128)S(1)}, /*in...) while((s32[]{:T(128)}, bf16[8,128,128]{1,2,0:T(8,128)(2,1)}, ...), condition=%wide.region_60.61_spmd.clone, body=%wide.region_58.60_spmd.clone.sunk | while | flops 170688256 | bytes 15645029 | solution.py:135
  1280.1 8.5 pad_maximum_fusion.3
  1295.5 80.0 %while.117 = (s32[]{:T(128)}, bf16[8,128,128]{1,2,0:T(8,128)(2,1)S(1)}, f32[8,1024,128]{1,2,0:T(8,128)}, f32[8,1024,128]{1,2,0:T(8,128)}, s32[8]{0:T(128)S(1)}, ...) while((s32[]{:T(128)}, ...), condition=%wide.region_47.48_spmd.clone, body=%wide.region_45.47_spmd.clone.sunk | while | flops 170688256 | bytes 15645029 | solution.py:135
  1375.5 8.5 pad_maximum_fusion.2
  1384.1 18.5 pad_maximum_fusion.1
  1402.7 17.7 pad_maximum_fusion
  1424.8 11.4 reduce-scatter.21.cloned.1.call-done
  1437.5 151.3 %reduce-scatter.19.cloned.1.call-done = f32[128,2048]{0,1:T(8,128)} async-done(((f32[1024,2048]{0,1:T(8,128)}), f32[128,2048]{0,1:T(8,128)}) %reduce-scatter.19.cloned.1.call-update) | async-done | bytes 1048592 | tf_op jit(solution)/shard_map/reduce_scatter | solution.py:379
  1591.0 404.3 %reduce-scatter.25.cloned.1.call-done = f32[384,2048]{0,1:T(8,128)} async-done(((f32[3072,2048]{0,1:T(8,128)}), f32[384,2048]{0,1:T(8,128)}) %reduce-scatter.25.cloned.1.call-update) | async-done | bytes 3145744 | tf_op jit(solution)/shard_map/reduce_scatter | solution.py:358
  1998.9 403.0 %reduce-scatter.23.cloned.1.call-done = f32[384,2048]{0,1:T(8,128)} async-done(((f32[3072,2048]{0,1:T(8,128)}), f32[384,2048]{0,1:T(8,128)}) %reduce-scatter.23.cloned.1.call-update) | async-done | bytes 3145744 | tf_op jit(solution)/shard_map/reduce_scatter | solution.py:358
  2405.7 4.9 convolution_add_fusion.8
  2425.7 6.3 add_bitcast_fusion
  2432.0 12.6 copy.119
  2449.4 9.5 convolution_add_fusion.1
  2459.9 11.1 fusion.155
  2471.0 13.3 convolution_add_fusion
  2488.7 5.7 add_bitcast_fusion.1
  2494.4 9.2 copy.121
  2504.4 39.6 %all-reduce.3 = (f32[4096]{0:T(1024)S(1)}, f32[1024]{0:T(1024)S(1)}) all-reduce(f32[4096]{0:T(1024)S(1)} %add.549, f32[1024]{0:T(1024)S(1)} %add.550), channel_id=14, replica_groups=mesh['ctx'=8,'fsdp'=4] {'ctx','fsdp'}, use_global_device_ids=true, to_apply=%region_98.99.clone | all-reduce | flops 5120 | bytes 40960
  2547.2 5.3 fusion.90
  2562.9 115.6 %reduce-scatter.27.cloned.1.call-done = f32[32,1024]{1,0:T(8,128)} async-done(((f32[1024,1024]{1,0:T(8,128)}), f32[32,1024]{1,0:T(8,128)}) %reduce-scatter.27.cloned.1.call-update) | async-done | bytes 131088 | tf_op jit(solution)/shard_map/reduce_scatter | solution.py:437
  2678.5 139.6 %reduce-scatter.29.cloned.1.call-done = f32[32,1024]{1,0:T(8,128)} async-done(((f32[1024,1024]{1,0:T(8,128)}), f32[32,1024]{1,0:T(8,128)}) %reduce-scatter.29.cloned.1.call-update) | async-done | bytes 131088 | tf_op jit(solution)/shard_map/reduce_scatter | solution.py:438
  2818.1 139.8 %reduce-scatter.31.cloned.1.call-done = f32[32,1024]{1,0:T(8,128)} async-done(((f32[1024,1024]{1,0:T(8,128)}), f32[32,1024]{1,0:T(8,128)}) %reduce-scatter.31.cloned.1.call-update) | async-done | bytes 131088 | tf_op jit(solution)/shard_map/reduce_scatter | solution.py:440
  2957.9 158.9 %reduce-scatter.37.cloned.1.call-done = f32[32,3072]{1,0:T(8,128)} async-done(((f32[1024,3072]{1,0:T(8,128)}), f32[32,3072]{1,0:T(8,128)}) %reduce-scatter.37.cloned.1.call-update) | async-done | bytes 393232
  3116.8 184.8 %reduce-scatter.33.cloned.1.call-done = f32[32,4096]{1,0:T(8,128)} async-done(((f32[1024,4096]{1,0:T(8,128)}), f32[32,4096]{1,0:T(8,128)}) %reduce-scatter.33.cloned.1.call-update) | async-done | bytes 524304 | tf_op jit(solution)/shard_map/reduce_scatter | solution.py:441
  3301.6 187.3 %reduce-scatter.35.cloned.1.call-done = f32[128,1024]{1,0:T(8,128)} async-done(((f32[4096,1024]{1,0:T(8,128)}), f32[128,1024]{1,0:T(8,128)}) %reduce-scatter.35.cloned.1.call-update) | async-done | bytes 524304 | tf_op jit(solution)/shard_map/reduce_scatter | solution.py:442
  3488.9 153.4 %reduce-scatter.39.cloned.1.call-done = f32[32,2048]{1,0:T(8,128)} async-done(((f32[1024,2048]{1,0:T(8,128)}), f32[32,2048]{1,0:T(8,128)}) %reduce-scatter.39.cloned.1.call-update) | async-done | bytes 262160
  (1419 shorter events, 612.1 us)
Async XLA Ops:
  7.2 51.5 %copy-start.32 = (bf16[2,128,1024]{2,1,0:T(8,128)(2,1)S(1)}, bf16[2,128,1024]{2,1,0:T(8,128)(2,1)}, u32[]{:S(2)}) copy-start(bf16[2,128,1024]{2,1,0:T(8,128)(2,1)} %param.32) | copy-start | bytes 1572868
  7.2 51.5 %all-gather.13.cloned.1.call-start = ((), (), s32[]{:S(2)}) async-start(), calls=%async_computation.12 | async-start | bytes 7864320 | tf_op jit(solution)/shard_map/all_gather | solution.py:167
  7.9 86.8 %all-gather.19.cloned.1.call-start = ((), (), s32[]{:S(2)}) async-start(), calls=%async_computation.15 | async-start | bytes 5242880 | tf_op jit(solution)/shard_map/all_gather | solution.py:170
  8.7 162.3 %all-gather.31.cloned.1.call-start = ((), (), s32[]{:S(2)}) async-start(), calls=%async_computation.21 | async-start | bytes 4718592 | tf_op jit(solution)/shard_map/all_gather | solution.py:228
  15.6 853.1 %copy-start.90 = (f32[1024,1]{0,1:T(1,128)}, f32[1024,1]{0,1:T(1,128)S(1)}, u32[]{:S(2)}) copy-start(f32[1024,1]{0,1:T(1,128)S(1)} %get-tuple-element.1290) | copy-start | bytes 12292
  15.6 859.4 %copy-start.68 = (f32[1024,1]{0,1:T(1,128)}, f32[1024,1]{0,1:T(1,128)S(1)}, u32[]{:S(2)}) copy-start(f32[1024,1]{0,1:T(1,128)S(1)} %get-tuple-element.1286) | copy-start | bytes 12292
  15.6 1023.6 %copy-start.64 = (f32[1024,1]{0,1:T(1,128)}, f32[1024,1]{0,1:T(1,128)S(1)}, u32[]{:S(2)}) copy-start(f32[1024,1]{0,1:T(1,128)S(1)} %get-tuple-element.1285) | copy-start | bytes 12292
  63.3 149.0 %all-gather.17.cloned.1.call-start = ((), (), s32[]{:S(2)}) async-start(), calls=%async_computation.14 | async-start | bytes 2621440 | tf_op jit(solution)/shard_map/all_gather | solution.py:168
  63.9 153.4 %all-gather.23.cloned.1.call-start = ((), (), s32[]{:S(2)}) async-start(), calls=%async_computation.17 | async-start | bytes 2621440 | tf_op jit(solution)/shard_map/all_gather | solution.py:169
  64.5 228.8 %all-gather.15.cloned.1.call-start = ((), (), s32[]{:S(2)}) async-start(), calls=%async_computation.13 | async-start | bytes 4718592 | tf_op jit(solution)/shard_map/all_gather | solution.py:228
  69.6 400.7 %all-gather.33.cloned.1.call-start = ((), (), s32[]{:S(2)}) async-start(), calls=%async_computation.22 | async-start | bytes 14155776 | tf_op jit(solution)/shard_map/all_gather | solution.py:249
  100.2 448.3 %all-gather.25.cloned.1.call-start = ((), (), s32[]{:S(2)}) async-start(), calls=%async_computation.18 | async-start | bytes 2621440 | tf_op jit(solution)/shard_map/all_gather | solution.py:171
  101.0 11.7 copy-start.132
  101.0 12.0 copy-start.130
  101.0 32.9 copy-start.133
  101.0 451.5 %all-gather.27.cloned.1.call-start = ((), (), s32[]{:S(2)}) async-start(), calls=%async_computation.19 | async-start | bytes 10485760 | tf_op jit(solution)/shard_map/all_gather | solution.py:172
  101.7 510.5 %all-gather.29.cloned.1.call-start = ((), (), s32[]{:S(2)}) async-start(), calls=%async_computation.20 | async-start | bytes 10485760 | tf_op jit(solution)/shard_map/all_gather | solution.py:173
  102.3 688.7 %all-gather.21.cloned.1.call-start = ((), (), s32[]{:S(2)}) async-start(), calls=%async_computation.16 | async-start | bytes 14155776 | tf_op jit(solution)/shard_map/all_gather | solution.py:249
  139.4 1296.8 %reduce-scatter.21.cloned.1.call-start = ((), (), s32[]{:S(2)}) async-start(), calls=%async_computation.24 | async-start | bytes 9437184 | tf_op jit(solution)/shard_map/reduce_scatter | solution.py:379
  215.4 333.1 %copy-start.11 = (f32[128,1024]{1,0:T(8,128)}, f32[128,1024]{1,0:T(8,128)S(1)}, u32[]{:S(2)}) copy-start(f32[128,1024]{1,0:T(8,128)S(1)} %get-tuple-element.1312) | copy-start | bytes 1572868
  215.4 333.1 %copy-start.108 = (f32[128]{0:T(128)}, f32[128]{0:T(128)S(1)}, u32[]{:S(2)}) copy-start(f32[128]{0:T(128)S(1)} %broadcast_multiply_fusion.14) | copy-start | bytes 1540
  215.6 332.9 %copy-start.127 = (f32[128]{0:T(128)}, f32[128]{0:T(128)S(1)}, u32[]{:S(2)}) copy-start(f32[128]{0:T(128)S(1)} %add_rsqrt_fusion.2) | copy-start | bytes 1540
  303.9 37.2 %copy-start.2 = (bf16[1024,1024]{1,0:T(8,128)(2,1)S(1)}, bf16[1024,1024]{1,0:T(8,128)(2,1)}, u32[]{:S(2)}) copy-start(bf16[1024,1024]{1,0:T(8,128)(2,1)} %all-gather.17.cloned.1.call-done) | copy-start | bytes 6291460
  342.8 525.9 %copy-start.9 = (f32[128,1024]{1,0:T(8,128)}, f32[128,1024]{1,0:T(8,128)S(1)}, u32[]{:S(2)}) copy-start(f32[128,1024]{1,0:T(8,128)S(1)} %get-tuple-element.1318) | copy-start | bytes 1572868
  548.4 10.1 copy-start.53
  550.7 61.6 %copy-start.14 = (f32[128,1024]{1,0:T(8,128)}, f32[128,1024]{1,0:T(8,128)S(1)}, u32[]{:S(2)}) copy-start(f32[128,1024]{1,0:T(8,128)S(1)} %get-tuple-element.1314) | copy-start | bytes 1572868
  550.7 488.5 %copy-start.97 = (f32[128]{0:T(128)}, f32[128]{0:T(128)S(1)}, u32[]{:S(2)}) copy-start(f32[128]{0:T(128)S(1)} %broadcast_multiply_fusion.13) | copy-start | bytes 1540
  551.0 488.3 %copy-start.104 = (f32[128]{0:T(128)}, f32[128]{0:T(128)S(1)}, u32[]{:S(2)}) copy-start(f32[128]{0:T(128)S(1)} %add_rsqrt_fusion.1) | copy-start | bytes 1540
  818.8 49.9 %copy-start.5 = (bf16[1024,1024]{1,0:T(8,128)(2,1)S(1)}, bf16[1024,1024]{1,0:T(8,128)(2,1)}, u32[]{:S(2)}) copy-start(bf16[1024,1024]{1,0:T(8,128)(2,1)} %all-gather.25.cloned.1.call-done) | copy-start | bytes 6291460
  869.3 25.8 copy-start.7
  869.3 25.8 copy-start.99
  869.6 25.6 copy-start.106
  883.8 11.4 copy-start.62
  1053.2 129.4 %copy-start.109 = (f32[128]{0:T(128)S(1)}, f32[128]{0:T(128)}, u32[]{:S(2)}) copy-start(f32[128]{0:T(128)} %copy-done.108) | copy-start | bytes 1540
  1053.2 129.4 %copy-start.128 = (f32[128]{0:T(128)S(1)}, f32[128]{0:T(128)}, u32[]{:S(2)}) copy-start(f32[128]{0:T(128)} %copy-done.127) | copy-start | bytes 1540
  1288.6 300.2 %reduce-scatter.19.cloned.1.call-start = ((), (), s32[]{:S(2)}) async-start(), calls=%async_computation.23 | async-start | bytes 9437184 | tf_op jit(solution)/shard_map/reduce_scatter | solution.py:379
  1384.0 611.2 %reduce-scatter.25.cloned.1.call-start = ((), (), s32[]{:S(2)}) async-start(), calls=%async_computation.26 | async-start | bytes 28311552 | tf_op jit(solution)/shard_map/reduce_scatter | solution.py:358
  1402.7 999.2 %reduce-scatter.23.cloned.1.call-start = ((), (), s32[]{:S(2)}) async-start(), calls=%async_computation.25 | async-start | bytes 28311552 | tf_op jit(solution)/shard_map/reduce_scatter | solution.py:358
  1420.5 1141.1 %reduce-scatter.41.cloned.1.call-start = ((), (), s32[]{:S(2)}) async-start(), calls=%async_computation.34 | async-start | bytes 540672
  1437.5 559.8 %copy-start.34 = (bf16[128,2048]{0,1:T(8,128)(2,1)}, bf16[128,2048]{0,1:T(8,128)(2,1)S(1)}, u32[]{:S(2)}) copy-start(bf16[128,2048]{0,1:T(8,128)(2,1)S(1)} %convert_element_type.370) | copy-start | bytes 1572868
  1998.7 405.5 %copy-start.114 = (f32[1024]{0:T(1024)S(1)}, f32[1024]{0:T(1024)}, u32[]{:S(2)}) copy-start(f32[1024]{0:T(1024)} %get-tuple-element.1010) | copy-start | bytes 12292
  1998.7 405.4 %copy-start.115 = (f32[1024]{0:T(1024)S(1)}, f32[1024]{0:T(1024)}, u32[]{:S(2)}) copy-start(f32[1024]{0:T(1024)} %get-tuple-element.1234) | copy-start | bytes 12292
  1998.8 405.4 %copy-start.118 = (f32[1024]{0:T(1024)S(1)}, f32[1024]{0:T(1024)}, u32[]{:S(2)}) copy-start(f32[1024]{0:T(1024)} %get-tuple-element.1301) | copy-start | bytes 12292
  1998.8 405.4 %copy-start.119 = (f32[1024]{0:T(1024)S(1)}, f32[1024]{0:T(1024)}, u32[]{:S(2)}) copy-start(f32[1024]{0:T(1024)} %get-tuple-element.1304) | copy-start | bytes 12292
  1998.8 405.4 %copy-start.122 = (f32[1024]{0:T(1024)S(1)}, f32[1024]{0:T(1024)}, u32[]{:S(2)}) copy-start(f32[1024]{0:T(1024)} %get-tuple-element.1236) | copy-start | bytes 12292
  1998.8 405.6 %copy-start.110 = (f32[1024]{0:T(1024)S(1)}, f32[1024]{0:T(1024)}, u32[]{:S(2)}) copy-start(f32[1024]{0:T(1024)} %get-tuple-element.1006) | copy-start | bytes 12292
  1998.8 405.6 %copy-start.111 = (f32[1024]{0:T(1024)S(1)}, f32[1024]{0:T(1024)}, u32[]{:S(2)}) copy-start(f32[1024]{0:T(1024)} %get-tuple-element.1026) | copy-start | bytes 12292
  1998.8 405.6 %copy-start.112 = (f32[1024]{0:T(1024)S(1)}, f32[1024]{0:T(1024)}, u32[]{:S(2)}) copy-start(f32[1024]{0:T(1024)} %get-tuple-element.1019) | copy-start | bytes 12292
  1998.8 405.6 %copy-start.113 = (f32[1024]{0:T(1024)S(1)}, f32[1024]{0:T(1024)}, u32[]{:S(2)}) copy-start(f32[1024]{0:T(1024)} %get-tuple-element.1281) | copy-start | bytes 12292
  1998.8 405.6 %copy-start.116 = (f32[1024]{0:T(1024)S(1)}, f32[1024]{0:T(1024)}, u32[]{:S(2)}) copy-start(f32[1024]{0:T(1024)} %get-tuple-element.1232) | copy-start | bytes 12292
  1998.8 405.6 %copy-start.125 = (f32[1024]{0:T(1024)S(1)}, f32[1024]{0:T(1024)}, u32[]{:S(2)}) copy-start(f32[1024]{0:T(1024)} %get-tuple-element.1008) | copy-start | bytes 12292
  1998.8 405.6 %copy-start.126 = (f32[1024]{0:T(1024)S(1)}, f32[1024]{0:T(1024)}, u32[]{:S(2)}) copy-start(f32[1024]{0:T(1024)} %get-tuple-element.1027) | copy-start | bytes 12292
  2403.9 84.8 %copy-start.18 = (bf16[384,2048]{0,1:T(8,128)(2,1)}, bf16[384,2048]{0,1:T(8,128)(2,1)S(1)}, u32[]{:S(2)}) copy-start(bf16[384,2048]{0,1:T(8,128)(2,1)S(1)} %convert_element_type.371) | copy-start | bytes 4718596
  2405.6 272.9 %reduce-scatter.27.cloned.1.call-start = ((), (), s32[]{:S(2)}) async-start(), calls=%async_computation.27 | async-start | bytes 4325376 | tf_op jit(solution)/shard_map/reduce_scatter | solution.py:437
  2410.6 407.5 %reduce-scatter.29.cloned.1.call-start = ((), (), s32[]{:S(2)}) async-start(), calls=%async_computation.28 | async-start | bytes 4325376 | tf_op jit(solution)/shard_map/reduce_scatter | solution.py:438
  2416.2 541.7 %reduce-scatter.31.cloned.1.call-start = ((), (), s32[]{:S(2)}) async-start(), calls=%async_computation.29 | async-start | bytes 4325376 | tf_op jit(solution)/shard_map/reduce_scatter | solution.py:440
  2421.7 695.1 %reduce-scatter.37.cloned.1.call-start = ((), (), s32[]{:S(2)}) async-start(), calls=%async_computation.32 | async-start | bytes 12976128
  2444.7 857.0 %reduce-scatter.33.cloned.1.call-start = ((), (), s32[]{:S(2)}) async-start(), calls=%async_computation.30 | async-start | bytes 17301504 | tf_op jit(solution)/shard_map/reduce_scatter | solution.py:441
  2458.9 12.1 copy-start.61
  2458.9 1030.1 %reduce-scatter.35.cloned.1.call-start = ((), (), s32[]{:S(2)}) async-start(), calls=%async_computation.31 | async-start | bytes 17301504 | tf_op jit(solution)/shard_map/reduce_scatter | solution.py:442
  2459.9 11.1 copy-start.58
  2484.3 1158.0 %reduce-scatter.39.cloned.1.call-start = ((), (), s32[]{:S(2)}) async-start(), calls=%async_computation.33 | async-start | bytes 8650752
  2503.7 43.5 %copy-start.31 = (f32[128,1024]{1,0:T(8,128)S(1)}, f32[128,1024]{1,0:T(8,128)}, u32[]{:S(2)}) copy-start(f32[128,1024]{1,0:T(8,128)} %copy-done.29) | copy-start | bytes 1572868
  2503.7 48.9 %slice-start.2 = ((s8[6291456]{0:T(1024)(128)(4,1)}), s8[2097152]{0:T(1024)(128)(4,1)S(1)}, s32[]{:S(2)}) async-start(s8[6291456]{0:T(1024)(128)(4,1)} %bitcast.598), calls=%async_computation.37 | async-start | bytes 4194304
  (171 other events, 511.5 us)
Sparse Core Ops, SparseCore 0:
  9.6 49.0 all-gather.12
  60.3 34.4 all-gather.18
  97.5 73.4 all-gather.30
  172.4 20.8 all-gather.16
  194.7 22.6 all-gather.22
  219.9 73.3 all-gather.14
  295.6 174.6 all-gather.32
  471.8 20.7 all-gather.24
  494.2 58.2 all-gather.26
  553.9 58.2 all-gather.28
  614.5 176.4 all-gather.20
  1288.7 147.5 reduce-scatter.20
  1440.3 148.4 reduce-scatter.18
  1592.5 402.7 reduce-scatter.24
  1999.0 402.8 reduce-scatter.22
  2405.7 132.8 reduce-scatter.40
  2541.5 137.0 reduce-scatter.26
  2681.3 136.7 reduce-scatter.28
  2821.0 136.8 reduce-scatter.30
  2965.4 151.3 reduce-scatter.36
  3119.7 181.9 reduce-scatter.32
  3304.5 184.4 reduce-scatter.34
  3491.8 150.4 reduce-scatter.38
where the time goes:
time: 3670 us; the launch traced here: 3650 us
  waiting for transfers between devices  2580 us (70%)
  local copies, waits for them, and re-layouts  443 us (12%)
  matrix products  309 us (8%)
  other arithmetic  117 us (3%)
  loops' own time  108 us (3%)
  blocking collectives  76.6 us (2%)
    reduce_scatter x2, waiting for transfers between devices, on_device(): lax.psum_scatter(enc_pair_terms, 'ctx', scatter_dimension=0, tiled=True)  807 us
    unnamed x26, waiting for transfers between devices  317 us
    all_gather x2, waiting for transfers between devices, on_device(): enc_table = lax.all_gather(enc_pairs, 'ctx', axis=0, tiled=True)  295 us
    reduce_scatter x1, waiting for transfers between devices, on_device(): lax.psum_scatter(total_down, ('ctx', 'fsdp'), scatter_dimension=0, tiled=...  187 us
    reduce_scatter x1, waiting for transfers between devices, on_device(): lax.psum_scatter(total_up, ('ctx', 'fsdp'), scatter_dimension=0, tiled=True)  185 us
    dynamic_slice x224, local copies, waits for them, and re-layouts, head_slice(): lax.dynamic_slice_in_dim(matrix, offset * group_width, group_width, 1)  171 us
    reduce_scatter x2, waiting for transfers between devices, on_device(): lax.psum_scatter(pair_terms, 'ctx', scatter_dimension=0, tiled=True)  163 us
    reduce_scatter x1, waiting for transfers between devices, on_device(): lax.psum_scatter(total_cross_out, ('ctx', 'fsdp'), scatter_dimension=0, t...  140 us
  transfers between devices with their start and end apart: 23, of which 20 were waited for; matrix products, arithmetic and copies ran while one was open for 12% of the time, Pallas kernels for 0%

commit v1 on v0

v1 whole, which is shorter than its diff:
```python
import functools

import jax
import jax.numpy as jnp
from jax import lax
from jax.experimental import pallas as pl
from jax.experimental.pallas import tpu as pltpu
from jax.sharding import Mesh
from jax.sharding import PartitionSpec as P

D = 1024
HD = 64
ENC = 1024
NSEQ = 3
MICRO = 2
DEPTH = 6

EPSILON = 1e-05
MASKED = -1e30
SCALE = HD ** (-0.5)
T_SIZE = 4
PAIR = 2
GROUP = ("y", "core")
ROWS = ("x", "core", "t", "s", "y")
BLOCKS = ("t", "s", "y", "x", "core")
MEMBERS = 4
WIDTH = D // MEMBERS
HEADS = WIDTH // HD
VMEM_LIMIT = 56 * 1024 * 1024


def norm_forward(resid, gain, offset):
    average = jnp.mean(resid, -1, keepdims=True)
    centered = resid - average
    inverse = lax.rsqrt(jnp.mean(centered * centered, -1, keepdims=True) + EPSILON)
    normed = centered * inverse
    return (normed * gain + offset, normed, inverse)


def norm_backward(grad_out, normed, inverse, gain):
    grad_normed = grad_out * gain
    first_mean = jnp.mean(grad_normed, -1, keepdims=True)
    second_mean = jnp.mean(grad_normed * normed, -1, keepdims=True)
    grad_resid = inverse * (grad_normed - first_mean - normed * second_mean)
    return (grad_resid, jnp.sum(grad_out * normed, 0), jnp.sum(grad_out, 0))


def gelu_slope(values):
    cumulative = 0.5 * (1.0 + jax.scipy.special.erf(values * 0.7071067811865476))
    density = jnp.exp(-0.5 * values * values) * 0.3989422804014327
    return cumulative + values * density


def column_sum(left, right):
    return lax.dot_general(
        left, right, (((0,), (0,)), ((), ())), preferred_element_type=jnp.float32
    )


def input_grad(grad_rows, weight):
    return lax.dot_general(
        grad_rows, weight, (((1,), (1,)), ((), ())), preferred_element_type=jnp.float32
    )


def linear(inputs, weight):
    return jnp.dot(inputs, weight, preferred_element_type=jnp.float32)


def pack_routes():
    straight, crossed = [], []
    for t in range(T_SIZE):
        for core in range(PAIR):
            here = t * PAIR + core
            straight.append((here, (2 * core + (t & 1)) * PAIR + (t >> 1)))
            crossed.append((here, (2 * core + 1 - (t & 1)) * PAIR + (t >> 1)))
    return straight, crossed


def to_packs(parts):
    straight, crossed = pack_routes()
    parity = lax.axis_index("t") & 1
    first = lax.dynamic_index_in_dim(parts, parity, 0, keepdims=False)
    second = lax.dynamic_index_in_dim(parts, 1 - parity, 0, keepdims=False)
    return (
        lax.ppermute(first, ("t", "core"), straight),
        lax.ppermute(second, ("t", "core"), crossed),
    )


def from_packs(first, second):
    straight, crossed = pack_routes()
    first = lax.ppermute(first, ("t", "core"), [(to, source) for source, to in straight])
    second = lax.ppermute(second, ("t", "core"), [(to, source) for source, to in crossed])
    parity = lax.axis_index("t") & 1
    return jnp.stack(
        [jnp.where(parity == 0, first, second), jnp.where(parity == 0, second, first)], 0
    )


def group_route(step):
    return [(member, member ^ step) for member in range(MEMBERS)]


def group_index():
    return lax.axis_index("y") * PAIR + lax.axis_index("core")


def share_in_group(block):
    return [block] + [
        lax.ppermute(block, GROUP, group_route(step)) for step in range(1, MEMBERS)
    ]


def to_heads(matrix):
    rows = matrix.shape[0]
    parts = matrix.shape[1] // D
    me = group_index()
    split = matrix.reshape(rows, parts, MEMBERS, WIDTH)
    blocks = []
    for step in range(MEMBERS):
        block = lax.dynamic_index_in_dim(split, me ^ step, 2, keepdims=False)
        block = block.reshape(rows, parts * WIDTH)
        blocks.append(block if step == 0 else lax.ppermute(block, GROUP, group_route(step)))
    return jnp.concatenate(blocks, 0)


def from_heads(matrix, parts):
    rows = matrix.shape[0] // MEMBERS
    me = group_index()
    blocks = []
    for step in range(MEMBERS):
        block = matrix[step * rows : (step + 1) * rows]
        blocks.append(block if step == 0 else lax.ppermute(block, GROUP, group_route(step)))
    table = jnp.stack(blocks, 0)
    columns = [
        lax.dynamic_index_in_dim(table, me ^ member, 0, keepdims=False) for member in range(MEMBERS)
    ]
    split = [block.reshape(rows, parts, WIDTH) for block in columns]
    return jnp.stack(split, 2).reshape(rows, parts * D)


def gather_sequence(matrix, count):
    if count == 1:
        return matrix
    return lax.all_gather(matrix, "s", axis=0, tiled=True)


def scatter_sequence(matrix, count):
    if count == 1:
        return matrix
    return lax.psum_scatter(matrix, "s", scatter_dimension=0, tiled=True)


def reduce_blocks(blocks, count, order):
    dtype = blocks.dtype
    names = ["t1", "t0", "s", "y", "x", "core"]
    sizes = [PAIR, PAIR, count, PAIR, PAIR, PAIR]
    value = blocks.reshape(tuple(sizes) + blocks.shape[1:])
    for name in order:
        place = names.index(name)
        names.pop(place)
        if name == "s":
            if count == 1:
                value = lax.squeeze(value, (place,))
            else:
                value = lax.psum_scatter(value, "s", scatter_dimension=place, tiled=False)
            continue
        axis = name[0] if name in ("t1", "t0") else name
        flip = {"t1": 2, "t0": 1}.get(name, 1)
        size = T_SIZE if axis == "t" else PAIR
        mine = lax.axis_index(axis)
        if name == "t1":
            mine = mine >> 1
        elif name == "t0":
            mine = mine & 1
        keep = lax.dynamic_index_in_dim(value, mine, place, keepdims=False)
        send = lax.dynamic_index_in_dim(value, 1 - mine, place, keepdims=False)
        arrived = lax.ppermute(send, axis, [(i, i ^ flip) for i in range(size)])
        value = (keep.astype(jnp.float32) + arrived.astype(jnp.float32)).astype(dtype)
    return value


def reduce_weight(gradient, count, order):
    blocks = T_SIZE * count * 8
    rows = gradient.shape[0] // blocks
    low = gradient.astype(jnp.bfloat16).reshape(blocks, rows, gradient.shape[1])
    return reduce_blocks(low, count, order).astype(jnp.float32)


def forward_kernel(
    chunk, flags_ref, q_ref, k_ref, v_ref, low_ref, high_ref, key_ref, out_ref, exact_ref, log_ref,
    masked_ref, top_ref, sum_ref, total_ref,
):
    step = pl.program_id(0)
    chunks = k_ref.shape[0] // chunk
    rows = q_ref.shape[0]
    lane = lax.broadcasted_iota(jnp.int32, (rows, 128), 1)
    for head in range(HEADS):
        pair = q_ref[:, (head // 2) * 128 : (head // 2 + 1) * 128] * SCALE
        masked_ref[head] = jnp.where((lane >= HD) == (head % 2 == 1), pair, 0).astype(jnp.bfloat16)
    top_ref[...] = jnp.full_like(top_ref, MASKED)
    sum_ref[...] = jnp.zeros_like(sum_ref)
    total_ref[...] = jnp.zeros_like(total_ref)

    def one_chunk(index, carry):
        @pl.when(flags_ref[step * chunks + index] != 0)
        def _():
            start = pl.multiple_of(index * chunk, chunk)
            keys = key_ref[:, pl.ds(start, chunk)]
            allow = (keys >= low_ref[...]) & (keys <= high_ref[...])
            bias = jnp.where(allow, 0.0, MASKED)
            for head in range(HEADS):
                columns = slice((head // 2) * 128, (head // 2 + 1) * 128)
                scores = lax.dot_general(
                    masked_ref[head],
                    k_ref[pl.ds(start, chunk), columns],
                    (((1,), (1,)), ((), ())),
                    preferred_element_type=jnp.float32,
                ) + bias
                before = top_ref[head]
                after = jnp.maximum(before, jnp.max(scores, 1, keepdims=True))
                exponent = jnp.exp(scores - after[:, :1])
                fade = jnp.exp(before - after)
                top_ref[head] = after
                sum_ref[head] = sum_ref[head] * fade + jnp.sum(exponent, 1, keepdims=True)
                total_ref[head] = total_ref[head] * fade + jnp.dot(
                    exponent.astype(jnp.bfloat16),
                    v_ref[pl.ds(start, chunk), columns],
                    preferred_element_type=jnp.float32,
                )

        return carry

    lax.fori_loop(0, chunks, one_chunk, 0)
    logs = jnp.zeros((rows, 128), jnp.float32)
    for head in range(0, HEADS, 2):
        first = total_ref[head] / sum_ref[head]
        second = total_ref[head + 1] / sum_ref[head + 1]
        both = jnp.where(lane < HD, first, second)
        columns = slice((head // 2) * 128, (head // 2 + 1) * 128)
        exact_ref[:, columns] = both
        out_ref[:, columns] = both.astype(jnp.bfloat16)
        for other in (head, head + 1):
            logs = jnp.where(lane == other, top_ref[other] + jnp.log(sum_ref[other]), logs)
    log_ref[...] = logs


def attend_forward(queries, keys, values, low, high, key_ids, flags, block, chunk):
    count, depth = queries[0].shape[0], keys[0].shape[0]
    whole = functools.partial(pl.BlockSpec, pipeline_mode=pl.Buffered(1))
    return pl.pallas_call(
        functools.partial(forward_kernel, chunk),
        grid_spec=pltpu.PrefetchScalarGridSpec(
            num_scalar_prefetch=1,
            grid=(count // block,),
            in_specs=[
                pl.BlockSpec((block, WIDTH), lambda i, f, c=queries[1]: (i, c)),
                whole((depth, WIDTH), lambda i, f, c=keys[1]: (0, c)),
                whole((depth, WIDTH), lambda i, f, c=values[1]: (0, c)),
                pl.BlockSpec((block, 1), lambda i, f: (i, 0)),
                pl.BlockSpec((block, 1), lambda i, f: (i, 0)),
                whole((1, depth), lambda i, f: (0, 0)),
            ],
            out_specs=[
                pl.BlockSpec((block, WIDTH), lambda i, f: (i, 0)),
                pl.BlockSpec((block, WIDTH), lambda i, f: (i, 0)),
                pl.BlockSpec((block, 128), lambda i, f: (i, 0)),
            ],
            scratch_shapes=[
                pltpu.VMEM((HEADS, block, 128), jnp.bfloat16),
                pltpu.VMEM((HEADS, block, 128), jnp.float32),
                pltpu.VMEM((HEADS, block, 128), jnp.float32),
                pltpu.VMEM((HEADS, block, 128), jnp.float32),
            ],
        ),
        out_shape=[
            jax.ShapeDtypeStruct((count, WIDTH), jnp.bfloat16),
            jax.ShapeDtypeStruct((count, WIDTH), jnp.float32),
            jax.ShapeDtypeStruct((count, 128), jnp.float32),
        ],
        compiler_params=pltpu.CompilerParams(vmem_limit_bytes=VMEM_LIMIT),
        cost_estimate=pl.CostEstimate(
            flops=4 * count * depth * WIDTH,
            bytes_accessed=8 * (count + depth) * WIDTH,
            transcendentals=count * depth * HEADS,
        ),
    )(flags.reshape(-1), queries[0], keys[0], values[0], low[:, None], high[:, None], key_ids[None, :])


def backward_kernel(
    chunk, flags_ref, q_ref, k_ref, v_ref, g_ref, log_ref, delta_ref, low_ref, high_ref, key_ref,
    dq_ref, dk_ref, dv_ref, q_masked, g_masked, turned_ref, dq_sum, dk_sum, dv_sum,
):
    step = pl.program_id(0)
    chunks = k_ref.shape[0] // chunk
    rows = q_ref.shape[0]
    lane = lax.broadcasted_iota(jnp.int32, (rows, 128), 1)

    @pl.when(step == 0)
    def _():
        dk_sum[...] = jnp.zeros_like(dk_sum)
        dv_sum[...] = jnp.zeros_like(dv_sum)

        def turn(index, carry):
            start = pl.multiple_of(index * chunk, chunk)
            turned_ref[:, pl.ds(start, chunk)] = k_ref[pl.ds(start, chunk), :].T
            return carry

        lax.fori_loop(0, chunks, turn, 0)

    for head in range(HEADS):
        columns = slice((head // 2) * 128, (head // 2 + 1) * 128)
        chosen = (lane >= HD) == (head % 2 == 1)
        q_masked[head] = jnp.where(chosen, q_ref[:, columns] * SCALE, 0).astype(jnp.bfloat16)
        g_masked[head] = jnp.where(chosen, g_ref[:, columns], 0).astype(jnp.bfloat16)
    dq_sum[...] = jnp.zeros_like(dq_sum)

    def one_chunk(index, carry):
        @pl.when(flags_ref[step * chunks + index] != 0)
        def _():
            start = pl.multiple_of(index * chunk, chunk)
            here = pl.ds(start, chunk)
            keys = key_ref[here, :]
            allow = (keys >= low_ref[...]) & (keys <= high_ref[...])
            bias = jnp.where(allow, 0.0, MASKED)
            for head in range(HEADS):
                columns = slice((head // 2) * 128, (head // 2 + 1) * 128)
                scores = lax.dot_general(
                    k_ref[here, columns],
                    q_masked[head],
                    (((1,), (1,)), ((), ())),
                    preferred_element_type=jnp.float32,
                )
                chances = jnp.exp(scores + bias - log_ref[head : head + 1, :])
                grads = lax.dot_general(
                    v_ref[here, columns],
                    g_masked[head],
                    (((1,), (1,)), ((), ())),
                    preferred_element_type=jnp.float32,
                )
                slopes = (chances * (grads - delta_ref[head : head + 1, :])).astype(jnp.bfloat16)
                dk_sum[here, columns] += jnp.dot(
                    slopes, q_masked[head], preferred_element_type=jnp.float32
                )
                dv_sum[here, columns] += jnp.dot(
                    chances.astype(jnp.bfloat16), g_masked[head], preferred_element_type=jnp.float32
                )
                dq_sum[head * HD : (head + 1) * HD, :] += jnp.dot(
                    turned_ref[head * HD : (head + 1) * HD, here],
                    slopes,
                    preferred_element_type=jnp.float32,
                )

        return carry

    lax.fori_loop(0, chunks, one_chunk, 0)
    dq_ref[...] = (dq_sum[...] * SCALE).T.astype(jnp.bfloat16)

    @pl.when(step == pl.num_programs(0) - 1)
    def _():
        dk_ref[...] = dk_sum[...].astype(jnp.bfloat16)
        dv_ref[...] = dv_sum[...].astype(jnp.bfloat16)


def attend_backward(
    queries, keys, values, grads, logs, delta, low, high, key_ids, flags, block, chunk
):
    count, depth = queries[0].shape[0], keys[0].shape[0]
    whole = functools.partial(pl.BlockSpec, pipeline_mode=pl.Buffered(1))
    return pl.pallas_call(
        functools.partial(backward_kernel, chunk),
        grid_spec=pltpu.PrefetchScalarGridSpec(
            num_scalar_prefetch=1,
            grid=(count // block,),
            in_specs=[
                pl.BlockSpec((block, WIDTH), lambda i, f, c=queries[1]: (i, c)),
                whole((depth, WIDTH), lambda i, f, c=keys[1]: (0, c)),
                whole((depth, WIDTH), lambda i, f, c=values[1]: (0, c)),
                pl.BlockSpec((block, WIDTH), lambda i, f: (i, 0)),
                pl.BlockSpec((HEADS, block), lambda i, f: (0, i)),
                pl.BlockSpec((HEADS, block), lambda i, f: (0, i)),
                pl.BlockSpec((1, block), lambda i, f: (0, i)),
                pl.BlockSpec((1, block), lambda i, f: (0, i)),
                whole((depth, 1), lambda i, f: (0, 0)),
            ],
            out_specs=[
                pl.BlockSpec((block, WIDTH), lambda i, f: (i, 0)),
                whole((depth, WIDTH), lambda i, f: (0, 0)),
                whole((depth, WIDTH), lambda i, f: (0, 0)),
            ],
            scratch_shapes=[
                pltpu.VMEM((HEADS, block, 128), jnp.bfloat16),
                pltpu.VMEM((HEADS, block, 128), jnp.bfloat16),
                pltpu.VMEM((WIDTH, depth), jnp.bfloat16),
                pltpu.VMEM((WIDTH, block), jnp.float32),
                pltpu.VMEM((depth, WIDTH), jnp.float32),
                pltpu.VMEM((depth, WIDTH), jnp.float32),
            ],
        ),
        out_shape=[
            jax.ShapeDtypeStruct((count, WIDTH), jnp.bfloat16),
            jax.ShapeDtypeStruct((depth, WIDTH), jnp.bfloat16),
            jax.ShapeDtypeStruct((depth, WIDTH), jnp.bfloat16),
        ],
        compiler_params=pltpu.CompilerParams(vmem_limit_bytes=VMEM_LIMIT),
        cost_estimate=pl.CostEstimate(
            flops=10 * count * depth * WIDTH,
            bytes_accessed=10 * (count + depth) * WIDTH,
            transcendentals=count * depth * HEADS,
        ),
    )(
        flags.reshape(-1), queries[0], keys[0], values[0], grads, logs, delta, low[None, :],
        high[None, :], key_ids[:, None],
    )


def needed_chunks(low, high, key_ids, block, chunk):
    first = jnp.min(low.reshape(-1, block), 1)[:, None]
    last = jnp.max(high.reshape(-1, block), 1)[:, None]
    smallest = jnp.min(key_ids.reshape(-1, chunk), 1)[None, :]
    largest = jnp.max(key_ids.reshape(-1, chunk), 1)[None, :]
    return ((largest >= first) & (smallest <= last)).astype(jnp.int32)


def log_rows(logs):
    return jnp.transpose(logs[:, :HEADS])


def delta_rows(grads, exact):
    products = grads.astype(jnp.float32) * exact
    return jnp.transpose(jnp.sum(products.reshape(-1, HEADS, HD), -1))


def on_device(
    count,
    tokens,
    encoder,
    seq_lengths,
    slot_ids,
    enc_lengths,
    cotangent,
    self_in,
    self_out,
    cross_query,
    cross_pair,
    cross_out,
    feed_up,
    feed_down,
    vectors,
    feed_bias,
    self_bias,
):
    residual_scale = (3.0 * DEPTH) ** 0.25
    fsdp = ("x", "core")

    def fetch(weight):
        return lax.all_gather(weight, fsdp, axis=0, tiled=True)

    full_self_in = fetch(self_in)
    facts = jnp.concatenate([slot_ids[0], seq_lengths[0], enc_lengths[0]], 1)
    slots = slot_ids.shape[2]
    facts_one, facts_two = to_packs(facts)
    tokens_in = jnp.concatenate(to_packs(tokens), 0)
    small = jnp.concatenate(
        [vectors.T, feed_bias.reshape(D // 4, 4).T, self_bias[None, :]], 0
    )
    full_small = lax.all_gather(small, fsdp, axis=1, tiled=True)
    encoder_in = jnp.concatenate(to_packs(encoder), 0)
    full_cross_pair = fetch(cross_pair)
    full_self_out = fetch(self_out)
    full_cross_q = fetch(cross_query)
    full_cross_out = fetch(cross_out)
    full_up = fetch(feed_up)
    full_down = fetch(feed_down)
    grad_in = jnp.concatenate(to_packs(cotangent), 0)

    vec = full_small[:12].astype(jnp.float32)
    bias_row = full_small[12:16].T.reshape(4 * D).astype(jnp.float32)
    self_bias_row = full_small[16].astype(jnp.float32)
    zero_row = jnp.zeros((D,), jnp.float32)

    lengths = facts_one[slots : slots + NSEQ]
    limits = facts_one[slots + NSEQ : slots + 2 * NSEQ]
    own_ids = jnp.concatenate([facts_one[:slots], facts_two[:slots]])
    ids = jnp.concatenate(share_in_group(own_ids))
    ends = jnp.cumsum(lengths)
    key_ids = gather_sequence(ids, count)
    rank = jnp.sum((ids[None, :] < ids[:, None]).astype(jnp.int32), 1)
    places = jnp.arange(ids.shape[0], dtype=jnp.int32)
    sorter = (places[:, None] == rank[None, :]).astype(jnp.bfloat16)
    sorted_ids = jnp.sum(jnp.where(places[:, None] == rank[None, :], ids[None, :], 0), 1)
    key_order = gather_sequence(sorted_ids, count)
    seq_of = jnp.sum((sorted_ids[:, None] >= ends[None, :]).astype(jnp.int32), 1)
    starts = jnp.concatenate([jnp.zeros((1,), jnp.int32), ends[:-1]])
    picked = seq_of[:, None] == jnp.arange(NSEQ, dtype=jnp.int32)[None, :]
    self_low = jnp.sum(jnp.where(picked, starts[None, :], 0), 1)
    self_high = sorted_ids
    cross_low = seq_of * ENC
    cross_high = cross_low + jnp.sum(jnp.where(picked, limits[None, :], 0), 1) - 1
    enc_rows = encoder.shape[1]
    micro = lax.axis_index("t") & 1
    enc_ids = []
    for place in range(count):
        index_s = place if count > 1 else 0
        for step in range(MEMBERS):
            core = lax.axis_index("core") ^ (step & 1)
            y_index = lax.axis_index("y") ^ (step >> 1)
            for part in range(2):
                t_index = 2 * core + (micro ^ part)
                row = ((t_index * count + index_s) * PAIR + y_index) * enc_rows
                enc_ids.append(row + jnp.arange(enc_rows, dtype=jnp.int32))
    enc_ids = jnp.concatenate(enc_ids)
    block = 256
    self_chunk, cross_chunk = 256, 384
    self_flags = needed_chunks(self_low, self_high, key_order, block, self_chunk)
    cross_flags = needed_chunks(cross_low, cross_high, enc_ids, block, cross_chunk)

    def sort_rows(matrix):
        return jnp.dot(sorter, matrix, preferred_element_type=jnp.float32).astype(jnp.bfloat16)

    def unsort_rows(matrix):
        return column_sum(sorter, matrix).astype(jnp.bfloat16)

    qkv = (
        linear(tokens_in, full_self_in) + jnp.concatenate([vec[6], zero_row, vec[7]])
    ).astype(jnp.bfloat16)
    own_heads = sort_rows(to_heads(qkv))
    if count > 1:
        pairs = gather_sequence(own_heads[:, WIDTH:], count)
        self_keys, self_values = (pairs, 0), (pairs, 1)
    else:
        self_keys, self_values = (own_heads, 1), (own_heads, 2)
    attended_heads, exact_self, log_self = attend_forward(
        (own_heads, 0), self_keys, self_values, self_low, self_high, key_order, self_flags,
        block, self_chunk,
    )
    attended = from_heads(unsort_rows(attended_heads), 1)

    enc_pairs = (
        linear(encoder_in, full_cross_pair) + jnp.concatenate([zero_row, vec[9]])
    ).astype(jnp.bfloat16)
    enc_heads = gather_sequence(to_heads(enc_pairs), count)

    resid_one = (
        residual_scale * tokens_in.astype(jnp.float32)
        + linear(attended, full_self_out)
        + self_bias_row
    )
    normed_one, unit_one, inverse_one = norm_forward(resid_one, vec[0], vec[3])
    normed_one_low = normed_one.astype(jnp.bfloat16)
    cross_queries = (linear(normed_one_low, full_cross_q) + vec[8]).astype(jnp.bfloat16)
    cross_heads = sort_rows(to_heads(cross_queries))
    crossed_heads, exact_cross, log_cross = attend_forward(
        (cross_heads, 0), (enc_heads, 0), (enc_heads, 1), cross_low, cross_high, enc_ids,
        cross_flags, block, cross_chunk,
    )
    crossed = from_heads(unsort_rows(crossed_heads), 1)
    resid_two = residual_scale * normed_one + linear(crossed, full_cross_out) + vec[10]
    normed_two, unit_two, inverse_two = norm_forward(resid_two, vec[1], vec[4])
    normed_two_low = normed_two.astype(jnp.bfloat16)
    pre_active = linear(normed_two_low, full_up) + bias_row
    hidden = jax.nn.gelu(pre_active, approximate=False).astype(jnp.bfloat16)
    resid_three = residual_scale * normed_two + linear(hidden, full_down) + vec[11]
    layer_value, unit_three, inverse_three = norm_forward(resid_three, vec[2], vec[5])
    layer_low = layer_value.astype(jnp.bfloat16)
    half = tokens_in.shape[0] // 2
    layer_out = from_packs(layer_low[:half], layer_low[half:])

    order_x = ("core", "x", "y", "t1", "t0", "s")
    order_y = ("core", "y", "x", "t1", "t0", "s")
    grad_three, gain_three, offset_three = norm_backward(
        grad_in.astype(jnp.float32), unit_three, inverse_three, vec[2]
    )
    grad_branch = grad_three.astype(jnp.bfloat16)
    grad_down = reduce_weight(column_sum(hidden, grad_branch), count, order_x)
    bias_down = jnp.sum(grad_branch.astype(jnp.float32), 0)
    grad_hidden = input_grad(grad_branch, full_down)
    grad_pre = (grad_hidden * gelu_slope(pre_active)).astype(jnp.bfloat16)
    grad_up = reduce_weight(column_sum(normed_two_low, grad_pre), count, order_y)
    bias_up = jnp.sum(grad_pre.astype(jnp.float32), 0)
    grad_two_in = residual_scale * grad_three + input_grad(grad_pre, full_up)
    grad_two, gain_two, offset_two = norm_backward(grad_two_in, unit_two, inverse_two, vec[1])
    grad_crossed_out = grad_two.astype(jnp.bfloat16)
    grad_cross_out = reduce_weight(column_sum(crossed, grad_crossed_out), count, order_x)
    bias_cross_out = jnp.sum(grad_crossed_out.astype(jnp.float32), 0)
    grad_crossed = input_grad(grad_crossed_out, full_cross_out).astype(jnp.bfloat16)
    grad_crossed_heads = sort_rows(to_heads(grad_crossed))
    dq_heads, dk_heads, dv_heads = attend_backward(
        (cross_heads, 0), (enc_heads, 0), (enc_heads, 1), grad_crossed_heads, log_rows(log_cross),
        delta_rows(grad_crossed_heads, exact_cross), cross_low, cross_high, enc_ids, cross_flags,
        block, cross_chunk,
    )
    grad_enc_heads = scatter_sequence(jnp.concatenate([dk_heads, dv_heads], 1), count)
    grad_enc_pairs = from_heads(grad_enc_heads, 2)
    grad_cross_queries = from_heads(unsort_rows(dq_heads), 1)
    grad_cross_q = reduce_weight(column_sum(normed_one_low, grad_cross_queries), count, order_y)
    bias_cross_q = jnp.sum(grad_cross_queries.astype(jnp.float32), 0)
    grad_cross_pair = reduce_weight(column_sum(encoder_in, grad_enc_pairs), count, order_x)
    bias_cross_value = jnp.sum(grad_enc_pairs[:, D:].astype(jnp.float32), 0)
    grad_enc = input_grad(grad_enc_pairs, full_cross_pair).astype(jnp.bfloat16)
    half_enc = encoder_in.shape[0] // 2
    grad_encoder = from_packs(grad_enc[:half_enc], grad_enc[half_enc:]).astype(jnp.float32)
    grad_one_in = residual_scale * grad_two + input_grad(grad_cross_queries, full_cross_q)
    grad_one, gain_one, offset_one = norm_backward(grad_one_in, unit_one, inverse_one, vec[0])
    grad_attended_out = grad_one.astype(jnp.bfloat16)
    grad_self_out = reduce_weight(column_sum(attended, grad_attended_out), count, order_y)
    bias_self_out = jnp.sum(grad_attended_out.astype(jnp.float32), 0)
    grad_attended = input_grad(grad_attended_out, full_self_out).astype(jnp.bfloat16)
    grad_attended_heads = sort_rows(to_heads(grad_attended))
    dq_heads, dk_heads, dv_heads = attend_backward(
        (own_heads, 0), self_keys, self_values, grad_attended_heads, log_rows(log_self),
        delta_rows(grad_attended_heads, exact_self), self_low, self_high, key_order, self_flags,
        block, self_chunk,
    )
    pair_heads = scatter_sequence(jnp.concatenate([dk_heads, dv_heads], 1), count)
    grad_qkv = from_heads(unsort_rows(jnp.concatenate([dq_heads, pair_heads], 1)), 3)
    grad_self_in = reduce_weight(column_sum(tokens_in, grad_qkv), count, order_x)
    bias_qkv = jnp.sum(grad_qkv.astype(jnp.float32), 0)
    grad_rows = (
        residual_scale * grad_one + input_grad(grad_qkv, full_self_in)
    ).astype(jnp.bfloat16)
    grad_tokens = from_packs(grad_rows[:half], grad_rows[half:]).astype(jnp.float32)

    blocks = T_SIZE * count * 8
    grad_vec = jnp.stack(
        [
            gain_one, gain_two, gain_three, offset_one, offset_two, offset_three, bias_qkv[:D],
            bias_qkv[2 * D :], bias_cross_q, bias_cross_value, bias_cross_out, bias_down,
        ],
        1,
    )
    small_grads = jnp.concatenate(
        [
            grad_vec.reshape(blocks, -1),
            bias_up.reshape(blocks, -1),
            bias_self_out.reshape(blocks, -1),
        ],
        1,
    )
    small_sum = reduce_blocks(small_grads, count, order_y)
    vec_end = 12 * D // blocks
    up_end = vec_end + 4 * D // blocks
    return (
        layer_out,
        grad_tokens,
        grad_encoder,
        grad_self_in,
        grad_self_out,
        grad_cross_q,
        grad_cross_pair,
        grad_cross_out,
        grad_up,
        grad_down,
        small_sum[:vec_end].reshape(D // blocks, 12),
        small_sum[vec_end:up_end],
        small_sum[up_end:],
    )


def solution(mesh):
    contexts = mesh.shape["ctx"]
    count = contexts // (T_SIZE * PAIR)
    fine = Mesh(
        mesh.devices.reshape(T_SIZE, count, PAIR, PAIR, PAIR), ("t", "s", "y", "x", "core")
    )
    fsdp, ctx = ("x", "core"), ("t", "s", "y")
    in_specs = (
        P(None, ROWS, None),
        P(None, ROWS, None),
        P(fsdp, None, None),
        P(fsdp, None, ctx),
        P(fsdp, None, None),
        P(None, ROWS, None),
        P(fsdp, None),
        P(fsdp, None),
        P(fsdp, None),
        P(fsdp, None),
        P(fsdp, None),
        P(fsdp, None),
        P(fsdp, None),
        P(fsdp, None),
        P(fsdp),
        P(fsdp),
    )
    out_specs = (P(None, ROWS, None),) * 3 + (P(BLOCKS, None),) * 8 + (P(BLOCKS),) * 2
    return jax.shard_map(
        functools.partial(on_device, count),
        mesh=fine,
        in_specs=in_specs,
        out_specs=out_specs,
        check_vma=False,
    )
```

time: 3670 us -> 848 us (0.23)
  waiting for transfers between devices: 2580 us -> 300 us
  local copies, waits for them, and re-layouts: 443 us -> 153 us
  matrix products: 309 us -> 104 us
  starting transfers between devices: 1.74 us -> 122 us
  loops' own time: 108 us -> 0 us
  Pallas kernels: 0 us -> 68.5 us
  blocking collectives: 76.6 us -> 13 us
  other arithmetic: 117 us -> 56.3 us
    reduce_scatter x9 -> x0, waiting for transfers between devices: 1740 us -> none  [the longest x2 807 us: on_device(): lax.psum_scatter(enc_pair_terms, 'ctx', scatter_dimension=0, tiled=True)]
    all_gather x11 -> x7, waiting for transfers between devices: 523 us -> 27.4 us  [fetch(): return lax.all_gather(weight, fsdp, axis=0, tiled=True)]
    unnamed x26 -> x7, waiting for transfers between devices: 317 us -> 3.65 us
    ppermute x0 -> x87, waiting for transfers between devices: none -> 269 us  [the longest x40 187 us: reduce_blocks(): arrived = lax.ppermute(send, axis, [(i, i ^ flip) for i in range(size)])]
    dot_general x224 -> x4, matrix products: 142 us -> 7.55 us  [sort_rows(): jnp.dot(sorter, matrix, preferred_element_type=jnp.float32)]
    dynamic_slice x288 -> x26, local copies, waits for them, and re-layouts: 209 us -> 78.1 us  [the longest x5 30.5 us: to_heads(): block = lax.dynamic_index_in_dim(split, me ^ step, 2, keepdims=False)]
    ppermute x0 -> x87, starting transfers between devices: none -> 122 us  [the longest x40 54 us: reduce_blocks(): arrived = lax.ppermute(send, axis, [(i, i ^ flip) for i in range(size)])]
    another operation x8 -> x0, loops' own time: 108 us -> none  [the longest x4 85.3 us: attend_backward(): lax.map(one_group, jnp.arange(queries.shape[1] // group_width, dtype=jnp....]
  transfers between devices with their start and end apart: 23 -> 94, of which waited for: 20 -> 43; matrix products, arithmetic and copies ran while one was open for 12% -> 33% of each run, Pallas kernels for 0% -> 8%
where the time goes in v1:
time: 848 us; the launch traced here: 834 us
  waiting for transfers between devices  300 us (35%)
  local copies, waits for them, and re-layouts  153 us (18%)
  starting transfers between devices  122 us (14%)
  matrix products  104 us (12%)
  Pallas kernels  68.5 us (8%)
  other arithmetic  56.3 us (7%)
  between operations  16.6 us (2%)
  blocking collectives  13 us (2%)
    ppermute x40, waiting for transfers between devices, reduce_blocks(): arrived = lax.ppermute(send, axis, [(i, i ^ flip) for i in range(size)])  187 us
    ppermute x40, starting transfers between devices, reduce_blocks(): arrived = lax.ppermute(send, axis, [(i, i ^ flip) for i in range(size)])  54 us
    dot_general x7, matrix products, linear(): return jnp.dot(inputs, weight, preferred_element_type=jnp.float32)  43.2 us
    ppermute x15, waiting for transfers between devices, from_heads(): lax.ppermute(block, GROUP, group_route(step))  42.3 us
    pallas_call x2, Pallas kernels, attend_forward(): pl.pallas_call(functools.partial(forward_kernel, chunk), grid_spec=pltpu....  36.1 us
    dot_general x11, matrix products, column_sum(): lax.dot_general(left, right, (((0,), (0,)), ((), ())), preferred_element_...  34.1 us
    pallas_call x2, Pallas kernels, attend_backward(): pl.pallas_call(functools.partial(backward_kernel, chunk), grid_spec=pltpu...  32.5 us
    dynamic_slice x5, local copies, waits for them, and re-layouts, to_heads(): block = lax.dynamic_index_in_dim(split, me ^ step, 2, keepdims=False)  30.5 us
  transfers between devices with their start and end apart: 94, of which 43 were waited for; matrix products, arithmetic and copies ran while one was open for 33% of the time, Pallas kernels for 8%

profile of v1, /device:TPU:0, one launch (start us, length us, event | category | flops | bytes accessed | tf_op | source)
XLA Modules:
  0.0 834.2 jit_solution(17437961533741404433)
XLA Ops:
  20.9 13.0 %all_gather.25 = bf16[17,1024]{1,0:T(8,128)(2,1)S(1)} all-gather(bf16[17,256]{1,0:T(8,128)(2,1)S(1)} %pad_maximum_fusion.13), channel_id=1, replica_groups=mesh['t'=4,'s'=1,'y'=2,'x'=2,'core'=2] {'x','core'}, dimensions={1}, use_global_device_ids=true | all-gather | bytes 43520 | tf_op jit(solution)/shard_map/all_gather | solution.py:468
  41.7 18.3 %collective-permute-start.4 = (s32[256]{0:T(256)S(1)}, s32[256]{0:T(256)S(1)}, u32[]{:S(2)}, u32[]{:S(2)}) collective-permute-start(s32[256]{0:T(256)S(1)} %pad_add_fusion.1), channel_id=1, source_target_pairs={{0,1},{1,0},{4,5},{5,4},{2,3},{3,2},{6,7},{7,6},{8,9},{9,8},{12,13... | collective-permute-start | bytes 3080 | tf_op jit(solution)/shard_map/ppermute | solution.py:111
  79.5 7.8 add_convert_fusion
  87.2 5.1 reshape.939
  92.3 23.0 %dynamic-slice_reduce_fusion = (bf16[768,2,256]{2,1,0:T(2,128)(2,1)}, bf16[768,2,256]{2,1,0:T(2,128)(2,1)}, bf16[768,2,256]{2,1,0:T(2,128)(2,1)}, bf16[768,2,256]{2,1,0:T(2,128)(2,1)}) fusion(bf16[768,2,4,256]{3,2,1,0:T(4,128)(2,1)S(1)} %reshape.939, s32[]{:T(128)S(6)} %select_n.247, s32[]{:T(128)S(6)} %select_n.246, s32[]{:T(128)S(6)} %select_n.245, ...), kind=kLoop, calls=%fused_computation.121 | loop fusion | bytes 6291472 | tf_op jit(solution)/shard_map/jit(dynamic_index_in_dim)/dynamic_slice | solution.py:122
  122.6 5.9 fusion.29
  128.5 3.3 reshape.927
  131.8 4.2 constant_dynamic-slice_fusion.45
  154.2 6.5 collective-permute-done.9
  160.7 4.4 fusion.45.q_ref.k_ref.v_ref
  165.1 13.6 %shard_map.255 = (bf16[1024,256]{1,0:T(8,128)(2,1)}, f32[1024,256]{1,0:T(8,128)}, f32[1024,128]{1,0:T(8,128)}) custom-call(s32[16]{0:T(128)} %reshape.961.flags_ref, bf16[1024,768]{1,0:T(8,128)(2,1)} %fusion.45.q_ref.k_ref.v_ref, bf16[1024,768]{1,0:T(8,128)(2,1)} %fusion.45.q_ref.k_ref.v_ref, bf16[1024,768]{1,0:T(8,128)(2,1)} %fusion.45.q_ref.k_ref.v_ref, ...), custom_call_target="tpu_custom_call" | custom-call | flops 1073741824 | bytes 4194304 | tf_op jit(solution)/shard_map/pallas_call | solution.py:252
  185.5 4.1 collective-permute-done.11
  201.1 4.3 collective-permute-done.14
  207.9 22.5 %shard_map.256 = (bf16[1024,256]{1,0:T(8,128)(2,1)}, f32[1024,256]{1,0:T(8,128)}, f32[1024,128]{1,0:T(8,128)}) custom-call(s32[32]{0:T(128)} %reshape.963.flags_ref, bf16[1024,256]{1,0:T(8,128)(2,1)} %fusion.66.q_ref, bf16[3072,512]{1,0:T(8,128)(2,1)} %constant_dynamic-update-slice_fusion.6.k_ref.v_ref, ...), custom_call_target="tpu_custom_call" | custom-call | flops 3221225472 | bytes 8388608 | tf_op jit(solution)/shard_map/pallas_call | solution.py:252
  236.0 4.1 collective-permute-done.22
  244.4 15.3 %fusion.6 = (bf16[256,4096]{1,0:T(8,128)(2,1)}, f32[256,4096]{1,0:T(8,128)}) fusion(f32[4096]{0:T(1024)S(1)} %copy-done.60, bf16[1024,4096]{1,0:T(8,128)(2,1)} %all-gather.18.cloned.1.call-done, f32[256,1024]{1,0:T(8,128)S(1)} %get-tuple-element.237, f32[1024]{0:T(1024)S(1)} %bitcast.581, f32[1024]{0:T(1024)S(1)} %bitcast.550, f32[256]{0:T(256)S(1)} %add_rsqrt_fusion.1, ...), kind=kOutput, calls=%fused_computation.17 | convolution fusion | flops 2218000384 | bytes 15755264 | tf_op jit(solution)/shard_map/dot_general | solution.py:67
  259.7 27.3 %all-gather.20.cloned.1.call-done = bf16[4096,1024]{1,0:T(8,128)(2,1)} async-done(((bf16[1024,1024]{1,0:T(8,128)(2,1)}), bf16[4096,1024]{1,0:T(8,128)(2,1)}) %all-gather.20.cloned.1.call-update) | async-done | bytes 8388624 | tf_op jit(solution)/shard_map/all_gather | solution.py:458
  287.0 6.5 fusion.175
  298.9 6.6 convolution_convert_fusion
  305.5 6.4 convert_reduce_fusion
  312.0 5.8 convolution_convert_fusion.1
  317.8 3.2 multiply_reduce_fusion
  328.5 8.6 %constant_dynamic-slice_fusion.9 = (bf16[2,2,1,2,2,1,128,1024]{7,6,5,4,3,1,0,2:T(8,128)(2,1)}, bf16[2,2,1,2,2,1,128,1024]{7,6,5,4,3,1,0,2:T(8,128)(2,1)}) fusion(bf16[2,2,1,2,2,2,128,1024]{7,6,5,4,3,1,0,2:T(8,128)(2,1)} %bitcast.508, s32[]{:T(128)S(6)} %select_n.256, s32[]{:T(128)S(6)} %select_n.257), kind=kLoop, calls=%fused_computation.350 | loop fusion | bytes 16777224 | tf_op jit(solution)/shard_map/jit(dynamic_index_in_dim)/dynamic_slice | solution.py:177
  337.1 4.8 copy.345
  341.9 3.9 constant_dynamic-slice_fusion.11
  345.8 4.9 copy.346
  353.8 4.1 collective-permute-start.24
  364.4 19.5 %shard_map.257 = (bf16[1024,256]{1,0:T(8,128)(2,1)}, bf16[3072,256]{1,0:T(8,128)(2,1)}, bf16[3072,256]{1,0:T(8,128)(2,1)}) custom-call(s32[32]{0:T(128)} %reshape.963.flags_ref, bf16[1024,256]{1,0:T(8,128)(2,1)} %fusion.66.q_ref, bf16[3072,512]{1,0:T(8,128)(2,1)} %constant_dynamic-update-slice_fusion.6.k_ref.v_ref, ...), custom_call_target="tpu_custom_call" | custom-call | flops 8053063680 | bytes 10485760 | tf_op jit(solution)/shard_map/pallas_call | solution.py:371
  391.3 3.1 collective-permute-done.32
  407.4 3.7 collective-permute-done.35
  419.2 12.9 %shard_map.258 = (bf16[1024,256]{1,0:T(8,128)(2,1)}, bf16[1024,256]{1,0:T(8,128)(2,1)}, bf16[1024,256]{1,0:T(8,128)(2,1)}) custom-call(s32[16]{0:T(128)} %reshape.961.flags_ref, bf16[1024,768]{1,0:T(8,128)(2,1)} %fusion.45.q_ref.k_ref.v_ref, bf16[1024,768]{1,0:T(8,128)(2,1)} %fusion.45.q_ref.k_ref.v_ref, bf16[1024,768]{1,0:T(8,128)(2,1)} %fusion.45.q_ref.k_ref.v_ref, ...), custom_call_target="tpu_custom_call" | custom-call | flops 2684354560 | bytes 5242880 | tf_op jit(solution)/shard_map/pallas_call | solution.py:371
  432.1 3.2 fusion.46
  450.7 5.9 collective-permute-done.39
  460.6 3.1 convolution_convert_fusion.2
  468.9 5.8 collective-permute-done.43
  474.6 14.9 %collective-permute-done.44 = bf16[768,512]{1,0:T(8,128)(2,1)S(1)} collective-permute-done((bf16[768,512]{1,0:T(8,128)(2,1)S(1)}, bf16[768,512]{1,0:T(8,128)(2,1)S(1)}, u32[]{:S(2)}, u32[]{:S(2)}) %collective-permute-start.44) | collective-permute-done | bytes 786464 | tf_op jit(solution)/shard_map/ppermute | solution.py:134
  514.2 3.5 convolution_convert_fusion.7
  517.7 8.9 %collective-permute-start.84 = (f32[2,2,1,544]{3,2,1,0:T(1,128)S(1)}, f32[2,2,1,544]{3,2,1,0:T(1,128)S(1)}, u32[]{:S(2)}, u32[]{:S(2)}) collective-permute-start(f32[2,2,1,544]{3,2,1,0:T(1,128)S(1)} %fusion.140), channel_id=1, source_target_pairs={{0,2},{2,0},{1,3},{3,1},{4,6},{6,4},{5,7},{7,5},{8,10},{10,8},{9,1... | collective-permute-start | bytes 26120 | tf_op jit(solution)/shard_map/ppermute | solution.py:179
  526.6 5.2 convolution_convert_fusion.3
  532.3 4.1 collective-permute-done.85
  540.1 3.6 collective-permute-start.40
  550.9 5.2 collective-permute-done.41
  564.0 7.8 collective-permute-done.68
  575.6 13.0 %collective-permute-done.46 = bf16[384,1024]{1,0:T(8,128)(2,1)S(1)} collective-permute-done((bf16[384,1024]{1,0:T(8,128)(2,1)S(1)}, bf16[384,1024]{1,0:T(8,128)(2,1)S(1)}, u32[]{:S(2)}, u32[]{:S(2)}) %collective-permute-start.46) | collective-permute-done | bytes 786464 | tf_op jit(solution)/shard_map/ppermute | solution.py:94
  591.8 3.6 collective-permute-done.69
  596.5 5.6 collective-permute-start.70
  602.4 4.3 collective-permute-done.53
  609.9 4.2 collective-permute-done.71
  616.6 7.5 collective-permute-done.54
  626.9 7.5 collective-permute-done.60
  634.5 5.8 collective-permute-done.55
  641.0 3.7 collective-permute-done.61
  652.3 20.6 %collective-permute-done.63 = bf16[2,2,1,2,32,2048]{5,4,1,0,3,2:T(8,128)(2,1)S(1)} collective-permute-done((bf16[2,2,1,2,32,2048]{5,4,1,0,3,2:T(8,128)(2,1)S(1)}, bf16[2,2,1,2,32,2048]{5,4,1,0,3,2:T(8,128)(2,1)S(1)}, u32[]{:S(2)}, u32[]{:S(2)}) %collective-permute-start.63) | collective-permute-done | bytes 1048608 | tf_op jit(solution)/shard_map/ppermute | solution.py:179
  675.2 4.3 fusion
  681.8 3.7 fusion.1
  690.4 6.6 collective-permute-done.65
  698.7 3.4 collective-permute-done.66
  702.8 3.8 collective-permute-done.48
  708.5 39.0 %collective-permute-done.78 = bf16[2,2,1,2,128,1024]{5,4,1,0,3,2:T(8,128)(2,1)S(1)} collective-permute-done((bf16[2,2,1,2,128,1024]{5,4,1,0,3,2:T(8,128)(2,1)S(1)}, bf16[2,2,1,2,128,1024]{5,4,1,0,3,2:T(8,128)(2,1)S(1)}, u32[]{:S(2)}, u32[]{:S(2)}) %collective-permute-start.78) | collective-permute-done | bytes 2097184 | tf_op jit(solution)/shard_map/ppermute | solution.py:179
  755.4 11.8 %collective-permute-done.50 = bf16[2,1,32,3072]{3,2,1,0:T(8,128)(2,1)S(1)} collective-permute-done((bf16[2,1,32,3072]{3,2,1,0:T(8,128)(2,1)S(1)}, bf16[2,1,32,3072]{3,2,1,0:T(8,128)(2,1)S(1)}, u32[]{:S(2)}, u32[]{:S(2)}) %collective-permute-start.50) | collective-permute-done | bytes 393248 | tf_op jit(solution)/shard_map/ppermute | solution.py:179
  776.2 27.8 %collective-permute-done.80 = bf16[2,1,128,1024]{3,2,1,0:T(8,128)(2,1)S(1)} collective-permute-done((bf16[2,1,128,1024]{3,2,1,0:T(8,128)(2,1)S(1)}, bf16[2,1,128,1024]{3,2,1,0:T(8,128)(2,1)S(1)}, u32[]{:S(2)}, u32[]{:S(2)}) %collective-permute-start.80) | collective-permute-done | bytes 524320 | tf_op jit(solution)/shard_map/ppermute | solution.py:179
  804.3 10.9 %collective-permute-done.75 = bf16[2,1,32,4096]{3,2,1,0:T(8,128)(2,1)S(1)} collective-permute-done((bf16[2,1,32,4096]{3,2,1,0:T(8,128)(2,1)S(1)}, bf16[2,1,32,4096]{3,2,1,0:T(8,128)(2,1)S(1)}, u32[]{:S(2)}, u32[]{:S(2)}) %collective-permute-start.75) | collective-permute-done | bytes 524320 | tf_op jit(solution)/shard_map/ppermute | solution.py:179
  816.3 4.6 collective-permute-done.81
  821.7 4.7 collective-permute-done.76
  (614 shorter events, 273.4 us)
Async XLA Ops:
  7.2 72.3 %all-gather.14.cloned.1.call-start = ((), (), s32[]{:S(2)}) async-start(), calls=%async_computation.3 | async-start | bytes 5242880 | tf_op jit(solution)/shard_map/all_gather | solution.py:458
  7.9 114.7 %all-gather.8.cloned.1.call-start = ((), (), s32[]{:S(2)}) async-start(), calls=%async_computation | async-start | bytes 7864320 | tf_op jit(solution)/shard_map/all_gather | solution.py:458
  8.7 182.0 %all-gather.10.cloned.1.call-start = ((), (), s32[]{:S(2)}) async-start(), calls=%async_computation.1 | async-start | bytes 2621440 | tf_op jit(solution)/shard_map/all_gather | solution.py:458
  9.4 184.2 %all-gather.12.cloned.1.call-start = ((), (), s32[]{:S(2)}) async-start(), calls=%async_computation.2 | async-start | bytes 2621440 | tf_op jit(solution)/shard_map/all_gather | solution.py:458
  10.0 231.3 %all-gather.16.cloned.1.call-start = ((), (), s32[]{:S(2)}) async-start(), calls=%async_computation.4 | async-start | bytes 2621440 | tf_op jit(solution)/shard_map/all_gather | solution.py:458
  10.6 233.7 %all-gather.18.cloned.1.call-start = ((), (), s32[]{:S(2)}) async-start(), calls=%async_computation.5 | async-start | bytes 10485760 | tf_op jit(solution)/shard_map/all_gather | solution.py:458
  11.2 275.8 %all-gather.20.cloned.1.call-start = ((), (), s32[]{:S(2)}) async-start(), calls=%async_computation.6 | async-start | bytes 10485760 | tf_op jit(solution)/shard_map/all_gather | solution.py:458
  12.3 65.2 %collective-permute-start.16 = (bf16[384,1024]{1,0:T(8,128)(2,1)}, bf16[384,1024]{1,0:T(8,128)(2,1)S(1)}, u32[]{:S(2)}, u32[]{:S(2)}) collective-permute-start(bf16[384,1024]{1,0:T(8,128)(2,1)} %get-tuple-element.160), channel_id=1, source_target_pairs={{0,0},{1,16},{8,8},{9,24},{16,1},{17,17},{24,9},{25,25},{2,2},{3,1... | collective-permute-start | bytes 2359304 | tf_op jit(solution)/shard_map/ppermute | solution.py:86
  14.1 64.4 %collective-permute-start.17 = (bf16[384,1024]{1,0:T(8,128)(2,1)S(1)}, bf16[384,1024]{1,0:T(8,128)(2,1)S(1)}, u32[]{:S(2)}, u32[]{:S(2)}) collective-permute-start(bf16[384,1024]{1,0:T(8,128)(2,1)S(1)} %get-tuple-element.159), channel_id=1, source_target_pairs={{0,8},{1,24},{8,0},{9,16},{16,9},{17,25},{24,1},{25,17},{2,10},{3,... | collective-permute-start | bytes 2359304 | tf_op jit(solution)/shard_map/ppermute | solution.py:87
  17.2 22.9 %collective-permute-start.2 = (s32[134]{0:T(256)S(1)}, s32[134]{0:T(256)S(1)}, u32[]{:S(2)}, u32[]{:S(2)}) collective-permute-start(s32[134]{0:T(256)S(1)} %bitcast.631), channel_id=1, source_target_pairs={{0,0},{1,16},{8,8},{9,24},{16,1},{17,17},{24,9},{25,25},{2,2},{3,1... | collective-permute-start | bytes 1616 | tf_op jit(solution)/shard_map/ppermute | solution.py:86
  17.8 23.8 %collective-permute-start.3 = (s32[134]{0:T(256)S(1)}, s32[134]{0:T(256)S(1)}, u32[]{:S(2)}, u32[]{:S(2)}) collective-permute-start(s32[134]{0:T(256)S(1)} %bitcast.630), channel_id=1, source_target_pairs={{0,8},{1,24},{8,0},{9,16},{16,9},{17,25},{24,1},{25,17},{2,10},{3,... | collective-permute-start | bytes 1616 | tf_op jit(solution)/shard_map/ppermute | solution.py:87
  18.8 56.4 %collective-permute-start = (bf16[128,1024]{1,0:T(8,128)(2,1)}, bf16[128,1024]{1,0:T(8,128)(2,1)S(1)}, u32[]{:S(2)}, u32[]{:S(2)}) collective-permute-start(bf16[128,1024]{1,0:T(8,128)(2,1)} %get-tuple-element.213), channel_id=1, source_target_pairs={{0,0},{1,16},{8,8},{9,24},{16,1},{17,17},{24,9},{25,25},{2,2},{3,1... | collective-permute-start | bytes 786440 | tf_op jit(solution)/shard_map/ppermute | solution.py:86
  40.1 35.8 %collective-permute-start.1 = (bf16[128,1024]{1,0:T(8,128)(2,1)S(1)}, bf16[128,1024]{1,0:T(8,128)(2,1)}, u32[]{:S(2)}, u32[]{:S(2)}) collective-permute-start(bf16[128,1024]{1,0:T(8,128)(2,1)S(1)} %copy-done.42), channel_id=1, source_target_pairs={{0,8},{1,24},{8,0},{9,16},{16,9},{17,25},{24,1},{25,17},{2,10},{3,... | collective-permute-start | bytes 786440 | tf_op jit(solution)/shard_map/ppermute | solution.py:87
  41.7 19.1 %collective-permute-start.4 = (s32[256]{0:T(256)S(1)}, s32[256]{0:T(256)S(1)}, u32[]{:S(2)}, u32[]{:S(2)}) collective-permute-start(s32[256]{0:T(256)S(1)} %pad_add_fusion.1), channel_id=1, source_target_pairs={{0,1},{1,0},{4,5},{5,4},{2,3},{3,2},{6,7},{7,6},{8,9},{9,8},{12,13... | collective-permute-start | bytes 3080 | tf_op jit(solution)/shard_map/ppermute | solution.py:111
  119.0 26.9 %collective-permute-start.18 = (bf16[768,512]{1,0:T(8,128)(2,1)}, bf16[768,512]{1,0:T(8,128)(2,1)}, u32[]{:S(2)}, u32[]{:S(2)}) collective-permute-start(bf16[768,512]{1,0:T(8,128)(2,1)} %bitcast.264), channel_id=1, source_target_pairs={{0,1},{1,0},{4,5},{5,4},{2,3},{3,2},{6,7},{7,6},{8,9},{9,8},{12,13... | collective-permute-start | bytes 2359304 | tf_op jit(solution)/shard_map/ppermute | solution.py:124
  120.3 28.3 %collective-permute-start.19 = (bf16[768,512]{1,0:T(8,128)(2,1)}, bf16[768,512]{1,0:T(8,128)(2,1)}, u32[]{:S(2)}, u32[]{:S(2)}) collective-permute-start(bf16[768,512]{1,0:T(8,128)(2,1)} %bitcast.266), channel_id=1, source_target_pairs={{0,4},{1,5},{4,0},{5,1},{2,6},{3,7},{6,2},{7,3},{8,12},{9,13},{12,... | collective-permute-start | bytes 2359304 | tf_op jit(solution)/shard_map/ppermute | solution.py:124
  138.1 14.3 %collective-permute-start.7 = (bf16[256,768]{0,1:T(8,128)(2,1)S(1)}, bf16[256,768]{0,1:T(8,128)(2,1)S(1)}, u32[]{:S(2)}, u32[]{:S(2)}) collective-permute-start(bf16[256,768]{0,1:T(8,128)(2,1)S(1)} %bitcast.547), channel_id=1, source_target_pairs={{0,1},{1,0},{4,5},{5,4},{2,3},{3,2},{6,7},{7,6},{8,9},{9,8},{12,13... | collective-permute-start | bytes 1179656 | tf_op jit(solution)/shard_map/ppermute | solution.py:124
  141.3 13.0 %collective-permute-start.8 = (bf16[256,768]{0,1:T(8,128)(2,1)}, bf16[256,768]{0,1:T(8,128)(2,1)}, u32[]{:S(2)}, u32[]{:S(2)}) collective-permute-start(bf16[256,768]{0,1:T(8,128)(2,1)} %bitcast.16), channel_id=1, source_target_pairs={{0,4},{1,5},{4,0},{5,1},{2,6},{3,7},{6,2},{7,3},{8,12},{9,13},{12,... | collective-permute-start | bytes 1179656 | tf_op jit(solution)/shard_map/ppermute | solution.py:124
  144.7 16.0 %collective-permute-start.9 = (bf16[256,768]{0,1:T(8,128)(2,1)}, bf16[256,768]{0,1:T(8,128)(2,1)}, u32[]{:S(2)}, u32[]{:S(2)}) collective-permute-start(bf16[256,768]{0,1:T(8,128)(2,1)} %bitcast.17), channel_id=1, source_target_pairs={{0,5},{1,4},{4,1},{5,0},{2,7},{3,6},{6,3},{7,2},{8,13},{9,12},{12,... | collective-permute-start | bytes 1179656 | tf_op jit(solution)/shard_map/ppermute | solution.py:124
  145.9 148.0 %collective-permute-start.26 = (bf16[128,1024]{1,0:T(8,128)(2,1)}, bf16[128,1024]{1,0:T(8,128)(2,1)S(1)}, u32[]{:S(2)}, u32[]{:S(2)}) collective-permute-start(bf16[128,1024]{1,0:T(8,128)(2,1)} %get-tuple-element.186), channel_id=1, source_target_pairs={{0,0},{1,16},{8,8},{9,24},{16,1},{17,17},{24,9},{25,25},{2,2},{3,1... | collective-permute-start | bytes 786440 | tf_op jit(solution)/shard_map/ppermute | solution.py:86
  148.7 145.2 %collective-permute-start.27 = (bf16[128,1024]{1,0:T(8,128)(2,1)}, bf16[128,1024]{1,0:T(8,128)(2,1)}, u32[]{:S(2)}, u32[]{:S(2)}) collective-permute-start(bf16[128,1024]{1,0:T(8,128)(2,1)} %get-tuple-element.187), channel_id=1, source_target_pairs={{0,8},{1,24},{8,0},{9,16},{16,9},{17,25},{24,1},{25,17},{2,10},{3,... | collective-permute-start | bytes 786440 | tf_op jit(solution)/shard_map/ppermute | solution.py:87
  153.2 30.2 %collective-permute-start.20 = (bf16[768,512]{1,0:T(8,128)(2,1)S(1)}, bf16[768,512]{1,0:T(8,128)(2,1)S(1)}, u32[]{:S(2)}, u32[]{:S(2)}) collective-permute-start(bf16[768,512]{1,0:T(8,128)(2,1)S(1)} %bitcast.546), channel_id=1, source_target_pairs={{0,5},{1,4},{4,1},{5,0},{2,7},{3,6},{6,3},{7,2},{8,13},{9,12},{12,... | collective-permute-start | bytes 2359304 | tf_op jit(solution)/shard_map/ppermute | solution.py:124
  326.4 33.0 %collective-permute-start.28 = (bf16[256,256]{1,0:T(8,128)(2,1)S(1)}, bf16[256,256]{1,0:T(8,128)(2,1)S(1)}, u32[]{:S(2)}, u32[]{:S(2)}) collective-permute-start(bf16[256,256]{1,0:T(8,128)(2,1)S(1)} %bitcast.555), channel_id=1, source_target_pairs={{0,1},{1,0},{4,5},{5,4},{2,3},{3,2},{6,7},{7,6},{8,9},{9,8},{12,13... | collective-permute-start | bytes 393224 | tf_op jit(solution)/shard_map/ppermute | solution.py:124
  326.7 32.7 %collective-permute-start.29 = (bf16[256,256]{1,0:T(8,128)(2,1)S(1)}, bf16[256,256]{1,0:T(8,128)(2,1)S(1)}, u32[]{:S(2)}, u32[]{:S(2)}) collective-permute-start(bf16[256,256]{1,0:T(8,128)(2,1)S(1)} %bitcast.556), channel_id=1, source_target_pairs={{0,4},{1,5},{4,0},{5,1},{2,6},{3,7},{6,2},{7,3},{8,12},{9,13},{12,... | collective-permute-start | bytes 393224 | tf_op jit(solution)/shard_map/ppermute | solution.py:124
  328.3 31.1 %collective-permute-start.30 = (bf16[256,256]{1,0:T(8,128)(2,1)S(1)}, bf16[256,256]{1,0:T(8,128)(2,1)S(1)}, u32[]{:S(2)}, u32[]{:S(2)}) collective-permute-start(bf16[256,256]{1,0:T(8,128)(2,1)S(1)} %bitcast.558), channel_id=1, source_target_pairs={{0,5},{1,4},{4,1},{5,0},{2,7},{3,6},{6,3},{7,2},{8,13},{9,12},{12,... | collective-permute-start | bytes 393224 | tf_op jit(solution)/shard_map/ppermute | solution.py:124
  353.8 91.0 %collective-permute-start.24 = (bf16[128,1024]{1,0:T(8,128)(2,1)}, bf16[128,1024]{1,0:T(8,128)(2,1)}, u32[]{:S(2)}, u32[]{:S(2)}) collective-permute-start(bf16[128,1024]{1,0:T(8,128)(2,1)} %get-tuple-element.190), channel_id=1, source_target_pairs={{0,0},{16,1},{8,8},{24,9},{1,16},{17,17},{9,24},{25,25},{2,2},{18,... | collective-permute-start | bytes 786440 | tf_op jit(solution)/shard_map/ppermute | solution.py:93
  357.9 87.7 %collective-permute-start.25 = (bf16[128,1024]{1,0:T(8,128)(2,1)}, bf16[128,1024]{1,0:T(8,128)(2,1)}, u32[]{:S(2)}, u32[]{:S(2)}) collective-permute-start(bf16[128,1024]{1,0:T(8,128)(2,1)} %get-tuple-element.191), channel_id=1, source_target_pairs={{8,0},{24,1},{0,8},{16,9},{9,16},{25,17},{1,24},{17,25},{10,2},{26... | collective-permute-start | bytes 786440 | tf_op jit(solution)/shard_map/ppermute | solution.py:94
  436.4 11.2 %collective-permute-start.37 = (bf16[256,768]{0,1:T(8,128)(2,1)}, bf16[256,768]{0,1:T(8,128)(2,1)}, u32[]{:S(2)}, u32[]{:S(2)}) collective-permute-start(bf16[256,768]{0,1:T(8,128)(2,1)} %get-tuple-element.158), channel_id=1, source_target_pairs={{0,1},{1,0},{4,5},{5,4},{2,3},{3,2},{6,7},{7,6},{8,9},{9,8},{12,13... | collective-permute-start | bytes 1179656 | tf_op jit(solution)/shard_map/ppermute | solution.py:134
  437.2 12.3 %collective-permute-start.38 = (bf16[256,768]{0,1:T(8,128)(2,1)}, bf16[256,768]{0,1:T(8,128)(2,1)}, u32[]{:S(2)}, u32[]{:S(2)}) collective-permute-start(bf16[256,768]{0,1:T(8,128)(2,1)} %get-tuple-element.157), channel_id=1, source_target_pairs={{0,4},{1,5},{4,0},{5,1},{2,6},{3,7},{6,2},{7,3},{8,12},{9,13},{12,... | collective-permute-start | bytes 1179656 | tf_op jit(solution)/shard_map/ppermute | solution.py:134
  438.4 18.2 %collective-permute-start.39 = (bf16[256,768]{0,1:T(8,128)(2,1)}, bf16[256,768]{0,1:T(8,128)(2,1)}, u32[]{:S(2)}, u32[]{:S(2)}) collective-permute-start(bf16[256,768]{0,1:T(8,128)(2,1)} %get-tuple-element.156), channel_id=1, source_target_pairs={{0,5},{1,4},{4,1},{5,0},{2,7},{3,6},{6,3},{7,2},{8,13},{9,12},{12,... | collective-permute-start | bytes 1179656 | tf_op jit(solution)/shard_map/ppermute | solution.py:134
  444.8 230.4 %collective-permute-start.77 = (bf16[2,2,1,2,2,128,1024]{6,5,1,0,3,4,2:T(8,128)(2,1)}, bf16[2,2,1,2,2,128,1024]{6,5,1,0,3,4,2:T(8,128)(2,1)}, u32[]{:S(2)}, u32[]{:S(2)}) collective-permute-start(bf16[2,2,1,2,2,128,1024]{6,5,1,0,3,4,2:T(8,128)(2,1)} %bitcast.489), channel_id=1, source_target_pairs={{0,1},{1,0},{2,3},{3,2},{4,5},{5,4},{6,7},{7,6},{8,9},{9,8},{10,11... | collective-permute-start | bytes 12582920 | tf_op jit(solution)/shard_map/ppermute | solution.py:179
  445.6 99.9 %collective-permute-start.67 = (bf16[2,2,1,2,2,32,1024]{6,5,1,0,3,4,2:T(8,128)(2,1)}, bf16[2,2,1,2,2,32,1024]{6,5,1,0,3,4,2:T(8,128)(2,1)}, u32[]{:S(2)}, u32[]{:S(2)}) collective-permute-start(bf16[2,2,1,2,2,32,1024]{6,5,1,0,3,4,2:T(8,128)(2,1)} %bitcast.493), channel_id=1, source_target_pairs={{0,1},{1,0},{2,3},{3,2},{4,5},{5,4},{6,7},{7,6},{8,9},{9,8},{10,11... | collective-permute-start | bytes 3145736 | tf_op jit(solution)/shard_map/ppermute | solution.py:179
  447.6 21.2 %collective-permute-start.42 = (bf16[768,512]{1,0:T(8,128)(2,1)S(1)}, bf16[768,512]{1,0:T(8,128)(2,1)S(1)}, u32[]{:S(2)}, u32[]{:S(2)}) collective-permute-start(bf16[768,512]{1,0:T(8,128)(2,1)S(1)} %copy-done.31), channel_id=1, source_target_pairs={{0,1},{1,0},{4,5},{5,4},{2,3},{3,2},{6,7},{7,6},{8,9},{9,8},{12,13... | collective-permute-start | bytes 2359304 | tf_op jit(solution)/shard_map/ppermute | solution.py:134
  449.5 25.2 %collective-permute-start.43 = (bf16[768,512]{1,0:T(8,128)(2,1)S(1)}, bf16[768,512]{1,0:T(8,128)(2,1)S(1)}, u32[]{:S(2)}, u32[]{:S(2)}) collective-permute-start(bf16[768,512]{1,0:T(8,128)(2,1)S(1)} %copy-done.30), channel_id=1, source_target_pairs={{0,4},{1,5},{4,0},{5,1},{2,6},{3,7},{6,2},{7,3},{8,12},{9,13},{12,... | collective-permute-start | bytes 2359304 | tf_op jit(solution)/shard_map/ppermute | solution.py:134
  456.6 33.0 %collective-permute-start.44 = (bf16[768,512]{1,0:T(8,128)(2,1)S(1)}, bf16[768,512]{1,0:T(8,128)(2,1)S(1)}, u32[]{:S(2)}, u32[]{:S(2)}) collective-permute-start(bf16[768,512]{1,0:T(8,128)(2,1)S(1)} %copy-done.29), channel_id=1, source_target_pairs={{0,5},{1,4},{4,1},{5,0},{2,7},{3,6},{6,3},{7,2},{8,13},{9,12},{12,... | collective-permute-start | bytes 2359304 | tf_op jit(solution)/shard_map/ppermute | solution.py:134
  468.8 90.4 %collective-permute-start.57 = (bf16[2,2,1,2,2,32,1024]{6,5,1,0,4,3,2:T(8,128)(2,1)}, bf16[2,2,1,2,2,32,1024]{6,5,1,0,4,3,2:T(8,128)(2,1)}, u32[]{:S(2)}, u32[]{:S(2)}) collective-permute-start(bf16[2,2,1,2,2,32,1024]{6,5,1,0,4,3,2:T(8,128)(2,1)} %bitcast.494), channel_id=1, source_target_pairs={{0,1},{1,0},{2,3},{3,2},{4,5},{5,4},{6,7},{7,6},{8,9},{9,8},{10,11... | collective-permute-start | bytes 3145736 | tf_op jit(solution)/shard_map/ppermute | solution.py:179
  474.6 87.5 %collective-permute-start.52 = (bf16[2,2,1,2,2,32,1024]{6,5,1,0,4,3,2:T(8,128)(2,1)}, bf16[2,2,1,2,2,32,1024]{6,5,1,0,4,3,2:T(8,128)(2,1)}, u32[]{:S(2)}, u32[]{:S(2)}) collective-permute-start(bf16[2,2,1,2,2,32,1024]{6,5,1,0,4,3,2:T(8,128)(2,1)} %bitcast.495), channel_id=1, source_target_pairs={{0,1},{1,0},{2,3},{3,2},{4,5},{5,4},{6,7},{7,6},{8,9},{9,8},{10,11... | collective-permute-start | bytes 3145736 | tf_op jit(solution)/shard_map/ppermute | solution.py:179
  517.7 14.1 %collective-permute-start.84 = (f32[2,2,1,544]{3,2,1,0:T(1,128)S(1)}, f32[2,2,1,544]{3,2,1,0:T(1,128)S(1)}, u32[]{:S(2)}, u32[]{:S(2)}) collective-permute-start(f32[2,2,1,544]{3,2,1,0:T(1,128)S(1)} %fusion.140), channel_id=1, source_target_pairs={{0,2},{2,0},{1,3},{3,1},{4,6},{6,4},{5,7},{7,5},{8,10},{10,8},{9,1... | collective-permute-start | bytes 26120 | tf_op jit(solution)/shard_map/ppermute | solution.py:179
  545.5 10.6 %collective-permute-start.41 = (bf16[128,1024]{1,0:T(8,128)(2,1)S(1)}, bf16[128,1024]{1,0:T(8,128)(2,1)S(1)}, u32[]{:S(2)}, u32[]{:S(2)}) collective-permute-start(bf16[128,1024]{1,0:T(8,128)(2,1)S(1)} %get-tuple-element.169), channel_id=1, source_target_pairs={{8,0},{24,1},{0,8},{16,9},{9,16},{25,17},{1,24},{17,25},{10,2},{26... | collective-permute-start | bytes 786440 | tf_op jit(solution)/shard_map/ppermute | solution.py:94
  548.6 100.2 %collective-permute-start.47 = (bf16[2,2,1,2,2,32,3072]{6,5,1,0,3,4,2:T(8,128)(2,1)S(1)}, bf16[2,2,1,2,2,32,3072]{6,5,1,0,3,4,2:T(8,128)(2,1)S(1)}, u32[]{:S(2)}, u32[]{:S(2)}) collective-permute-start(bf16[2,2,1,2,2,32,3072]{6,5,1,0,3,4,2:T(8,128)(2,1)S(1)} %bitcast.534), channel_id=1, source_target_pairs={{0,1},{1,0},{2,3},{3,2},{4,5},{5,4},{6,7},{7,6},{8,9},{9,8},{10,11... | collective-permute-start | bytes 9437192 | tf_op jit(solution)/shard_map/ppermute | solution.py:179
  556.1 18.3 %collective-permute-start.45 = (bf16[384,1024]{1,0:T(8,128)(2,1)S(1)}, bf16[384,1024]{1,0:T(8,128)(2,1)S(1)}, u32[]{:S(2)}, u32[]{:S(2)}) collective-permute-start(bf16[384,1024]{1,0:T(8,128)(2,1)S(1)} %copy-done.34), channel_id=1, source_target_pairs={{0,0},{16,1},{8,8},{24,9},{1,16},{17,17},{9,24},{25,25},{2,2},{18,... | collective-permute-start | bytes 2359304 | tf_op jit(solution)/shard_map/ppermute | solution.py:93
  559.3 12.5 %collective-permute-start.68 = (bf16[2,2,1,2,32,1024]{5,4,1,0,3,2:T(8,128)(2,1)S(1)}, bf16[2,2,1,2,32,1024]{5,4,1,0,3,2:T(8,128)(2,1)S(1)}, u32[]{:S(2)}, u32[]{:S(2)}) collective-permute-start(bf16[2,2,1,2,32,1024]{5,4,1,0,3,2:T(8,128)(2,1)S(1)} %dynamic-slice_bitcast_fusion.11), channel_id=1, source_target_pairs={{0,2},{2,0},{1,3},{3,1},{4,6},{6,4},{5,7},{7,5},{8,10},{10,8},{9,1... | collective-permute-start | bytes 1572872 | tf_op jit(solution)/shard_map/ppermute | solution.py:179
  562.1 26.5 %collective-permute-start.46 = (bf16[384,1024]{1,0:T(8,128)(2,1)S(1)}, bf16[384,1024]{1,0:T(8,128)(2,1)S(1)}, u32[]{:S(2)}, u32[]{:S(2)}) collective-permute-start(bf16[384,1024]{1,0:T(8,128)(2,1)S(1)} %copy-done.33), channel_id=1, source_target_pairs={{8,0},{24,1},{0,8},{16,9},{9,16},{25,17},{1,24},{17,25},{10,2},{26... | collective-permute-start | bytes 2359304 | tf_op jit(solution)/shard_map/ppermute | solution.py:94
  571.8 73.6 %collective-permute-start.62 = (bf16[2,2,1,2,2,32,2048]{6,5,1,0,3,4,2:T(8,128)(2,1)S(1)}, bf16[2,2,1,2,2,32,2048]{6,5,1,0,3,4,2:T(8,128)(2,1)S(1)}, u32[]{:S(2)}, u32[]{:S(2)}) collective-permute-start(bf16[2,2,1,2,2,32,2048]{6,5,1,0,3,4,2:T(8,128)(2,1)S(1)} %bitcast.538), channel_id=1, source_target_pairs={{0,1},{1,0},{2,3},{3,2},{4,5},{5,4},{6,7},{7,6},{8,9},{9,8},{10,11... | collective-permute-start | bytes 6291464 | tf_op jit(solution)/shard_map/ppermute | solution.py:179
  574.5 22.1 %collective-permute-start.58 = (bf16[2,2,1,2,32,1024]{5,4,1,0,3,2:T(8,128)(2,1)S(1)}, bf16[2,2,1,2,32,1024]{5,4,1,0,3,2:T(8,128)(2,1)S(1)}, u32[]{:S(2)}, u32[]{:S(2)}) collective-permute-start(bf16[2,2,1,2,32,1024]{5,4,1,0,3,2:T(8,128)(2,1)S(1)} %dynamic-slice_bitcast_fusion.13), channel_id=1, source_target_pairs={{0,4},{4,0},{1,5},{5,1},{2,6},{6,2},{3,7},{7,3},{8,12},{12,8},{9,1... | collective-permute-start | bytes 1572872 | tf_op jit(solution)/shard_map/ppermute | solution.py:179
  595.3 11.4 %collective-permute-start.53 = (bf16[2,2,1,2,32,1024]{5,4,1,0,3,2:T(8,128)(2,1)S(1)}, bf16[2,2,1,2,32,1024]{5,4,1,0,3,2:T(8,128)(2,1)S(1)}, u32[]{:S(2)}, u32[]{:S(2)}) collective-permute-start(bf16[2,2,1,2,32,1024]{5,4,1,0,3,2:T(8,128)(2,1)S(1)} %dynamic-slice_bitcast_fusion.14), channel_id=1, source_target_pairs={{0,4},{4,0},{1,5},{5,1},{2,6},{6,2},{3,7},{7,3},{8,12},{12,8},{9,1... | collective-permute-start | bytes 1572872 | tf_op jit(solution)/shard_map/ppermute | solution.py:179
  596.5 13.2 %collective-permute-start.70 = (bf16[2,1,32,1024]{3,2,1,0:T(8,128)(2,1)S(1)}, bf16[2,1,32,1024]{3,2,1,0:T(8,128)(2,1)S(1)}, u32[]{:S(2)}, u32[]{:S(2)}) collective-permute-start(bf16[2,1,32,1024]{3,2,1,0:T(8,128)(2,1)S(1)} %dynamic-slice_bitcast_fusion.27), channel_id=1, source_target_pairs={{0,16},{8,24},{16,0},{24,8},{1,17},{9,25},{17,1},{25,9},{2,18},{10... | collective-permute-start | bytes 393224 | tf_op jit(solution)/shard_map/ppermute | solution.py:179
  614.2 67.7 %collective-permute-start.72 = (bf16[2,2,1,2,2,32,4096]{6,5,1,0,4,3,2:T(8,128)(2,1)}, bf16[2,2,1,2,2,32,4096]{6,5,1,0,4,3,2:T(8,128)(2,1)}, u32[]{:S(2)}, u32[]{:S(2)}) collective-permute-start(bf16[2,2,1,2,2,32,4096]{6,5,1,0,4,3,2:T(8,128)(2,1)} %bitcast.490), channel_id=1, source_target_pairs={{0,1},{1,0},{2,3},{3,2},{4,5},{5,4},{6,7},{7,6},{8,9},{9,8},{10,11... | collective-permute-start | bytes 12582920 | tf_op jit(solution)/shard_map/ppermute | solution.py:179
  624.2 10.2 %collective-permute-start.60 = (bf16[2,1,32,1024]{3,2,1,0:T(8,128)(2,1)S(1)}, bf16[2,1,32,1024]{3,2,1,0:T(8,128)(2,1)S(1)}, u32[]{:S(2)}, u32[]{:S(2)}) collective-permute-start(bf16[2,1,32,1024]{3,2,1,0:T(8,128)(2,1)S(1)} %dynamic-slice_bitcast_fusion.29), channel_id=1, source_target_pairs={{0,16},{8,24},{16,0},{24,8},{1,17},{9,25},{17,1},{25,9},{2,18},{10... | collective-permute-start | bytes 393224 | tf_op jit(solution)/shard_map/ppermute | solution.py:179
  644.7 52.4 %collective-permute-start.56 = (bf16[1,32,1024]{2,1,0:T(8,128)(2,1)}, bf16[1,32,1024]{2,1,0:T(8,128)(2,1)}, u32[]{:S(2)}, u32[]{:S(2)}) collective-permute-start(bf16[1,32,1024]{2,1,0:T(8,128)(2,1)} %dynamic-slice_bitcast_fusion.45), channel_id=1, source_target_pairs={{0,8},{8,0},{16,24},{24,16},{1,9},{9,1},{17,25},{25,17},{2,10},{10... | collective-permute-start | bytes 196616 | tf_op jit(solution)/shard_map/ppermute | solution.py:179
  646.3 26.6 %collective-permute-start.63 = (bf16[2,2,1,2,32,2048]{5,4,1,0,3,2:T(8,128)(2,1)S(1)}, bf16[2,2,1,2,32,2048]{5,4,1,0,3,2:T(8,128)(2,1)S(1)}, u32[]{:S(2)}, u32[]{:S(2)}) collective-permute-start(bf16[2,2,1,2,32,2048]{5,4,1,0,3,2:T(8,128)(2,1)S(1)} %dynamic-slice_bitcast_fusion.5), channel_id=1, source_target_pairs={{0,2},{2,0},{1,3},{3,1},{4,6},{6,4},{5,7},{7,5},{8,10},{10,8},{9,1... | collective-permute-start | bytes 3145736 | tf_op jit(solution)/shard_map/ppermute | solution.py:179
  651.4 55.2 %collective-permute-start.48 = (bf16[2,2,1,2,32,3072]{5,4,1,0,3,2:T(8,128)(2,1)}, bf16[2,2,1,2,32,3072]{5,4,1,0,3,2:T(8,128)(2,1)S(1)}, u32[]{:S(2)}, u32[]{:S(2)}) collective-permute-start(bf16[2,2,1,2,32,3072]{5,4,1,0,3,2:T(8,128)(2,1)} %dynamic-slice_bitcast_fusion.2), channel_id=1, source_target_pairs={{0,2},{2,0},{1,3},{3,1},{4,6},{6,4},{5,7},{7,5},{8,10},{10,8},{9,1... | collective-permute-start | bytes 4718600 | tf_op jit(solution)/shard_map/ppermute | solution.py:179
  674.1 11.4 %collective-permute-start.64 = (bf16[2,2,1,32,2048]{4,3,1,2,0:T(8,128)(2,1)}, bf16[2,2,1,32,2048]{4,3,1,2,0:T(8,128)(2,1)}, u32[]{:S(2)}, u32[]{:S(2)}) collective-permute-start(bf16[2,2,1,32,2048]{4,3,1,2,0:T(8,128)(2,1)} %dynamic-slice_bitcast_fusion.12), channel_id=1, source_target_pairs={{0,4},{4,0},{1,5},{5,1},{2,6},{6,2},{3,7},{7,3},{8,12},{12,8},{9,1... | collective-permute-start | bytes 1572872 | tf_op jit(solution)/shard_map/ppermute | solution.py:179
  679.7 67.8 %collective-permute-start.78 = (bf16[2,2,1,2,128,1024]{5,4,1,0,3,2:T(8,128)(2,1)S(1)}, bf16[2,2,1,2,128,1024]{5,4,1,0,3,2:T(8,128)(2,1)S(1)}, u32[]{:S(2)}, u32[]{:S(2)}) collective-permute-start(bf16[2,2,1,2,128,1024]{5,4,1,0,3,2:T(8,128)(2,1)S(1)} %dynamic-slice_bitcast_fusion), channel_id=1, source_target_pairs={{0,2},{2,0},{1,3},{3,1},{4,6},{6,4},{5,7},{7,5},{8,10},{10,8},{9,1... | collective-permute-start | bytes 6291464 | tf_op jit(solution)/shard_map/ppermute | solution.py:179
  689.2 60.7 %collective-permute-start.73 = (bf16[2,2,1,2,32,4096]{5,4,1,0,3,2:T(8,128)(2,1)S(1)}, bf16[2,2,1,2,32,4096]{5,4,1,0,3,2:T(8,128)(2,1)S(1)}, u32[]{:S(2)}, u32[]{:S(2)}) collective-permute-start(bf16[2,2,1,2,32,4096]{5,4,1,0,3,2:T(8,128)(2,1)S(1)} %dynamic-slice_bitcast_fusion.1), channel_id=1, source_target_pairs={{0,4},{4,0},{1,5},{5,1},{2,6},{6,2},{3,7},{7,3},{8,12},{12,8},{9,1... | collective-permute-start | bytes 6291464 | tf_op jit(solution)/shard_map/ppermute | solution.py:179
  707.3 43.6 %collective-permute-start.49 = (bf16[2,2,1,32,3072]{4,3,1,2,0:T(8,128)(2,1)S(1)}, bf16[2,2,1,32,3072]{4,3,1,2,0:T(8,128)(2,1)S(1)}, u32[]{:S(2)}, u32[]{:S(2)}) collective-permute-start(bf16[2,2,1,32,3072]{4,3,1,2,0:T(8,128)(2,1)S(1)} %dynamic-slice_bitcast_fusion.6), channel_id=1, source_target_pairs={{0,4},{4,0},{1,5},{5,1},{2,6},{6,2},{3,7},{7,3},{8,12},{12,8},{9,1... | collective-permute-start | bytes 2359304 | tf_op jit(solution)/shard_map/ppermute | solution.py:179
  748.8 21.2 %collective-permute-start.79 = (bf16[2,2,1,128,1024]{4,3,1,2,0:T(8,128)(2,1)S(1)}, bf16[2,2,1,128,1024]{4,3,1,2,0:T(8,128)(2,1)S(1)}, u32[]{:S(2)}, u32[]{:S(2)}) collective-permute-start(bf16[2,2,1,128,1024]{4,3,1,2,0:T(8,128)(2,1)S(1)} %dynamic-slice_bitcast_fusion.3), channel_id=1, source_target_pairs={{0,4},{4,0},{1,5},{5,1},{2,6},{6,2},{3,7},{7,3},{8,12},{12,8},{9,1... | collective-permute-start | bytes 3145736 | tf_op jit(solution)/shard_map/ppermute | solution.py:179
  751.1 16.0 %collective-permute-start.50 = (bf16[2,1,32,3072]{3,2,1,0:T(8,128)(2,1)S(1)}, bf16[2,1,32,3072]{3,2,1,0:T(8,128)(2,1)S(1)}, u32[]{:S(2)}, u32[]{:S(2)}) collective-permute-start(bf16[2,1,32,3072]{3,2,1,0:T(8,128)(2,1)S(1)} %dynamic-slice_bitcast_fusion.15), channel_id=1, source_target_pairs={{0,16},{8,24},{16,0},{24,8},{1,17},{9,25},{17,1},{25,9},{2,18},{10... | collective-permute-start | bytes 1179656 | tf_op jit(solution)/shard_map/ppermute | solution.py:179
  753.6 21.3 %collective-permute-start.74 = (bf16[2,2,1,32,4096]{4,3,1,2,0:T(8,128)(2,1)S(1)}, bf16[2,2,1,32,4096]{4,3,1,2,0:T(8,128)(2,1)S(1)}, u32[]{:S(2)}, u32[]{:S(2)}) collective-permute-start(bf16[2,2,1,32,4096]{4,3,1,2,0:T(8,128)(2,1)S(1)} %dynamic-slice_bitcast_fusion.4), channel_id=1, source_target_pairs={{0,2},{2,0},{1,3},{3,1},{4,6},{6,4},{5,7},{7,5},{8,10},{10,8},{9,1... | collective-permute-start | bytes 3145736 | tf_op jit(solution)/shard_map/ppermute | solution.py:179
  770.4 33.5 %collective-permute-start.80 = (bf16[2,1,128,1024]{3,2,1,0:T(8,128)(2,1)S(1)}, bf16[2,1,128,1024]{3,2,1,0:T(8,128)(2,1)S(1)}, u32[]{:S(2)}, u32[]{:S(2)}) collective-permute-start(bf16[2,1,128,1024]{3,2,1,0:T(8,128)(2,1)S(1)} %dynamic-slice_bitcast_fusion.9), channel_id=1, source_target_pairs={{0,16},{8,24},{16,0},{24,8},{1,17},{9,25},{17,1},{25,9},{2,18},{10... | collective-permute-start | bytes 1572872 | tf_op jit(solution)/shard_map/ppermute | solution.py:179
  775.2 40.0 %collective-permute-start.75 = (bf16[2,1,32,4096]{3,2,1,0:T(8,128)(2,1)S(1)}, bf16[2,1,32,4096]{3,2,1,0:T(8,128)(2,1)S(1)}, u32[]{:S(2)}, u32[]{:S(2)}) collective-permute-start(bf16[2,1,32,4096]{3,2,1,0:T(8,128)(2,1)S(1)} %dynamic-slice_bitcast_fusion.10), channel_id=1, source_target_pairs={{0,16},{8,24},{16,0},{24,8},{1,17},{9,25},{17,1},{25,9},{2,18},{10... | collective-permute-start | bytes 1572872 | tf_op jit(solution)/shard_map/ppermute | solution.py:179
  775.6 39.9 %collective-permute-start.51 = (bf16[1,32,3072]{2,1,0:T(8,128)(2,1)S(1)}, bf16[1,32,3072]{2,1,0:T(8,128)(2,1)S(1)}, u32[]{:S(2)}, u32[]{:S(2)}) collective-permute-start(bf16[1,32,3072]{2,1,0:T(8,128)(2,1)S(1)} %dynamic-slice_bitcast_fusion.26), channel_id=1, source_target_pairs={{0,8},{8,0},{16,24},{24,16},{1,9},{9,1},{17,25},{25,17},{2,10},{10... | collective-permute-start | bytes 589832 | tf_op jit(solution)/shard_map/ppermute | solution.py:179
  804.2 16.6 %collective-permute-start.81 = (bf16[1,128,1024]{2,1,0:T(8,128)(2,1)S(1)}, bf16[1,128,1024]{2,1,0:T(8,128)(2,1)S(1)}, u32[]{:S(2)}, u32[]{:S(2)}) collective-permute-start(bf16[1,128,1024]{2,1,0:T(8,128)(2,1)S(1)} %dynamic-slice_bitcast_fusion.16), channel_id=1, source_target_pairs={{0,8},{8,0},{16,24},{24,16},{1,9},{9,1},{17,25},{25,17},{2,10},{10... | collective-permute-start | bytes 786440 | tf_op jit(solution)/shard_map/ppermute | solution.py:179
  815.4 11.0 %collective-permute-start.76 = (bf16[1,32,4096]{2,1,0:T(8,128)(2,1)S(1)}, bf16[1,32,4096]{2,1,0:T(8,128)(2,1)S(1)}, u32[]{:S(2)}, u32[]{:S(2)}) collective-permute-start(bf16[1,32,4096]{2,1,0:T(8,128)(2,1)S(1)} %dynamic-slice_bitcast_fusion.17), channel_id=1, source_target_pairs={{0,8},{8,0},{16,24},{24,16},{1,9},{9,1},{17,25},{25,17},{2,10},{10... | collective-permute-start | bytes 786440 | tf_op jit(solution)/shard_map/ppermute | solution.py:179
  (119 other events, 921.1 us)
Sparse Core Ops, SparseCore 0:
  9.6 37.4 all-gather.13
  48.7 46.3 all-gather.7
  96.6 22.6 all-gather.9
  120.7 22.6 all-gather.11
  144.7 22.5 all-gather.15
  168.8 58.3 all-gather.17
  228.7 58.2 all-gather.19

commit v2 on v1

v2 whole, which is shorter than its diff:
```python
import functools

import jax
import jax.numpy as jnp
from jax import lax
from jax.experimental import pallas as pl
from jax.experimental.pallas import tpu as pltpu
from jax.sharding import Mesh
from jax.sharding import PartitionSpec as P

D = 1024
HD = 64
ENC = 1024
NSEQ = 3
MICRO = 2
DEPTH = 6

EPSILON = 1e-05
MASKED = -1e30
SCALE = HD ** (-0.5)
T_SIZE = 4
PAIR = 2
GROUP = ("y", "core")
ROWS = ("x", "core", "t", "s", "y")
BLOCKS = ("t", "s", "y", "x", "core")
MEMBERS = 4
WIDTH = D // MEMBERS
HEADS = WIDTH // HD
VMEM_LIMIT = 56 * 1024 * 1024
RESIDUAL = (3.0 * DEPTH) ** 0.25
COST = pl.CostEstimate(flops=0, bytes_accessed=0, transcendentals=0)


def norm_forward(resid, gain, offset):
    average = jnp.mean(resid, -1, keepdims=True)
    centered = resid - average
    inverse = lax.rsqrt(jnp.mean(centered * centered, -1, keepdims=True) + EPSILON)
    normed = centered * inverse
    return (normed * gain + offset, normed, inverse)


def norm_backward(grad_out, normed, inverse, gain):
    grad_normed = grad_out * gain
    first_mean = jnp.mean(grad_normed, -1, keepdims=True)
    second_mean = jnp.mean(grad_normed * normed, -1, keepdims=True)
    grad_resid = inverse * (grad_normed - first_mean - normed * second_mean)
    return (grad_resid, jnp.sum(grad_out * normed, 0), jnp.sum(grad_out, 0))


def gelu_slope(values):
    cumulative = 0.5 * (1.0 + lax.erf(values * 0.7071067811865476))
    density = jnp.exp(-0.5 * values * values) * 0.3989422804014327
    return cumulative + values * density


def column_sum(left, right):
    return lax.dot_general(
        left, right, (((0,), (0,)), ((), ())), preferred_element_type=jnp.float32
    )


def input_grad(grad_rows, weight):
    return lax.dot_general(
        grad_rows, weight, (((1,), (1,)), ((), ())), preferred_element_type=jnp.float32
    )


def linear(inputs, weight):
    return jnp.dot(inputs, weight, preferred_element_type=jnp.float32)


def pack_routes():
    straight, crossed = [], []
    for t in range(T_SIZE):
        for core in range(PAIR):
            here = t * PAIR + core
            straight.append((here, (2 * core + (t & 1)) * PAIR + (t >> 1)))
            crossed.append((here, (2 * core + 1 - (t & 1)) * PAIR + (t >> 1)))
    return straight, crossed


def to_packs(parts):
    straight, crossed = pack_routes()
    parity = lax.axis_index("t") & 1
    first = lax.dynamic_index_in_dim(parts, parity, 0, keepdims=False)
    second = lax.dynamic_index_in_dim(parts, 1 - parity, 0, keepdims=False)
    return (
        lax.ppermute(first, ("t", "core"), straight),
        lax.ppermute(second, ("t", "core"), crossed),
    )


def from_packs(first, second):
    straight, crossed = pack_routes()
    first = lax.ppermute(first, ("t", "core"), [(to, source) for source, to in straight])
    second = lax.ppermute(second, ("t", "core"), [(to, source) for source, to in crossed])
    parity = lax.axis_index("t") & 1
    return jnp.stack(
        [jnp.where(parity == 0, first, second), jnp.where(parity == 0, second, first)], 0
    )


def group_route(step):
    return [(member, member ^ step) for member in range(MEMBERS)]


def group_index():
    return lax.axis_index("y") * PAIR + lax.axis_index("core")


def join_kernel(parts, me_ref, *refs):
    matrix_ref = refs[-1]
    for step, block_ref in enumerate(refs[:-1]):
        for part in range(parts):
            start = pl.multiple_of(part * D + (me_ref[0] ^ step) * WIDTH, WIDTH)
            matrix_ref[:, pl.ds(start, WIDTH)] = block_ref[:, part * WIDTH : (part + 1) * WIDTH]


def join_members_kernel(blocks_ref, matrix_ref):
    rows = matrix_ref.shape[0]
    for member in range(MEMBERS):
        for part in range(matrix_ref.shape[1] // D):
            start = part * D + member * WIDTH
            matrix_ref[:, start : start + WIDTH] = blocks_ref[
                member * rows : (member + 1) * rows, part * WIDTH : (part + 1) * WIDTH
            ]


def in_vmem(count):
    return [pl.BlockSpec(memory_space=pltpu.VMEM)] * count


def small_kernel(body, scalars, operands, outs, work=0):
    return pl.pallas_call(
        body,
        in_specs=[pl.BlockSpec(memory_space=pltpu.SMEM)] * len(scalars) + in_vmem(len(operands)),
        out_specs=in_vmem(len(outs)),
        out_shape=outs,
        compiler_params=pltpu.CompilerParams(vmem_limit_bytes=VMEM_LIMIT),
        cost_estimate=COST,
    )(*scalars, *operands)


def gelu(values):
    return 0.5 * values * (1.0 + lax.erf(values * 0.7071067811865476))


def fetch(weight):
    return lax.all_gather(weight, ("x", "core"), axis=0, tiled=True)


SWAP = [(0, 1), (1, 0)]


def stack_feed(up, down):
    return jnp.concatenate([down] + [up[:, part * D : (part + 1) * D] for part in range(4)], 0)


def up_specs(column):
    def block(i, p):
        place = column(i, p)
        return (MEMBERS + place // 2, place % 2)

    return [pl.BlockSpec((D // MEMBERS, FEED_TILE), block)] * MEMBERS


def shard_index():
    return (lax.axis_index("x") * PAIR + lax.axis_index("core"))[None]


def product(rows_ref, weight_ref, start=0, width=None):
    columns = slice(start, weight_ref.shape[1] if width is None else start + width)
    if len(rows_ref.shape) == 2:
        return linear(rows_ref[...], weight_ref[:, columns])
    total = None
    for member in range(MEMBERS):
        lines = slice(member * WIDTH, (member + 1) * WIDTH)
        term = linear(rows_ref[member], weight_ref[lines, columns])
        total = term if total is None else total + term
    return total


def back_product(grads_ref, weight_ref, lines=slice(None), offset=0):
    if len(grads_ref.shape) == 2:
        return input_grad(
            grads_ref[...], weight_ref[lines, offset : offset + grads_ref.shape[1]]
        )
    total = None
    for member in range(MEMBERS):
        columns = slice(offset + member * WIDTH, offset + (member + 1) * WIDTH)
        term = input_grad(grads_ref[member], weight_ref[lines, columns])
        total = term if total is None else total + term
    return total


def put_heads(rows_ref, weight_ref, bias_ref, out_ref, offset=0):
    count = out_ref.shape[0] // MEMBERS
    for member in range(MEMBERS):
        for part in range(out_ref.shape[1] // WIDTH):
            start = part * D + member * WIDTH
            value = product(rows_ref, weight_ref, offset + start, WIDTH)
            value = value + bias_ref[:, start : start + WIDTH]
            out_ref[
                member * count : (member + 1) * count, part * WIDTH : (part + 1) * WIDTH
            ] = value.astype(jnp.bfloat16)


def put_back_heads(grads_ref, weight_ref, out_ref):
    count = out_ref.shape[0] // MEMBERS
    for member in range(MEMBERS):
        value = back_product(grads_ref, weight_ref, slice(member * WIDTH, (member + 1) * WIDTH))
        out_ref[member * count : (member + 1) * count, :] = value.astype(jnp.bfloat16)


def heads_kernel(rows_ref, weight_ref, bias_ref, out_ref):
    put_heads(rows_ref, weight_ref, bias_ref, out_ref)


def project_heads(rows, weight, bias):
    shape = jax.ShapeDtypeStruct((rows.shape[0] * MEMBERS, weight.shape[1] // MEMBERS), jnp.bfloat16)
    work = 2 * rows.shape[0] * weight.size
    return small_kernel(heads_kernel, [], [rows, weight, bias[None, :]], [shape], work)[0]


def own_heads_kernel(me_ref, rows_ref, weight_ref, bias_ref, *outs):
    for step, out_ref in reversed(list(enumerate(outs))):
        for part in range(out_ref.shape[1] // WIDTH):
            start = pl.multiple_of(part * D + (me_ref[0] ^ step) * WIDTH, WIDTH)
            value = linear(rows_ref[...], weight_ref[:, pl.ds(start, WIDTH)])
            value = value + bias_ref[:, pl.ds(start, WIDTH)]
            out_ref[:, part * WIDTH : (part + 1) * WIDTH] = value.astype(jnp.bfloat16)


def project_blocks(rows, weight, bias):
    shape = jax.ShapeDtypeStruct((rows.shape[0], weight.shape[1] // MEMBERS), jnp.bfloat16)
    work = 2 * rows.shape[0] * weight.size
    return small_kernel(
        own_heads_kernel, [group_index()[None]], [rows, weight, bias[None, :]], [shape] * MEMBERS,
        work,
    )


def norm_kernel(
    rows_ref, weight_ref, bias_ref, base_ref, gain_ref, offset_ref, *refs
):
    outs = refs if len(refs) == 4 else refs[1:]
    resid = (
        RESIDUAL * base_ref[...].astype(jnp.float32)
        + product(rows_ref, weight_ref, 0, D)
        + bias_ref[...]
    )
    normed, unit, inverse = norm_forward(resid, gain_ref[...], offset_ref[...])
    outs[0][...] = normed
    outs[1][...] = normed.astype(jnp.bfloat16)
    outs[2][...] = unit
    outs[3][...] = inverse
    if len(refs) > 4:
        put_heads(outs[1], weight_ref, refs[0], outs[4], D)


def project_norm(rows, weight, bias, base, gain, offset, after=()):
    count = base.shape[0]
    outs = [
        jax.ShapeDtypeStruct((count, D), jnp.float32),
        jax.ShapeDtypeStruct((count, D), jnp.bfloat16),
        jax.ShapeDtypeStruct((count, D), jnp.float32),
        jax.ShapeDtypeStruct((count, 1), jnp.float32),
    ]
    if after:
        outs.append(jax.ShapeDtypeStruct((count * MEMBERS, WIDTH), jnp.bfloat16))
    return small_kernel(
        norm_kernel, [],
        [rows, weight, bias[None, :], base, gain[None, :], offset[None, :]]
        + [row[None, :] for row in after],
        outs,
    )


FEED_TILE = 512


def feed_column(step, me, tiles):
    return (me ^ (step // tiles)) * tiles + step % tiles


def up_kernel(me_ref, rows_ref, *refs):
    shards, (bias_ref, active_ref, hidden_ref) = refs[:MEMBERS], refs[MEMBERS:]
    depth = shards[0].shape[0]
    active = bias_ref[...]
    for index, shard in enumerate(shards):
        start = pl.multiple_of((me_ref[0] ^ index) * depth, depth)
        active = active + linear(rows_ref[:, pl.ds(start, depth)], shard[...])
    active_ref[...] = active
    hidden_ref[...] = gelu(active).astype(jnp.bfloat16)


def feed_up_gelu(rows, shards, bias):
    count, width = rows.shape[0], 4 * D
    column = lambda i, p: (0, i)
    return pl.pallas_call(
        up_kernel,
        grid_spec=pltpu.PrefetchScalarGridSpec(
            num_scalar_prefetch=1,
            grid=(width // FEED_TILE,),
            in_specs=[pl.BlockSpec((count, D), lambda i, p: (0, 0))]
            + up_specs(lambda i, p: i)
            + [pl.BlockSpec((1, FEED_TILE), column)],
            out_specs=[pl.BlockSpec((count, FEED_TILE), column)] * 2,
        ),
        out_shape=[
            jax.ShapeDtypeStruct((count, width), jnp.float32),
            jax.ShapeDtypeStruct((count, width), jnp.bfloat16),
        ],
        compiler_params=pltpu.CompilerParams(vmem_limit_bytes=VMEM_LIMIT),
        cost_estimate=COST,
    )(shard_index(), rows, *shards, bias[None, :])


def put_norm_back(grads, unit, inverse, gain, resid_ref, low_ref, sums_ref):
    resid, gain_sum, offset_sum = norm_backward(grads, unit, inverse, gain)
    low = resid.astype(jnp.bfloat16)
    resid_ref[...] = resid
    low_ref[...] = low
    sums_ref[0:1, :] = gain_sum[None, :]
    sums_ref[1:2, :] = offset_sum[None, :]
    sums_ref[2:3, :] = jnp.sum(low.astype(jnp.float32), 0)[None, :]
    sums_ref[3:8, :] = jnp.zeros((5, D), jnp.float32)


def down_kernel(tiles, me_ref, hidden_ref, *refs):
    shards = refs[:MEMBERS]
    bias_ref, base_ref, gain_ref, offset_ref, grads_ref = refs[MEMBERS : MEMBERS + 5]
    layer_ref, resid_ref, low_ref, sums_ref, total_ref = refs[MEMBERS + 5 :]
    step = pl.program_id(0)

    @pl.when(step == 0)
    def _():
        total_ref[...] = RESIDUAL * base_ref[...] + bias_ref[...]

    for index, shard in enumerate(shards):

        @pl.when(step // tiles == index)
        def _(shard=shard):
            total_ref[...] += linear(hidden_ref[...], shard[...])

    @pl.when(step == pl.num_programs(0) - 1)
    def _():
        layer, unit, inverse = norm_forward(total_ref[...], gain_ref[...], offset_ref[...])
        layer_ref[...] = layer.astype(jnp.bfloat16)
        put_norm_back(
            grads_ref[...].astype(jnp.float32), unit, inverse, gain_ref[...], resid_ref, low_ref,
            sums_ref,
        )


def one_block(array):
    return pl.BlockSpec(array.shape, lambda i, p: (0,) * len(array.shape))


def down_specs(tiles):
    return [
        pl.BlockSpec((FEED_TILE, D), lambda i, p, s=s: (jnp.clip(i - s * tiles, 0, tiles - 1), 0))
        for s in range(MEMBERS)
    ]


def feed_down_norm(hidden, shards, bias, base, gain, offset, grads):
    count = base.shape[0]
    tiles = D // FEED_TILE
    fixed = [bias[None, :], base, gain[None, :], offset[None, :], grads]
    outs = [
        jax.ShapeDtypeStruct((count, D), jnp.bfloat16),
        jax.ShapeDtypeStruct((count, D), jnp.float32),
        jax.ShapeDtypeStruct((count, D), jnp.bfloat16),
        jax.ShapeDtypeStruct((8, D), jnp.float32),
    ]
    return pl.pallas_call(
        functools.partial(down_kernel, tiles),
        grid_spec=pltpu.PrefetchScalarGridSpec(
            num_scalar_prefetch=1,
            grid=(MEMBERS * tiles,),
            in_specs=[
                pl.BlockSpec((count, FEED_TILE), lambda i, p: (0, feed_column(i, p[0], tiles)))
            ]
            + down_specs(tiles)
            + [one_block(array) for array in fixed],
            out_specs=[one_block(out) for out in outs],
            scratch_shapes=[pltpu.VMEM((count, D), jnp.float32)],
        ),
        out_shape=outs,
        compiler_params=pltpu.CompilerParams(vmem_limit_bytes=VMEM_LIMIT),
        cost_estimate=COST,
    )(shard_index(), hidden, *shards, *fixed)


def feed_back_kernel(tiles, me_ref, active_ref, *refs):
    downs, ups, refs = refs[:MEMBERS], refs[MEMBERS : 2 * MEMBERS], refs[2 * MEMBERS :]
    grads_ref, resid_ref, unit_ref, inverse_ref, gain_ref, out_ref = refs[:6]
    du_ref, bias_ref, next_resid_ref, next_low_ref, sums_ref, heads_ref, total_ref = refs[6:]
    step = pl.program_id(0)
    depth = ups[0].shape[0]

    @pl.when(step == 0)
    def _():
        total_ref[...] = RESIDUAL * resid_ref[...]

    slope = gelu_slope(active_ref[...])
    for index, shard in enumerate(downs):

        @pl.when(step // tiles == index)
        def _(shard=shard):
            du_ref[...] = (back_product(grads_ref, shard) * slope).astype(jnp.bfloat16)

    du = du_ref[...]
    bias_ref[...] = jnp.sum(du.astype(jnp.float32), 0, keepdims=True)
    for index, shard in enumerate(ups):
        start = pl.multiple_of((me_ref[0] ^ index) * depth, depth)
        total_ref[:, pl.ds(start, depth)] += input_grad(du, shard[...])

    @pl.when(step == pl.num_programs(0) - 1)
    def _():
        put_norm_back(
            total_ref[...], unit_ref[...], inverse_ref[...], gain_ref[...], next_resid_ref,
            next_low_ref, sums_ref,
        )
        put_back_heads(next_low_ref, out_ref, heads_ref)


def feed_back(active, shards, grads, resid, unit, inverse, gain, out_weight):
    count, width = active.shape
    tiles = D // FEED_TILE
    fixed = [grads, resid, unit, inverse, gain[None, :], out_weight]
    column = lambda i, p: (0, feed_column(i, p[0], tiles))
    outs = [
        jax.ShapeDtypeStruct((count, width), jnp.bfloat16),
        jax.ShapeDtypeStruct((1, width), jnp.float32),
        jax.ShapeDtypeStruct((count, D), jnp.float32),
        jax.ShapeDtypeStruct((count, D), jnp.bfloat16),
        jax.ShapeDtypeStruct((8, D), jnp.float32),
        jax.ShapeDtypeStruct((count * MEMBERS, WIDTH), jnp.bfloat16),
    ]
    return pl.pallas_call(
        functools.partial(feed_back_kernel, tiles),
        grid_spec=pltpu.PrefetchScalarGridSpec(
            num_scalar_prefetch=1,
            grid=(MEMBERS * tiles,),
            in_specs=[pl.BlockSpec((count, FEED_TILE), column)]
            + down_specs(tiles)
            + up_specs(lambda i, p: feed_column(i, p[0], tiles))
            + [one_block(array) for array in fixed],
            out_specs=[
                pl.BlockSpec((count, FEED_TILE), column), pl.BlockSpec((1, FEED_TILE), column)
            ]
            + [one_block(out) for out in outs[2:]],
            scratch_shapes=[pltpu.VMEM((count, D), jnp.float32)],
        ),
        out_shape=outs,
        compiler_params=pltpu.CompilerParams(vmem_limit_bytes=VMEM_LIMIT),
        cost_estimate=COST,
    )(shard_index(), active, *shards, *shards, *fixed)


def norm_back_kernel(
    grads_ref, weight_ref, resid_ref, unit_ref, inverse_ref, gain_ref,
    next_resid_ref, next_low_ref, sums_ref, heads_ref,
):
    total = RESIDUAL * resid_ref[...] + back_product(grads_ref, weight_ref, offset=D)
    put_norm_back(
        total, unit_ref[...], inverse_ref[...], gain_ref[...], next_resid_ref, next_low_ref, sums_ref
    )
    put_back_heads(next_low_ref, weight_ref, heads_ref)


def back_norm(grads, weight, resid, unit, inverse, gain):
    count = resid.shape[0]
    outs = [
        jax.ShapeDtypeStruct((count, D), jnp.float32),
        jax.ShapeDtypeStruct((count, D), jnp.bfloat16),
        jax.ShapeDtypeStruct((8, D), jnp.float32),
        jax.ShapeDtypeStruct((count * MEMBERS, WIDTH), jnp.bfloat16),
    ]
    return small_kernel(
        norm_back_kernel, [], [grads, weight, resid, unit, inverse, gain[None, :]], outs
    )


def back_kernel(grads_ref, weight_ref, out_ref):
    out_ref[...] = back_product(grads_ref, weight_ref).astype(out_ref.dtype)


def back_project(grads, weight, dtype=jnp.bfloat16):
    count, width = grads.shape
    rows = 256
    return pl.pallas_call(
        back_kernel,
        grid=(weight.shape[0] // rows,),
        in_specs=[
            pl.BlockSpec((count, width), lambda i: (0, 0)),
            pl.BlockSpec((rows, width), lambda i: (i, 0)),
        ],
        out_specs=pl.BlockSpec((count, rows), lambda i: (0, i)),
        out_shape=jax.ShapeDtypeStruct((count, weight.shape[0]), dtype),
        compiler_params=pltpu.CompilerParams(vmem_limit_bytes=VMEM_LIMIT),
        cost_estimate=COST,
    )(grads, weight)


def to_members(blocks):
    return lax.all_to_all(blocks, GROUP, 0, 0, tiled=True)


def by_member(blocks):
    return blocks.reshape(MEMBERS, blocks.shape[0] // MEMBERS, blocks.shape[1])


def as_columns(blocks):
    shape = (blocks.shape[0] // MEMBERS, blocks.shape[1] * MEMBERS)
    return small_kernel(
        join_members_kernel, [], [blocks], [jax.ShapeDtypeStruct(shape, blocks.dtype)]
    )[0]


def chain(first, second):
    return lax.optimization_barrier((first, second))


def exchange(blocks):
    return [
        block if step == 0 else lax.ppermute(block, GROUP, group_route(step))
        for step, block in enumerate(blocks)
    ]


def during(blocks, work, inputs):
    own, inputs = chain(blocks[0], inputs)
    results, received = chain(work(*inputs), exchange(blocks)[1:])
    return [own, *received], results


def during_members(blocks, work, inputs):
    blocks, inputs = chain(blocks, inputs)
    results, received = chain(work(*inputs), to_members(blocks))
    return received, results


def join_heads(blocks, me):
    rows, parts = blocks[0].shape[0], blocks[0].shape[1] // WIDTH
    shape = jax.ShapeDtypeStruct((rows, parts * D), blocks[0].dtype)
    return small_kernel(
        functools.partial(join_kernel, parts), [me], blocks, [shape]
    )[0]


def cut(matrix):
    rows = matrix.shape[0] // MEMBERS
    return [matrix[step * rows : (step + 1) * rows] for step in range(MEMBERS)]


def sort_kernel(rank_ref, blocks_ref, sorted_ref):
    rows = blocks_ref.shape[0] // MEMBERS
    for place in range(MEMBERS):
        wanted = lax.broadcasted_iota(jnp.int32, (rows, rows * MEMBERS), 0) + place * rows
        pick = (rank_ref[...] == wanted).astype(jnp.bfloat16)
        sorted_ref[place * rows : (place + 1) * rows, :] = linear(pick, blocks_ref[...]).astype(
            jnp.bfloat16
        )


def put_unsorted(ranks, parts, block_ref, lines):
    rows = ranks.shape[0]
    wanted = lax.broadcasted_iota(jnp.int32, (rows, rows * MEMBERS), 1)
    pick = (ranks == wanted).astype(jnp.bfloat16)
    start = 0
    for sorted_ref in parts:
        end = start + sorted_ref.shape[1]
        block_ref[lines, start:end] = linear(pick, sorted_ref[...]).astype(jnp.bfloat16)
        start = end


def unsort_kernel(rank_ref, *refs):
    blocks_ref = refs[-1]
    rows = blocks_ref.shape[0] // MEMBERS
    for member in range(MEMBERS):
        lines = slice(member * rows, (member + 1) * rows)
        put_unsorted(rank_ref[lines, :], refs[:-1], blocks_ref, lines)


def sort_rows(blocks, rank):
    shape = jax.ShapeDtypeStruct(blocks.shape, jnp.bfloat16)
    work = 2 * blocks.size * blocks.shape[0]
    return small_kernel(sort_kernel, [], [rank[None, :], blocks], [shape], work)[0]


def unsort_rows(parts, rank):
    width = sum(part.shape[1] for part in parts)
    shape = jax.ShapeDtypeStruct((parts[0].shape[0], width), jnp.bfloat16)
    work = 2 * shape.size * shape.shape[0]
    return small_kernel(unsort_kernel, [], [rank[:, None], *parts], [shape], work)[0]


def gather_sequence(matrix, count):
    if count == 1:
        return matrix
    return lax.all_gather(matrix, "s", axis=0, tiled=True)


def scatter_sequence(matrix, count):
    if count == 1:
        return matrix
    return lax.psum_scatter(matrix, "s", scatter_dimension=0, tiled=True)


def own_bits():
    t_index = lax.axis_index("t")
    return {
        "t1": t_index >> 1,
        "t0": t_index & 1,
        "y": lax.axis_index("y"),
        "x": lax.axis_index("x"),
        "core": lax.axis_index("core"),
    }


def flip(block, name):
    if name in ("t1", "t0"):
        step = 2 if name == "t1" else 1
        return lax.ppermute(block, "t", [(i, i ^ step) for i in range(T_SIZE)])
    return lax.ppermute(block, name, [(i, i ^ 1) for i in range(PAIR)])


def relative_index(total, count, order):
    rows = total // (32 * count)
    place = jnp.arange(total, dtype=jnp.int32)
    bits, mine = {"r": place % rows, "s": place // rows % count}, own_bits()
    for index, name in enumerate(order):
        bits[name] = (place // (rows * count) >> (len(order) - 1 - index) & 1) ^ mine[name]
    row = (bits["t1"] * PAIR + bits["t0"]) * count + bits["s"]
    for name in ("y", "x", "core"):
        row = row * PAIR + bits[name]
    return row * rows + bits["r"]


def relative_columns(matrix, count, order):
    index = relative_index(matrix.shape[1], count, order)
    pick = jnp.arange(matrix.shape[1], dtype=jnp.int32)[:, None] == index[None, :]
    return linear(matrix, pick.astype(jnp.bfloat16)).astype(jnp.bfloat16)


def put_grads(pairs, outs):
    half, start = outs[0].shape[0], 0
    for left_ref, right in pairs:
        end = start + right.shape[1]
        for out_ref, lines in zip(outs, (slice(half, 2 * half), slice(0, half))):
            value = column_sum(left_ref[:, lines], right)
            out_ref[:, start:end] = value.astype(jnp.bfloat16)
        start = end
    return start


def grads_kernel(count, *refs):
    put_grads([(refs[i], refs[count + i][...]) for i in range(count)], refs[-2:])


def weight_grads(lefts, rights):
    half = lefts[0].shape[1] // 2
    shape = jax.ShapeDtypeStruct((half, sum(right.shape[1] for right in rights)), jnp.bfloat16)
    return small_kernel(
        functools.partial(grads_kernel, len(lefts)), [], [*lefts, *rights], [shape] * 2
    )


def self_in_kernel(
    left_ref, right_ref, grads_ref, pick_ref, one_ref, two_ref, three_ref, up_ref, query_ref,
    pair_ref, left_sent, left_kept, right_sent, right_kept, small_ref,
):
    middle = grads_ref.shape[1] // 2
    put_grads([(left_ref, grads_ref[:, :middle])], [left_sent, left_kept])
    start = put_grads([(right_ref, grads_ref[:, middle:])], [right_sent, right_kept])

    def total(rows):
        return jnp.sum(rows.astype(jnp.float32), 0, keepdims=True)

    small_ref[...] = jnp.zeros_like(small_ref)
    rows = [one_ref[0:1, :], two_ref[0:1, :], three_ref[0:1, :]]
    rows += [one_ref[1:2, :], two_ref[1:2, :], three_ref[1:2, :]]
    rows += [total(grads_ref[:, :D]), total(grads_ref[:, 2 * D :]), total(query_ref[...])]
    rows += [total(pair_ref[:, D:]), two_ref[2:3, :], three_ref[2:3, :], one_ref[2:3, :]]
    for place, row in enumerate(rows):
        small_ref[place : place + 1, :] = row
    small_ref[13:17, :] = up_ref[...]
    half = right_sent.shape[0]
    low = small_ref[...].astype(jnp.bfloat16)
    for out_ref, lines in ((right_sent, slice(half, 2 * half)), (right_kept, slice(0, half))):
        out_ref[:, start:] = input_grad(pick_ref[lines, :], low).astype(jnp.bfloat16)


def self_in_grads(left, right, grads, pick, one, two, three, up, query, pair):
    half, middle = D // 2, grads.shape[1] // 2
    outs = [jax.ShapeDtypeStruct((half, middle), jnp.bfloat16)] * 2
    outs += [jax.ShapeDtypeStruct((half, middle + 128), jnp.bfloat16)] * 2
    operands = [left, right, grads, pick, one, two, three, up.reshape(D, 4).T, query, pair]
    results = pl.pallas_call(
        self_in_kernel,
        in_specs=in_vmem(len(operands)),
        out_specs=in_vmem(len(outs)),
        out_shape=outs,
        scratch_shapes=[pltpu.VMEM((128, D), jnp.float32)],
        compiler_params=pltpu.CompilerParams(vmem_limit_bytes=VMEM_LIMIT),
        cost_estimate=COST,
    )(*operands)
    return results[:2], results[2:]


class Halving:
    def __init__(self, parts, count, order):
        sent, self.value = parts
        self.count, self.order = count, list(order)
        self.send(sent)

    def send(self, block):
        self.sent = block.astype(jnp.bfloat16)
        self.pending = flip(self.sent, self.order.pop(0))

    def step(self):
        total = self.value.astype(jnp.float32) + self.pending.astype(jnp.float32)
        half = total.shape[0] // 2
        self.value = total[:half]
        self.send(total[half:])

    def finish(self):
        total = self.value + self.pending.astype(jnp.float32)
        if self.count > 1:
            total = lax.psum_scatter(
                total.astype(jnp.bfloat16), "s", scatter_dimension=0, tiled=True
            ).astype(jnp.float32)
        return total


def feed_grads_kernel(hidden_ref, grads_ref, rows_ref, active_grads_ref, out_ref):
    others, _, _, rows, _ = out_ref.shape

    @pl.when(pl.program_id(0) == 0)
    def _():
        value = column_sum(hidden_ref[...], grads_ref[...]).astype(jnp.bfloat16)
        value = value.reshape(PAIR, others, 4, rows, D)
        for y_index in range(PAIR):
            out_ref[:, y_index] = value[y_index]

    @pl.when(pl.program_id(0) == 1)
    def _():
        for part in range(4):
            value = column_sum(rows_ref[...], active_grads_ref[:, part * D : (part + 1) * D])
            value = value.astype(jnp.bfloat16).reshape(PAIR, others, rows, D)
            for y_index in range(PAIR):
                out_ref[:, y_index, part] = value[y_index]


def feed_grads(hidden, grads, rows, active_grads, count):
    blocks = 32 * count
    lines = D // blocks
    size = rows.shape[0]
    if count > 1:
        parts = [column_sum(hidden, grads).astype(jnp.bfloat16).reshape(-1, PAIR, 4, 4, lines, D)]
        for part in range(4):
            up = column_sum(rows, active_grads[:, part * D : (part + 1) * D])
            parts.append(up.astype(jnp.bfloat16).reshape(-1, PAIR, 4, 1, lines, D))
        return jnp.swapaxes(jnp.concatenate(parts, 3), 1, 2).reshape(-1, PAIR, 8, lines, D)
    return pl.pallas_call(
        feed_grads_kernel,
        grid=(2, T_SIZE),
        in_specs=[
            pl.BlockSpec((size, D), lambda p, i: (0, jnp.where(p == 0, i, T_SIZE - 1))),
            pl.BlockSpec((size, D), lambda p, i: (0, 0)),
            pl.BlockSpec((size, D // T_SIZE), lambda p, i: (0, jnp.where(p == 0, 0, i))),
            pl.BlockSpec((size, 4 * D), lambda p, i: (0, 0)),
        ],
        out_specs=pl.BlockSpec((4, PAIR, 4, lines, D), lambda p, i: (i, 0, p, 0, 0)),
        out_shape=jax.ShapeDtypeStruct((blocks // PAIR, PAIR, 8, lines, D), jnp.bfloat16),
        compiler_params=pltpu.CompilerParams(vmem_limit_bytes=VMEM_LIMIT),
        cost_estimate=COST,
    )(hidden, grads, rows, active_grads)


def reduce_feed(parts):
    return lax.psum_scatter(parts, ("t", "s", "x", "core"), scatter_dimension=0, tiled=True)[0]


def split_feed(halves):
    mine = lax.axis_index("y")
    keep = lax.dynamic_index_in_dim(halves, mine, 0, keepdims=False)
    sent = lax.dynamic_index_in_dim(halves, 1 - mine, 0, keepdims=False)
    total = keep.astype(jnp.float32) + flip(sent, "y").astype(jnp.float32)
    return jnp.concatenate([total[4 + part] for part in range(4)], 1), total[:4].reshape(-1, D)


def forward_kernel(
    chunk, flags_ref, q_ref, k_ref, v_ref, low_ref, high_ref, key_ref, out_ref, exact_ref, log_ref,
    masked_ref, turned_ref, top_ref, sum_ref, total_ref,
):
    step = pl.program_id(0)
    chunks = k_ref.shape[0] // chunk
    rows = q_ref.shape[0]
    lane = lax.broadcasted_iota(jnp.int32, (rows, 128), 1)

    @pl.when(step == 0)
    def _():
        def turn(index, carry):
            start = pl.multiple_of(index * chunk, chunk)
            turned_ref[:, pl.ds(start, chunk)] = v_ref[pl.ds(start, chunk), :].T
            return carry

        lax.fori_loop(0, chunks, turn, 0)

    for head in range(HEADS):
        pair = q_ref[:, (head // 2) * 128 : (head // 2 + 1) * 128] * SCALE
        masked_ref[head] = jnp.where((lane >= HD) == (head % 2 == 1), pair, 0).astype(jnp.bfloat16)
    top_ref[...] = jnp.full_like(top_ref, MASKED)
    sum_ref[...] = jnp.zeros_like(sum_ref)
    total_ref[...] = jnp.zeros_like(total_ref)

    def one_chunk(index, carry):
        @pl.when(flags_ref[step * chunks + index] != 0)
        def _():
            start = pl.multiple_of(index * chunk, chunk)
            here = pl.ds(start, chunk)
            keys = key_ref[here, :]
            allow = (keys >= low_ref[...]) & (keys <= high_ref[...])
            bias = jnp.where(allow, 0.0, MASKED)
            for head in range(HEADS):
                columns = slice((head // 2) * 128, (head // 2 + 1) * 128)
                lines = slice(head * HD, (head + 1) * HD)
                scores = lax.dot_general(
                    k_ref[here, columns],
                    masked_ref[head],
                    (((1,), (1,)), ((), ())),
                    preferred_element_type=jnp.float32,
                ) + bias
                before = top_ref[head : head + 1, :]
                after = jnp.maximum(before, jnp.max(scores, 0, keepdims=True))
                exponent = jnp.exp(scores - after)
                fade = jnp.exp(before - after)
                top_ref[head : head + 1, :] = after
                sum_ref[head : head + 1, :] = sum_ref[head : head + 1, :] * fade + jnp.sum(
                    exponent, 0, keepdims=True
                )
                total_ref[lines, :] = total_ref[lines, :] * fade + jnp.dot(
                    turned_ref[lines, here],
                    exponent.astype(jnp.bfloat16),
                    preferred_element_type=jnp.float32,
                )

        return carry

    lax.fori_loop(0, chunks, one_chunk, 0)
    for head in range(HEADS):
        lines = slice(head * HD, (head + 1) * HD)
        total_ref[lines, :] = total_ref[lines, :] / sum_ref[head : head + 1, :]
    exact = total_ref[...].T
    exact_ref[...] = exact
    out_ref[...] = exact.astype(jnp.bfloat16)
    log_ref[:HEADS, :] = top_ref[:HEADS, :] + jnp.log(sum_ref[:HEADS, :])
    log_ref[HEADS:, :] = jnp.zeros((8 - HEADS, rows), jnp.float32)


def attend_forward(queries, keys, values, low, high, key_ids, flags, block, chunk):
    count, depth = queries[0].shape[0], keys[0].shape[0]
    whole = functools.partial(pl.BlockSpec, pipeline_mode=pl.Buffered(1))
    return pl.pallas_call(
        functools.partial(forward_kernel, chunk),
        grid_spec=pltpu.PrefetchScalarGridSpec(
            num_scalar_prefetch=1,
            grid=(count // block,),
            in_specs=[
                pl.BlockSpec((block, WIDTH), lambda i, f, c=queries[1]: (i, c)),
                whole((depth, WIDTH), lambda i, f, c=keys[1]: (0, c)),
                whole((depth, WIDTH), lambda i, f, c=values[1]: (0, c)),
                pl.BlockSpec((1, block), lambda i, f: (0, i)),
                pl.BlockSpec((1, block), lambda i, f: (0, i)),
                whole((depth, 1), lambda i, f: (0, 0)),
            ],
            out_specs=[
                pl.BlockSpec((block, WIDTH), lambda i, f: (i, 0)),
                pl.BlockSpec((block, WIDTH), lambda i, f: (i, 0)),
                pl.BlockSpec((8, block), lambda i, f: (0, i)),
            ],
            scratch_shapes=[
                pltpu.VMEM((HEADS, block, 128), jnp.bfloat16),
                pltpu.VMEM((WIDTH, depth), jnp.bfloat16),
                pltpu.VMEM((8, block), jnp.float32),
                pltpu.VMEM((8, block), jnp.float32),
                pltpu.VMEM((WIDTH, block), jnp.float32),
            ],
        ),
        out_shape=[
            jax.ShapeDtypeStruct((count, WIDTH), jnp.bfloat16),
            jax.ShapeDtypeStruct((count, WIDTH), jnp.float32),
            jax.ShapeDtypeStruct((8, count), jnp.float32),
        ],
        compiler_params=pltpu.CompilerParams(vmem_limit_bytes=VMEM_LIMIT),
        cost_estimate=COST,
    )(
        flags.reshape(-1), queries[0], keys[0], values[0], low[None, :], high[None, :],
        key_ids[:, None],
    )


def backward_kernel(
    chunk, flags_ref, q_ref, k_ref, v_ref, g_ref, log_ref, exact_ref, low_ref, high_ref, key_ref,
    dq_ref, *refs,
):
    pair_refs, (q_masked, g_masked, delta_ref, turned_ref, dq_sum, dk_sum, dv_sum) = (
        refs[:-7], refs[-7:]
    )
    step = pl.program_id(0)
    chunks = k_ref.shape[0] // chunk
    rows = q_ref.shape[0]
    lane = lax.broadcasted_iota(jnp.int32, (rows, 128), 1)

    @pl.when(step == 0)
    def _():
        dk_sum[...] = jnp.zeros_like(dk_sum)
        dv_sum[...] = jnp.zeros_like(dv_sum)

        def turn(index, carry):
            start = pl.multiple_of(index * chunk, chunk)
            turned_ref[:, pl.ds(start, chunk)] = k_ref[pl.ds(start, chunk), :].T
            return carry

        lax.fori_loop(0, chunks, turn, 0)

    for head in range(HEADS):
        columns = slice((head // 2) * 128, (head // 2 + 1) * 128)
        chosen = (lane >= HD) == (head % 2 == 1)
        q_masked[head] = jnp.where(chosen, q_ref[:, columns] * SCALE, 0).astype(jnp.bfloat16)
        g_masked[head] = jnp.where(chosen, g_ref[:, columns], 0).astype(jnp.bfloat16)
    dq_sum[...] = jnp.zeros_like(dq_sum)
    members = lax.broadcasted_iota(jnp.int32, (8, WIDTH), 1) // HD
    members = (members == lax.broadcasted_iota(jnp.int32, (8, WIDTH), 0)).astype(jnp.float32)
    delta_ref[...] = lax.dot_general(
        members,
        g_ref[...].astype(jnp.float32) * exact_ref[...],
        (((1,), (1,)), ((), ())),
        precision=lax.Precision.HIGHEST,
        preferred_element_type=jnp.float32,
    )

    def one_chunk(index, carry):
        @pl.when(flags_ref[step * chunks + index] != 0)
        def _():
            start = pl.multiple_of(index * chunk, chunk)
            here = pl.ds(start, chunk)
            keys = key_ref[here, :]
            allow = (keys >= low_ref[...]) & (keys <= high_ref[...])
            bias = jnp.where(allow, 0.0, MASKED)
            for head in range(HEADS):
                columns = slice((head // 2) * 128, (head // 2 + 1) * 128)
                scores = lax.dot_general(
                    k_ref[here, columns],
                    q_masked[head],
                    (((1,), (1,)), ((), ())),
                    preferred_element_type=jnp.float32,
                )
                chances = jnp.exp(scores + bias - log_ref[head : head + 1, :])
                grads = lax.dot_general(
                    v_ref[here, columns],
                    g_masked[head],
                    (((1,), (1,)), ((), ())),
                    preferred_element_type=jnp.float32,
                )
                slopes = (chances * (grads - delta_ref[head : head + 1, :])).astype(jnp.bfloat16)
                dk_sum[here, columns] += jnp.dot(
                    slopes, q_masked[head], preferred_element_type=jnp.float32
                )
                dv_sum[here, columns] += jnp.dot(
                    chances.astype(jnp.bfloat16), g_masked[head], preferred_element_type=jnp.float32
                )
                dq_sum[head * HD : (head + 1) * HD, :] += jnp.dot(
                    turned_ref[head * HD : (head + 1) * HD, here],
                    slopes,
                    preferred_element_type=jnp.float32,
                )

        return carry

    lax.fori_loop(0, chunks, one_chunk, 0)
    dq_ref[...] = (dq_sum[...] * SCALE).T.astype(jnp.bfloat16)

    @pl.when(step == pl.num_programs(0) - 1)
    def _():
        for place, pair_ref in enumerate(pair_refs):
            size = pair_ref.shape[0]
            lines = slice(place * size, (place + 1) * size)
            pair_ref[:, :WIDTH] = dk_sum[lines, :].astype(jnp.bfloat16)
            pair_ref[:, WIDTH:] = dv_sum[lines, :].astype(jnp.bfloat16)


def attend_backward(
    queries, keys, values, grads, logs, exact, low, high, key_ids, flags, block, chunk, splits
):
    count, depth = queries[0].shape[0], keys[0].shape[0]
    whole = functools.partial(pl.BlockSpec, pipeline_mode=pl.Buffered(1))
    return pl.pallas_call(
        functools.partial(backward_kernel, chunk),
        grid_spec=pltpu.PrefetchScalarGridSpec(
            num_scalar_prefetch=1,
            grid=(count // block,),
            in_specs=[
                pl.BlockSpec((block, WIDTH), lambda i, f, c=queries[1]: (i, c)),
                whole((depth, WIDTH), lambda i, f, c=keys[1]: (0, c)),
                whole((depth, WIDTH), lambda i, f, c=values[1]: (0, c)),
                pl.BlockSpec((block, WIDTH), lambda i, f: (i, 0)),
                pl.BlockSpec((8, block), lambda i, f: (0, i)),
                pl.BlockSpec((block, WIDTH), lambda i, f: (i, 0)),
                pl.BlockSpec((1, block), lambda i, f: (0, i)),
                pl.BlockSpec((1, block), lambda i, f: (0, i)),
                whole((depth, 1), lambda i, f: (0, 0)),
            ],
            out_specs=[
                pl.BlockSpec((block, WIDTH), lambda i, f: (i, 0)),
            ]
            + [whole((depth // splits, 2 * WIDTH), lambda i, f: (0, 0))] * splits,
            scratch_shapes=[
                pltpu.VMEM((HEADS, block, 128), jnp.bfloat16),
                pltpu.VMEM((HEADS, block, 128), jnp.bfloat16),
                pltpu.VMEM((8, block), jnp.float32),
                pltpu.VMEM((WIDTH, depth), jnp.bfloat16),
                pltpu.VMEM((WIDTH, block), jnp.float32),
                pltpu.VMEM((depth, WIDTH), jnp.float32),
                pltpu.VMEM((depth, WIDTH), jnp.float32),
            ],
        ),
        out_shape=[
            jax.ShapeDtypeStruct((count, WIDTH), jnp.bfloat16),
        ]
        + [jax.ShapeDtypeStruct((depth // splits, 2 * WIDTH), jnp.bfloat16)] * splits,
        compiler_params=pltpu.CompilerParams(vmem_limit_bytes=VMEM_LIMIT),
        cost_estimate=COST,
    )(
        flags.reshape(-1), queries[0], keys[0], values[0], grads, logs, exact, low[None, :],
        high[None, :], key_ids[:, None],
    )


def needed_chunks(low, high, key_ids, block, chunk):
    first = jnp.min(low.reshape(-1, block), 1)[:, None]
    last = jnp.max(high.reshape(-1, block), 1)[:, None]
    smallest = jnp.min(key_ids.reshape(-1, chunk), 1)[None, :]
    largest = jnp.max(key_ids.reshape(-1, chunk), 1)[None, :]
    return ((largest >= first) & (smallest <= last)).astype(jnp.int32)


def on_device(
    count,
    tokens,
    encoder,
    seq_lengths,
    slot_ids,
    enc_lengths,
    cotangent,
    self_in,
    self_out,
    cross_query,
    cross_pair,
    cross_out,
    feed_up,
    feed_down,
    vectors,
    feed_bias,
    self_bias,
):

    full_self_in = fetch(self_in)
    facts = jnp.concatenate([slot_ids[0], seq_lengths[0], enc_lengths[0]], 1)
    slots = slot_ids.shape[2]
    facts_one, facts_two = to_packs(facts)
    tokens_in = jnp.concatenate(to_packs(tokens), 0)
    small = jnp.concatenate([vectors.T, feed_bias.reshape(D // 4, 4).T, self_bias[None, :]], 0)
    full_small = lax.all_gather(small, ("x", "core"), axis=1, tiled=True)
    vec = full_small[:12].astype(jnp.float32)
    bias_row = full_small[12:16].T.reshape(4 * D).astype(jnp.float32)
    self_bias_row = full_small[16].astype(jnp.float32)
    zero_row = jnp.zeros((D,), jnp.float32)
    facts_one, (self_out, cross_query) = chain(facts_one, (self_out, cross_query))
    full_out_query = fetch(jnp.concatenate([self_out, cross_query], 1))
    encoder_in = jnp.concatenate(to_packs(encoder), 0)
    tokens_in, (cross_pair, cross_out) = chain(tokens_in, (cross_pair, cross_out))
    full_cross_pair = fetch(cross_pair)
    full_cross_out = fetch(cross_out)

    lengths = facts_one[slots : slots + NSEQ]
    limits = facts_one[slots + NSEQ : slots + 2 * NSEQ]
    own_ids = jnp.concatenate([facts_one[:slots], facts_two[:slots]])
    ids = lax.all_gather(own_ids, GROUP, axis=0, tiled=True)
    ends = jnp.cumsum(lengths)
    key_ids = gather_sequence(ids, count)
    rank = jnp.sum((ids[None, :] < ids[:, None]).astype(jnp.int32), 1)
    places = jnp.arange(ids.shape[0], dtype=jnp.int32)
    sorted_ids = jnp.sum(jnp.where(places[:, None] == rank[None, :], ids[None, :], 0), 1)
    key_order = gather_sequence(sorted_ids, count)
    seq_of = jnp.sum((sorted_ids[:, None] >= ends[None, :]).astype(jnp.int32), 1)
    starts = jnp.concatenate([jnp.zeros((1,), jnp.int32), ends[:-1]])
    picked = seq_of[:, None] == jnp.arange(NSEQ, dtype=jnp.int32)[None, :]
    self_low = jnp.sum(jnp.where(picked, starts[None, :], 0), 1)
    self_high = sorted_ids
    cross_low = seq_of * ENC
    cross_high = cross_low + jnp.sum(jnp.where(picked, limits[None, :], 0), 1) - 1
    enc_rows = encoder.shape[1]
    micro = lax.axis_index("t") & 1
    enc_ids = []
    for place in range(count):
        index_s = place if count > 1 else 0
        for step in range(MEMBERS):
            core = lax.axis_index("core") ^ (step & 1)
            y_index = lax.axis_index("y") ^ (step >> 1)
            for part in range(2):
                t_index = 2 * core + (micro ^ part)
                row = ((t_index * count + index_s) * PAIR + y_index) * enc_rows
                enc_ids.append(row + jnp.arange(enc_rows, dtype=jnp.int32))
    enc_ids = jnp.concatenate(enc_ids)
    block = 256
    self_chunk, cross_chunk = 256, 384
    self_flags = needed_chunks(self_low, self_high, key_order, block, self_chunk)
    cross_flags = needed_chunks(cross_low, cross_high, enc_ids, block, cross_chunk)

    orders = {
        "x": ("core", "x", "y", "t0", "t1"),
        "y": ("core", "y", "x", "t0", "t1"),
    }

    def relative(matrix, name):
        return relative_columns(matrix, count, orders[name])

    facts_known = (rank, self_flags, cross_flags, key_order, enc_ids, self_low, cross_low, cross_high)
    tokens_in, facts_known = chain(tokens_in, facts_known)
    rank, self_flags, cross_flags, key_order, enc_ids, self_low, cross_low, cross_high = facts_known
    qkv = project_heads(tokens_in, full_self_in, jnp.concatenate([vec[6], zero_row, vec[7]]))
    feed_own = stack_feed(feed_up, feed_down)
    own_heads = sort_rows(to_members(qkv), rank)
    if count > 1:
        pairs = gather_sequence(own_heads[:, WIDTH:], count)
        self_keys, self_values = (pairs, 0), (pairs, 1)
    else:
        self_keys, self_values = (own_heads, 1), (own_heads, 2)
    tokens_x, tokens_y = relative(tokens_in, "x"), relative(tokens_in, "y")
    encoder_x = relative(encoder_in, "x")
    index = relative_index(D, count, orders["y"])
    pick_y = (index[:, None] == jnp.arange(D, dtype=jnp.int32)[None, :]).astype(jnp.bfloat16)
    (tokens_x, tokens_y, encoder_x, pick_y, own_heads), (encoder_in, cotangent) = chain(
        (tokens_x, tokens_y, encoder_x, pick_y, own_heads), (encoder_in, cotangent)
    )
    grad_in = jnp.concatenate(to_packs(cotangent), 0)
    attended_heads, exact_self, log_self = attend_forward(
        (own_heads, 0), self_keys, self_values, self_low, self_high, key_order, self_flags,
        block, self_chunk,
    )
    attended_heads, feed_own = chain(attended_heads, feed_own)
    feed_far = lax.ppermute(feed_own, "x", SWAP)
    enc_pairs = project_blocks(
        encoder_in, full_cross_pair, jnp.concatenate([zero_row, vec[9]])
    )
    attended = to_members(unsort_rows([attended_heads], rank))
    attended, enc_pairs = chain(attended, enc_pairs)
    enc_heads = gather_sequence(jnp.concatenate(exchange(enc_pairs), 0), count)
    normed_one, normed_one_low, unit_one, inverse_one, cross_queries = project_norm(
        by_member(attended), full_out_query, self_bias_row, tokens_in, vec[0], vec[3],
        after=(vec[8],),
    )
    cross_heads = sort_rows(to_members(cross_queries), rank)
    attended_x = relative(as_columns(attended), "x")
    normed_one_x = relative(normed_one_low, "x")
    (attended_x, normed_one_x), cross_heads = chain((attended_x, normed_one_x), cross_heads)
    crossed_heads, exact_cross, log_cross = attend_forward(
        (cross_heads, 0), (enc_heads, 0), (enc_heads, 1), cross_low, cross_high, enc_ids,
        cross_flags, block, cross_chunk,
    )
    cross_heads, feed_own = chain(cross_heads, feed_own)
    feed_near = lax.ppermute(feed_own, "core", SWAP)
    crossed_heads, feed_far = chain(crossed_heads, feed_far)
    feed_shards = [feed_own, feed_near, feed_far, lax.ppermute(feed_far, "core", SWAP)]
    crossed = to_members(unsort_rows([crossed_heads], rank))
    normed_two, normed_two_low, unit_two, inverse_two = project_norm(
        by_member(crossed), full_cross_out, vec[10], normed_one, vec[1], vec[4]
    )
    crossed_x = relative(as_columns(crossed), "x")
    crossed_x, normed_two_low = chain(crossed_x, normed_two_low)
    pre_active, hidden = feed_up_gelu(normed_two_low, feed_shards, bias_row)
    layer_low, grad_three, grad_branch, sums_three = feed_down_norm(
        hidden, feed_shards, vec[11], normed_two, vec[2], vec[5], grad_in
    )
    half = tokens_in.shape[0] // 2

    grad_pre, bias_up, grad_two, grad_crossed_out, sums_two, grad_crossed = feed_back(
        pre_active, feed_shards, grad_branch, grad_three, unit_two, inverse_two, vec[1],
        full_cross_out,
    )
    received, (feed_parts, layer_low) = during_members(
        grad_crossed, lambda layer, *rows: (feed_grads(*rows, count), layer),
        (layer_low, hidden, grad_branch, normed_two_low, grad_pre),
    )
    layer_out = from_packs(layer_low[:half], layer_low[half:])
    feed_sum = reduce_feed(feed_parts)
    grad_crossed_heads = sort_rows(received, rank)
    dq_heads, *enc_pair_grads = attend_backward(
        (cross_heads, 0), (enc_heads, 0), (enc_heads, 1), grad_crossed_heads, log_cross,
        exact_cross, cross_low, cross_high, enc_ids, cross_flags, block, cross_chunk,
        MEMBERS if count == 1 else 1,
    )
    layer_out, dq_heads = chain(layer_out, dq_heads)
    if count > 1:
        enc_pair_grads = cut(scatter_sequence(enc_pair_grads[0], count))
    dq_blocks, (enc_pair_grads,) = during_members(
        unsort_rows([dq_heads], rank), lambda *rest: rest, (enc_pair_grads,)
    )
    enc_blocks = exchange(enc_pair_grads)
    grad_one, grad_attended_out, sums_one, grad_attended = back_norm(
        by_member(dq_blocks), full_out_query, grad_two, unit_one, inverse_one, vec[0]
    )

    def three_side(dq_blocks, *lefts):
        grads = as_columns(dq_blocks)
        return grads, weight_grads(lefts, [grad_attended_out, grads, grad_crossed_out])

    received, (grad_cross_queries, three_parts) = during_members(
        grad_attended, three_side, (dq_blocks, attended_x, normed_one_x, crossed_x)
    )
    three_sum = Halving(three_parts, count, orders["x"])
    grad_attended_heads = sort_rows(received, rank)
    dq_heads, pair_heads = attend_backward(
        (own_heads, 0), self_keys, self_values, grad_attended_heads, log_self, exact_self,
        self_low, self_high, key_order, self_flags, block, self_chunk, 1,
    )
    pair_heads = scatter_sequence(pair_heads, count)
    half_enc = encoder_in.shape[0] // 2

    dq_heads, enc_blocks = chain(dq_heads, enc_blocks)

    def encoder_side(pending, me):
        three_sum.pending = pending
        three_sum.step()
        grads = join_heads(enc_blocks, me)
        parts = weight_grads([encoder_x], [grads])
        return grads, back_project(grads, full_cross_pair), parts, three_sum.sent, three_sum.value

    received, (grad_enc_pairs, grad_enc, pair_parts, three_sum.sent, three_sum.value) = (
        during_members(
            unsort_rows([dq_heads, pair_heads], rank), encoder_side,
            (three_sum.pending, group_index()[None]),
        )
    )
    pair_sum = Halving(pair_parts, count, orders["x"])
    grad_encoder = from_packs(grad_enc[:half_enc], grad_enc[half_enc:])
    grad_qkv = as_columns(received)
    left_parts, right_parts = self_in_grads(
        tokens_x, tokens_y, grad_qkv, pick_y, sums_one, sums_two, sums_three, bias_up,
        grad_cross_queries, grad_enc_pairs,
    )
    left_sum = Halving(left_parts, count, orders["x"])
    right_sum = Halving(right_parts, count, orders["y"])
    (left_sum.sent, right_sum.sent), grad_qkv = chain((left_sum.sent, right_sum.sent), grad_qkv)
    grad_rows = (RESIDUAL * grad_one + back_project(grad_qkv, full_self_in, jnp.float32)).astype(
        jnp.bfloat16
    )
    turn, grad_encoder = chain(right_sum.sent, grad_encoder)
    grad_tokens = from_packs(grad_rows[:half], grad_rows[half:]).astype(jnp.float32)
    for halving in [pair_sum, left_sum, right_sum, three_sum] * 5:
        if halving.order:
            turn, halving.pending = chain(turn, halving.pending)
            halving.step()
            turn = halving.sent
    three, pair = three_sum.finish(), pair_sum.finish()
    left, right = left_sum.finish(), right_sum.finish()
    up_sum, down_sum = split_feed(feed_sum)
    small = right[:, 3 * D // 2 :]
    return (
        layer_out,
        grad_tokens,
        grad_encoder.astype(jnp.float32),
        jnp.concatenate([left, right[:, : 3 * D // 2]], 1),
        three[:, :D],
        three[:, D : 2 * D],
        pair,
        three[:, 2 * D :],
        up_sum,
        down_sum,
        small[:, :12],
        small[:, 13:17].reshape(-1),
        small[:, 12],
    )


def solution(mesh):
    contexts = mesh.shape["ctx"]
    count = contexts // (T_SIZE * PAIR)
    fine = Mesh(
        mesh.devices.reshape(T_SIZE, count, PAIR, PAIR, PAIR), ("t", "s", "y", "x", "core")
    )
    fsdp, ctx = ("x", "core"), ("t", "s", "y")
    in_specs = (
        P(None, ROWS, None),
        P(None, ROWS, None),
        P(fsdp, None, None),
        P(fsdp, None, ctx),
        P(fsdp, None, None),
        P(None, ROWS, None),
        P(fsdp, None),
        P(fsdp, None),
        P(fsdp, None),
        P(fsdp, None),
        P(fsdp, None),
        P(fsdp, None),
        P(fsdp, None),
        P(fsdp, None),
        P(fsdp),
        P(fsdp),
    )
    out_specs = (P(None, ROWS, None),) * 3 + (P(BLOCKS, None),) * 8 + (P(BLOCKS),) * 2
    return jax.shard_map(
        functools.partial(on_device, count),
        mesh=fine,
        in_specs=in_specs,
        out_specs=out_specs,
        check_vma=False,
    )
```

time: 848 us -> 634 us (0.75)
  Pallas kernels: 68.5 us -> 235 us
  waiting for transfers between devices: 300 us -> 145 us
  local copies, waits for them, and re-layouts: 153 us -> 39.9 us
  matrix products: 104 us -> 14.2 us
  other arithmetic: 56.3 us -> 27.7 us
  blocking collectives: 13 us -> 41.3 us
  starting transfers between devices: 122 us -> 107 us
    pallas_call x0 -> x27, Pallas kernels: none -> 155 us  [the longest x20 80.2 us: small_kernel(): pl.pallas_call(body, in_specs=[pl.BlockSpec(memory_space=pltpu.SMEM)] * l...]
    ppermute x73 -> x30, waiting for transfers between devices: 251 us -> 114 us  [the longest x13 50.7 us: flip(): return lax.ppermute(block, name, [(i, i ^ 1) for i in range(PAIR)])]
    dynamic_slice x26 -> x1, local copies, waits for them, and re-layouts: 78.1 us -> 0.01 us  [to_packs(): first = lax.dynamic_index_in_dim(parts, parity, 0, keepdims=False)]
    dot_general x22 -> x0, matrix products: 60.6 us -> none  [the longest x11 34.1 us: column_sum(): lax.dot_general(left, right, (((0,), (0,)), ((), ())), preferred_element_...]
    ppermute x73 -> x30, starting transfers between devices: 99.9 us -> 63.4 us  [the longest x13 32 us: flip(): return lax.ppermute(block, name, [(i, i ^ 1) for i in range(PAIR)])]
    dot_general x7 -> x6, matrix products: 43.2 us -> 14.2 us  [linear(): return jnp.dot(inputs, weight, preferred_element_type=jnp.float32)]
    all_to_all x0 -> x7, starting transfers between devices: none -> 26.5 us  [to_members(): return lax.all_to_all(blocks, GROUP, 0, 0, tiled=True)]
    convert_element_type x36 -> x4, other arithmetic: 29.7 us -> 5.95 us  [the longest x1 2.05 us: on_device(): grad_encoder.astype(jnp.float32)]
  transfers between devices with their start and end apart: 94 -> 56, of which waited for: 43 -> 23; matrix products, arithmetic and copies ran while one was open for 33% -> 11% of each run, Pallas kernels for 8% -> 31%
where the time goes in v2:
time: 634 us; the launch traced here: 625 us
  Pallas kernels  235 us (37%)
  waiting for transfers between devices  145 us (23%)
  starting transfers between devices  107 us (17%)
  blocking collectives  41.3 us (7%)
  local copies, waits for them, and re-layouts  39.9 us (6%)
  other arithmetic  27.7 us (4%)
  between operations  15.2 us (2%)
  matrix products  14.2 us (2%)
    pallas_call x20, Pallas kernels, small_kernel(): pl.pallas_call(body, in_specs=[pl.BlockSpec(memory_space=pltpu.SMEM)] * l...  80.2 us
    ppermute x13, waiting for transfers between devices, flip(): return lax.ppermute(block, name, [(i, i ^ 1) for i in range(PAIR)])  50.7 us
    pallas_call x2, Pallas kernels, attend_backward(): pl.pallas_call(functools.partial(backward_kernel, chunk), grid_spec=pltpu...  40.9 us
    pallas_call x2, Pallas kernels, attend_forward(): pl.pallas_call(functools.partial(forward_kernel, chunk), grid_spec=pltpu....  39.1 us
    ppermute x13, starting transfers between devices, flip(): return lax.ppermute(block, name, [(i, i ^ 1) for i in range(PAIR)])  32 us
    ppermute x6, waiting for transfers between devices, exchange(): lax.ppermute(block, GROUP, group_route(step))  28.3 us
    all_to_all x7, starting transfers between devices, to_members(): return lax.all_to_all(blocks, GROUP, 0, 0, tiled=True)  26.5 us
    ppermute x8, waiting for transfers between devices, flip(): return lax.ppermute(block, 't', [(i, i ^ step) for i in range(T_SIZE)])  22.2 us
  transfers between devices with their start and end apart: 56, of which 23 were waited for; matrix products, arithmetic and copies ran while one was open for 11% of the time, Pallas kernels for 31%

profile of v2, /device:TPU:0, one launch (start us, length us, event | category | flops | bytes accessed | tf_op | source)
XLA Modules:
  0.0 625.1 jit_solution(15003999967847497505)
XLA Ops:
  9.9 3.1 collective-permute-start.1
  13.0 6.0 collective-permute-done.1
  27.2 19.6 %all_gather.20 = bf16[17,1024]{1,0:T(8,128)(2,1)S(1)} all-gather(bf16[17,256]{1,0:T(8,128)(2,1)S(1)} %pad_maximum_fusion.7), channel_id=1, replica_groups=mesh['t'=4,'s'=1,'y'=2,'x'=2,'core'=2] {'x','core'}, dimensions={1}, use_global_device_ids=true | all-gather | bytes 43520 | tf_op jit(solution)/shard_map/all_gather | solution.py:1078
  56.3 5.1 all-gather
  65.4 6.5 %shard_map.255 = bf16[1024,768]{1,0:T(8,128)(2,1)} custom-call(bf16[256,1024]{1,0:T(8,128)(2,1)} %pad_maximum_fusion.2.rows_ref.base_ref, bf16[1024,3072]{1,0:T(8,128)(2,1)} %all-gather.6.cloned.1.call-done.weight_ref, f32[1,3072]{1,0:T(1,128)} %bitcast.125), custom_call_target="tpu_custom_call" | custom-call | tf_op jit(solution)/shard_map/pallas_call | solution.py:134
  71.9 3.9 all-to-all-start
  81.9 3.0 fusion.13.refs_0_
  84.9 11.0 %all-to-all-done = bf16[4,256,768]{2,1,0:T(8,128)(2,1)S(1)} async-done(((bf16[4,256,768]{2,1,0:T(8,128)(2,1)}), bf16[4,256,768]{2,1,0:T(8,128)(2,1)S(1)}, u32[]{:S(2)}, u32[]{:S(2)}) %all-to-all-start) | async-done | bytes 1572896 | tf_op jit(solution)/shard_map/all_to_all | solution.py:509
  97.0 4.4 shard_map.256.q_ref.k_ref.v_ref
  101.4 13.5 %shard_map.257 = (bf16[1024,256]{1,0:T(8,128)(2,1)}, f32[1024,256]{1,0:T(8,128)}, f32[8,1024]{1,0:T(8,128)}) custom-call(s32[16]{0:T(128)} %reshape.236.flags_ref, bf16[1024,768]{1,0:T(8,128)(2,1)} %shard_map.256.q_ref.k_ref.v_ref, bf16[1024,768]{1,0:T(8,128)(2,1)} %shard_map.256.q_ref.k_ref.v_ref, bf16[1024,768]{1,0:T(8,128)(2,1)} %shard_map.256.q_ref.k_ref.v_ref, ...), custom_call_target="tpu_custom_call" | custom-call | tf_op jit(solution)/shard_map/pallas_call | solution.py:868
  114.9 4.5 collective-permute-start.9
  120.4 2.7 shard_map.258
  123.2 3.5 all-to-all-start.1
  127.3 7.0 %shard_map.259 = (bf16[768,512]{1,0:T(8,128)(2,1)}, bf16[768,512]{1,0:T(8,128)(2,1)}, bf16[768,512]{1,0:T(8,128)(2,1)}, bf16[768,512]{1,0:T(8,128)(2,1)}) custom-call(s32[1]{0:T(128)} %bitcast.29.me_ref, bf16[768,1024]{1,0:T(8,128)(2,1)} %copy-done.8, bf16[1024,2048]{1,0:T(8,128)(2,1)} %all-gather.8.cloned.1.call-done.weight_ref, f32[1,2048]{1,0:T(1,128)} %bitcast.129), custom_call_target="tpu_custom_call" | custom-call | tf_op jit(solution)/shard_map/pallas_call | solution.py:134
  140.6 5.3 shard_map.261
  145.9 4.1 all-to-all-start.2
  152.8 2.8 fusion.17.refs_1_
  158.8 2.9 fusion.16.refs_0_
  161.7 2.5 shard_map.262.q_ref
  166.8 11.0 %collective-permute-done.8 = bf16[768,512]{1,0:T(8,128)(2,1)} collective-permute-done((bf16[768,512]{1,0:T(8,128)(2,1)}, bf16[768,512]{1,0:T(8,128)(2,1)}, u32[]{:S(2)}, u32[]{:S(2)}) %collective-permute-start.8) | collective-permute-done | bytes 786464 | tf_op jit(solution)/shard_map/ppermute | solution.py:529
  180.7 25.6 %shard_map.263 = (bf16[1024,256]{1,0:T(8,128)(2,1)}, f32[1024,256]{1,0:T(8,128)}, f32[8,1024]{1,0:T(8,128)}) custom-call(s32[32]{0:T(128)} %reshape.235.flags_ref, bf16[1024,256]{1,0:T(8,128)(2,1)} %shard_map.262.q_ref, bf16[3072,512]{1,0:T(8,128)(2,1)} %copy-done, bf16[3072,512]{1,0:T(8,128)(2,1)} %copy-done, s32[1,1024]{1,0:T(1,128)} %bitcast.118, ...), custom_call_target="tpu_custom_call" | custom-call | tf_op jit(solution)/shard_map/pallas_call | solution.py:868
  206.3 13.3 %collective-permute-done.9.refs_2_.refs_6_ = bf16[2048,1024]{1,0:T(8,128)(2,1)} collective-permute-done((bf16[2048,1024]{1,0:T(8,128)(2,1)}, bf16[2048,1024]{1,0:T(8,128)(2,1)}, u32[]{:S(2)}, u32[]{:S(2)}) %collective-permute-start.9) | collective-permute-done | bytes 4194336 | tf_op jit(solution)/shard_map/ppermute | solution.py:1157
  219.6 2.8 shard_map.264
  222.4 3.5 all-to-all-start.3
  229.3 5.3 collective-permute-done.13
  238.2 4.3 all-gather.12.cloned.1.call-done.weight_ref.refs_13_
  242.5 4.6 shard_map.266
  248.9 9.8 %shard_map.267 = (f32[256,4096]{1,0:T(8,128)}, bf16[256,4096]{1,0:T(8,128)(2,1)}) custom-call(s32[1]{0:T(128)} %bitcast.me_ref, bf16[256,1024]{1,0:T(8,128)(2,1)} %get-tuple-element.212.rows_ref, bf16[2048,1024]{1,0:T(8,128)(2,1)} %slice_dynamic-update-slice_fusion.refs_0_.refs_4_, bf16[2048,1024]{1,0:T(8,128)(2,1)} %collective-permute-done.10.refs_1_.refs_5_, ...), custom_call_target="tpu_custom_call" | custom-call | tf_op jit(solution)/shard_map/pallas_call | solution.py:300
  258.7 11.9 %shard_map.268 = (bf16[256,1024]{1,0:T(8,128)(2,1)}, f32[256,1024]{1,0:T(8,128)}, bf16[256,1024]{1,0:T(8,128)(2,1)}, f32[8,1024]{1,0:T(8,128)}) custom-call(s32[1]{0:T(128)} %bitcast.me_ref, bf16[256,4096]{1,0:T(8,128)(2,1)} %get-tuple-element.210.hidden_ref, bf16[2048,1024]{1,0:T(8,128)(2,1)} %slice_dynamic-update-slice_fusion.refs_0_.refs_4_, ...), custom_call_target="tpu_custom_call" | custom-call | tf_op jit(solution)/shard_map/pallas_call | solution.py:377
  270.6 19.4 %shard_map.269 = (bf16[256,4096]{1,0:T(8,128)(2,1)}, f32[1,4096]{1,0:T(1,128)}, f32[256,1024]{1,0:T(8,128)}, bf16[256,1024]{1,0:T(8,128)(2,1)}, f32[8,1024]{1,0:T(8,128)}, /*index=5*/bf16[1024,256]{1,0:T(8,128)(2,1)}) custom-call(s32[1]{0:T(128)} %bitcast.me_ref, f32[256,4096]{1,0:T(8,128)} %get-tuple-element.199.active_ref, ...), custom_call_target="tpu_custom_call" | custom-call | tf_op jit(solution)/shard_map/pallas_call | solution.py:442
  290.0 4.3 all-to-all-start.4
  294.3 11.7 %shard_map.270 = bf16[16,2,8,32,1024]{4,3,2,1,0:T(8,128)(2,1)} custom-call(bf16[256,4096]{1,0:T(8,128)(2,1)} %get-tuple-element.210.hidden_ref, bf16[256,1024]{1,0:T(8,128)(2,1)} %get-tuple-element.211.refs_8_.grads_ref, bf16[256,1024]{1,0:T(8,128)(2,1)} %get-tuple-element.212.rows_ref, bf16[256,4096]{1,0:T(8,128)(2,1)} %get-tuple-element.213.active_grads_ref), custom_call_target="tpu_custom_call" | custom-call | tf_op jit(solution)/shard_map/pallas_call | solution.py:768
  308.1 3.4 collective-permute-start.15
  314.1 26.7 %shard_map.272 = (bf16[1024,256]{1,0:T(8,128)(2,1)}, bf16[768,512]{1,0:T(8,128)(2,1)}, bf16[768,512]{1,0:T(8,128)(2,1)}, bf16[768,512]{1,0:T(8,128)(2,1)}, bf16[768,512]{1,0:T(8,128)(2,1)}) custom-call(s32[32]{0:T(128)} %reshape.235.flags_ref, bf16[1024,256]{1,0:T(8,128)(2,1)} %shard_map.262.q_ref, bf16[3072,512]{1,0:T(8,128)(2,1)} %copy-done, ...), custom_call_target="tpu_custom_call" | custom-call | tf_op jit(solution)/shard_map/pallas_call | solution.py:1002
  341.6 2.7 shard_map.273
  344.4 16.6 %all_to_all.93 = bf16[4,256,256]{2,1,0:T(8,128)(2,1)} all-to-all(bf16[4,256,256]{2,1,0:T(8,128)(2,1)} %bitcast.103), channel_id=1, replica_groups=mesh['t'=4,'s'=1,'y'=2,'x'=2,'core'=2] {'y','core'}, dimensions={0} | all-to-all | bytes 1048576 | tf_op jit(solution)/shard_map/all_to_all | solution.py:509
  361.0 5.8 shard_map.274
  366.8 3.5 all-to-all-start.6
  372.2 6.2 shard_map.276
  380.9 2.6 shard_map.277.g_ref
  383.6 14.3 %shard_map.278 = (bf16[1024,256]{1,0:T(8,128)(2,1)}, bf16[1024,512]{1,0:T(8,128)(2,1)}) custom-call(s32[16]{0:T(128)} %reshape.236.flags_ref, bf16[1024,768]{1,0:T(8,128)(2,1)} %shard_map.256.q_ref.k_ref.v_ref, bf16[1024,768]{1,0:T(8,128)(2,1)} %shard_map.256.q_ref.k_ref.v_ref, bf16[1024,768]{1,0:T(8,128)(2,1)} %shard_map.256.q_ref.k_ref.v_ref, ...), custom_call_target="tpu_custom_call" | custom-call | tf_op jit(solution)/shard_map/pallas_call | solution.py:1002
  400.2 15.0 %collective-permute-done.18.refs_3_ = bf16[768,512]{1,0:T(8,128)(2,1)S(1)} collective-permute-done((bf16[768,512]{1,0:T(8,128)(2,1)}, bf16[768,512]{1,0:T(8,128)(2,1)S(1)}, u32[]{:S(2)}, u32[]{:S(2)}) %collective-permute-start.18) | collective-permute-done | bytes 786464 | tf_op jit(solution)/shard_map/ppermute | solution.py:529
  415.2 4.8 shard_map.279
  420.0 3.8 all-to-all-start.7
  423.8 4.1 convert_add_fusion
  428.0 2.7 copy-done.1
  432.1 4.0 shard_map.280.grads_ref.refs_1_.pair_ref
  436.0 7.1 %shard_map.282 = (bf16[512,2048]{1,0:T(8,128)(2,1)}, bf16[512,2048]{1,0:T(8,128)(2,1)}) custom-call(bf16[768,1024]{1,0:T(8,128)(2,1)} %fusion.13.refs_0_, bf16[768,2048]{1,0:T(8,128)(2,1)} %shard_map.280.grads_ref.refs_1_.pair_ref), custom_call_target="tpu_custom_call" | custom-call | tf_op jit(solution)/shard_map/pallas_call | solution.py:134
  443.1 7.5 %shard_map.281 = bf16[768,1024]{1,0:T(8,128)(2,1)} custom-call(bf16[768,2048]{1,0:T(8,128)(2,1)} %shard_map.280.grads_ref.refs_1_.pair_ref, bf16[1024,2048]{1,0:T(8,128)(2,1)} %all-gather.8.cloned.1.call-done.weight_ref), custom_call_target="tpu_custom_call" | custom-call | tf_op jit(solution)/shard_map/pallas_call | solution.py:494
  454.8 6.7 %collective-permute-start.27 = (bf16[256,3072]{1,0:T(8,128)(2,1)}, bf16[256,3072]{1,0:T(8,128)(2,1)S(1)}, u32[]{:S(2)}, u32[]{:S(2)}) collective-permute-start(bf16[256,3072]{1,0:T(8,128)(2,1)} %slice.428), channel_id=1, source_target_pairs={{0,2},{2,0},{1,3},{3,1},{4,6},{6,4},{5,7},{7,5},{8,10},{10,8},{9,1... | collective-permute-start | bytes 4718600 | tf_op jit(solution)/shard_map/ppermute | solution.py:628
  461.5 2.8 shard_map.283.grads_ref
  464.4 8.3 %shard_map.284 = (bf16[512,1536]{1,0:T(8,128)(2,1)}, bf16[512,1536]{1,0:T(8,128)(2,1)}, bf16[512,1664]{1,0:T(8,128)(2,1)}, bf16[512,1664]{1,0:T(8,128)(2,1)}) custom-call(bf16[256,1024]{1,0:T(8,128)(2,1)} %fusion.15.left_ref, bf16[256,1024]{1,0:T(8,128)(2,1)} %fusion.14.right_ref, bf16[256,3072]{1,0:T(8,128)(2,1)} %shard_map.283.grads_ref, ...), custom_call_target="tpu_custom_call" | custom-call | tf_op jit(solution)/shard_map/pallas_call | solution.py:702
  472.7 6.2 shard_map.285
  481.5 11.0 %collective-permute-start.26 = (bf16[512,1664]{1,0:T(8,128)(2,1)S(1)}, bf16[512,1664]{1,0:T(8,128)(2,1)S(1)}, u32[]{:S(2)}, u32[]{:S(2)}) collective-permute-start(bf16[512,1664]{1,0:T(8,128)(2,1)S(1)} %copy-done.36), channel_id=1, source_target_pairs={{0,1},{1,0},{2,3},{3,2},{4,5},{5,4},{6,7},{7,6},{8,9},{9,8},{10,11... | collective-permute-start | bytes 5111816 | tf_op jit(solution)/shard_map/ppermute | solution.py:628
  504.0 11.0 %collective-permute-done.28 = bf16[256,2048]{1,0:T(8,128)(2,1)S(1)} collective-permute-done((bf16[256,2048]{1,0:T(8,128)(2,1)S(1)}, bf16[256,2048]{1,0:T(8,128)(2,1)S(1)}, u32[]{:S(2)}, u32[]{:S(2)}) %collective-permute-start.28) | collective-permute-done | bytes 1048608 | tf_op jit(solution)/shard_map/ppermute | solution.py:628
  516.9 15.0 %collective-permute-done.29 = bf16[256,1536]{1,0:T(8,128)(2,1)S(1)} collective-permute-done((bf16[256,1536]{1,0:T(8,128)(2,1)S(1)}, bf16[256,1536]{1,0:T(8,128)(2,1)S(1)}, u32[]{:S(2)}, u32[]{:S(2)}) %collective-permute-start.29) | collective-permute-done | bytes 786464 | tf_op jit(solution)/shard_map/ppermute | solution.py:628
  537.2 9.4 %collective-permute-done.32 = bf16[128,2048]{1,0:T(8,128)(2,1)S(1)} collective-permute-done((bf16[128,2048]{1,0:T(8,128)(2,1)S(1)}, bf16[128,2048]{1,0:T(8,128)(2,1)S(1)}, u32[]{:S(2)}, u32[]{:S(2)}) %collective-permute-start.32) | collective-permute-done | bytes 524320 | tf_op jit(solution)/shard_map/ppermute | solution.py:628
  549.3 5.8 collective-permute-done.33
  555.5 13.4 %collective-permute-start.41 = (bf16[32,3072]{1,0:T(8,128)(2,1)S(1)}, bf16[32,3072]{1,0:T(8,128)(2,1)S(1)}, u32[]{:S(2)}, u32[]{:S(2)}) collective-permute-start(bf16[32,3072]{1,0:T(8,128)(2,1)S(1)} %slice.439), channel_id=1, source_target_pairs={{0,16},{8,24},{16,0},{24,8},{1,17},{9,25},{17,1},{25,9},{2,18},{10... | collective-permute-start | bytes 589832 | tf_op jit(solution)/shard_map/ppermute | solution.py:627
  574.5 2.7 collective-permute-done.41
  578.1 7.2 %collective-permute-done.36 = bf16[64,2048]{1,0:T(8,128)(2,1)S(1)} collective-permute-done((bf16[64,2048]{1,0:T(8,128)(2,1)S(1)}, bf16[64,2048]{1,0:T(8,128)(2,1)S(1)}, u32[]{:S(2)}, u32[]{:S(2)}) %collective-permute-start.36) | collective-permute-done | bytes 262176 | tf_op jit(solution)/shard_map/ppermute | solution.py:627
  585.4 2.9 collective-permute-done.37
  592.7 6.0 collective-permute-done.38
  605.9 9.4 %collective-permute-done.43 = bf16[8,32,1024]{2,1,0:T(8,128)(2,1)S(1)} collective-permute-done((bf16[8,32,1024]{2,1,0:T(8,128)(2,1)S(1)}, bf16[8,32,1024]{2,1,0:T(8,128)(2,1)S(1)}, u32[]{:S(2)}, u32[]{:S(2)}) %collective-permute-start.43) | collective-permute-done | bytes 524320 | tf_op jit(solution)/shard_map/ppermute | solution.py:628
  (306 shorter events, 122.4 us)
Async XLA Ops:
  7.2 58.2 %all-gather.6.cloned.1.call-start = ((), (), s32[]{:S(2)}) async-start(), calls=%async_computation.9 | async-start | bytes 7864320 | tf_op jit(solution)/shard_map/all_gather | solution.py:149
  7.9 119.3 %all-gather.8.cloned.1.call-start = ((), (), s32[]{:S(2)}) async-start(), calls=%async_computation.10 | async-start | bytes 5242880 | tf_op jit(solution)/shard_map/all_gather | solution.py:149
  8.0 18.9 %copy-start.32 = (bf16[1024]{0:T(1024)(128)(2,1)S(1)}, bf16[1024]{0:T(1024)(128)(2,1)}, u32[]{:S(2)}) copy-start(bf16[1024]{0:T(1024)(128)(2,1)} %param.30) | copy-start | bytes 6148
  8.0 19.2 %copy-start.37 = (bf16[256]{0:T(256)(128)(2,1)S(1)}, bf16[256]{0:T(256)(128)(2,1)}, u32[]{:S(2)}) copy-start(bf16[256]{0:T(256)(128)(2,1)} %param.31) | copy-start | bytes 1540
  8.0 19.2 %copy-start.31 = (bf16[256,12]{0,1:T(8,128)(2,1)S(1)}, bf16[256,12]{0,1:T(8,128)(2,1)}, u32[]{:S(2)}) copy-start(bf16[256,12]{0,1:T(8,128)(2,1)} %param.29) | copy-start | bytes 18436
  9.1 39.2 %copy-start.9 = (bf16[1024,1024]{1,0:T(8,128)(2,1)S(1)}, bf16[1024,1024]{1,0:T(8,128)(2,1)}, u32[]{:S(2)}) copy-start(bf16[1024,1024]{1,0:T(8,128)(2,1)} %param.28) | copy-start | bytes 6291460
  9.1 3.9 collective-permute-start
  9.9 9.1 %collective-permute-start.1 = (bf16[128,1024]{1,0:T(8,128)(2,1)S(1)}, bf16[128,1024]{1,0:T(8,128)(2,1)S(1)}, u32[]{:S(2)}, u32[]{:S(2)}) collective-permute-start(bf16[128,1024]{1,0:T(8,128)(2,1)S(1)} %get-tuple-element.388), channel_id=1, source_target_pairs={{0,8},{1,24},{8,0},{9,16},{16,9},{17,25},{24,1},{25,17},{2,10},{3,... | collective-permute-start | bytes 786440 | tf_op jit(solution)/shard_map/ppermute | solution.py:89
  19.9 120.7 %all-gather.10.cloned.1.call-start = ((), (), s32[]{:S(2)}) async-start(), calls=%async_computation.11 | async-start | bytes 5242880 | tf_op jit(solution)/shard_map/all_gather | solution.py:149
  20.0 34.8 %collective-permute-start.2 = (s32[134]{0:T(256)S(1)}, s32[134]{0:T(256)S(1)}, u32[]{:S(2)}, u32[]{:S(2)}) collective-permute-start(s32[134]{0:T(256)S(1)} %bitcast.140), channel_id=1, source_target_pairs={{0,0},{1,16},{8,8},{9,24},{16,1},{17,17},{24,9},{25,25},{2,2},{3,1... | collective-permute-start | bytes 1616 | tf_op jit(solution)/shard_map/ppermute | solution.py:88
  20.7 35.6 %collective-permute-start.3 = (s32[134]{0:T(256)S(1)}, s32[134]{0:T(256)S(1)}, u32[]{:S(2)}, u32[]{:S(2)}) collective-permute-start(s32[134]{0:T(256)S(1)} %bitcast.139), channel_id=1, source_target_pairs={{0,8},{1,24},{8,0},{9,16},{16,9},{17,25},{24,1},{25,17},{2,10},{3,... | collective-permute-start | bytes 1616 | tf_op jit(solution)/shard_map/ppermute | solution.py:89
  24.8 54.6 %collective-permute-start.4 = (bf16[384,1024]{1,0:T(8,128)(2,1)S(1)}, bf16[384,1024]{1,0:T(8,128)(2,1)}, u32[]{:S(2)}, u32[]{:S(2)}) collective-permute-start(bf16[384,1024]{1,0:T(8,128)(2,1)S(1)} %get-tuple-element.372), channel_id=1, source_target_pairs={{0,0},{1,16},{8,8},{9,24},{16,1},{17,17},{24,9},{25,25},{2,2},{3,1... | collective-permute-start | bytes 2359304 | tf_op jit(solution)/shard_map/ppermute | solution.py:88
  26.3 54.3 %collective-permute-start.5 = (bf16[384,1024]{1,0:T(8,128)(2,1)}, bf16[384,1024]{1,0:T(8,128)(2,1)}, u32[]{:S(2)}, u32[]{:S(2)}) collective-permute-start(bf16[384,1024]{1,0:T(8,128)(2,1)} %get-tuple-element.371), channel_id=1, source_target_pairs={{0,8},{1,24},{8,0},{9,16},{16,9},{17,25},{24,1},{25,17},{2,10},{3,... | collective-permute-start | bytes 2359304 | tf_op jit(solution)/shard_map/ppermute | solution.py:89
  27.2 22.6 %copy-start.10 = (bf16[256,4096]{1,0:T(8,128)(2,1)S(1)}, bf16[256,4096]{1,0:T(8,128)(2,1)}, u32[]{:S(2)}) copy-start(bf16[256,4096]{1,0:T(8,128)(2,1)} %param.27) | copy-start | bytes 6291460
  71.9 23.9 %all-to-all-start = ((bf16[4,256,768]{2,1,0:T(8,128)(2,1)}), bf16[4,256,768]{2,1,0:T(8,128)(2,1)S(1)}, u32[]{:S(2)}, u32[]{:S(2)}) async-start(bf16[4,256,768]{2,1,0:T(8,128)(2,1)} %bitcast.97), calls=%async_computation | async-start | bytes 3145728 | tf_op jit(solution)/shard_map/all_to_all | solution.py:509
  114.9 104.7 %collective-permute-start.9 = (bf16[2048,1024]{1,0:T(8,128)(2,1)}, bf16[2048,1024]{1,0:T(8,128)(2,1)}, u32[]{:S(2)}, u32[]{:S(2)}) collective-permute-start(bf16[2048,1024]{1,0:T(8,128)(2,1)} %slice_dynamic-update-slice_fusion.refs_0_.refs_4_), channel_id=1, source_target_pairs={{0,2},{2,0},{1,3},{3,1},{4,6},{6,4},{5,7},{7,5},{8,10},{10,8},{9,1... | collective-permute-start | bytes 12582920 | tf_op jit(solution)/shard_map/ppermute | solution.py:1157
  123.2 12.3 %all-to-all-start.1 = ((bf16[4,256,256]{2,1,0:T(8,128)(2,1)}), bf16[4,256,256]{2,1,0:T(8,128)(2,1)S(1)}, u32[]{:S(2)}, u32[]{:S(2)}) async-start(bf16[4,256,256]{2,1,0:T(8,128)(2,1)} %bitcast.102), calls=%async_computation.1 | async-start | bytes 1048576 | tf_op jit(solution)/shard_map/all_to_all | solution.py:509
  135.5 29.0 %collective-permute-start.6 = (bf16[768,512]{1,0:T(8,128)(2,1)}, bf16[768,512]{1,0:T(8,128)(2,1)}, u32[]{:S(2)}, u32[]{:S(2)}) collective-permute-start(bf16[768,512]{1,0:T(8,128)(2,1)} %get-tuple-element.184), channel_id=1, source_target_pairs={{0,1},{1,0},{4,5},{5,4},{2,3},{3,2},{6,7},{7,6},{8,9},{9,8},{12,13... | collective-permute-start | bytes 2359304 | tf_op jit(solution)/shard_map/ppermute | solution.py:529
  135.5 30.2 %collective-permute-start.7 = (bf16[768,512]{1,0:T(8,128)(2,1)}, bf16[768,512]{1,0:T(8,128)(2,1)}, u32[]{:S(2)}, u32[]{:S(2)}) collective-permute-start(bf16[768,512]{1,0:T(8,128)(2,1)} %get-tuple-element.185), channel_id=1, source_target_pairs={{0,4},{1,5},{4,0},{5,1},{2,6},{3,7},{6,2},{7,3},{8,12},{9,13},{12,... | collective-permute-start | bytes 2359304 | tf_op jit(solution)/shard_map/ppermute | solution.py:529
  145.9 15.8 %all-to-all-start.2 = ((bf16[4,256,256]{2,1,0:T(8,128)(2,1)}), bf16[4,256,256]{2,1,0:T(8,128)(2,1)}, u32[]{:S(2)}, u32[]{:S(2)}) async-start(bf16[4,256,256]{2,1,0:T(8,128)(2,1)} %bitcast.108), calls=%async_computation.2 | async-start | bytes 1048576 | tf_op jit(solution)/shard_map/all_to_all | solution.py:509
  150.0 92.4 %all-gather.12.cloned.1.call-start = ((), (), s32[]{:S(2)}) async-start(), calls=%async_computation.12 | async-start | bytes 2621440 | tf_op jit(solution)/shard_map/all_gather | solution.py:149
  150.5 27.3 %collective-permute-start.8 = (bf16[768,512]{1,0:T(8,128)(2,1)}, bf16[768,512]{1,0:T(8,128)(2,1)}, u32[]{:S(2)}, u32[]{:S(2)}) collective-permute-start(bf16[768,512]{1,0:T(8,128)(2,1)} %get-tuple-element.186), channel_id=1, source_target_pairs={{0,5},{1,4},{4,1},{5,0},{2,7},{3,6},{6,3},{7,2},{8,13},{9,12},{12,... | collective-permute-start | bytes 2359304 | tf_op jit(solution)/shard_map/ppermute | solution.py:529
  164.3 84.6 %collective-permute-start.10 = (bf16[2048,1024]{1,0:T(8,128)(2,1)}, bf16[2048,1024]{1,0:T(8,128)(2,1)}, u32[]{:S(2)}, u32[]{:S(2)}) collective-permute-start(bf16[2048,1024]{1,0:T(8,128)(2,1)} %slice_dynamic-update-slice_fusion.refs_0_.refs_4_), channel_id=1, source_target_pairs={{0,1},{1,0},{2,3},{3,2},{4,5},{5,4},{6,7},{7,6},{8,9},{9,8},{10,11... | collective-permute-start | bytes 12582920 | tf_op jit(solution)/shard_map/ppermute | solution.py:1177
  206.3 19.6 %copy-start.20 = (bf16[2,128,1024]{2,1,0:T(8,128)(2,1)S(1)}, bf16[2,128,1024]{2,1,0:T(8,128)(2,1)}, u32[]{:S(2)}) copy-start(bf16[2,128,1024]{2,1,0:T(8,128)(2,1)} %param.21) | copy-start | bytes 1572868
  219.6 29.3 %collective-permute-start.11 = (bf16[2048,1024]{1,0:T(8,128)(2,1)}, bf16[2048,1024]{1,0:T(8,128)(2,1)}, u32[]{:S(2)}, u32[]{:S(2)}) collective-permute-start(bf16[2048,1024]{1,0:T(8,128)(2,1)} %collective-permute-done.9.refs_2_.refs_6_), channel_id=1, source_target_pairs={{0,1},{1,0},{2,3},{3,2},{4,5},{5,4},{6,7},{7,6},{8,9},{9,8},{10,11... | collective-permute-start | bytes 12582920 | tf_op jit(solution)/shard_map/ppermute | solution.py:1179
  222.4 13.1 %all-to-all-start.3 = ((bf16[4,256,256]{2,1,0:T(8,128)(2,1)}), bf16[4,256,256]{2,1,0:T(8,128)(2,1)S(1)}, u32[]{:S(2)}, u32[]{:S(2)}) async-start(bf16[4,256,256]{2,1,0:T(8,128)(2,1)} %bitcast.101), calls=%async_computation.3 | async-start | bytes 1048576 | tf_op jit(solution)/shard_map/all_to_all | solution.py:509
  225.9 3.4 collective-permute-start.12
  226.6 8.0 %collective-permute-start.13 = (bf16[128,1024]{1,0:T(8,128)(2,1)S(1)}, bf16[128,1024]{1,0:T(8,128)(2,1)S(1)}, u32[]{:S(2)}, u32[]{:S(2)}) collective-permute-start(bf16[128,1024]{1,0:T(8,128)(2,1)S(1)} %get-tuple-element.386), channel_id=1, source_target_pairs={{0,8},{1,24},{8,0},{9,16},{16,9},{17,25},{24,1},{25,17},{2,10},{3,... | collective-permute-start | bytes 786440 | tf_op jit(solution)/shard_map/ppermute | solution.py:89
  290.0 16.0 %all-to-all-start.4 = ((bf16[4,256,256]{2,1,0:T(8,128)(2,1)}), bf16[4,256,256]{2,1,0:T(8,128)(2,1)S(1)}, u32[]{:S(2)}, u32[]{:S(2)}) async-start(bf16[4,256,256]{2,1,0:T(8,128)(2,1)} %bitcast.107), calls=%async_computation.4 | async-start | bytes 1048576 | tf_op jit(solution)/shard_map/all_to_all | solution.py:509
  294.3 307.9 %reduce-scatter.2.cloned.1.call-start = ((), (), s32[]{:S(2)}) async-start(), calls=%async_computation.13 | async-start | bytes 17825792 | tf_op jit(solution)/shard_map/reduce_scatter | solution.py:785
  307.2 33.5 %collective-permute-start.14 = (bf16[128,1024]{1,0:T(8,128)(2,1)S(1)}, bf16[128,1024]{1,0:T(8,128)(2,1)S(1)}, u32[]{:S(2)}, u32[]{:S(2)}) collective-permute-start(bf16[128,1024]{1,0:T(8,128)(2,1)S(1)} %get-tuple-element.383), channel_id=1, source_target_pairs={{0,0},{16,1},{8,8},{24,9},{1,16},{17,17},{9,24},{25,25},{2,2},{18,... | collective-permute-start | bytes 786440 | tf_op jit(solution)/shard_map/ppermute | solution.py:95
  308.1 32.7 %collective-permute-start.15 = (bf16[128,1024]{1,0:T(8,128)(2,1)S(1)}, bf16[128,1024]{1,0:T(8,128)(2,1)S(1)}, u32[]{:S(2)}, u32[]{:S(2)}) collective-permute-start(bf16[128,1024]{1,0:T(8,128)(2,1)S(1)} %get-tuple-element.384), channel_id=1, source_target_pairs={{8,0},{24,1},{0,8},{16,9},{9,16},{25,17},{1,24},{17,25},{10,2},{26... | collective-permute-start | bytes 786440 | tf_op jit(solution)/shard_map/ppermute | solution.py:96
  366.8 12.3 %all-to-all-start.6 = ((bf16[4,256,256]{2,1,0:T(8,128)(2,1)}), bf16[4,256,256]{2,1,0:T(8,128)(2,1)S(1)}, u32[]{:S(2)}, u32[]{:S(2)}) async-start(bf16[4,256,256]{2,1,0:T(8,128)(2,1)} %bitcast.109), calls=%async_computation.6 | async-start | bytes 1048576 | tf_op jit(solution)/shard_map/all_to_all | solution.py:509
  379.0 41.0 %collective-permute-start.19 = (bf16[512,3072]{1,0:T(8,128)(2,1)}, bf16[512,3072]{1,0:T(8,128)(2,1)}, u32[]{:S(2)}, u32[]{:S(2)}) collective-permute-start(bf16[512,3072]{1,0:T(8,128)(2,1)} %get-tuple-element.263), channel_id=1, source_target_pairs={{0,1},{1,0},{2,3},{3,2},{4,5},{5,4},{6,7},{7,6},{8,9},{9,8},{10,11... | collective-permute-start | bytes 9437192 | tf_op jit(solution)/shard_map/ppermute | solution.py:628
  379.1 18.8 %collective-permute-start.16 = (bf16[768,512]{1,0:T(8,128)(2,1)}, bf16[768,512]{1,0:T(8,128)(2,1)S(1)}, u32[]{:S(2)}, u32[]{:S(2)}) collective-permute-start(bf16[768,512]{1,0:T(8,128)(2,1)} %get-tuple-element.258), channel_id=1, source_target_pairs={{0,1},{1,0},{4,5},{5,4},{2,3},{3,2},{6,7},{7,6},{8,9},{9,8},{12,13... | collective-permute-start | bytes 2359304 | tf_op jit(solution)/shard_map/ppermute | solution.py:529
  379.6 20.6 %collective-permute-start.17 = (bf16[768,512]{1,0:T(8,128)(2,1)}, bf16[768,512]{1,0:T(8,128)(2,1)S(1)}, u32[]{:S(2)}, u32[]{:S(2)}) collective-permute-start(bf16[768,512]{1,0:T(8,128)(2,1)} %get-tuple-element.259), channel_id=1, source_target_pairs={{0,4},{1,5},{4,0},{5,1},{2,6},{3,7},{6,2},{7,3},{8,12},{9,13},{12,... | collective-permute-start | bytes 2359304 | tf_op jit(solution)/shard_map/ppermute | solution.py:529
  380.9 34.3 %collective-permute-start.18 = (bf16[768,512]{1,0:T(8,128)(2,1)}, bf16[768,512]{1,0:T(8,128)(2,1)S(1)}, u32[]{:S(2)}, u32[]{:S(2)}) collective-permute-start(bf16[768,512]{1,0:T(8,128)(2,1)} %get-tuple-element.260), channel_id=1, source_target_pairs={{0,5},{1,4},{4,1},{5,0},{2,7},{3,6},{6,3},{7,2},{8,13},{9,12},{12,... | collective-permute-start | bytes 2359304 | tf_op jit(solution)/shard_map/ppermute | solution.py:529
  397.9 22.1 %copy-start.17 = (bf16[768,512]{1,0:T(8,128)(2,1)}, bf16[768,512]{1,0:T(8,128)(2,1)S(1)}, u32[]{:S(2)}) copy-start(bf16[768,512]{1,0:T(8,128)(2,1)S(1)} %collective-permute-done.16.refs_1_) | copy-start | bytes 2359300
  400.2 19.8 %copy-start.18 = (bf16[768,512]{1,0:T(8,128)(2,1)}, bf16[768,512]{1,0:T(8,128)(2,1)S(1)}, u32[]{:S(2)}) copy-start(bf16[768,512]{1,0:T(8,128)(2,1)S(1)} %collective-permute-done.17.refs_2_) | copy-start | bytes 2359300
  420.0 30.6 %all-to-all-start.7 = ((bf16[4,256,768]{2,1,0:T(8,128)(2,1)}), bf16[4,256,768]{2,1,0:T(8,128)(2,1)S(1)}, u32[]{:S(2)}, u32[]{:S(2)}) async-start(bf16[4,256,768]{2,1,0:T(8,128)(2,1)} %bitcast.95), calls=%async_computation.7 | async-start | bytes 3145728 | tf_op jit(solution)/shard_map/all_to_all | solution.py:509
  450.7 43.9 %collective-permute-start.24 = (bf16[512,2048]{1,0:T(8,128)(2,1)}, bf16[512,2048]{1,0:T(8,128)(2,1)}, u32[]{:S(2)}, u32[]{:S(2)}) collective-permute-start(bf16[512,2048]{1,0:T(8,128)(2,1)} %get-tuple-element.289), channel_id=1, source_target_pairs={{0,1},{1,0},{2,3},{3,2},{4,5},{5,4},{6,7},{7,6},{8,9},{9,8},{10,11... | collective-permute-start | bytes 6291464 | tf_op jit(solution)/shard_map/ppermute | solution.py:628
  454.8 47.0 %collective-permute-start.27 = (bf16[256,3072]{1,0:T(8,128)(2,1)}, bf16[256,3072]{1,0:T(8,128)(2,1)S(1)}, u32[]{:S(2)}, u32[]{:S(2)}) collective-permute-start(bf16[256,3072]{1,0:T(8,128)(2,1)} %slice.428), channel_id=1, source_target_pairs={{0,2},{2,0},{1,3},{3,1},{4,6},{6,4},{5,7},{7,5},{8,10},{10,8},{9,1... | collective-permute-start | bytes 4718600 | tf_op jit(solution)/shard_map/ppermute | solution.py:628
  472.6 24.5 %collective-permute-start.25 = (bf16[512,1536]{1,0:T(8,128)(2,1)}, bf16[512,1536]{1,0:T(8,128)(2,1)S(1)}, u32[]{:S(2)}, u32[]{:S(2)}) collective-permute-start(bf16[512,1536]{1,0:T(8,128)(2,1)} %get-tuple-element.283), channel_id=1, source_target_pairs={{0,1},{1,0},{2,3},{3,2},{4,5},{5,4},{6,7},{7,6},{8,9},{9,8},{10,11... | collective-permute-start | bytes 4718600 | tf_op jit(solution)/shard_map/ppermute | solution.py:628
  480.5 1.0 collective-permute-start.20
  481.3 11.2 %collective-permute-start.21 = (bf16[128,1024]{1,0:T(8,128)(2,1)S(1)}, bf16[128,1024]{1,0:T(8,128)(2,1)S(1)}, u32[]{:S(2)}, u32[]{:S(2)}) collective-permute-start(bf16[128,1024]{1,0:T(8,128)(2,1)S(1)} %get-tuple-element.380), channel_id=1, source_target_pairs={{8,0},{24,1},{0,8},{16,9},{9,16},{25,17},{1,24},{17,25},{10,2},{26... | collective-permute-start | bytes 786440 | tf_op jit(solution)/shard_map/ppermute | solution.py:96
  481.5 18.6 %collective-permute-start.26 = (bf16[512,1664]{1,0:T(8,128)(2,1)S(1)}, bf16[512,1664]{1,0:T(8,128)(2,1)S(1)}, u32[]{:S(2)}, u32[]{:S(2)}) collective-permute-start(bf16[512,1664]{1,0:T(8,128)(2,1)S(1)} %copy-done.36), channel_id=1, source_target_pairs={{0,1},{1,0},{2,3},{3,2},{4,5},{5,4},{6,7},{7,6},{8,9},{9,8},{10,11... | collective-permute-start | bytes 5111816 | tf_op jit(solution)/shard_map/ppermute | solution.py:628
  492.5 76.4 %collective-permute-start.22 = (bf16[384,1024]{1,0:T(8,128)(2,1)S(1)}, bf16[384,1024]{1,0:T(8,128)(2,1)S(1)}, u32[]{:S(2)}, u32[]{:S(2)}) collective-permute-start(bf16[384,1024]{1,0:T(8,128)(2,1)S(1)} %get-tuple-element.369), channel_id=1, source_target_pairs={{0,0},{16,1},{8,8},{24,9},{1,16},{17,17},{9,24},{25,25},{2,2},{18,... | collective-permute-start | bytes 2359304 | tf_op jit(solution)/shard_map/ppermute | solution.py:95
  494.6 74.3 %collective-permute-start.23 = (bf16[384,1024]{1,0:T(8,128)(2,1)S(1)}, bf16[384,1024]{1,0:T(8,128)(2,1)S(1)}, u32[]{:S(2)}, u32[]{:S(2)}) collective-permute-start(bf16[384,1024]{1,0:T(8,128)(2,1)S(1)} %get-tuple-element.370), channel_id=1, source_target_pairs={{8,0},{24,1},{0,8},{16,9},{9,16},{25,17},{1,24},{17,25},{10,2},{26... | collective-permute-start | bytes 2359304 | tf_op jit(solution)/shard_map/ppermute | solution.py:96
  497.1 17.9 %collective-permute-start.28 = (bf16[256,2048]{1,0:T(8,128)(2,1)S(1)}, bf16[256,2048]{1,0:T(8,128)(2,1)S(1)}, u32[]{:S(2)}, u32[]{:S(2)}) collective-permute-start(bf16[256,2048]{1,0:T(8,128)(2,1)S(1)} %slice.429), channel_id=1, source_target_pairs={{0,2},{2,0},{1,3},{3,1},{4,6},{6,4},{5,7},{7,5},{8,10},{10,8},{9,1... | collective-permute-start | bytes 3145736 | tf_op jit(solution)/shard_map/ppermute | solution.py:628
  500.1 31.8 %collective-permute-start.29 = (bf16[256,1536]{1,0:T(8,128)(2,1)S(1)}, bf16[256,1536]{1,0:T(8,128)(2,1)S(1)}, u32[]{:S(2)}, u32[]{:S(2)}) collective-permute-start(bf16[256,1536]{1,0:T(8,128)(2,1)S(1)} %slice.432), channel_id=1, source_target_pairs={{0,2},{2,0},{1,3},{3,1},{4,6},{6,4},{5,7},{7,5},{8,10},{10,8},{9,1... | collective-permute-start | bytes 2359304 | tf_op jit(solution)/shard_map/ppermute | solution.py:628
  501.8 31.9 %collective-permute-start.30 = (bf16[256,1664]{1,0:T(8,128)(2,1)S(1)}, bf16[256,1664]{1,0:T(8,128)(2,1)S(1)}, u32[]{:S(2)}, u32[]{:S(2)}) collective-permute-start(bf16[256,1664]{1,0:T(8,128)(2,1)S(1)} %slice.430), channel_id=1, source_target_pairs={{0,4},{4,0},{1,5},{5,1},{2,6},{6,2},{3,7},{7,3},{8,12},{12,8},{9,1... | collective-permute-start | bytes 2555912 | tf_op jit(solution)/shard_map/ppermute | solution.py:628
  515.0 19.4 %collective-permute-start.31 = (bf16[128,3072]{1,0:T(8,128)(2,1)S(1)}, bf16[128,3072]{1,0:T(8,128)(2,1)S(1)}, u32[]{:S(2)}, u32[]{:S(2)}) collective-permute-start(bf16[128,3072]{1,0:T(8,128)(2,1)S(1)} %slice.431), channel_id=1, source_target_pairs={{0,4},{4,0},{1,5},{5,1},{2,6},{6,2},{3,7},{7,3},{8,12},{12,8},{9,1... | collective-permute-start | bytes 2359304 | tf_op jit(solution)/shard_map/ppermute | solution.py:628
  531.9 14.8 %collective-permute-start.32 = (bf16[128,2048]{1,0:T(8,128)(2,1)S(1)}, bf16[128,2048]{1,0:T(8,128)(2,1)S(1)}, u32[]{:S(2)}, u32[]{:S(2)}) collective-permute-start(bf16[128,2048]{1,0:T(8,128)(2,1)S(1)} %slice.433), channel_id=1, source_target_pairs={{0,4},{4,0},{1,5},{5,1},{2,6},{6,2},{3,7},{7,3},{8,12},{12,8},{9,1... | collective-permute-start | bytes 1572872 | tf_op jit(solution)/shard_map/ppermute | solution.py:628
  533.7 21.4 %collective-permute-start.33 = (bf16[128,1536]{1,0:T(8,128)(2,1)S(1)}, bf16[128,1536]{1,0:T(8,128)(2,1)S(1)}, u32[]{:S(2)}, u32[]{:S(2)}) collective-permute-start(bf16[128,1536]{1,0:T(8,128)(2,1)S(1)} %slice.436), channel_id=1, source_target_pairs={{0,4},{4,0},{1,5},{5,1},{2,6},{6,2},{3,7},{7,3},{8,12},{12,8},{9,1... | collective-permute-start | bytes 1179656 | tf_op jit(solution)/shard_map/ppermute | solution.py:628
  534.5 20.8 %collective-permute-start.34 = (bf16[128,1664]{1,0:T(8,128)(2,1)S(1)}, bf16[128,1664]{1,0:T(8,128)(2,1)S(1)}, u32[]{:S(2)}, u32[]{:S(2)}) collective-permute-start(bf16[128,1664]{1,0:T(8,128)(2,1)S(1)} %slice.434), channel_id=1, source_target_pairs={{0,2},{2,0},{1,3},{3,1},{4,6},{6,4},{5,7},{7,5},{8,10},{10,8},{9,1... | collective-permute-start | bytes 1277960 | tf_op jit(solution)/shard_map/ppermute | solution.py:628
  546.7 8.7 %collective-permute-start.35 = (bf16[64,3072]{1,0:T(8,128)(2,1)S(1)}, bf16[64,3072]{1,0:T(8,128)(2,1)S(1)}, u32[]{:S(2)}, u32[]{:S(2)}) collective-permute-start(bf16[64,3072]{1,0:T(8,128)(2,1)S(1)} %slice.435), channel_id=1, source_target_pairs={{0,8},{8,0},{16,24},{24,16},{1,9},{9,1},{17,25},{25,17},{2,10},{10... | collective-permute-start | bytes 1179656 | tf_op jit(solution)/shard_map/ppermute | solution.py:627
  555.5 21.8 %collective-permute-start.41 = (bf16[32,3072]{1,0:T(8,128)(2,1)S(1)}, bf16[32,3072]{1,0:T(8,128)(2,1)S(1)}, u32[]{:S(2)}, u32[]{:S(2)}) collective-permute-start(bf16[32,3072]{1,0:T(8,128)(2,1)S(1)} %slice.439), channel_id=1, source_target_pairs={{0,16},{8,24},{16,0},{24,8},{1,17},{9,25},{17,1},{25,9},{2,18},{10... | collective-permute-start | bytes 589832 | tf_op jit(solution)/shard_map/ppermute | solution.py:627
  571.2 14.0 %collective-permute-start.36 = (bf16[64,2048]{1,0:T(8,128)(2,1)S(1)}, bf16[64,2048]{1,0:T(8,128)(2,1)S(1)}, u32[]{:S(2)}, u32[]{:S(2)}) collective-permute-start(bf16[64,2048]{1,0:T(8,128)(2,1)S(1)} %slice.437), channel_id=1, source_target_pairs={{0,8},{8,0},{16,24},{24,16},{1,9},{9,1},{17,25},{25,17},{2,10},{10... | collective-permute-start | bytes 786440 | tf_op jit(solution)/shard_map/ppermute | solution.py:627
  572.5 15.8 %collective-permute-start.37 = (bf16[64,1536]{1,0:T(8,128)(2,1)S(1)}, bf16[64,1536]{1,0:T(8,128)(2,1)S(1)}, u32[]{:S(2)}, u32[]{:S(2)}) collective-permute-start(bf16[64,1536]{1,0:T(8,128)(2,1)S(1)} %slice.440), channel_id=1, source_target_pairs={{0,8},{8,0},{16,24},{24,16},{1,9},{9,1},{17,25},{25,17},{2,10},{10... | collective-permute-start | bytes 589832 | tf_op jit(solution)/shard_map/ppermute | solution.py:627
  573.2 17.4 %collective-permute-start.39 = (bf16[64,1664]{1,0:T(8,128)(2,1)S(1)}, bf16[64,1664]{1,0:T(8,128)(2,1)S(1)}, u32[]{:S(2)}, u32[]{:S(2)}) collective-permute-start(bf16[64,1664]{1,0:T(8,128)(2,1)S(1)} %slice.438), channel_id=1, source_target_pairs={{0,8},{8,0},{16,24},{24,16},{1,9},{9,1},{17,25},{25,17},{2,10},{10... | collective-permute-start | bytes 638984 | tf_op jit(solution)/shard_map/ppermute | solution.py:627
  585.3 19.8 %collective-permute-start.42 = (bf16[32,2048]{1,0:T(8,128)(2,1)S(1)}, bf16[32,2048]{1,0:T(8,128)(2,1)S(1)}, u32[]{:S(2)}, u32[]{:S(2)}) collective-permute-start(bf16[32,2048]{1,0:T(8,128)(2,1)S(1)} %slice.441), channel_id=1, source_target_pairs={{0,16},{8,24},{16,0},{24,8},{1,17},{9,25},{17,1},{25,9},{2,18},{10... | collective-permute-start | bytes 393224 | tf_op jit(solution)/shard_map/ppermute | solution.py:627
  588.4 10.4 %collective-permute-start.38 = (bf16[32,1536]{1,0:T(8,128)(2,1)S(1)}, bf16[32,1536]{1,0:T(8,128)(2,1)S(1)}, u32[]{:S(2)}, u32[]{:S(2)}) collective-permute-start(bf16[32,1536]{1,0:T(8,128)(2,1)S(1)} %slice.443), channel_id=1, source_target_pairs={{0,16},{8,24},{16,0},{24,8},{1,17},{9,25},{17,1},{25,9},{2,18},{10... | collective-permute-start | bytes 294920 | tf_op jit(solution)/shard_map/ppermute | solution.py:627
  590.7 9.2 %collective-permute-start.40 = (bf16[32,1664]{1,0:T(8,128)(2,1)S(1)}, bf16[32,1664]{1,0:T(8,128)(2,1)S(1)}, u32[]{:S(2)}, u32[]{:S(2)}) collective-permute-start(bf16[32,1664]{1,0:T(8,128)(2,1)S(1)} %slice.442), channel_id=1, source_target_pairs={{0,16},{8,24},{16,0},{24,8},{1,17},{9,25},{17,1},{25,9},{2,18},{10... | collective-permute-start | bytes 319496 | tf_op jit(solution)/shard_map/ppermute | solution.py:627
  603.2 12.1 %collective-permute-start.43 = (bf16[8,32,1024]{2,1,0:T(8,128)(2,1)S(1)}, bf16[8,32,1024]{2,1,0:T(8,128)(2,1)S(1)}, u32[]{:S(2)}, u32[]{:S(2)}) collective-permute-start(bf16[8,32,1024]{2,1,0:T(8,128)(2,1)S(1)} %dynamic-slice_bitcast_fusion.2), channel_id=1, source_target_pairs={{0,4},{4,0},{1,5},{5,1},{2,6},{6,2},{3,7},{7,3},{8,12},{12,8},{9,1... | collective-permute-start | bytes 1572872 | tf_op jit(solution)/shard_map/ppermute | solution.py:628
  (31 other events, 192.2 us)
Sparse Core Ops, SparseCore 0:
  9.6 49.3 all-gather.5
  60.5 34.4 all-gather.7
  96.6 43.9 all-gather.9
  219.7 22.6 all-gather.11
  306.1 180.4 reduce-scatter.1

commit v3 on v2

--- a/solution.py
+++ b/solution.py
@@ -47,12 +47,6 @@
     return (grad_resid, jnp.sum(grad_out * normed, 0), jnp.sum(grad_out, 0))
 
 
-def gelu_slope(values):
-    cumulative = 0.5 * (1.0 + lax.erf(values * 0.7071067811865476))
-    density = jnp.exp(-0.5 * values * values) * 0.3989422804014327
-    return cumulative + values * density
-
-
 def column_sum(left, right):
     return lax.dot_general(
         left, right, (((0,), (0,)), ((), ())), preferred_element_type=jnp.float32
@@ -90,14 +84,20 @@
     )
 
 
-def from_packs(first, second):
-    straight, crossed = pack_routes()
-    first = lax.ppermute(first, ("t", "core"), [(to, source) for source, to in straight])
-    second = lax.ppermute(second, ("t", "core"), [(to, source) for source, to in crossed])
+def send_back(part, place):
+    route = pack_routes()[place]
+    return lax.ppermute(part, ("t", "core"), [(to, source) for source, to in route])
+
+
+def order_back(first, second):
     parity = lax.axis_index("t") & 1
     return jnp.stack(
         [jnp.where(parity == 0, first, second), jnp.where(parity == 0, second, first)], 0
     )
+
+
+def from_packs(first, second):
+    return order_back(send_back(first, 0), send_back(second, 1))
 
 
 def group_route(step):
@@ -139,10 +139,6 @@
         compiler_params=pltpu.CompilerParams(vmem_limit_bytes=VMEM_LIMIT),
         cost_estimate=COST,
     )(*scalars, *operands)
-
-
-def gelu(values):
-    return 0.5 * values * (1.0 + lax.erf(values * 0.7071067811865476))
 
 
 def fetch(weight):
@@ -218,8 +214,7 @@
 
 def project_heads(rows, weight, bias):
     shape = jax.ShapeDtypeStruct((rows.shape[0] * MEMBERS, weight.shape[1] // MEMBERS), jnp.bfloat16)
-    work = 2 * rows.shape[0] * weight.size
-    return small_kernel(heads_kernel, [], [rows, weight, bias[None, :]], [shape], work)[0]
+    return small_kernel(heads_kernel, [], [rows, weight, bias[None, :]], [shape])[0]
 
 
 def own_heads_kernel(me_ref, rows_ref, weight_ref, bias_ref, *outs):
@@ -284,14 +279,16 @@
 
 
 def up_kernel(me_ref, rows_ref, *refs):
-    shards, (bias_ref, active_ref, hidden_ref) = refs[:MEMBERS], refs[MEMBERS:]
+    shards, (bias_ref, slope_ref, hidden_ref) = refs[:MEMBERS], refs[MEMBERS:]
     depth = shards[0].shape[0]
     active = bias_ref[...]
     for index, shard in enumerate(shards):
         start = pl.multiple_of((me_ref[0] ^ index) * depth, depth)
         active = active + linear(rows_ref[:, pl.ds(start, depth)], shard[...])
-    active_ref[...] = active
-    hidden_ref[...] = gelu(active).astype(jnp.bfloat16)
+    cumulative = 0.5 * (1.0 + lax.erf(active * 0.7071067811865476))
+    density = jnp.exp(-0.5 * active * active) * 0.3989422804014327
+    slope_ref[...] = cumulative + active * density
+    hidden_ref[...] = (active * cumulative).astype(jnp.bfloat16)
 
 
 def feed_up_gelu(rows, shards, bias):
@@ -393,7 +390,7 @@
     )(shard_index(), hidden, *shards, *fixed)
 
 
-def feed_back_kernel(tiles, me_ref, active_ref, *refs):
+def feed_back_kernel(tiles, me_ref, slope_ref, *refs):
     downs, ups, refs = refs[:MEMBERS], refs[MEMBERS : 2 * MEMBERS], refs[2 * MEMBERS :]
     grads_ref, resid_ref, unit_ref, inverse_ref, gain_ref, out_ref = refs[:6]
     du_ref, bias_ref, next_resid_ref, next_low_ref, sums_ref, heads_ref, total_ref = refs[6:]
@@ -404,7 +401,7 @@
     def _():
         total_ref[...] = RESIDUAL * resid_ref[...]
 
-    slope = gelu_slope(active_ref[...])
+    slope = slope_ref[...]
     for index, shard in enumerate(downs):
 
         @pl.when(step // tiles == index)
@@ -426,8 +423,8 @@
         put_back_heads(next_low_ref, out_ref, heads_ref)
 
 
-def feed_back(active, shards, grads, resid, unit, inverse, gain, out_weight):
-    count, width = active.shape
+def feed_back(slope, shards, grads, resid, unit, inverse, gain, out_weight):
+    count, width = slope.shape
     tiles = D // FEED_TILE
     fixed = [grads, resid, unit, inverse, gain[None, :], out_weight]
     column = lambda i, p: (0, feed_column(i, p[0], tiles))
@@ -457,7 +454,7 @@
         out_shape=outs,
         compiler_params=pltpu.CompilerParams(vmem_limit_bytes=VMEM_LIMIT),
         cost_estimate=COST,
-    )(shard_index(), active, *shards, *shards, *fixed)
+    )(shard_index(), slope, *shards, *shards, *fixed)
 
 
 def norm_back_kernel(
@@ -484,11 +481,12 @@
     )
 
 
-def back_kernel(grads_ref, weight_ref, out_ref):
-    out_ref[...] = back_product(grads_ref, weight_ref).astype(out_ref.dtype)
-
-
-def back_project(grads, weight, dtype=jnp.bfloat16):
+def back_kernel(grads_ref, weight_ref, resid_ref, out_ref):
+    value = RESIDUAL * resid_ref[...] + back_product(grads_ref, weight_ref)
+    out_ref[...] = value.astype(out_ref.dtype)
+
+
+def back_project(grads, weight, resid):
     count, width = grads.shape
     rows = 256
     return pl.pallas_call(
@@ -497,12 +495,13 @@
         in_specs=[
             pl.BlockSpec((count, width), lambda i: (0, 0)),
             pl.BlockSpec((rows, width), lambda i: (i, 0)),
+            pl.BlockSpec((count, rows), lambda i: (0, i)),
         ],
         out_specs=pl.BlockSpec((count, rows), lambda i: (0, i)),
-        out_shape=jax.ShapeDtypeStruct((count, weight.shape[0]), dtype),
+        out_shape=jax.ShapeDtypeStruct((count, weight.shape[0]), jnp.bfloat16),
         compiler_params=pltpu.CompilerParams(vmem_limit_bytes=VMEM_LIMIT),
         cost_estimate=COST,
-    )(grads, weight)
+    )(grads, weight, resid)
 
 
 def to_members(blocks):
@@ -541,14 +540,6 @@
     blocks, inputs = chain(blocks, inputs)
     results, received = chain(work(*inputs), to_members(blocks))
     return received, results
-
-
-def join_heads(blocks, me):
-    rows, parts = blocks[0].shape[0], blocks[0].shape[1] // WIDTH
-    shape = jax.ShapeDtypeStruct((rows, parts * D), blocks[0].dtype)
-    return small_kernel(
-        functools.partial(join_kernel, parts), [me], blocks, [shape]
-    )[0]
 
 
 def cut(matrix):
@@ -585,6 +576,21 @@
         put_unsorted(rank_ref[lines, :], refs[:-1], blocks_ref, lines)
 
 
+def unsort_blocks_kernel(me_ref, rank_ref, *refs):
+    for step, block_ref in enumerate(refs[-MEMBERS:]):
+        rows = block_ref.shape[0]
+        start = pl.multiple_of((me_ref[0] ^ step) * rows, rows)
+        put_unsorted(rank_ref[pl.ds(start, rows), :], refs[:-MEMBERS], block_ref, slice(None))
+
+
+def unsort_blocks(parts, rank):
+    rows, width = parts[0].shape[0] // MEMBERS, sum(part.shape[1] for part in parts)
+    shape = jax.ShapeDtypeStruct((rows, width), jnp.bfloat16)
+    return small_kernel(
+        unsort_blocks_kernel, [group_index()[None]], [rank[:, None], *parts], [shape] * MEMBERS
+    )
+
+
 def sort_rows(blocks, rank):
     shape = jax.ShapeDtypeStruct(blocks.shape, jnp.bfloat16)
     work = 2 * blocks.size * blocks.shape[0]
@@ -596,6 +602,20 @@
     shape = jax.ShapeDtypeStruct((parts[0].shape[0], width), jnp.bfloat16)
     work = 2 * shape.size * shape.shape[0]
     return small_kernel(unsort_kernel, [], [rank[:, None], *parts], [shape], work)[0]
+
+
+def assemble_kernel(places_ref, *refs):
+    blocks, whole_ref = refs[:-1], refs[-1]
+    for place, block_ref in enumerate(blocks):
+        size = block_ref.shape[0] // 2
+        for half in range(2):
+            start = pl.multiple_of(places_ref[2 * place + half], 128)
+            whole_ref[pl.ds(start, size), :] = block_ref[half * size : (half + 1) * size, :]
+
+
+def assemble(blocks, places):
+    shape = jax.ShapeDtypeStruct((len(blocks) * blocks[0].shape[0], blocks[0].shape[1]), jnp.bfloat16)
+    return small_kernel(assemble_kernel, [places], blocks, [shape])[0]
 
 
 def gather_sequence(matrix, count):
@@ -657,34 +677,82 @@
     return start
 
 
-def grads_kernel(count, *refs):
-    put_grads([(refs[i], refs[count + i][...]) for i in range(count)], refs[-2:])
-
-
-def weight_grads(lefts, rights):
-    half = lefts[0].shape[1] // 2
-    shape = jax.ShapeDtypeStruct((half, sum(right.shape[1] for right in rights)), jnp.bfloat16)
-    return small_kernel(
-        functools.partial(grads_kernel, len(lefts)), [], [*lefts, *rights], [shape] * 2
-    )
+def total_rows(rows):
+    return jnp.sum(rows.astype(jnp.float32), 0, keepdims=True)
+
+
+def three_kernel(
+    out_left, query_left, cross_left, out_grads, query_blocks, cross_grads,
+    sent_ref, kept_ref, sums_ref, columns_ref,
+):
+    rows = columns_ref.shape[0]
+    for member in range(MEMBERS):
+        columns_ref[:, member * WIDTH : (member + 1) * WIDTH] = query_blocks[
+            member * rows : (member + 1) * rows, :
+        ]
+    pairs = [(out_left, out_grads), (query_left, columns_ref), (cross_left, cross_grads)]
+    put_grads([(left, right[...]) for left, right in pairs], [sent_ref, kept_ref])
+    sums_ref[...] = total_rows(columns_ref[...])
+
+
+def three_grads(out_left, query_left, cross_left, out_grads, query_blocks, cross_grads):
+    operands = [out_left, query_left, cross_left, out_grads, query_blocks, cross_grads]
+    return pl.pallas_call(
+        three_kernel,
+        in_specs=in_vmem(6),
+        out_specs=in_vmem(3),
+        out_shape=[jax.ShapeDtypeStruct((D // 2, 3 * D), jnp.bfloat16)] * 2
+        + [jax.ShapeDtypeStruct((1, D), jnp.float32)],
+        scratch_shapes=[pltpu.VMEM(out_grads.shape, jnp.bfloat16)],
+        compiler_params=pltpu.CompilerParams(vmem_limit_bytes=VMEM_LIMIT),
+        cost_estimate=COST,
+    )(*operands)
+
+
+def encoder_kernel(
+    me_ref, left_ref, weight_ref, *refs
+):
+    blocks, refs = refs[:MEMBERS], refs[MEMBERS:]
+    sent_ref, kept_ref, first_ref, second_ref, sums_ref, grads_ref = refs
+    join_kernel(2, me_ref, *blocks, grads_ref)
+    put_grads([(left_ref, grads_ref[...])], [sent_ref, kept_ref])
+    half = first_ref.shape[0]
+    first_ref[...] = input_grad(grads_ref[:half, :], weight_ref[...]).astype(jnp.bfloat16)
+    second_ref[...] = input_grad(grads_ref[half:, :], weight_ref[...]).astype(jnp.bfloat16)
+    sums_ref[...] = total_rows(grads_ref[:, D:])
+
+
+def encoder_grads(me, left, weight, blocks):
+    rows = left.shape[0]
+    return pl.pallas_call(
+        encoder_kernel,
+        in_specs=[pl.BlockSpec(memory_space=pltpu.SMEM)] + in_vmem(2 + MEMBERS),
+        out_specs=in_vmem(5),
+        out_shape=[jax.ShapeDtypeStruct((D // 2, 2 * D), jnp.bfloat16)] * 2
+        + [jax.ShapeDtypeStruct((rows // 2, D), jnp.bfloat16)] * 2
+        + [jax.ShapeDtypeStruct((1, D), jnp.float32)],
+        scratch_shapes=[pltpu.VMEM((rows, 2 * D), jnp.bfloat16)],
+        compiler_params=pltpu.CompilerParams(vmem_limit_bytes=VMEM_LIMIT),
+        cost_estimate=COST,
+    )(me, left, weight, *blocks)
 
 
 def self_in_kernel(
-    left_ref, right_ref, grads_ref, pick_ref, one_ref, two_ref, three_ref, up_ref, query_ref,
-    pair_ref, left_sent, left_kept, right_sent, right_kept, small_ref,
+    me_ref, left_ref, right_ref, pick_ref, one_ref, two_ref, three_ref, up_ref, query_ref,
+    value_ref, *refs
 ):
+    blocks, refs = refs[:MEMBERS], refs[MEMBERS:]
+    left_sent, left_kept, right_sent, right_kept, grads_ref, small_ref = refs
+    join_kernel(3, me_ref, *blocks, grads_ref)
     middle = grads_ref.shape[1] // 2
     put_grads([(left_ref, grads_ref[:, :middle])], [left_sent, left_kept])
     start = put_grads([(right_ref, grads_ref[:, middle:])], [right_sent, right_kept])
 
-    def total(rows):
-        return jnp.sum(rows.astype(jnp.float32), 0, keepdims=True)
-
     small_ref[...] = jnp.zeros_like(small_ref)
     rows = [one_ref[0:1, :], two_ref[0:1, :], three_ref[0:1, :]]
     rows += [one_ref[1:2, :], two_ref[1:2, :], three_ref[1:2, :]]
-    rows += [total(grads_ref[:, :D]), total(grads_ref[:, 2 * D :]), total(query_ref[...])]
-    rows += [total(pair_ref[:, D:]), two_ref[2:3, :], three_ref[2:3, :], one_ref[2:3, :]]
+    rows += [total_rows(grads_ref[:, :D]), total_rows(grads_ref[:, 2 * D :]), query_ref[...]]
+    rows += [value_ref[...], two_ref[2:3, :], three_ref[2:3, :], one_ref[2:3, :]]
     for place, row in enumerate(rows):
         small_ref[place : place + 1, :] = row
     small_ref[13:17, :] = up_ref[...]
@@ -694,21 +762,23 @@
         out_ref[:, start:] = input_grad(pick_ref[lines, :], low).astype(jnp.bfloat16)
 
 
-def self_in_grads(left, right, grads, pick, one, two, three, up, query, pair):
-    half, middle = D // 2, grads.shape[1] // 2
+def self_in_grads(me, left, right, pick, one, two, three, up, query, value, blocks):
+    rows = left.shape[0]
+    half, middle = D // 2, 3 * D // 2
     outs = [jax.ShapeDtypeStruct((half, middle), jnp.bfloat16)] * 2
     outs += [jax.ShapeDtypeStruct((half, middle + 128), jnp.bfloat16)] * 2
-    operands = [left, right, grads, pick, one, two, three, up.reshape(D, 4).T, query, pair]
+    outs += [jax.ShapeDtypeStruct((rows, 3 * D), jnp.bfloat16)]
+    operands = [left, right, pick, one, two, three, up.reshape(D, 4).T, query, value, *blocks]
     results = pl.pallas_call(
         self_in_kernel,
-        in_specs=in_vmem(len(operands)),
+        in_specs=[pl.BlockSpec(memory_space=pltpu.SMEM)] + in_vmem(len(operands)),
         out_specs=in_vmem(len(outs)),
         out_shape=outs,
         scratch_shapes=[pltpu.VMEM((128, D), jnp.float32)],
         compiler_params=pltpu.CompilerParams(vmem_limit_bytes=VMEM_LIMIT),
         cost_estimate=COST,
-    )(*operands)
-    return results[:2], results[2:]
+    )(me, *operands)
+    return results[:2], results[2:4], results[4]
 
 
 class Halving:
@@ -787,35 +857,31 @@
 
 def split_feed(halves):
     mine = lax.axis_index("y")
-    keep = lax.dynamic_index_in_dim(halves, mine, 0, keepdims=False)
-    sent = lax.dynamic_index_in_dim(halves, 1 - mine, 0, keepdims=False)
-    total = keep.astype(jnp.float32) + flip(sent, "y").astype(jnp.float32)
+    return [
+        lax.dynamic_index_in_dim(halves, place, 0, keepdims=False) for place in (mine, 1 - mine)
+    ]
+
+
+def merge_feed(kept, arrived):
+    total = kept.astype(jnp.float32) + arrived.astype(jnp.float32)
     return jnp.concatenate([total[4 + part] for part in range(4)], 1), total[:4].reshape(-1, D)
 
 
 def forward_kernel(
     chunk, flags_ref, q_ref, k_ref, v_ref, low_ref, high_ref, key_ref, out_ref, exact_ref, log_ref,
-    masked_ref, turned_ref, top_ref, sum_ref, total_ref,
+    masked_ref, top_ref, sum_ref, fade_ref, total_ref,
 ):
     step = pl.program_id(0)
     chunks = k_ref.shape[0] // chunk
     rows = q_ref.shape[0]
     lane = lax.broadcasted_iota(jnp.int32, (rows, 128), 1)
-
-    @pl.when(step == 0)
-    def _():
-        def turn(index, carry):
-            start = pl.multiple_of(index * chunk, chunk)
-            turned_ref[:, pl.ds(start, chunk)] = v_ref[pl.ds(start, chunk), :].T
-            return carry
-
-        lax.fori_loop(0, chunks, turn, 0)
-
     for head in range(HEADS):
         pair = q_ref[:, (head // 2) * 128 : (head // 2 + 1) * 128] * SCALE
         masked_ref[head] = jnp.where((lane >= HD) == (head % 2 == 1), pair, 0).astype(jnp.bfloat16)
     top_ref[...] = jnp.full_like(top_ref, MASKED)
-    sum_ref[...] = jnp.zeros_like(sum_ref)
+    sum_ref[...] = jnp.ones_like(sum_ref)
+    sum_ref[:HEADS, :] = jnp.zeros((HEADS, rows), jnp.float32)
+    fade_ref[...] = jnp.zeros_like(fade_ref)
     total_ref[...] = jnp.zeros_like(total_ref)
 
     def one_chunk(index, carry):
@@ -826,38 +892,52 @@
             keys = key_ref[here, :]
             allow = (keys >= low_ref[...]) & (keys <= high_ref[...])
             bias = jnp.where(allow, 0.0, MASKED)
-            for head in range(HEADS):
-                columns = slice((head // 2) * 128, (head // 2 + 1) * 128)
-                lines = slice(head * HD, (head + 1) * HD)
-                scores = lax.dot_general(
-                    k_ref[here, columns],
+            def pair_of(head):
+                return slice((head // 2) * 128, (head // 2 + 1) * 128)
+
+            scores = [
+                lax.dot_general(
+                    k_ref[here, pair_of(head)],
                     masked_ref[head],
                     (((1,), (1,)), ((), ())),
                     preferred_element_type=jnp.float32,
                 ) + bias
-                before = top_ref[head : head + 1, :]
-                after = jnp.maximum(before, jnp.max(scores, 0, keepdims=True))
-                exponent = jnp.exp(scores - after)
-                fade = jnp.exp(before - after)
-                top_ref[head : head + 1, :] = after
+                for head in range(HEADS)
+            ]
+            befores = [top_ref[head : head + 1, :] for head in range(HEADS)]
+            afters = [
+                jnp.maximum(before, jnp.max(score, 0, keepdims=True))
+                for before, score in zip(befores, scores)
+            ]
+            exponents = [jnp.exp(score - after) for score, after in zip(scores, afters)]
+            chances = [exponent.astype(jnp.bfloat16) for exponent in exponents]
+            for head in range(HEADS):
+                fade = jnp.exp(befores[head] - afters[head])
+                top_ref[head : head + 1, :] = afters[head]
+                fade_ref[head : head + 1, :] = fade
                 sum_ref[head : head + 1, :] = sum_ref[head : head + 1, :] * fade + jnp.sum(
-                    exponent, 0, keepdims=True
+                    exponents[head], 0, keepdims=True
                 )
-                total_ref[lines, :] = total_ref[lines, :] * fade + jnp.dot(
-                    turned_ref[lines, here],
-                    exponent.astype(jnp.bfloat16),
-                    preferred_element_type=jnp.float32,
+            fades = fade_ref[...].T
+            for head in range(HEADS):
+                columns = slice((head // 2) * 128, (head // 2 + 1) * 128)
+                total_ref[head] = total_ref[head] * fades[:, head : head + 1] + column_sum(
+                    chances[head], v_ref[here, columns]
                 )
 
         return carry
 
     lax.fori_loop(0, chunks, one_chunk, 0)
-    for head in range(HEADS):
-        lines = slice(head * HD, (head + 1) * HD)
-        total_ref[lines, :] = total_ref[lines, :] / sum_ref[head : head + 1, :]
-    exact = total_ref[...].T
-    exact_ref[...] = exact
-    out_ref[...] = exact.astype(jnp.bfloat16)
+    shares = (1.0 / sum_ref[...]).T
+    for head in range(0, HEADS, 2):
+        columns = slice((head // 2) * 128, (head // 2 + 1) * 128)
+        exact = jnp.where(
+            lane < HD,
+            total_ref[head] * shares[:, head : head + 1],
+            total_ref[head + 1] * shares[:, head + 1 : head + 2],
+        )
+        exact_ref[:, columns] = exact
+        out_ref[:, columns] = exact.astype(jnp.bfloat16)
     log_ref[:HEADS, :] = top_ref[:HEADS, :] + jnp.log(sum_ref[:HEADS, :])
     log_ref[HEADS:, :] = jnp.zeros((8 - HEADS, rows), jnp.float32)
 
@@ -885,10 +965,10 @@
             ],
             scratch_shapes=[
                 pltpu.VMEM((HEADS, block, 128), jnp.bfloat16),
-                pltpu.VMEM((WIDTH, depth), jnp.bfloat16),
                 pltpu.VMEM((8, block), jnp.float32),
                 pltpu.VMEM((8, block), jnp.float32),
-                pltpu.VMEM((WIDTH, block), jnp.float32),
+                pltpu.VMEM((8, block), jnp.float32),
+                pltpu.VMEM((HEADS, block, 128), jnp.float32),
             ],
         ),
         out_shape=[
@@ -905,7 +985,7 @@
 
 
 def backward_kernel(
-    chunk, flags_ref, q_ref, k_ref, v_ref, g_ref, log_ref, exact_ref, low_ref, high_ref, key_ref,
+    chunk, flags_ref, places_ref, q_ref, k_ref, v_ref, g_ref, log_ref, exact_ref, low_ref, high_ref, key_ref,
     dq_ref, *refs,
 ):
     pair_refs, (q_masked, g_masked, delta_ref, turned_ref, dq_sum, dk_sum, dv_sum) = (
@@ -952,33 +1032,36 @@
             keys = key_ref[here, :]
             allow = (keys >= low_ref[...]) & (keys <= high_ref[...])
             bias = jnp.where(allow, 0.0, MASKED)
-            for head in range(HEADS):
-                columns = slice((head // 2) * 128, (head // 2 + 1) * 128)
-                scores = lax.dot_general(
-                    k_ref[here, columns],
-                    q_masked[head],
+
+            def pair_of(head):
+                return slice((head // 2) * 128, (head // 2 + 1) * 128)
+
+            def against(keys_ref, head, masked):
+                return lax.dot_general(
+                    keys_ref[here, pair_of(head)],
+                    masked[head],
                     (((1,), (1,)), ((), ())),
                     preferred_element_type=jnp.float32,
                 )
-                chances = jnp.exp(scores + bias - log_ref[head : head + 1, :])
-                grads = lax.dot_general(
-                    v_ref[here, columns],
-                    g_masked[head],
-                    (((1,), (1,)), ((), ())),
-                    preferred_element_type=jnp.float32,
-                )
-                slopes = (chances * (grads - delta_ref[head : head + 1, :])).astype(jnp.bfloat16)
-                dk_sum[here, columns] += jnp.dot(
-                    slopes, q_masked[head], preferred_element_type=jnp.float32
-                )
-                dv_sum[here, columns] += jnp.dot(
-                    chances.astype(jnp.bfloat16), g_masked[head], preferred_element_type=jnp.float32
-                )
-                dq_sum[head * HD : (head + 1) * HD, :] += jnp.dot(
-                    turned_ref[head * HD : (head + 1) * HD, here],
-                    slopes,
-                    preferred_element_type=jnp.float32,
-                )
+
+            heads = range(HEADS)
+            scores = [against(k_ref, head, q_masked) for head in heads]
+            grads = [against(v_ref, head, g_masked) for head in heads]
+            chances = [
+                jnp.exp(scores[head] + bias - log_ref[head : head + 1, :]) for head in heads
+            ]
+            slopes = [
+                (chances[head] * (grads[head] - delta_ref[head : head + 1, :])).astype(jnp.bfloat16)
+                for head in heads
+            ]
+            chances = [chance.astype(jnp.bfloat16) for chance in chances]
+            for head in heads:
+                dv_sum[here, pair_of(head)] += linear(chances[head], g_masked[head])
+            for head in heads:
+                dk_sum[here, pair_of(head)] += linear(slopes[head], q_masked[head])
+            for head in heads:
+                lines = slice(head * HD, (head + 1) * HD)
+                dq_sum[lines, :] += linear(turned_ref[lines, here], slopes[head])
 
         return carry
 
@@ -988,37 +1071,40 @@
     @pl.when(step == pl.num_programs(0) - 1)
     def _():
         for place, pair_ref in enumerate(pair_refs):
-            size = pair_ref.shape[0]
-            lines = slice(place * size, (place + 1) * size)
-            pair_ref[:, :WIDTH] = dk_sum[lines, :].astype(jnp.bfloat16)
-            pair_ref[:, WIDTH:] = dv_sum[lines, :].astype(jnp.bfloat16)
+            size = pair_ref.shape[0] // 2
+            for half in range(2):
+                start = pl.multiple_of(places_ref[2 * place + half], 128)
+                lines = slice(half * size, (half + 1) * size)
+                pair_ref[lines, :WIDTH] = dk_sum[pl.ds(start, size), :].astype(jnp.bfloat16)
+                pair_ref[lines, WIDTH:] = dv_sum[pl.ds(start, size), :].astype(jnp.bfloat16)
 
 
 def attend_backward(
-    queries, keys, values, grads, logs, exact, low, high, key_ids, flags, block, chunk, splits
+    queries, keys, values, grads, logs, exact, low, high, key_ids, flags, block, chunk, places
 ):
+    splits = places.shape[0] // 2
     count, depth = queries[0].shape[0], keys[0].shape[0]
     whole = functools.partial(pl.BlockSpec, pipeline_mode=pl.Buffered(1))
     return pl.pallas_call(
         functools.partial(backward_kernel, chunk),
         grid_spec=pltpu.PrefetchScalarGridSpec(
-            num_scalar_prefetch=1,
+            num_scalar_prefetch=2,
             grid=(count // block,),
             in_specs=[
-                pl.BlockSpec((block, WIDTH), lambda i, f, c=queries[1]: (i, c)),
-                whole((depth, WIDTH), lambda i, f, c=keys[1]: (0, c)),
-                whole((depth, WIDTH), lambda i, f, c=values[1]: (0, c)),
-                pl.BlockSpec((block, WIDTH), lambda i, f: (i, 0)),
-                pl.BlockSpec((8, block), lambda i, f: (0, i)),
-                pl.BlockSpec((block, WIDTH), lambda i, f: (i, 0)),
-                pl.BlockSpec((1, block), lambda i, f: (0, i)),
-                pl.BlockSpec((1, block), lambda i, f: (0, i)),
-                whole((depth, 1), lambda i, f: (0, 0)),
+                pl.BlockSpec((block, WIDTH), lambda i, f, p, c=queries[1]: (i, c)),
+                whole((depth, WIDTH), lambda i, f, p, c=keys[1]: (0, c)),
+                whole((depth, WIDTH), lambda i, f, p, c=values[1]: (0, c)),
+                pl.BlockSpec((block, WIDTH), lambda i, f, p: (i, 0)),
+                pl.BlockSpec((8, block), lambda i, f, p: (0, i)),
+                pl.BlockSpec((block, WIDTH), lambda i, f, p: (i, 0)),
+                pl.BlockSpec((1, block), lambda i, f, p: (0, i)),
+                pl.BlockSpec((1, block), lambda i, f, p: (0, i)),
+                whole((depth, 1), lambda i, f, p: (0, 0)),
             ],
             out_specs=[
-                pl.BlockSpec((block, WIDTH), lambda i, f: (i, 0)),
+                pl.BlockSpec((block, WIDTH), lambda i, f, p: (i, 0)),
             ]
-            + [whole((depth // splits, 2 * WIDTH), lambda i, f: (0, 0))] * splits,
+            + [whole((depth // splits, 2 * WIDTH), lambda i, f, p: (0, 0))] * splits,
             scratch_shapes=[
                 pltpu.VMEM((HEADS, block, 128), jnp.bfloat16),
                 pltpu.VMEM((HEADS, block, 128), jnp.bfloat16),
@@ -1036,7 +1122,7 @@
         compiler_params=pltpu.CompilerParams(vmem_limit_bytes=VMEM_LIMIT),
         cost_estimate=COST,
     )(
-        flags.reshape(-1), queries[0], keys[0], values[0], grads, logs, exact, low[None, :],
+        flags.reshape(-1), places, queries[0], keys[0], values[0], grads, logs, exact, low[None, :],
         high[None, :], key_ids[:, None],
     )
 
@@ -1106,19 +1192,22 @@
     cross_high = cross_low + jnp.sum(jnp.where(picked, limits[None, :], 0), 1) - 1
     enc_rows = encoder.shape[1]
     micro = lax.axis_index("t") & 1
-    enc_ids = []
-    for place in range(count):
-        index_s = place if count > 1 else 0
+    starts_of = []
+    for index_s in range(count):
         for step in range(MEMBERS):
             core = lax.axis_index("core") ^ (step & 1)
             y_index = lax.axis_index("y") ^ (step >> 1)
             for part in range(2):
                 t_index = 2 * core + (micro ^ part)
-                row = ((t_index * count + index_s) * PAIR + y_index) * enc_rows
-                enc_ids.append(row + jnp.arange(enc_rows, dtype=jnp.int32))
-    enc_ids = jnp.concatenate(enc_ids)
+                starts_of.append(((t_index * count + index_s) * PAIR + y_index) * enc_rows)
+    enc_places = jnp.stack(starts_of)
+    enc_ids = jnp.arange(NSEQ * ENC, dtype=jnp.int32)
+    if count > 1:
+        enc_ids = (enc_places[:, None] + jnp.arange(enc_rows, dtype=jnp.int32)[None, :]).reshape(-1)
+        enc_places = jnp.array([0, NSEQ * ENC // 2], jnp.int32)
+    self_places = jnp.array([0, key_order.shape[0] // 2], jnp.int32)
     block = 256
-    self_chunk, cross_chunk = 256, 384
+    self_chunk, cross_chunk = 256, 512 if count == 1 else 384
     self_flags = needed_chunks(self_low, self_high, key_order, block, self_chunk)
     cross_flags = needed_chunks(cross_low, cross_high, enc_ids, block, cross_chunk)
 
@@ -1130,9 +1219,9 @@
     def relative(matrix, name):
         return relative_columns(matrix, count, orders[name])
 
-    facts_known = (rank, self_flags, cross_flags, key_order, enc_ids, self_low, cross_low, cross_high)
+    facts_known = (rank, self_flags, cross_flags, key_order, enc_places, self_low, cross_low, cross_high)
     tokens_in, facts_known = chain(tokens_in, facts_known)
-    rank, self_flags, cross_flags, key_order, enc_ids, self_low, cross_low, cross_high = facts_known
+    rank, self_flags, cross_flags, key_order, enc_places, self_low, cross_low, cross_high = facts_known
     qkv = project_heads(tokens_in, full_self_in, jnp.concatenate([vec[6], zero_row, vec[7]]))
     feed_own = stack_feed(feed_up, feed_down)
     own_heads = sort_rows(to_members(qkv), rank)
@@ -1142,11 +1231,11 @@
     else:
         self_keys, self_values = (own_heads, 1), (own_heads, 2)
     tokens_x, tokens_y = relative(tokens_in, "x"), relative(tokens_in, "y")
-    encoder_x = relative(encoder_in, "x")
+    encoder_y = relative(encoder_in, "y")
     index = relative_index(D, count, orders["y"])
     pick_y = (index[:, None] == jnp.arange(D, dtype=jnp.int32)[None, :]).astype(jnp.bfloat16)
-    (tokens_x, tokens_y, encoder_x, pick_y, own_heads), (encoder_in, cotangent) = chain(
-        (tokens_x, tokens_y, encoder_x, pick_y, own_heads), (encoder_in, cotangent)
+    (tokens_x, tokens_y, encoder_y, pick_y, own_heads), (encoder_in, cotangent) = chain(
+        (tokens_x, tokens_y, encoder_y, pick_y, own_heads), (encoder_in, cotangent)
     )
     grad_in = jnp.concatenate(to_packs(cotangent), 0)
     attended_heads, exact_self, log_self = attend_forward(
@@ -1160,37 +1249,41 @@
     )
     attended = to_members(unsort_rows([attended_heads], rank))
     attended, enc_pairs = chain(attended, enc_pairs)
-    enc_heads = gather_sequence(jnp.concatenate(exchange(enc_pairs), 0), count)
+    if count == 1:
+        enc_heads = assemble(exchange(enc_pairs), enc_places)
+    else:
+        enc_heads = gather_sequence(jnp.concatenate(exchange(enc_pairs), 0), count)
     normed_one, normed_one_low, unit_one, inverse_one, cross_queries = project_norm(
         by_member(attended), full_out_query, self_bias_row, tokens_in, vec[0], vec[3],
         after=(vec[8],),
     )
     cross_heads = sort_rows(to_members(cross_queries), rank)
-    attended_x = relative(as_columns(attended), "x")
-    normed_one_x = relative(normed_one_low, "x")
-    (attended_x, normed_one_x), cross_heads = chain((attended_x, normed_one_x), cross_heads)
+    attended_y = relative(as_columns(attended), "y")
+    normed_one_y = relative(normed_one_low, "y")
+    (attended_y, normed_one_y), cross_heads = chain((attended_y, normed_one_y), cross_heads)
     crossed_heads, exact_cross, log_cross = attend_forward(
         (cross_heads, 0), (enc_heads, 0), (enc_heads, 1), cross_low, cross_high, enc_ids,
         cross_flags, block, cross_chunk,
     )
-    cross_heads, feed_own = chain(cross_heads, feed_own)
+    cross_heads, (feed_own, full_cross_out) = chain(cross_heads, (feed_own, full_cross_out))
     feed_near = lax.ppermute(feed_own, "core", SWAP)
-    crossed_heads, feed_far = chain(crossed_heads, feed_far)
+    crossed_heads, grad_in = chain(crossed_heads, grad_in)
+    crossed = to_members(unsort_rows([crossed_heads], rank))
+    crossed, feed_far = chain(crossed, feed_far)
     feed_shards = [feed_own, feed_near, feed_far, lax.ppermute(feed_far, "core", SWAP)]
-    crossed = to_members(unsort_rows([crossed_heads], rank))
     normed_two, normed_two_low, unit_two, inverse_two = project_norm(
         by_member(crossed), full_cross_out, vec[10], normed_one, vec[1], vec[4]
     )
-    crossed_x = relative(as_columns(crossed), "x")
-    crossed_x, normed_two_low = chain(crossed_x, normed_two_low)
-    pre_active, hidden = feed_up_gelu(normed_two_low, feed_shards, bias_row)
+    crossed_y = relative(as_columns(crossed), "y")
+    crossed_y, normed_two_low = chain(crossed_y, normed_two_low)
+    slope, hidden = feed_up_gelu(normed_two_low, feed_shards, bias_row)
     layer_low, grad_three, grad_branch, sums_three = feed_down_norm(
         hidden, feed_shards, vec[11], normed_two, vec[2], vec[5], grad_in
     )
     half = tokens_in.shape[0] // 2
 
     grad_pre, bias_up, grad_two, grad_crossed_out, sums_two, grad_crossed = feed_back(
-        pre_active, feed_shards, grad_branch, grad_three, unit_two, inverse_two, vec[1],
+        slope, feed_shards, grad_branch, grad_three, unit_two, inverse_two, vec[1],
         full_cross_out,
     )
     received, (feed_parts, layer_low) = during_members(
@@ -1202,8 +1295,7 @@
     grad_crossed_heads = sort_rows(received, rank)
     dq_heads, *enc_pair_grads = attend_backward(
         (cross_heads, 0), (enc_heads, 0), (enc_heads, 1), grad_crossed_heads, log_cross,
-        exact_cross, cross_low, cross_high, enc_ids, cross_flags, block, cross_chunk,
-        MEMBERS if count == 1 else 1,
+        exact_cross, cross_low, cross_high, enc_ids, cross_flags, block, cross_chunk, enc_places,
     )
     layer_out, dq_heads = chain(layer_out, dq_heads)
     if count > 1:
@@ -1216,60 +1308,75 @@
         by_member(dq_blocks), full_out_query, grad_two, unit_one, inverse_one, vec[0]
     )
 
-    def three_side(dq_blocks, *lefts):
-        grads = as_columns(dq_blocks)
-        return grads, weight_grads(lefts, [grad_attended_out, grads, grad_crossed_out])
-
-    received, (grad_cross_queries, three_parts) = during_members(
-        grad_attended, three_side, (dq_blocks, attended_x, normed_one_x, crossed_x)
-    )
-    three_sum = Halving(three_parts, count, orders["x"])
+    received, (*three_parts, query_sums) = during_members(
+        grad_attended,
+        lambda blocks: three_grads(
+            attended_y, normed_one_y, crossed_y, grad_attended_out, blocks, grad_crossed_out
+        ),
+        (dq_blocks,),
+    )
+    three_sum = Halving(three_parts, count, orders["y"])
     grad_attended_heads = sort_rows(received, rank)
     dq_heads, pair_heads = attend_backward(
         (own_heads, 0), self_keys, self_values, grad_attended_heads, log_self, exact_self,
-        self_low, self_high, key_order, self_flags, block, self_chunk, 1,
+        self_low, self_high, key_order, self_flags, block, self_chunk, self_places,
     )
     pair_heads = scatter_sequence(pair_heads, count)
-    half_enc = encoder_in.shape[0] // 2
-
-    dq_heads, enc_blocks = chain(dq_heads, enc_blocks)
-
-    def encoder_side(pending, me):
-        three_sum.pending = pending
-        three_sum.step()
-        grads = join_heads(enc_blocks, me)
-        parts = weight_grads([encoder_x], [grads])
-        return grads, back_project(grads, full_cross_pair), parts, three_sum.sent, three_sum.value
-
-    received, (grad_enc_pairs, grad_enc, pair_parts, three_sum.sent, three_sum.value) = (
-        during_members(
-            unsort_rows([dq_heads, pair_heads], rank), encoder_side,
-            (three_sum.pending, group_index()[None]),
-        )
-    )
-    pair_sum = Halving(pair_parts, count, orders["x"])
-    grad_encoder = from_packs(grad_enc[:half_enc], grad_enc[half_enc:])
-    grad_qkv = as_columns(received)
-    left_parts, right_parts = self_in_grads(
-        tokens_x, tokens_y, grad_qkv, pick_y, sums_one, sums_two, sums_three, bias_up,
-        grad_cross_queries, grad_enc_pairs,
+
+    dq_heads, three_sum.pending = chain(dq_heads, three_sum.pending)
+    three_sum.step()
+    (dq_heads, three_sum.sent, three_sum.value), enc_blocks = chain(
+        (dq_heads, three_sum.sent, three_sum.value), enc_blocks
+    )
+
+    blocks, me = chain(unsort_blocks([dq_heads, pair_heads], rank), group_index()[None])
+    received = exchange(blocks)
+    *pair_parts, enc_first, enc_rest, value_sums = encoder_grads(
+        me, encoder_y, full_cross_pair, enc_blocks
+    )
+    (pair_parts, enc_first, enc_rest), received = chain((pair_parts, enc_first, enc_rest), received)
+    pair_sum = Halving(pair_parts, count, orders["y"])
+    enc_first = send_back(enc_first, 0)
+    left_parts, right_parts, grad_qkv = self_in_grads(
+        group_index()[None], tokens_x, tokens_y, pick_y, sums_one, sums_two, sums_three, bias_up,
+        query_sums, value_sums, received,
     )
     left_sum = Halving(left_parts, count, orders["x"])
     right_sum = Halving(right_parts, count, orders["y"])
-    (left_sum.sent, right_sum.sent), grad_qkv = chain((left_sum.sent, right_sum.sent), grad_qkv)
-    grad_rows = (RESIDUAL * grad_one + back_project(grad_qkv, full_self_in, jnp.float32)).astype(
-        jnp.bfloat16
-    )
-    turn, grad_encoder = chain(right_sum.sent, grad_encoder)
-    grad_tokens = from_packs(grad_rows[:half], grad_rows[half:]).astype(jnp.float32)
-    for halving in [pair_sum, left_sum, right_sum, three_sum] * 5:
-        if halving.order:
-            turn, halving.pending = chain(turn, halving.pending)
+    def steps(last, *halvings):
+        for halving in halvings:
+            last.value, halving.pending = chain(last.value, halving.pending)
             halving.step()
-            turn = halving.sent
+            last = halving
+        return last
+
+    last = right_sum
+    last.value, grad_qkv = chain(last.value, grad_qkv)
+    grad_rows = back_project(grad_qkv, full_self_in, grad_one)
+    last.value, grad_rows = chain(last.value, grad_rows)
+    last = steps(last, left_sum, right_sum, pair_sum, three_sum)
+    last.value, (enc_first, enc_rest) = chain(last.value, (enc_first, enc_rest))
+    enc_second = send_back(enc_rest, 1)
+    last = steps(last, right_sum, left_sum, pair_sum)
+    last.value, feed_sum = chain(last.value, feed_sum)
+    feed_kept, feed_sent = split_feed(feed_sum)
+    feed_arrived = flip(feed_sent, "y")
+    last = steps(last, three_sum)
+    last.value, enc_second = chain(last.value, enc_second)
+    last = steps(last, right_sum)
+    last.value, rows_first = chain(last.value, grad_rows[:half])
+    rows_first = send_back(rows_first, 0)
+    last = steps(last, left_sum, three_sum)
+    last.value, (rows_first, rows_second) = chain(last.value, (rows_first, grad_rows[half:]))
+    rows_second = send_back(rows_second, 1)
+    last = steps(last, pair_sum)
+    last.value, feed_arrived = chain(last.value, feed_arrived)
+    last = steps(last, right_sum, left_sum, pair_sum)
+    grad_encoder = order_back(enc_first, enc_second)
+    grad_tokens = order_back(rows_first, rows_second).astype(jnp.float32)
     three, pair = three_sum.finish(), pair_sum.finish()
     left, right = left_sum.finish(), right_sum.finish()
-    up_sum, down_sum = split_feed(feed_sum)
+    up_sum, down_sum = merge_feed(feed_kept, feed_arrived)
     small = right[:, 3 * D // 2 :]
     return (
         layer_out,

time: 634 us -> 595 us (0.938)
  starting transfers between devices: 107 us -> 76.2 us
  Pallas kernels: 235 us -> 220 us
  local copies, waits for them, and re-layouts: 39.9 us -> 50.3 us
    all_to_all x7 -> x6, waiting for transfers between devices: 12.9 us -> 43.3 us  [to_members(): return lax.all_to_all(blocks, GROUP, 0, 0, tiled=True)]
    ppermute x13, starting transfers between devices: 32 us -> 4.47 us  [flip(): return lax.ppermute(block, name, [(i, i ^ 1) for i in range(PAIR)])]
    pallas_call x20 -> x16, Pallas kernels: 80.2 us -> 61.4 us  [small_kernel(): pl.pallas_call(body, in_specs=[pl.BlockSpec(memory_space=pltpu.SMEM)] * l...]
    pallas_call x1 -> x3, Pallas kernels: 8.28 us -> 25.6 us  [the longest x1 11.9 us: encoder_grads(): pl.pallas_call(encoder_kernel, in_specs=[pl.BlockSpec(memory_space=pltpu....]
    ppermute x6 -> x9, waiting for transfers between devices: 28.3 us -> 13.1 us  [exchange(): lax.ppermute(block, GROUP, group_route(step))]
    unnamed x85 -> x122, local copies, waits for them, and re-layouts: 17 us -> 24 us
    pallas_call x2, Pallas kernels: 39.1 us -> 32.3 us  [attend_forward(): pl.pallas_call(functools.partial(forward_kernel, chunk), grid_spec=pltpu....]
    pallas_call x2 -> x1, Pallas kernels: 13.7 us -> 7.07 us  [back_project(): pl.pallas_call(back_kernel, grid=(weight.shape[0] // rows,), in_specs=[pl...]
  transfers between devices with their start and end apart: 56 -> 58, of which waited for: 23 -> 15; matrix products, arithmetic and copies ran while one was open for 11% -> 12% of each run, Pallas kernels for 31% -> 31%
where the time goes in v3:
time: 595 us; the launch traced here: 588 us
  Pallas kernels  220 us (37%)
  waiting for transfers between devices  144 us (24%)
  starting transfers between devices  76.2 us (13%)
  local copies, waits for them, and re-layouts  50.3 us (8%)
  blocking collectives  40.3 us (7%)
  other arithmetic  29 us (5%)
  between operations  15.3 us (3%)
  matrix products  13.1 us (2%)
    pallas_call x16, Pallas kernels, small_kernel(): pl.pallas_call(body, in_specs=[pl.BlockSpec(memory_space=pltpu.SMEM)] * l...  61.4 us
    ppermute x13, waiting for transfers between devices, flip(): return lax.ppermute(block, name, [(i, i ^ 1) for i in range(PAIR)])  47 us
    all_to_all x6, waiting for transfers between devices, to_members(): return lax.all_to_all(blocks, GROUP, 0, 0, tiled=True)  43.3 us
    pallas_call x2, Pallas kernels, attend_backward(): pl.pallas_call(functools.partial(backward_kernel, chunk), grid_spec=pltpu...  41.5 us
    pallas_call x2, Pallas kernels, attend_forward(): pl.pallas_call(functools.partial(forward_kernel, chunk), grid_spec=pltpu....  32.3 us
    ppermute x8, waiting for transfers between devices, flip(): return lax.ppermute(block, 't', [(i, i ^ step) for i in range(T_SIZE)])  24.3 us
    unnamed x122, local copies, waits for them, and re-layouts  24 us
    all_to_all x6, starting transfers between devices, to_members(): return lax.all_to_all(blocks, GROUP, 0, 0, tiled=True)  21.6 us
  transfers between devices with their start and end apart: 58, of which 15 were waited for; matrix products, arithmetic and copies ran while one was open for 12% of the time, Pallas kernels for 31%

profile of v3, /device:TPU:0, one launch (start us, length us, event | category | flops | bytes accessed | tf_op | source)
XLA Modules:
  0.0 588.0 jit_solution(9006120615219211075)
XLA Ops:
  9.8 3.1 collective-permute-start.1
  12.9 6.0 %collective-permute-done.1 = bf16[128,1024]{1,0:T(8,128)(2,1)S(1)} collective-permute-done((bf16[128,1024]{1,0:T(8,128)(2,1)S(1)}, bf16[128,1024]{1,0:T(8,128)(2,1)S(1)}, u32[]{:S(2)}, u32[]{:S(2)}) %collective-permute-start.1) | collective-permute-done | bytes 262176 | tf_op jit(solution)/shard_map/ppermute | solution.py:83
  26.3 19.6 %all_gather.20 = bf16[17,1024]{1,0:T(8,128)(2,1)S(1)} all-gather(bf16[17,256]{1,0:T(8,128)(2,1)S(1)} %pad_maximum_fusion.6), channel_id=1, replica_groups=mesh['t'=4,'s'=1,'y'=2,'x'=2,'core'=2] {'x','core'}, dimensions={1}, use_global_device_ids=true | all-gather | bytes 43520 | tf_op jit(solution)/shard_map/all_gather | solution.py:1164
  46.2 2.1 pad_maximum_fusion
  57.4 5.1 all-gather
  66.5 6.6 %shard_map.264 = bf16[1024,768]{1,0:T(8,128)(2,1)} custom-call(bf16[256,1024]{1,0:T(8,128)(2,1)} %pad_maximum_fusion.1.rows_ref.base_ref, bf16[1024,3072]{1,0:T(8,128)(2,1)} %all-gather.6.cloned.1.call-done.weight_ref, f32[1,3072]{1,0:T(1,128)} %bitcast.133), custom_call_target="tpu_custom_call" | custom-call | tf_op jit(solution)/shard_map/pallas_call | solution.py:134
  73.1 3.7 all-to-all-start
  83.1 3.0 fusion.13.left_ref
  86.1 10.8 %all-to-all-done = bf16[4,256,768]{2,1,0:T(8,128)(2,1)S(1)} async-done(((bf16[4,256,768]{2,1,0:T(8,128)(2,1)}), bf16[4,256,768]{2,1,0:T(8,128)(2,1)S(1)}, u32[]{:S(2)}, u32[]{:S(2)}) %all-to-all-start) | async-done | bytes 1572896 | tf_op jit(solution)/shard_map/all_to_all | solution.py:508
  98.0 4.4 shard_map.265.q_ref.k_ref.v_ref
  102.3 14.1 %shard_map.266 = (bf16[1024,256]{1,0:T(8,128)(2,1)}, f32[1024,256]{1,0:T(8,128)}, f32[8,1024]{1,0:T(8,128)}) custom-call(s32[16]{0:T(128)} %reshape.241.flags_ref, bf16[1024,768]{1,0:T(8,128)(2,1)} %shard_map.265.q_ref.k_ref.v_ref, bf16[1024,768]{1,0:T(8,128)(2,1)} %shard_map.265.q_ref.k_ref.v_ref, bf16[1024,768]{1,0:T(8,128)(2,1)} %shard_map.265.q_ref.k_ref.v_ref, ...), custom_call_target="tpu_custom_call" | custom-call | tf_op jit(solution)/shard_map/pallas_call | solution.py:948
  117.6 2.8 shard_map.267
  120.4 3.5 all-to-all-start.1
  126.0 7.0 %shard_map.268 = (bf16[768,512]{1,0:T(8,128)(2,1)}, bf16[768,512]{1,0:T(8,128)(2,1)}, bf16[768,512]{1,0:T(8,128)(2,1)}, bf16[768,512]{1,0:T(8,128)(2,1)}) custom-call(s32[1]{0:T(128)} %bitcast.37.me_ref, bf16[768,1024]{1,0:T(8,128)(2,1)} %copy-done.13, bf16[1024,2048]{1,0:T(8,128)(2,1)} %all-gather.8.cloned.1.call-done.weight_ref, f32[1,2048]{1,0:T(1,128)} %bitcast.136), custom_call_target="tpu_custom_call" | custom-call | tf_op jit(solution)/shard_map/pallas_call | solution.py:134
  133.0 2.2 collective-permute-start.6
  135.1 2.0 collective-permute-start.7
  140.1 1.9 shard_map.269
  142.0 5.3 shard_map.270
  147.3 4.0 all-to-all-start.2
  151.3 2.8 fusion.17.query_left
  156.0 21.6 %all-to-all-done.2 = bf16[4,256,256]{2,1,0:T(8,128)(2,1)S(1)} async-done(((bf16[4,256,256]{2,1,0:T(8,128)(2,1)}), bf16[4,256,256]{2,1,0:T(8,128)(2,1)S(1)}, u32[]{:S(2)}, u32[]{:S(2)}) %all-to-all-start.2) | async-done | bytes 524320 | tf_op jit(solution)/shard_map/all_to_all | solution.py:508
  178.4 2.5 shard_map.271.q_ref
  182.9 3.7 shard_map.272.k_ref.v_ref
  187.9 18.2 %shard_map.273 = (bf16[1024,256]{1,0:T(8,128)(2,1)}, f32[1024,256]{1,0:T(8,128)}, f32[8,1024]{1,0:T(8,128)}) custom-call(s32[24]{0:T(128)} %reshape.240.flags_ref, bf16[1024,256]{1,0:T(8,128)(2,1)} %shard_map.271.q_ref, bf16[3072,512]{1,0:T(8,128)(2,1)} %shard_map.272.k_ref.v_ref, bf16[3072,512]{1,0:T(8,128)(2,1)} %shard_map.272.k_ref.v_ref, ...), custom_call_target="tpu_custom_call" | custom-call | tf_op jit(solution)/shard_map/pallas_call | solution.py:948
  206.1 2.7 shard_map.274
  208.8 3.5 all-to-all-start.3
  212.8 8.3 %all-to-all-done.3 = bf16[4,256,256]{2,1,0:T(8,128)(2,1)S(1)} async-done(((bf16[4,256,256]{2,1,0:T(8,128)(2,1)}), bf16[4,256,256]{2,1,0:T(8,128)(2,1)S(1)}, u32[]{:S(2)}, u32[]{:S(2)}) %all-to-all-start.3) | async-done | bytes 524320 | tf_op jit(solution)/shard_map/all_to_all | solution.py:508
  221.1 9.7 %collective-permute-done.11.refs_2_.refs_6_ = bf16[2048,1024]{1,0:T(8,128)(2,1)} collective-permute-done((bf16[2048,1024]{1,0:T(8,128)(2,1)}, bf16[2048,1024]{1,0:T(8,128)(2,1)}, u32[]{:S(2)}, u32[]{:S(2)}) %collective-permute-start.11) | collective-permute-done | bytes 4194336 | tf_op jit(solution)/shard_map/ppermute | solution.py:1246
  233.8 4.7 shard_map.276
  240.3 10.3 %shard_map.277 = (f32[256,4096]{1,0:T(8,128)}, bf16[256,4096]{1,0:T(8,128)(2,1)}) custom-call(s32[1]{0:T(128)} %bitcast.me_ref, bf16[256,1024]{1,0:T(8,128)(2,1)} %get-tuple-element.264.rows_ref, bf16[2048,1024]{1,0:T(8,128)(2,1)} %slice_dynamic-update-slice_fusion.refs_0_.refs_4_, bf16[2048,1024]{1,0:T(8,128)(2,1)} %collective-permute-done.12.refs_1_.refs_5_, ...), custom_call_target="tpu_custom_call" | custom-call | tf_op jit(solution)/shard_map/pallas_call | solution.py:297
  250.6 11.9 %shard_map.278 = (bf16[256,1024]{1,0:T(8,128)(2,1)}, f32[256,1024]{1,0:T(8,128)}, bf16[256,1024]{1,0:T(8,128)(2,1)}, f32[8,1024]{1,0:T(8,128)}) custom-call(s32[1]{0:T(128)} %bitcast.me_ref, bf16[256,4096]{1,0:T(8,128)(2,1)} %get-tuple-element.262.hidden_ref, bf16[2048,1024]{1,0:T(8,128)(2,1)} %slice_dynamic-update-slice_fusion.refs_0_.refs_4_, ...), custom_call_target="tpu_custom_call" | custom-call | tf_op jit(solution)/shard_map/pallas_call | solution.py:374
  262.5 18.0 %shard_map.279 = (bf16[256,4096]{1,0:T(8,128)(2,1)}, f32[1,4096]{1,0:T(1,128)}, f32[256,1024]{1,0:T(8,128)}, bf16[256,1024]{1,0:T(8,128)(2,1)}, f32[8,1024]{1,0:T(8,128)}, /*index=5*/bf16[1024,256]{1,0:T(8,128)(2,1)}) custom-call(s32[1]{0:T(128)} %bitcast.me_ref, f32[256,4096]{1,0:T(8,128)} %get-tuple-element.251.slope_ref, ...), custom_call_target="tpu_custom_call" | custom-call | tf_op jit(solution)/shard_map/pallas_call | solution.py:439
  280.5 3.5 all-to-all-start.4
  284.1 11.7 %shard_map.280 = bf16[16,2,8,32,1024]{4,3,2,1,0:T(8,128)(2,1)} custom-call(bf16[256,4096]{1,0:T(8,128)(2,1)} %get-tuple-element.262.hidden_ref, bf16[256,1024]{1,0:T(8,128)(2,1)} %get-tuple-element.263.refs_8_.grads_ref, bf16[256,1024]{1,0:T(8,128)(2,1)} %get-tuple-element.264.rows_ref, bf16[256,4096]{1,0:T(8,128)(2,1)} %get-tuple-element.265.active_grads_ref), custom_call_target="tpu_custom_call" | custom-call | tf_op jit(solution)/shard_map/pallas_call | solution.py:838
  299.5 2.5 shard_map.281.g_ref
  303.3 25.3 %shard_map.282 = (bf16[1024,256]{1,0:T(8,128)(2,1)}, bf16[768,512]{1,0:T(8,128)(2,1)}, bf16[768,512]{1,0:T(8,128)(2,1)}, bf16[768,512]{1,0:T(8,128)(2,1)}, bf16[768,512]{1,0:T(8,128)(2,1)}) custom-call(s32[24]{0:T(128)} %reshape.240.flags_ref, s32[8]{0:T(128)} %stack.62.places_ref, bf16[1024,256]{1,0:T(8,128)(2,1)} %shard_map.271.q_ref, ...), custom_call_target="tpu_custom_call" | custom-call | tf_op jit(solution)/shard_map/pallas_call | solution.py:1088
  329.5 2.7 shard_map.283
  332.2 15.6 %all_to_all.82 = bf16[4,256,256]{2,1,0:T(8,128)(2,1)} all-to-all(bf16[4,256,256]{2,1,0:T(8,128)(2,1)} %bitcast.108), channel_id=1, replica_groups=mesh['t'=4,'s'=1,'y'=2,'x'=2,'core'=2] {'y','core'}, dimensions={0} | all-to-all | bytes 1048576 | tf_op jit(solution)/shard_map/all_to_all | solution.py:508
  347.9 5.8 shard_map.284
  353.6 3.5 all-to-all-start.6
  357.1 6.2 %shard_map.285 = (bf16[512,3072]{1,0:T(8,128)(2,1)}, bf16[512,3072]{1,0:T(8,128)(2,1)}, f32[1,1024]{1,0:T(1,128)}) custom-call(bf16[256,1024]{1,0:T(8,128)(2,1)} %fusion.16.out_left, bf16[256,1024]{1,0:T(8,128)(2,1)} %fusion.17.query_left, bf16[256,1024]{1,0:T(8,128)(2,1)} %fusion.18.cross_left, bf16[256,1024]{1,0:T(8,128)(2,1)} %get-tuple-element.292.out_grads, ...), custom_call_target="tpu_custom_call" | custom-call | tf_op jit(solution)/shard_map/pallas_call | solution.py:700
  363.3 2.6 all-to-all-done.6
  368.3 2.6 shard_map.286.g_ref
  370.9 16.2 %shard_map.287 = (bf16[1024,256]{1,0:T(8,128)(2,1)}, bf16[1024,512]{1,0:T(8,128)(2,1)}) custom-call(s32[16]{0:T(128)} %reshape.241.flags_ref, s32[2]{0:T(128)} %iota_multiply_fusion.places_ref, bf16[1024,768]{1,0:T(8,128)(2,1)} %shard_map.265.q_ref.k_ref.v_ref, bf16[1024,768]{1,0:T(8,128)(2,1)} %shard_map.265.q_ref.k_ref.v_ref, ...), custom_call_target="tpu_custom_call" | custom-call | tf_op jit(solution)/shard_map/pallas_call | solution.py:1088
  388.3 2.7 copy-done
  392.4 10.3 %collective-permute-done.19.refs_3_ = bf16[768,512]{1,0:T(8,128)(2,1)} collective-permute-done((bf16[768,512]{1,0:T(8,128)(2,1)}, bf16[768,512]{1,0:T(8,128)(2,1)}, u32[]{:S(2)}, u32[]{:S(2)}) %collective-permute-start.19) | collective-permute-done | bytes 786464 | tf_op jit(solution)/shard_map/ppermute | solution.py:528
  402.7 4.2 shard_map.288
  411.7 11.9 %shard_map.289 = (bf16[512,2048]{1,0:T(8,128)(2,1)}, bf16[512,2048]{1,0:T(8,128)(2,1)}, bf16[384,1024]{1,0:T(8,128)(2,1)}, bf16[384,1024]{1,0:T(8,128)(2,1)}, f32[1,1024]{1,0:T(1,128)}) custom-call(s32[1]{0:T(128)} %bitcast.37.me_ref, bf16[768,1024]{1,0:T(8,128)(2,1)} %fusion.13.left_ref, bf16[1024,2048]{1,0:T(8,128)(2,1)} %all-gather.8.cloned.1.call-done.weight_ref, ...), custom_call_target="tpu_custom_call" | custom-call | tf_op jit(solution)/shard_map/pallas_call | solution.py:727
  423.7 2.8 collective-permute-done.22.refs_3_
  427.3 7.5 %shard_map.290 = (bf16[512,1536]{1,0:T(8,128)(2,1)}, bf16[512,1536]{1,0:T(8,128)(2,1)}, bf16[512,1664]{1,0:T(8,128)(2,1)}, bf16[512,1664]{1,0:T(8,128)(2,1)}, bf16[256,3072]{1,0:T(8,128)(2,1)}) custom-call(s32[1]{0:T(128)} %bitcast.37.me_ref, bf16[256,1024]{1,0:T(8,128)(2,1)} %fusion.14.left_ref, bf16[256,1024]{1,0:T(8,128)(2,1)} %fusion.15.right_ref, ...), custom_call_target="tpu_custom_call" | custom-call | tf_op jit(solution)/shard_map/pallas_call | solution.py:772
  436.3 7.1 %shard_map.291 = bf16[256,1024]{1,0:T(8,128)(2,1)} custom-call(bf16[256,3072]{1,0:T(8,128)(2,1)} %get-tuple-element.350.grads_ref, bf16[1024,3072]{1,0:T(8,128)(2,1)} %all-gather.6.cloned.1.call-done.weight_ref, f32[256,1024]{1,0:T(8,128)} %get-tuple-element.351.resid_ref), custom_call_target="tpu_custom_call" | custom-call | tf_op jit(solution)/shard_map/pallas_call | solution.py:492
  443.4 2.0 collective-permute-start.27
  457.9 15.5 %collective-permute-done.26 = bf16[256,3072]{1,0:T(8,128)(2,1)S(1)} collective-permute-done((bf16[256,3072]{1,0:T(8,128)(2,1)}, bf16[256,3072]{1,0:T(8,128)(2,1)S(1)}, u32[]{:S(2)}, u32[]{:S(2)}) %collective-permute-start.26) | collective-permute-done | bytes 1572896 | tf_op jit(solution)/shard_map/ppermute | solution.py:648
  477.0 2.6 collective-permute-start.32
  479.6 11.2 %collective-permute-done.28 = bf16[256,1664]{1,0:T(8,128)(2,1)S(1)} collective-permute-done((bf16[256,1664]{1,0:T(8,128)(2,1)S(1)}, bf16[256,1664]{1,0:T(8,128)(2,1)S(1)}, u32[]{:S(2)}, u32[]{:S(2)}) %collective-permute-start.28) | collective-permute-done | bytes 852000 | tf_op jit(solution)/shard_map/ppermute | solution.py:648
  493.6 17.5 %collective-permute-done.30 = bf16[256,2048]{1,0:T(8,128)(2,1)S(1)} collective-permute-done((bf16[256,2048]{1,0:T(8,128)(2,1)S(1)}, bf16[256,2048]{1,0:T(8,128)(2,1)S(1)}, u32[]{:S(2)}, u32[]{:S(2)}) %collective-permute-start.30) | collective-permute-done | bytes 1048608 | tf_op jit(solution)/shard_map/ppermute | solution.py:648
  516.8 2.8 collective-permute-done.34
  526.9 4.8 collective-permute-done.35
  531.7 2.5 collective-permute-start.41
  535.3 10.8 %collective-permute-start.45 = (bf16[32,3072]{1,0:T(8,128)(2,1)S(1)}, bf16[32,3072]{1,0:T(8,128)(2,1)S(1)}, u32[]{:S(2)}, u32[]{:S(2)}) collective-permute-start(bf16[32,3072]{1,0:T(8,128)(2,1)S(1)} %slice.415), channel_id=1, source_target_pairs={{0,16},{8,24},{16,0},{24,8},{1,17},{9,25},{17,1},{25,9},{2,18},{10... | collective-permute-start | bytes 589832 | tf_op jit(solution)/shard_map/ppermute | solution.py:647
  546.1 1.9 collective-permute-start.37
  550.1 5.9 collective-permute-start.43
  556.9 13.6 %collective-permute-done.44 = bf16[32,1664]{1,0:T(8,128)(2,1)S(1)} collective-permute-done((bf16[32,1664]{1,0:T(8,128)(2,1)S(1)}, bf16[32,1664]{1,0:T(8,128)(2,1)S(1)}, u32[]{:S(2)}, u32[]{:S(2)}) %collective-permute-start.44) | collective-permute-done | bytes 106528 | tf_op jit(solution)/shard_map/ppermute | solution.py:647
  574.7 5.8 collective-permute-done.46
  (361 shorter events, 106.2 us)
Async XLA Ops:
  7.2 59.2 %all-gather.6.cloned.1.call-start = ((), (), s32[]{:S(2)}) async-start(), calls=%async_computation.8 | async-start | bytes 7864320 | tf_op jit(solution)/shard_map/all_gather | solution.py:145
  8.0 118.0 %all-gather.8.cloned.1.call-start = ((), (), s32[]{:S(2)}) async-start(), calls=%async_computation.9 | async-start | bytes 5242880 | tf_op jit(solution)/shard_map/all_gather | solution.py:145
  9.1 3.8 collective-permute-start
  9.8 9.1 %collective-permute-start.1 = (bf16[128,1024]{1,0:T(8,128)(2,1)S(1)}, bf16[128,1024]{1,0:T(8,128)(2,1)S(1)}, u32[]{:S(2)}, u32[]{:S(2)}) collective-permute-start(bf16[128,1024]{1,0:T(8,128)(2,1)S(1)} %get-tuple-element.482), channel_id=1, source_target_pairs={{0,8},{1,24},{8,0},{9,16},{16,9},{17,25},{24,1},{25,17},{2,10},{3,... | collective-permute-start | bytes 786440 | tf_op jit(solution)/shard_map/ppermute | solution.py:83
  19.7 26.6 %copy-start.40 = (bf16[256,1024]{1,0:T(8,128)(2,1)S(1)}, bf16[256,1024]{1,0:T(8,128)(2,1)}, u32[]{:S(2)}) copy-start(bf16[256,1024]{1,0:T(8,128)(2,1)} %param.25) | copy-start | bytes 1572868
  19.7 122.3 %all-gather.10.cloned.1.call-start = ((), (), s32[]{:S(2)}) async-start(), calls=%async_computation.10 | async-start | bytes 5242880 | tf_op jit(solution)/shard_map/all_gather | solution.py:145
  19.9 26.4 %collective-permute-start.2 = (s32[134]{0:T(256)S(1)}, s32[134]{0:T(256)S(1)}, u32[]{:S(2)}, u32[]{:S(2)}) collective-permute-start(s32[134]{0:T(256)S(1)} %bitcast.147), channel_id=1, source_target_pairs={{0,0},{1,16},{8,8},{9,24},{16,1},{17,17},{24,9},{25,25},{2,2},{3,1... | collective-permute-start | bytes 1616 | tf_op jit(solution)/shard_map/ppermute | solution.py:82
  20.7 36.7 %collective-permute-start.3 = (s32[134]{0:T(256)S(1)}, s32[134]{0:T(256)S(1)}, u32[]{:S(2)}, u32[]{:S(2)}) collective-permute-start(s32[134]{0:T(256)S(1)} %bitcast.146), channel_id=1, source_target_pairs={{0,8},{1,24},{8,0},{9,16},{16,9},{17,25},{24,1},{25,17},{2,10},{3,... | collective-permute-start | bytes 1616 | tf_op jit(solution)/shard_map/ppermute | solution.py:83
  23.3 26.4 %copy-start.19 = (bf16[1024,1024]{1,0:T(8,128)(2,1)S(1)}, bf16[1024,1024]{1,0:T(8,128)(2,1)}, u32[]{:S(2)}) copy-start(bf16[1024,1024]{1,0:T(8,128)(2,1)} %param.29) | copy-start | bytes 6291460
  23.3 57.4 %collective-permute-start.4 = (bf16[384,1024]{1,0:T(8,128)(2,1)S(1)}, bf16[384,1024]{1,0:T(8,128)(2,1)}, u32[]{:S(2)}, u32[]{:S(2)}) collective-permute-start(bf16[384,1024]{1,0:T(8,128)(2,1)S(1)} %get-tuple-element.466), channel_id=1, source_target_pairs={{0,0},{1,16},{8,8},{9,24},{16,1},{17,17},{24,9},{25,25},{2,2},{3,1... | collective-permute-start | bytes 2359304 | tf_op jit(solution)/shard_map/ppermute | solution.py:82
  24.9 56.9 %collective-permute-start.5 = (bf16[384,1024]{1,0:T(8,128)(2,1)}, bf16[384,1024]{1,0:T(8,128)(2,1)}, u32[]{:S(2)}, u32[]{:S(2)}) collective-permute-start(bf16[384,1024]{1,0:T(8,128)(2,1)} %get-tuple-element.465), channel_id=1, source_target_pairs={{0,8},{1,24},{8,0},{9,16},{16,9},{17,25},{24,1},{25,17},{2,10},{3,... | collective-permute-start | bytes 2359304 | tf_op jit(solution)/shard_map/ppermute | solution.py:83
  73.1 23.8 %all-to-all-start = ((bf16[4,256,768]{2,1,0:T(8,128)(2,1)}), bf16[4,256,768]{2,1,0:T(8,128)(2,1)S(1)}, u32[]{:S(2)}, u32[]{:S(2)}) async-start(bf16[4,256,768]{2,1,0:T(8,128)(2,1)} %bitcast.102), calls=%async_computation | async-start | bytes 3145728 | tf_op jit(solution)/shard_map/all_to_all | solution.py:508
  76.8 135.5 %all-gather.12.cloned.1.call-start = ((), (), s32[]{:S(2)}) async-start(), calls=%async_computation.11 | async-start | bytes 2621440 | tf_op jit(solution)/shard_map/all_gather | solution.py:145
  116.5 114.3 %collective-permute-start.11 = (bf16[2048,1024]{1,0:T(8,128)(2,1)}, bf16[2048,1024]{1,0:T(8,128)(2,1)}, u32[]{:S(2)}, u32[]{:S(2)}) collective-permute-start(bf16[2048,1024]{1,0:T(8,128)(2,1)} %slice_dynamic-update-slice_fusion.refs_0_.refs_4_), channel_id=1, source_target_pairs={{0,2},{2,0},{1,3},{3,1},{4,6},{6,4},{5,7},{7,5},{8,10},{10,8},{9,1... | collective-permute-start | bytes 12582920 | tf_op jit(solution)/shard_map/ppermute | solution.py:1246
  120.4 12.6 %all-to-all-start.1 = ((bf16[4,256,256]{2,1,0:T(8,128)(2,1)}), bf16[4,256,256]{2,1,0:T(8,128)(2,1)S(1)}, u32[]{:S(2)}, u32[]{:S(2)}) async-start(bf16[4,256,256]{2,1,0:T(8,128)(2,1)} %bitcast.106), calls=%async_computation.1 | async-start | bytes 1048576 | tf_op jit(solution)/shard_map/all_to_all | solution.py:508
  123.9 13.2 %collective-permute-start.10 = (bf16[128,1024]{1,0:T(8,128)(2,1)S(1)}, bf16[128,1024]{1,0:T(8,128)(2,1)S(1)}, u32[]{:S(2)}, u32[]{:S(2)}) collective-permute-start(bf16[128,1024]{1,0:T(8,128)(2,1)S(1)} %get-tuple-element.480), channel_id=1, source_target_pairs={{0,8},{1,24},{8,0},{9,16},{16,9},{17,25},{24,1},{25,17},{2,10},{3,... | collective-permute-start | bytes 786440 | tf_op jit(solution)/shard_map/ppermute | solution.py:83
  124.0 14.3 %collective-permute-start.9 = (bf16[128,1024]{1,0:T(8,128)(2,1)S(1)}, bf16[128,1024]{1,0:T(8,128)(2,1)}, u32[]{:S(2)}, u32[]{:S(2)}) collective-permute-start(bf16[128,1024]{1,0:T(8,128)(2,1)S(1)} %get-tuple-element.479), channel_id=1, source_target_pairs={{0,0},{1,16},{8,8},{9,24},{16,1},{17,17},{24,9},{25,25},{2,2},{3,1... | collective-permute-start | bytes 786440 | tf_op jit(solution)/shard_map/ppermute | solution.py:82
  133.0 47.9 %collective-permute-start.6 = (bf16[768,512]{1,0:T(8,128)(2,1)}, bf16[768,512]{1,0:T(8,128)(2,1)S(1)}, u32[]{:S(2)}, u32[]{:S(2)}) collective-permute-start(bf16[768,512]{1,0:T(8,128)(2,1)} %get-tuple-element.234), channel_id=1, source_target_pairs={{0,1},{1,0},{4,5},{5,4},{2,3},{3,2},{6,7},{7,6},{8,9},{9,8},{12,13... | collective-permute-start | bytes 2359304 | tf_op jit(solution)/shard_map/ppermute | solution.py:528
  135.1 45.8 %collective-permute-start.7 = (bf16[768,512]{1,0:T(8,128)(2,1)}, bf16[768,512]{1,0:T(8,128)(2,1)S(1)}, u32[]{:S(2)}, u32[]{:S(2)}) collective-permute-start(bf16[768,512]{1,0:T(8,128)(2,1)} %get-tuple-element.235), channel_id=1, source_target_pairs={{0,4},{1,5},{4,0},{5,1},{2,6},{3,7},{6,2},{7,3},{8,12},{9,13},{12,... | collective-permute-start | bytes 2359304 | tf_op jit(solution)/shard_map/ppermute | solution.py:528
  137.1 43.8 %collective-permute-start.8 = (bf16[768,512]{1,0:T(8,128)(2,1)}, bf16[768,512]{1,0:T(8,128)(2,1)S(1)}, u32[]{:S(2)}, u32[]{:S(2)}) collective-permute-start(bf16[768,512]{1,0:T(8,128)(2,1)} %get-tuple-element.236), channel_id=1, source_target_pairs={{0,5},{1,4},{4,1},{5,0},{2,7},{3,6},{6,3},{7,2},{8,13},{9,12},{12,... | collective-permute-start | bytes 2359304 | tf_op jit(solution)/shard_map/ppermute | solution.py:528
  147.3 30.2 %all-to-all-start.2 = ((bf16[4,256,256]{2,1,0:T(8,128)(2,1)}), bf16[4,256,256]{2,1,0:T(8,128)(2,1)S(1)}, u32[]{:S(2)}, u32[]{:S(2)}) async-start(bf16[4,256,256]{2,1,0:T(8,128)(2,1)} %bitcast.117), calls=%async_computation.2 | async-start | bytes 1048576 | tf_op jit(solution)/shard_map/all_to_all | solution.py:508
  208.8 12.3 %all-to-all-start.3 = ((bf16[4,256,256]{2,1,0:T(8,128)(2,1)}), bf16[4,256,256]{2,1,0:T(8,128)(2,1)S(1)}, u32[]{:S(2)}, u32[]{:S(2)}) async-start(bf16[4,256,256]{2,1,0:T(8,128)(2,1)} %bitcast.107), calls=%async_computation.3 | async-start | bytes 1048576 | tf_op jit(solution)/shard_map/all_to_all | solution.py:508
  212.3 28.0 %collective-permute-start.12 = (bf16[2048,1024]{1,0:T(8,128)(2,1)}, bf16[2048,1024]{1,0:T(8,128)(2,1)}, u32[]{:S(2)}, u32[]{:S(2)}) collective-permute-start(bf16[2048,1024]{1,0:T(8,128)(2,1)} %slice_dynamic-update-slice_fusion.refs_0_.refs_4_), channel_id=1, source_target_pairs={{0,1},{1,0},{2,3},{3,2},{4,5},{5,4},{6,7},{7,6},{8,9},{9,8},{10,11... | collective-permute-start | bytes 12582920 | tf_op jit(solution)/shard_map/ppermute | solution.py:1269
  230.8 9.6 %collective-permute-start.13 = (bf16[2048,1024]{1,0:T(8,128)(2,1)}, bf16[2048,1024]{1,0:T(8,128)(2,1)}, u32[]{:S(2)}, u32[]{:S(2)}) collective-permute-start(bf16[2048,1024]{1,0:T(8,128)(2,1)} %collective-permute-done.11.refs_2_.refs_6_), channel_id=1, source_target_pairs={{0,1},{1,0},{2,3},{3,2},{4,5},{5,4},{6,7},{7,6},{8,9},{9,8},{10,11... | collective-permute-start | bytes 12582920 | tf_op jit(solution)/shard_map/ppermute | solution.py:1273
  280.5 15.3 %all-to-all-start.4 = ((bf16[4,256,256]{2,1,0:T(8,128)(2,1)}), bf16[4,256,256]{2,1,0:T(8,128)(2,1)S(1)}, u32[]{:S(2)}, u32[]{:S(2)}) async-start(bf16[4,256,256]{2,1,0:T(8,128)(2,1)} %bitcast.115), calls=%async_computation.4 | async-start | bytes 1048576 | tf_op jit(solution)/shard_map/all_to_all | solution.py:508
  284.0 228.9 %reduce-scatter.2.cloned.1.call-start = ((), (), s32[]{:S(2)}) async-start(), calls=%async_computation.12 | async-start | bytes 17825792 | tf_op jit(solution)/shard_map/reduce_scatter | solution.py:855
  297.1 31.5 %collective-permute-start.14 = (bf16[128,1024]{1,0:T(8,128)(2,1)S(1)}, bf16[128,1024]{1,0:T(8,128)(2,1)S(1)}, u32[]{:S(2)}, u32[]{:S(2)}) collective-permute-start(bf16[128,1024]{1,0:T(8,128)(2,1)S(1)} %get-tuple-element.477), channel_id=1, source_target_pairs={{0,0},{16,1},{8,8},{24,9},{1,16},{17,17},{9,24},{25,25},{2,2},{18,... | collective-permute-start | bytes 786440 | tf_op jit(solution)/shard_map/ppermute | solution.py:89
  297.9 30.7 %collective-permute-start.15 = (bf16[128,1024]{1,0:T(8,128)(2,1)S(1)}, bf16[128,1024]{1,0:T(8,128)(2,1)S(1)}, u32[]{:S(2)}, u32[]{:S(2)}) collective-permute-start(bf16[128,1024]{1,0:T(8,128)(2,1)S(1)} %get-tuple-element.478), channel_id=1, source_target_pairs={{8,0},{24,1},{0,8},{16,9},{9,16},{25,17},{1,24},{17,25},{10,2},{26... | collective-permute-start | bytes 786440 | tf_op jit(solution)/shard_map/ppermute | solution.py:89
  353.6 12.3 %all-to-all-start.6 = ((bf16[4,256,256]{2,1,0:T(8,128)(2,1)}), bf16[4,256,256]{2,1,0:T(8,128)(2,1)S(1)}, u32[]{:S(2)}, u32[]{:S(2)}) async-start(bf16[4,256,256]{2,1,0:T(8,128)(2,1)} %bitcast.116), calls=%async_computation.6 | async-start | bytes 1048576 | tf_op jit(solution)/shard_map/all_to_all | solution.py:508
  365.9 21.2 %collective-permute-start.16 = (bf16[512,3072]{1,0:T(8,128)(2,1)}, bf16[512,3072]{1,0:T(8,128)(2,1)S(1)}, u32[]{:S(2)}, u32[]{:S(2)}) collective-permute-start(bf16[512,3072]{1,0:T(8,128)(2,1)} %get-tuple-element.304), channel_id=1, source_target_pairs={{0,1},{1,0},{2,3},{3,2},{4,5},{5,4},{6,7},{7,6},{8,9},{9,8},{10,11... | collective-permute-start | bytes 9437192 | tf_op jit(solution)/shard_map/ppermute | solution.py:648
  366.5 25.9 %collective-permute-start.17 = (bf16[768,512]{1,0:T(8,128)(2,1)}, bf16[768,512]{1,0:T(8,128)(2,1)S(1)}, u32[]{:S(2)}, u32[]{:S(2)}) collective-permute-start(bf16[768,512]{1,0:T(8,128)(2,1)} %get-tuple-element.309), channel_id=1, source_target_pairs={{0,1},{1,0},{4,5},{5,4},{2,3},{3,2},{6,7},{7,6},{8,9},{9,8},{12,13... | collective-permute-start | bytes 2359304 | tf_op jit(solution)/shard_map/ppermute | solution.py:528
  366.9 25.4 %collective-permute-start.18 = (bf16[768,512]{1,0:T(8,128)(2,1)}, bf16[768,512]{1,0:T(8,128)(2,1)}, u32[]{:S(2)}, u32[]{:S(2)}) collective-permute-start(bf16[768,512]{1,0:T(8,128)(2,1)} %get-tuple-element.310), channel_id=1, source_target_pairs={{0,4},{1,5},{4,0},{5,1},{2,6},{3,7},{6,2},{7,3},{8,12},{9,13},{12,... | collective-permute-start | bytes 2359304 | tf_op jit(solution)/shard_map/ppermute | solution.py:528
  367.3 35.4 %collective-permute-start.19 = (bf16[768,512]{1,0:T(8,128)(2,1)}, bf16[768,512]{1,0:T(8,128)(2,1)}, u32[]{:S(2)}, u32[]{:S(2)}) collective-permute-start(bf16[768,512]{1,0:T(8,128)(2,1)} %get-tuple-element.311), channel_id=1, source_target_pairs={{0,5},{1,4},{4,1},{5,0},{2,7},{3,6},{6,3},{7,2},{8,13},{9,12},{12,... | collective-permute-start | bytes 2359304 | tf_op jit(solution)/shard_map/ppermute | solution.py:528
  391.0 18.7 %copy-start.51 = (f32[1,4096]{1,0:T(1,128)S(1)}, f32[1,4096]{1,0:T(1,128)}, u32[]{:S(2)}) copy-start(f32[1,4096]{1,0:T(1,128)} %get-tuple-element.340) | copy-start | bytes 49156
  392.4 19.4 %copy-start.30 = (bf16[768,512]{1,0:T(8,128)(2,1)}, bf16[768,512]{1,0:T(8,128)(2,1)S(1)}, u32[]{:S(2)}) copy-start(bf16[768,512]{1,0:T(8,128)(2,1)S(1)} %collective-permute-done.17.refs_1_) | copy-start | bytes 2359300
  406.9 16.8 %collective-permute-start.20 = (bf16[256,768]{1,0:T(8,128)(2,1)}, bf16[256,768]{1,0:T(8,128)(2,1)S(1)}, u32[]{:S(2)}, u32[]{:S(2)}) collective-permute-start(bf16[256,768]{1,0:T(8,128)(2,1)} %get-tuple-element.330), channel_id=1, source_target_pairs={{0,1},{1,0},{4,5},{5,4},{2,3},{3,2},{6,7},{7,6},{8,9},{9,8},{12,13... | collective-permute-start | bytes 1179656 | tf_op jit(solution)/shard_map/ppermute | solution.py:528
  407.8 15.9 %collective-permute-start.21 = (bf16[256,768]{1,0:T(8,128)(2,1)}, bf16[256,768]{1,0:T(8,128)(2,1)S(1)}, u32[]{:S(2)}, u32[]{:S(2)}) collective-permute-start(bf16[256,768]{1,0:T(8,128)(2,1)} %get-tuple-element.331), channel_id=1, source_target_pairs={{0,4},{1,5},{4,0},{5,1},{2,6},{3,7},{6,2},{7,3},{8,12},{9,13},{12,... | collective-permute-start | bytes 1179656 | tf_op jit(solution)/shard_map/ppermute | solution.py:528
  408.2 18.3 %collective-permute-start.22 = (bf16[256,768]{1,0:T(8,128)(2,1)}, bf16[256,768]{1,0:T(8,128)(2,1)S(1)}, u32[]{:S(2)}, u32[]{:S(2)}) collective-permute-start(bf16[256,768]{1,0:T(8,128)(2,1)} %get-tuple-element.332), channel_id=1, source_target_pairs={{0,5},{1,4},{4,1},{5,0},{2,7},{3,6},{6,3},{7,2},{8,13},{9,12},{12,... | collective-permute-start | bytes 1179656 | tf_op jit(solution)/shard_map/ppermute | solution.py:528
  434.8 12.6 %collective-permute-start.23 = (bf16[512,1536]{1,0:T(8,128)(2,1)}, bf16[512,1536]{1,0:T(8,128)(2,1)}, u32[]{:S(2)}, u32[]{:S(2)}) collective-permute-start(bf16[512,1536]{1,0:T(8,128)(2,1)} %get-tuple-element.353), channel_id=1, source_target_pairs={{0,1},{1,0},{2,3},{3,2},{4,5},{5,4},{6,7},{7,6},{8,9},{9,8},{10,11... | collective-permute-start | bytes 4718600 | tf_op jit(solution)/shard_map/ppermute | solution.py:648
  435.4 15.4 %collective-permute-start.24 = (bf16[512,1664]{1,0:T(8,128)(2,1)}, bf16[512,1664]{1,0:T(8,128)(2,1)}, u32[]{:S(2)}, u32[]{:S(2)}) collective-permute-start(bf16[512,1664]{1,0:T(8,128)(2,1)} %get-tuple-element.357), channel_id=1, source_target_pairs={{0,1},{1,0},{2,3},{3,2},{4,5},{5,4},{6,7},{7,6},{8,9},{9,8},{10,11... | collective-permute-start | bytes 5111816 | tf_op jit(solution)/shard_map/ppermute | solution.py:648
  435.5 21.6 %collective-permute-start.25 = (bf16[512,2048]{1,0:T(8,128)(2,1)}, bf16[512,2048]{1,0:T(8,128)(2,1)S(1)}, u32[]{:S(2)}, u32[]{:S(2)}) collective-permute-start(bf16[512,2048]{1,0:T(8,128)(2,1)} %get-tuple-element.359), channel_id=1, source_target_pairs={{0,1},{1,0},{2,3},{3,2},{4,5},{5,4},{6,7},{7,6},{8,9},{9,8},{10,11... | collective-permute-start | bytes 6291464 | tf_op jit(solution)/shard_map/ppermute | solution.py:648
  435.9 37.5 %collective-permute-start.26 = (bf16[256,3072]{1,0:T(8,128)(2,1)}, bf16[256,3072]{1,0:T(8,128)(2,1)S(1)}, u32[]{:S(2)}, u32[]{:S(2)}) collective-permute-start(bf16[256,3072]{1,0:T(8,128)(2,1)} %slice.404), channel_id=1, source_target_pairs={{0,4},{4,0},{1,5},{5,1},{2,6},{6,2},{3,7},{7,3},{8,12},{12,8},{9,1... | collective-permute-start | bytes 4718600 | tf_op jit(solution)/shard_map/ppermute | solution.py:648
  443.4 33.1 %collective-permute-start.27 = (bf16[384,1024]{1,0:T(8,128)(2,1)}, bf16[384,1024]{1,0:T(8,128)(2,1)S(1)}, u32[]{:S(2)}, u32[]{:S(2)}) collective-permute-start(bf16[384,1024]{1,0:T(8,128)(2,1)} %get-tuple-element.362), channel_id=1, source_target_pairs={{0,0},{16,1},{8,8},{24,9},{1,16},{17,17},{9,24},{25,25},{2,2},{18,... | collective-permute-start | bytes 2359304 | tf_op jit(solution)/shard_map/ppermute | solution.py:89
  450.8 40.2 %collective-permute-start.29 = (bf16[256,1536]{1,0:T(8,128)(2,1)S(1)}, bf16[256,1536]{1,0:T(8,128)(2,1)S(1)}, u32[]{:S(2)}, u32[]{:S(2)}) collective-permute-start(bf16[256,1536]{1,0:T(8,128)(2,1)S(1)} %slice.408), channel_id=1, source_target_pairs={{0,2},{2,0},{1,3},{3,1},{4,6},{6,4},{5,7},{7,5},{8,10},{10,8},{9,1... | collective-permute-start | bytes 2359304 | tf_op jit(solution)/shard_map/ppermute | solution.py:648
  455.3 35.5 %collective-permute-start.28 = (bf16[256,1664]{1,0:T(8,128)(2,1)S(1)}, bf16[256,1664]{1,0:T(8,128)(2,1)S(1)}, u32[]{:S(2)}, u32[]{:S(2)}) collective-permute-start(bf16[256,1664]{1,0:T(8,128)(2,1)S(1)} %slice.406), channel_id=1, source_target_pairs={{0,4},{4,0},{1,5},{5,1},{2,6},{6,2},{3,7},{7,3},{8,12},{12,8},{9,1... | collective-permute-start | bytes 2555912 | tf_op jit(solution)/shard_map/ppermute | solution.py:648
  476.5 34.5 %collective-permute-start.30 = (bf16[256,2048]{1,0:T(8,128)(2,1)S(1)}, bf16[256,2048]{1,0:T(8,128)(2,1)S(1)}, u32[]{:S(2)}, u32[]{:S(2)}) collective-permute-start(bf16[256,2048]{1,0:T(8,128)(2,1)S(1)} %slice.405), channel_id=1, source_target_pairs={{0,4},{4,0},{1,5},{5,1},{2,6},{6,2},{3,7},{7,3},{8,12},{12,8},{9,1... | collective-permute-start | bytes 3145736 | tf_op jit(solution)/shard_map/ppermute | solution.py:648
  477.0 35.9 %collective-permute-start.31 = (bf16[128,3072]{1,0:T(8,128)(2,1)}, bf16[128,3072]{1,0:T(8,128)(2,1)}, u32[]{:S(2)}, u32[]{:S(2)}) collective-permute-start(bf16[128,3072]{1,0:T(8,128)(2,1)} %slice.407), channel_id=1, source_target_pairs={{0,2},{2,0},{1,3},{3,1},{4,6},{6,4},{5,7},{7,5},{8,10},{10,8},{9,1... | collective-permute-start | bytes 2359304 | tf_op jit(solution)/shard_map/ppermute | solution.py:648
  477.0 38.0 %collective-permute-start.32 = (bf16[384,1024]{1,0:T(8,128)(2,1)}, bf16[384,1024]{1,0:T(8,128)(2,1)}, u32[]{:S(2)}, u32[]{:S(2)}) collective-permute-start(bf16[384,1024]{1,0:T(8,128)(2,1)} %get-tuple-element.375), channel_id=1, source_target_pairs={{8,0},{24,1},{0,8},{16,9},{9,16},{25,17},{1,24},{17,25},{10,2},{26... | collective-permute-start | bytes 2359304 | tf_op jit(solution)/shard_map/ppermute | solution.py:89
  492.2 18.9 %slice-start.1 = ((f32[512,2048]{1,0:T(8,128)}), f32[256,2048]{1,0:T(8,128)S(1)}, s32[]{:S(2)}) async-start(f32[512,2048]{1,0:T(8,128)} %copy-done.1), calls=%async_computation.14 | async-start | bytes 4194304 | tf_op jit(solution)/shard_map/slice | solution.py:797
  493.0 21.9 %collective-permute-start.33 = (bf16[128,1664]{1,0:T(8,128)(2,1)}, bf16[128,1664]{1,0:T(8,128)(2,1)S(1)}, u32[]{:S(2)}, u32[]{:S(2)}) collective-permute-start(bf16[128,1664]{1,0:T(8,128)(2,1)} %slice.410), channel_id=1, source_target_pairs={{0,2},{2,0},{1,3},{3,1},{4,6},{6,4},{5,7},{7,5},{8,10},{10,8},{9,1... | collective-permute-start | bytes 1277960 | tf_op jit(solution)/shard_map/ppermute | solution.py:648
  493.1 26.5 %collective-permute-start.34 = (bf16[128,1536]{1,0:T(8,128)(2,1)S(1)}, bf16[128,1536]{1,0:T(8,128)(2,1)}, u32[]{:S(2)}, u32[]{:S(2)}) collective-permute-start(bf16[128,1536]{1,0:T(8,128)(2,1)S(1)} %slice.412), channel_id=1, source_target_pairs={{0,4},{4,0},{1,5},{5,1},{2,6},{6,2},{3,7},{7,3},{8,12},{12,8},{9,1... | collective-permute-start | bytes 1179656 | tf_op jit(solution)/shard_map/ppermute | solution.py:648
  512.8 21.5 %collective-permute-start.38 = (bf16[128,2048]{1,0:T(8,128)(2,1)S(1)}, bf16[128,2048]{1,0:T(8,128)(2,1)S(1)}, u32[]{:S(2)}, u32[]{:S(2)}) collective-permute-start(bf16[128,2048]{1,0:T(8,128)(2,1)S(1)} %slice.409), channel_id=1, source_target_pairs={{0,2},{2,0},{1,3},{3,1},{4,6},{6,4},{5,7},{7,5},{8,10},{10,8},{9,1... | collective-permute-start | bytes 1572872 | tf_op jit(solution)/shard_map/ppermute | solution.py:648
  520.7 11.0 %collective-permute-start.35 = (bf16[64,3072]{1,0:T(8,128)(2,1)S(1)}, bf16[64,3072]{1,0:T(8,128)(2,1)S(1)}, u32[]{:S(2)}, u32[]{:S(2)}) collective-permute-start(bf16[64,3072]{1,0:T(8,128)(2,1)S(1)} %slice.411), channel_id=1, source_target_pairs={{0,8},{8,0},{16,24},{24,16},{1,9},{9,1},{17,25},{25,17},{2,10},{10... | collective-permute-start | bytes 1179656 | tf_op jit(solution)/shard_map/ppermute | solution.py:647
  522.5 11.8 %collective-permute-start.36 = (bf16[128,1024]{1,0:T(8,128)(2,1)S(1)}, bf16[128,1024]{1,0:T(8,128)(2,1)S(1)}, u32[]{:S(2)}, u32[]{:S(2)}) collective-permute-start(bf16[128,1024]{1,0:T(8,128)(2,1)S(1)} %copy-done.45), channel_id=1, source_target_pairs={{0,0},{16,1},{8,8},{24,9},{1,16},{17,17},{9,24},{25,25},{2,2},{18,... | collective-permute-start | bytes 786440 | tf_op jit(solution)/shard_map/ppermute | solution.py:89
  523.2 22.8 %collective-permute-start.39 = (bf16[8,32,1024]{2,1,0:T(8,128)(2,1)S(1)}, bf16[8,32,1024]{2,1,0:T(8,128)(2,1)S(1)}, u32[]{:S(2)}, u32[]{:S(2)}) collective-permute-start(bf16[8,32,1024]{2,1,0:T(8,128)(2,1)S(1)} %dynamic-slice_bitcast_fusion.2), channel_id=1, source_target_pairs={{0,4},{4,0},{1,5},{5,1},{2,6},{6,2},{3,7},{7,3},{8,12},{12,8},{9,1... | collective-permute-start | bytes 1572872 | tf_op jit(solution)/shard_map/ppermute | solution.py:648
  523.3 24.7 %collective-permute-start.40 = (bf16[64,1664]{1,0:T(8,128)(2,1)S(1)}, bf16[64,1664]{1,0:T(8,128)(2,1)S(1)}, u32[]{:S(2)}, u32[]{:S(2)}) collective-permute-start(bf16[64,1664]{1,0:T(8,128)(2,1)S(1)} %slice.414), channel_id=1, source_target_pairs={{0,8},{8,0},{16,24},{24,16},{1,9},{9,1},{17,25},{25,17},{2,10},{10... | collective-permute-start | bytes 638984 | tf_op jit(solution)/shard_map/ppermute | solution.py:647
  531.7 16.7 %collective-permute-start.41 = (bf16[64,1536]{1,0:T(8,128)(2,1)S(1)}, bf16[64,1536]{1,0:T(8,128)(2,1)S(1)}, u32[]{:S(2)}, u32[]{:S(2)}) collective-permute-start(bf16[64,1536]{1,0:T(8,128)(2,1)S(1)} %slice.416), channel_id=1, source_target_pairs={{0,8},{8,0},{16,24},{24,16},{1,9},{9,1},{17,25},{25,17},{2,10},{10... | collective-permute-start | bytes 589832 | tf_op jit(solution)/shard_map/ppermute | solution.py:647
  535.2 37.4 %collective-permute-start.42 = (bf16[64,2048]{1,0:T(8,128)(2,1)S(1)}, bf16[64,2048]{1,0:T(8,128)(2,1)S(1)}, u32[]{:S(2)}, u32[]{:S(2)}) collective-permute-start(bf16[64,2048]{1,0:T(8,128)(2,1)S(1)} %slice.413), channel_id=1, source_target_pairs={{0,8},{8,0},{16,24},{24,16},{1,9},{9,1},{17,25},{25,17},{2,10},{10... | collective-permute-start | bytes 786440 | tf_op jit(solution)/shard_map/ppermute | solution.py:647
  535.3 20.8 %collective-permute-start.45 = (bf16[32,3072]{1,0:T(8,128)(2,1)S(1)}, bf16[32,3072]{1,0:T(8,128)(2,1)S(1)}, u32[]{:S(2)}, u32[]{:S(2)}) collective-permute-start(bf16[32,3072]{1,0:T(8,128)(2,1)S(1)} %slice.415), channel_id=1, source_target_pairs={{0,16},{8,24},{16,0},{24,8},{1,17},{9,25},{17,1},{25,9},{2,18},{10... | collective-permute-start | bytes 589832 | tf_op jit(solution)/shard_map/ppermute | solution.py:647
  546.1 27.5 %collective-permute-start.37 = (bf16[128,1024]{1,0:T(8,128)(2,1)S(1)}, bf16[128,1024]{1,0:T(8,128)(2,1)S(1)}, u32[]{:S(2)}, u32[]{:S(2)}) collective-permute-start(bf16[128,1024]{1,0:T(8,128)(2,1)S(1)} %copy-done.44), channel_id=1, source_target_pairs={{8,0},{24,1},{0,8},{16,9},{9,16},{25,17},{1,24},{17,25},{10,2},{26... | collective-permute-start | bytes 786440 | tf_op jit(solution)/shard_map/ppermute | solution.py:89
  549.3 23.4 %slice-start.9 = ((f32[128,2048]{1,0:T(8,128)}), f32[64,2048]{1,0:T(8,128)S(1)}, s32[]{:S(2)}) async-start(f32[128,2048]{1,0:T(8,128)} %copy-done.14), calls=%async_computation.22 | async-start | bytes 1048576 | tf_op jit(solution)/shard_map/slice | solution.py:797
  550.1 22.6 %collective-permute-start.43 = (bf16[32,1536]{1,0:T(8,128)(2,1)S(1)}, bf16[32,1536]{1,0:T(8,128)(2,1)S(1)}, u32[]{:S(2)}, u32[]{:S(2)}) collective-permute-start(bf16[32,1536]{1,0:T(8,128)(2,1)S(1)} %slice.419), channel_id=1, source_target_pairs={{0,16},{8,24},{16,0},{24,8},{1,17},{9,25},{17,1},{25,9},{2,18},{10... | collective-permute-start | bytes 294920 | tf_op jit(solution)/shard_map/ppermute | solution.py:647
  556.0 14.5 %collective-permute-start.44 = (bf16[32,1664]{1,0:T(8,128)(2,1)S(1)}, bf16[32,1664]{1,0:T(8,128)(2,1)S(1)}, u32[]{:S(2)}, u32[]{:S(2)}) collective-permute-start(bf16[32,1664]{1,0:T(8,128)(2,1)S(1)} %slice.418), channel_id=1, source_target_pairs={{0,16},{8,24},{16,0},{24,8},{1,17},{9,25},{17,1},{25,9},{2,18},{10... | collective-permute-start | bytes 319496 | tf_op jit(solution)/shard_map/ppermute | solution.py:647
  572.7 7.8 %collective-permute-start.46 = (bf16[32,2048]{1,0:T(8,128)(2,1)S(1)}, bf16[32,2048]{1,0:T(8,128)(2,1)S(1)}, u32[]{:S(2)}, u32[]{:S(2)}) collective-permute-start(bf16[32,2048]{1,0:T(8,128)(2,1)S(1)} %slice.417), channel_id=1, source_target_pairs={{0,16},{8,24},{16,0},{24,8},{1,17},{9,25},{17,1},{25,9},{2,18},{10... | collective-permute-start | bytes 393224 | tf_op jit(solution)/shard_map/ppermute | solution.py:647
  (66 other events, 433.7 us)
Sparse Core Ops, SparseCore 0:
  9.6 49.3 all-gather.5
  60.5 34.4 all-gather.7
  96.6 44.8 all-gather.9
  143.0 38.2 all-gather.11
  295.9 193.3 reduce-scatter.1

commit v4 on v3

--- a/solution.py
+++ b/solution.py
@@ -530,12 +530,6 @@
     ]
 
 
-def during(blocks, work, inputs):
-    own, inputs = chain(blocks[0], inputs)
-    results, received = chain(work(*inputs), exchange(blocks)[1:])
-    return [own, *received], results
-
-
 def during_members(blocks, work, inputs):
     blocks, inputs = chain(blocks, inputs)
     results, received = chain(work(*inputs), to_members(blocks))
@@ -679,6 +673,16 @@
 
 def total_rows(rows):
     return jnp.sum(rows.astype(jnp.float32), 0, keepdims=True)
+
+
+def three_lefts_kernel(*refs):
+    for rows_ref, out_ref in zip(refs[:3], refs[4:]):
+        out_ref[...] = back_product(rows_ref, refs[3]).astype(jnp.bfloat16)
+
+
+def three_lefts(attended, normed, crossed, pick):
+    shape = jax.ShapeDtypeStruct(normed.shape, jnp.bfloat16)
+    return small_kernel(three_lefts_kernel, [], [attended, normed, crossed, pick], [shape] * 3)
 
 
 def three_kernel(
@@ -794,11 +798,11 @@
     def step(self):
         total = self.value.astype(jnp.float32) + self.pending.astype(jnp.float32)
         half = total.shape[0] // 2
-        self.value = total[:half]
+        self.value = total[:half].astype(jnp.bfloat16)
         self.send(total[half:])
 
     def finish(self):
-        total = self.value + self.pending.astype(jnp.float32)
+        total = self.value.astype(jnp.float32) + self.pending.astype(jnp.float32)
         if self.count > 1:
             total = lax.psum_scatter(
                 total.astype(jnp.bfloat16), "s", scatter_dimension=0, tiled=True
@@ -1161,6 +1165,9 @@
     facts_one, facts_two = to_packs(facts)
     tokens_in = jnp.concatenate(to_packs(tokens), 0)
     small = jnp.concatenate([vectors.T, feed_bias.reshape(D // 4, 4).T, self_bias[None, :]], 0)
+    own_ids = jnp.concatenate([facts_one[:slots], facts_two[:slots]])
+    ids = lax.all_gather(own_ids, GROUP, axis=0, tiled=True)
+    ids, small = chain(ids, small)
     full_small = lax.all_gather(small, ("x", "core"), axis=1, tiled=True)
     vec = full_small[:12].astype(jnp.float32)
     bias_row = full_small[12:16].T.reshape(4 * D).astype(jnp.float32)
@@ -1175,8 +1182,6 @@
 
     lengths = facts_one[slots : slots + NSEQ]
     limits = facts_one[slots + NSEQ : slots + 2 * NSEQ]
-    own_ids = jnp.concatenate([facts_one[:slots], facts_two[:slots]])
-    ids = lax.all_gather(own_ids, GROUP, axis=0, tiled=True)
     ends = jnp.cumsum(lengths)
     key_ids = gather_sequence(ids, count)
     rank = jnp.sum((ids[None, :] < ids[:, None]).astype(jnp.int32), 1)
@@ -1219,9 +1224,6 @@
     def relative(matrix, name):
         return relative_columns(matrix, count, orders[name])
 
-    facts_known = (rank, self_flags, cross_flags, key_order, enc_places, self_low, cross_low, cross_high)
-    tokens_in, facts_known = chain(tokens_in, facts_known)
-    rank, self_flags, cross_flags, key_order, enc_places, self_low, cross_low, cross_high = facts_known
     qkv = project_heads(tokens_in, full_self_in, jnp.concatenate([vec[6], zero_row, vec[7]]))
     feed_own = stack_feed(feed_up, feed_down)
     own_heads = sort_rows(to_members(qkv), rank)
@@ -1258,9 +1260,6 @@
         after=(vec[8],),
     )
     cross_heads = sort_rows(to_members(cross_queries), rank)
-    attended_y = relative(as_columns(attended), "y")
-    normed_one_y = relative(normed_one_low, "y")
-    (attended_y, normed_one_y), cross_heads = chain((attended_y, normed_one_y), cross_heads)
     crossed_heads, exact_cross, log_cross = attend_forward(
         (cross_heads, 0), (enc_heads, 0), (enc_heads, 1), cross_low, cross_high, enc_ids,
         cross_flags, block, cross_chunk,
@@ -1274,8 +1273,6 @@
     normed_two, normed_two_low, unit_two, inverse_two = project_norm(
         by_member(crossed), full_cross_out, vec[10], normed_one, vec[1], vec[4]
     )
-    crossed_y = relative(as_columns(crossed), "y")
-    crossed_y, normed_two_low = chain(crossed_y, normed_two_low)
     slope, hidden = feed_up_gelu(normed_two_low, feed_shards, bias_row)
     layer_low, grad_three, grad_branch, sums_three = feed_down_norm(
         hidden, feed_shards, vec[11], normed_two, vec[2], vec[5], grad_in
@@ -1300,8 +1297,10 @@
     layer_out, dq_heads = chain(layer_out, dq_heads)
     if count > 1:
         enc_pair_grads = cut(scatter_sequence(enc_pair_grads[0], count))
-    dq_blocks, (enc_pair_grads,) = during_members(
-        unsort_rows([dq_heads], rank), lambda *rest: rest, (enc_pair_grads,)
+    dq_blocks, (enc_pair_grads, lefts) = during_members(
+        unsort_rows([dq_heads], rank),
+        lambda pairs, *rows: (pairs, three_lefts(*rows, pick_y)),
+        (enc_pair_grads, by_member(attended), normed_one_low, by_member(crossed)),
     )
     enc_blocks = exchange(enc_pair_grads)
     grad_one, grad_attended_out, sums_one, grad_attended = back_norm(
@@ -1311,7 +1310,7 @@
     received, (*three_parts, query_sums) = during_members(
         grad_attended,
         lambda blocks: three_grads(
-            attended_y, normed_one_y, crossed_y, grad_attended_out, blocks, grad_crossed_out
+            *lefts, grad_attended_out, blocks, grad_crossed_out
         ),
         (dq_blocks,),
     )
@@ -1325,11 +1324,11 @@
 
     dq_heads, three_sum.pending = chain(dq_heads, three_sum.pending)
     three_sum.step()
-    (dq_heads, three_sum.sent, three_sum.value), enc_blocks = chain(
-        (dq_heads, three_sum.sent, three_sum.value), enc_blocks
-    )
-
-    blocks, me = chain(unsort_blocks([dq_heads, pair_heads], rank), group_index()[None])
+    dq_heads, three_sum.value = chain(dq_heads, three_sum.value)
+
+    blocks, (me, enc_blocks) = chain(
+        unsort_blocks([dq_heads, pair_heads], rank), (group_index()[None], enc_blocks)
+    )
     received = exchange(blocks)
     *pair_parts, enc_first, enc_rest, value_sums = encoder_grads(
         me, encoder_y, full_cross_pair, enc_blocks

time: 595 us -> 586 us (0.985)
  waiting for transfers between devices: 144 us -> 162 us
  blocking collectives: 40.3 us -> 24.4 us
  starting transfers between devices: 76.2 us -> 89.2 us
  local copies, waits for them, and re-layouts: 50.3 us -> 37.9 us
  matrix products: 13.1 us -> 6.63 us
    all_to_all x1 -> x0, blocking collectives: 15.6 us -> none  [to_members(): return lax.all_to_all(blocks, GROUP, 0, 0, tiled=True)]
    all_gather x1, blocking collectives: 19.6 us -> 5.22 us  [on_device(): full_small = lax.all_gather(small, ('x', 'core'), axis=1, tiled=True)]
    all_gather x1, blocking collectives: 5.07 us -> 19.1 us  [on_device(): ids = lax.all_gather(own_ids, GROUP, axis=0, tiled=True)]
    all_gather x4, waiting for transfers between devices: 0.03 us -> 11 us  [fetch(): return lax.all_gather(weight, ('x', 'core'), axis=0, tiled=True)]
    unnamed x122 -> x92, local copies, waits for them, and re-layouts: 24 us -> 13.1 us
    another operation x2 -> x18, other arithmetic: 0.72 us -> 10.4 us
    add x20 -> x4, other arithmetic: 10.3 us -> 0.83 us  [finish(): total = self.value.astype(jnp.float32) + self.pending.astype(jnp.float32)]
    ppermute x13, waiting for transfers between devices: 47 us -> 55.2 us  [flip(): return lax.ppermute(block, name, [(i, i ^ 1) for i in range(PAIR)])]
  transfers between devices with their start and end apart: 58 -> 59, of which waited for: 15 -> 18; matrix products, arithmetic and copies ran while one was open for 12% -> 11% of each run, Pallas kernels for 31% -> 30%
where the time goes in v4:
time: 586 us; the launch traced here: 582 us
  Pallas kernels  217 us (37%)
  waiting for transfers between devices  162 us (28%)
  starting transfers between devices  89.2 us (15%)
  local copies, waits for them, and re-layouts  37.9 us (6%)
  other arithmetic  29.2 us (5%)
  blocking collectives  24.4 us (4%)
  between operations  15.3 us (3%)
  matrix products  6.63 us (1%)
    pallas_call x15, Pallas kernels, small_kernel(): pl.pallas_call(body, in_specs=[pl.BlockSpec(memory_space=pltpu.SMEM)] * l...  61.9 us
    ppermute x13, waiting for transfers between devices, flip(): return lax.ppermute(block, name, [(i, i ^ 1) for i in range(PAIR)])  55.2 us
    all_to_all x7, waiting for transfers between devices, to_members(): return lax.all_to_all(blocks, GROUP, 0, 0, tiled=True)  41.9 us
    pallas_call x2, Pallas kernels, attend_backward(): pl.pallas_call(functools.partial(backward_kernel, chunk), grid_spec=pltpu...  40.2 us
    pallas_call x2, Pallas kernels, attend_forward(): pl.pallas_call(functools.partial(forward_kernel, chunk), grid_spec=pltpu....  31 us
    ppermute x8, starting transfers between devices, flip(): return lax.ppermute(block, 't', [(i, i ^ step) for i in range(T_SIZE)])  28.8 us
    all_to_all x7, starting transfers between devices, to_members(): return lax.all_to_all(blocks, GROUP, 0, 0, tiled=True)  27.6 us
    ppermute x8, waiting for transfers between devices, flip(): return lax.ppermute(block, 't', [(i, i ^ step) for i in range(T_SIZE)])  19.4 us
  transfers between devices with their start and end apart: 59, of which 18 were waited for; matrix products, arithmetic and copies ran while one was open for 11% of the time, Pallas kernels for 30%

profile of v4, /device:TPU:0, one launch (start us, length us, event | category | flops | bytes accessed | tf_op | source)
XLA Modules:
  0.0 581.5 jit_solution(12109740301632537303)
XLA Ops:
  9.8 3.1 collective-permute-start.3
  12.9 6.0 %collective-permute-done.3 = bf16[128,1024]{1,0:T(8,128)(2,1)S(1)} collective-permute-done((bf16[128,1024]{1,0:T(8,128)(2,1)S(1)}, bf16[128,1024]{1,0:T(8,128)(2,1)S(1)}, u32[]{:S(2)}, u32[]{:S(2)}) %collective-permute-start.3) | collective-permute-done | bytes 262176 | tf_op jit(solution)/shard_map/ppermute | solution.py:83
  25.7 2.1 pad_maximum_fusion
  35.4 19.1 %all-gather = s32[4,1,256]{2,1,0:T(1,128)S(1)} all-gather(s32[1,1,256]{2,1,0:T(1,128)S(1)} %bitcast.137), channel_id=1, replica_groups=mesh['t'=4,'s'=1,'y'=2,'x'=2,'core'=2] {'y','core'}, dimensions={0}, use_global_device_ids=true | all-gather | bytes 5120 | tf_op jit(solution)/shard_map/all_gather | solution.py:1169
  56.3 5.2 all_gather.20
  64.7 6.3 %shard_map.264 = bf16[1024,768]{1,0:T(8,128)(2,1)} custom-call(bf16[256,1024]{1,0:T(8,128)(2,1)} %pad_maximum_fusion.1.rows_ref.base_ref, bf16[1024,3072]{1,0:T(8,128)(2,1)} %all-gather.6.cloned.1.call-done.weight_ref, f32[1,3072]{1,0:T(1,128)} %bitcast.129), custom_call_target="tpu_custom_call" | custom-call | tf_op jit(solution)/shard_map/pallas_call | solution.py:134
  71.1 3.7 all-to-all-start
  81.1 3.0 fusion.7.left_ref
  84.1 10.7 %all-to-all-done = bf16[4,256,768]{2,1,0:T(8,128)(2,1)S(1)} async-done(((bf16[4,256,768]{2,1,0:T(8,128)(2,1)}), bf16[4,256,768]{2,1,0:T(8,128)(2,1)S(1)}, u32[]{:S(2)}, u32[]{:S(2)}) %all-to-all-start) | async-done | bytes 1572896 | tf_op jit(solution)/shard_map/all_to_all | solution.py:508
  96.0 4.3 shard_map.265.q_ref.k_ref.v_ref
  100.3 11.5 %shard_map.266 = (bf16[1024,256]{1,0:T(8,128)(2,1)}, f32[1024,256]{1,0:T(8,128)}, f32[8,1024]{1,0:T(8,128)}) custom-call(s32[16]{0:T(128)} %reshape.287.flags_ref, bf16[1024,768]{1,0:T(8,128)(2,1)} %shard_map.265.q_ref.k_ref.v_ref, bf16[1024,768]{1,0:T(8,128)(2,1)} %shard_map.265.q_ref.k_ref.v_ref, bf16[1024,768]{1,0:T(8,128)(2,1)} %shard_map.265.q_ref.k_ref.v_ref, ...), custom_call_target="tpu_custom_call" | custom-call | tf_op jit(solution)/shard_map/pallas_call | solution.py:952
  114.2 2.8 shard_map.267
  116.9 3.5 all-to-all-start.1
  122.4 7.0 %shard_map.268 = (bf16[768,512]{1,0:T(8,128)(2,1)}, bf16[768,512]{1,0:T(8,128)(2,1)}, bf16[768,512]{1,0:T(8,128)(2,1)}, bf16[768,512]{1,0:T(8,128)(2,1)}) custom-call(s32[1]{0:T(128)} %bitcast.29.me_ref, bf16[768,1024]{1,0:T(8,128)(2,1)} %copy-done.5, bf16[1024,2048]{1,0:T(8,128)(2,1)} %all-gather.8.cloned.1.call-done.weight_ref, f32[1,2048]{1,0:T(1,128)} %bitcast.131), custom_call_target="tpu_custom_call" | custom-call | tf_op jit(solution)/shard_map/pallas_call | solution.py:134
  129.4 2.8 collective-permute-start.6
  132.2 2.0 collective-permute-start.7
  134.8 11.0 %all-gather.10.cloned.1.call-done.weight_ref = bf16[1024,2048]{1,0:T(8,128)(2,1)} async-done(((bf16[256,2048]{1,0:T(8,128)(2,1)}), bf16[1024,2048]{1,0:T(8,128)(2,1)}) %all-gather.10.cloned.1.call-update) | async-done | bytes 4194320 | tf_op jit(solution)/shard_map/all_gather | solution.py:145
  145.8 5.3 shard_map.269
  151.1 3.7 all-to-all-start.2
  159.0 15.7 %all-to-all-done.2 = bf16[4,256,256]{2,1,0:T(8,128)(2,1)S(1)} async-done(((bf16[4,256,256]{2,1,0:T(8,128)(2,1)}), bf16[4,256,256]{2,1,0:T(8,128)(2,1)S(1)}, u32[]{:S(2)}, u32[]{:S(2)}) %all-to-all-start.2) | async-done | bytes 524320 | tf_op jit(solution)/shard_map/all_to_all | solution.py:508
  175.5 2.5 shard_map.270.q_ref
  180.1 3.7 shard_map.271.k_ref.v_ref
  185.1 19.5 %shard_map.272 = (bf16[1024,256]{1,0:T(8,128)(2,1)}, f32[1024,256]{1,0:T(8,128)}, f32[8,1024]{1,0:T(8,128)}) custom-call(s32[24]{0:T(128)} %reshape.286.flags_ref, bf16[1024,256]{1,0:T(8,128)(2,1)} %shard_map.270.q_ref, bf16[3072,512]{1,0:T(8,128)(2,1)} %shard_map.271.k_ref.v_ref, bf16[3072,512]{1,0:T(8,128)(2,1)} %shard_map.271.k_ref.v_ref, ...), custom_call_target="tpu_custom_call" | custom-call | tf_op jit(solution)/shard_map/pallas_call | solution.py:952
  204.6 2.8 shard_map.273
  207.4 3.5 all-to-all-start.3
  211.3 8.3 %all-to-all-done.3 = bf16[4,256,256]{2,1,0:T(8,128)(2,1)S(1)} async-done(((bf16[4,256,256]{2,1,0:T(8,128)(2,1)}), bf16[4,256,256]{2,1,0:T(8,128)(2,1)S(1)}, u32[]{:S(2)}, u32[]{:S(2)}) %all-to-all-start.3) | async-done | bytes 524320 | tf_op jit(solution)/shard_map/all_to_all | solution.py:508
  219.7 10.8 %collective-permute-done.11.refs_2_.refs_6_ = bf16[2048,1024]{1,0:T(8,128)(2,1)} collective-permute-done((bf16[2048,1024]{1,0:T(8,128)(2,1)}, bf16[2048,1024]{1,0:T(8,128)(2,1)}, u32[]{:S(2)}, u32[]{:S(2)}) %collective-permute-start.11) | collective-permute-done | bytes 4194336 | tf_op jit(solution)/shard_map/ppermute | solution.py:1248
  231.7 4.6 shard_map.274
  238.0 10.4 %shard_map.275 = (f32[256,4096]{1,0:T(8,128)}, bf16[256,4096]{1,0:T(8,128)(2,1)}) custom-call(s32[1]{0:T(128)} %bitcast.me_ref, bf16[256,1024]{1,0:T(8,128)(2,1)} %get-tuple-element.251.rows_ref, bf16[2048,1024]{1,0:T(8,128)(2,1)} %slice_dynamic-update-slice_fusion.refs_0_.refs_4_, bf16[2048,1024]{1,0:T(8,128)(2,1)} %collective-permute-done.12.refs_1_.refs_5_, ...), custom_call_target="tpu_custom_call" | custom-call | tf_op jit(solution)/shard_map/pallas_call | solution.py:297
  248.4 12.0 %shard_map.276 = (bf16[256,1024]{1,0:T(8,128)(2,1)}, f32[256,1024]{1,0:T(8,128)}, bf16[256,1024]{1,0:T(8,128)(2,1)}, f32[8,1024]{1,0:T(8,128)}) custom-call(s32[1]{0:T(128)} %bitcast.me_ref, bf16[256,4096]{1,0:T(8,128)(2,1)} %get-tuple-element.249.hidden_ref, bf16[2048,1024]{1,0:T(8,128)(2,1)} %slice_dynamic-update-slice_fusion.refs_0_.refs_4_, ...), custom_call_target="tpu_custom_call" | custom-call | tf_op jit(solution)/shard_map/pallas_call | solution.py:374
  260.3 18.1 %shard_map.277 = (bf16[256,4096]{1,0:T(8,128)(2,1)}, f32[1,4096]{1,0:T(1,128)}, f32[256,1024]{1,0:T(8,128)}, bf16[256,1024]{1,0:T(8,128)(2,1)}, f32[8,1024]{1,0:T(8,128)}, /*index=5*/bf16[1024,256]{1,0:T(8,128)(2,1)}) custom-call(s32[1]{0:T(128)} %bitcast.me_ref, f32[256,4096]{1,0:T(8,128)} %get-tuple-element.238.slope_ref, ...), custom_call_target="tpu_custom_call" | custom-call | tf_op jit(solution)/shard_map/pallas_call | solution.py:439
  278.4 3.5 all-to-all-start.4
  282.1 11.7 %shard_map.278 = bf16[16,2,8,32,1024]{4,3,2,1,0:T(8,128)(2,1)} custom-call(bf16[256,4096]{1,0:T(8,128)(2,1)} %get-tuple-element.249.hidden_ref, bf16[256,1024]{1,0:T(8,128)(2,1)} %get-tuple-element.250.refs_8_.grads_ref, bf16[256,1024]{1,0:T(8,128)(2,1)} %get-tuple-element.251.rows_ref, bf16[256,4096]{1,0:T(8,128)(2,1)} %get-tuple-element.252.active_grads_ref), custom_call_target="tpu_custom_call" | custom-call | tf_op jit(solution)/shard_map/pallas_call | solution.py:842
  297.3 2.6 shard_map.279.g_ref
  301.1 26.9 %shard_map.280 = (bf16[1024,256]{1,0:T(8,128)(2,1)}, bf16[768,512]{1,0:T(8,128)(2,1)}, bf16[768,512]{1,0:T(8,128)(2,1)}, bf16[768,512]{1,0:T(8,128)(2,1)}, bf16[768,512]{1,0:T(8,128)(2,1)}) custom-call(s32[24]{0:T(128)} %reshape.286.flags_ref, s32[8]{0:T(128)} %stack.62.places_ref, bf16[1024,256]{1,0:T(8,128)(2,1)} %shard_map.270.q_ref, ...), custom_call_target="tpu_custom_call" | custom-call | tf_op jit(solution)/shard_map/pallas_call | solution.py:1092
  329.0 2.7 shard_map.281
  331.7 6.2 %all-to-all-start.5 = ((bf16[4,256,256]{2,1,0:T(8,128)(2,1)}), bf16[4,256,256]{2,1,0:T(8,128)(2,1)S(1)}, u32[]{:S(2)}, u32[]{:S(2)}) async-start(bf16[4,256,256]{2,1,0:T(8,128)(2,1)} %bitcast.102), calls=%async_computation.5 | async-start | bytes 1048576 | tf_op jit(solution)/shard_map/all_to_all | solution.py:508
  337.9 4.8 shard_map.282
  342.7 4.5 all-to-all-done.5
  348.0 5.8 shard_map.283
  353.8 3.5 all-to-all-start.6
  357.2 6.1 %shard_map.284 = (bf16[512,3072]{1,0:T(8,128)(2,1)}, bf16[512,3072]{1,0:T(8,128)(2,1)}, f32[1,1024]{1,0:T(1,128)}) custom-call(bf16[256,1024]{1,0:T(8,128)(2,1)} %get-tuple-element.280.out_left, bf16[256,1024]{1,0:T(8,128)(2,1)} %get-tuple-element.281.query_left, bf16[256,1024]{1,0:T(8,128)(2,1)} %get-tuple-element.282.cross_left, ...), custom_call_target="tpu_custom_call" | custom-call | tf_op jit(solution)/shard_map/pallas_call | solution.py:704
  363.4 2.7 all-to-all-done.6
  368.5 2.6 shard_map.285.g_ref
  371.1 13.3 %shard_map.286 = (bf16[1024,256]{1,0:T(8,128)(2,1)}, bf16[1024,512]{1,0:T(8,128)(2,1)}) custom-call(s32[16]{0:T(128)} %reshape.287.flags_ref, s32[2]{0:T(128)} %iota_multiply_fusion.places_ref, bf16[1024,768]{1,0:T(8,128)(2,1)} %shard_map.265.q_ref.k_ref.v_ref, bf16[1024,768]{1,0:T(8,128)(2,1)} %shard_map.265.q_ref.k_ref.v_ref, ...), custom_call_target="tpu_custom_call" | custom-call | tf_op jit(solution)/shard_map/pallas_call | solution.py:1092
  386.9 4.1 shard_map.287
  391.0 11.8 %collective-permute-done.19.refs_3_ = bf16[768,512]{1,0:T(8,128)(2,1)} collective-permute-done((bf16[768,512]{1,0:T(8,128)(2,1)}, bf16[768,512]{1,0:T(8,128)(2,1)}, u32[]{:S(2)}, u32[]{:S(2)}) %collective-permute-start.19) | collective-permute-done | bytes 786464 | tf_op jit(solution)/shard_map/ppermute | solution.py:528
  407.7 11.8 %shard_map.288 = (bf16[512,2048]{1,0:T(8,128)(2,1)}, bf16[512,2048]{1,0:T(8,128)(2,1)}, bf16[384,1024]{1,0:T(8,128)(2,1)}, bf16[384,1024]{1,0:T(8,128)(2,1)}, f32[1,1024]{1,0:T(1,128)}) custom-call(s32[1]{0:T(128)} %bitcast.29.me_ref, bf16[768,1024]{1,0:T(8,128)(2,1)} %fusion.7.left_ref, bf16[1024,2048]{1,0:T(8,128)(2,1)} %all-gather.8.cloned.1.call-done.weight_ref, ...), custom_call_target="tpu_custom_call" | custom-call | tf_op jit(solution)/shard_map/pallas_call | solution.py:731
  419.6 3.1 collective-permute-done.22.refs_3_
  422.6 7.5 %shard_map.289 = (bf16[512,1536]{1,0:T(8,128)(2,1)}, bf16[512,1536]{1,0:T(8,128)(2,1)}, bf16[512,1664]{1,0:T(8,128)(2,1)}, bf16[512,1664]{1,0:T(8,128)(2,1)}, bf16[256,3072]{1,0:T(8,128)(2,1)}) custom-call(s32[1]{0:T(128)} %bitcast.29.me_ref, bf16[256,1024]{1,0:T(8,128)(2,1)} %fusion.8.left_ref, bf16[256,1024]{1,0:T(8,128)(2,1)} %fusion.9.right_ref, ...), custom_call_target="tpu_custom_call" | custom-call | tf_op jit(solution)/shard_map/pallas_call | solution.py:776
  431.6 6.7 %shard_map.290 = bf16[256,1024]{1,0:T(8,128)(2,1)} custom-call(bf16[256,3072]{1,0:T(8,128)(2,1)} %get-tuple-element.344.grads_ref, bf16[1024,3072]{1,0:T(8,128)(2,1)} %all-gather.6.cloned.1.call-done.weight_ref, f32[256,1024]{1,0:T(8,128)} %get-tuple-element.345.resid_ref), custom_call_target="tpu_custom_call" | custom-call | tf_op jit(solution)/shard_map/pallas_call | solution.py:492
  438.6 2.0 collective-permute-start.27
  440.6 1.9 fusion.65
  449.1 19.6 %collective-permute-done.26 = bf16[256,3072]{1,0:T(8,128)(2,1)S(1)} collective-permute-done((bf16[256,3072]{1,0:T(8,128)(2,1)}, bf16[256,3072]{1,0:T(8,128)(2,1)S(1)}, u32[]{:S(2)}, u32[]{:S(2)}) %collective-permute-start.26) | collective-permute-done | bytes 1572896 | tf_op jit(solution)/shard_map/ppermute | solution.py:642
  470.7 15.9 %collective-permute-done.28 = bf16[256,1664]{1,0:T(8,128)(2,1)S(1)} collective-permute-done((bf16[256,1664]{1,0:T(8,128)(2,1)S(1)}, bf16[256,1664]{1,0:T(8,128)(2,1)S(1)}, u32[]{:S(2)}, u32[]{:S(2)}) %collective-permute-start.28) | collective-permute-done | bytes 852000 | tf_op jit(solution)/shard_map/ppermute | solution.py:642
  489.4 15.2 %collective-permute-done.30 = bf16[256,2048]{1,0:T(8,128)(2,1)S(1)} collective-permute-done((bf16[256,2048]{1,0:T(8,128)(2,1)S(1)}, bf16[256,2048]{1,0:T(8,128)(2,1)S(1)}, u32[]{:S(2)}, u32[]{:S(2)}) %collective-permute-start.30) | collective-permute-done | bytes 1048608 | tf_op jit(solution)/shard_map/ppermute | solution.py:642
  508.6 4.5 collective-permute-done.34
  513.9 2.1 collective-permute-start.40
  518.4 1.9 maximum_convert_fusion
  521.7 2.1 collective-permute-start.42
  523.8 15.9 %collective-permute-start.45 = (bf16[32,3072]{1,0:T(8,128)(2,1)S(1)}, bf16[32,3072]{1,0:T(8,128)(2,1)S(1)}, u32[]{:S(2)}, u32[]{:S(2)}) collective-permute-start(bf16[32,3072]{1,0:T(8,128)(2,1)S(1)} %get-tuple-element.502), channel_id=1, source_target_pairs={{0,16},{8,24},{16,0},{24,8},{1,17},{9,25},{17,1},{25,9},{2,18},{10... | collective-permute-start | bytes 589832 | tf_op jit(solution)/shard_map/ppermute | solution.py:641
  541.9 8.6 %collective-permute-start.43 = (bf16[32,1536]{1,0:T(8,128)(2,1)S(1)}, bf16[32,1536]{1,0:T(8,128)(2,1)S(1)}, u32[]{:S(2)}, u32[]{:S(2)}) collective-permute-start(bf16[32,1536]{1,0:T(8,128)(2,1)S(1)} %get-tuple-element.509), channel_id=1, source_target_pairs={{0,16},{8,24},{16,0},{24,8},{1,17},{9,25},{17,1},{25,9},{2,18},{10... | collective-permute-start | bytes 294920 | tf_op jit(solution)/shard_map/ppermute | solution.py:641
  551.3 14.3 %collective-permute-done.44 = bf16[32,1664]{1,0:T(8,128)(2,1)S(1)} collective-permute-done((bf16[32,1664]{1,0:T(8,128)(2,1)S(1)}, bf16[32,1664]{1,0:T(8,128)(2,1)S(1)}, u32[]{:S(2)}, u32[]{:S(2)}) %collective-permute-start.44) | collective-permute-done | bytes 106528 | tf_op jit(solution)/shard_map/ppermute | solution.py:641
  569.9 3.9 collective-permute-done.46
  (299 shorter events, 91.6 us)
Async XLA Ops:
  7.2 57.5 %all-gather.6.cloned.1.call-start = ((), (), s32[]{:S(2)}) async-start(), calls=%async_computation.8 | async-start | bytes 7864320 | tf_op jit(solution)/shard_map/all_gather | solution.py:145
  8.0 114.4 %all-gather.8.cloned.1.call-start = ((), (), s32[]{:S(2)}) async-start(), calls=%async_computation.9 | async-start | bytes 5242880 | tf_op jit(solution)/shard_map/all_gather | solution.py:145
  9.1 3.8 collective-permute-start.2
  9.8 9.1 %collective-permute-start.3 = (bf16[128,1024]{1,0:T(8,128)(2,1)S(1)}, bf16[128,1024]{1,0:T(8,128)(2,1)S(1)}, u32[]{:S(2)}, u32[]{:S(2)}) collective-permute-start(bf16[128,1024]{1,0:T(8,128)(2,1)S(1)} %get-tuple-element.496), channel_id=1, source_target_pairs={{0,8},{1,24},{8,0},{9,16},{16,9},{17,25},{24,1},{25,17},{2,10},{3,... | collective-permute-start | bytes 786440 | tf_op jit(solution)/shard_map/ppermute | solution.py:83
  19.7 126.1 %all-gather.10.cloned.1.call-start = ((), (), s32[]{:S(2)}) async-start(), calls=%async_computation.10 | async-start | bytes 5242880 | tf_op jit(solution)/shard_map/all_gather | solution.py:145
  19.9 5.8 %collective-permute-start = (s32[134]{0:T(256)S(1)}, s32[134]{0:T(256)S(1)}, u32[]{:S(2)}, u32[]{:S(2)}) collective-permute-start(s32[134]{0:T(256)S(1)} %bitcast.142), channel_id=1, source_target_pairs={{0,0},{1,16},{8,8},{9,24},{16,1},{17,17},{24,9},{25,25},{2,2},{3,1... | collective-permute-start | bytes 1616 | tf_op jit(solution)/shard_map/ppermute | solution.py:82
  20.6 14.7 %collective-permute-start.1 = (s32[134]{0:T(256)S(1)}, s32[134]{0:T(256)S(1)}, u32[]{:S(2)}, u32[]{:S(2)}) collective-permute-start(s32[134]{0:T(256)S(1)} %bitcast.141), channel_id=1, source_target_pairs={{0,8},{1,24},{8,0},{9,16},{16,9},{17,25},{24,1},{25,17},{2,10},{3,... | collective-permute-start | bytes 1616 | tf_op jit(solution)/shard_map/ppermute | solution.py:83
  23.3 55.4 %collective-permute-start.4 = (bf16[384,1024]{1,0:T(8,128)(2,1)S(1)}, bf16[384,1024]{1,0:T(8,128)(2,1)}, u32[]{:S(2)}, u32[]{:S(2)}) collective-permute-start(bf16[384,1024]{1,0:T(8,128)(2,1)S(1)} %get-tuple-element.470), channel_id=1, source_target_pairs={{0,0},{1,16},{8,8},{9,24},{16,1},{17,17},{24,9},{25,25},{2,2},{3,1... | collective-permute-start | bytes 2359304 | tf_op jit(solution)/shard_map/ppermute | solution.py:82
  24.9 54.9 %collective-permute-start.5 = (bf16[384,1024]{1,0:T(8,128)(2,1)}, bf16[384,1024]{1,0:T(8,128)(2,1)}, u32[]{:S(2)}, u32[]{:S(2)}) collective-permute-start(bf16[384,1024]{1,0:T(8,128)(2,1)} %get-tuple-element.469), channel_id=1, source_target_pairs={{0,8},{1,24},{8,0},{9,16},{16,9},{17,25},{24,1},{25,17},{2,10},{3,... | collective-permute-start | bytes 2359304 | tf_op jit(solution)/shard_map/ppermute | solution.py:83
  56.2 100.4 %copy-start.34 = (s32[1024]{0:T(1024)}, s32[1024]{0:T(1024)S(1)}, u32[]{:S(2)}) copy-start(s32[1024]{0:T(1024)S(1)} %broadcast_multiply_fusion) | copy-start | bytes 12292
  71.1 23.8 %all-to-all-start = ((bf16[4,256,768]{2,1,0:T(8,128)(2,1)}), bf16[4,256,768]{2,1,0:T(8,128)(2,1)S(1)}, u32[]{:S(2)}, u32[]{:S(2)}) async-start(bf16[4,256,768]{2,1,0:T(8,128)(2,1)} %bitcast.99), calls=%async_computation | async-start | bytes 3145728 | tf_op jit(solution)/shard_map/all_to_all | solution.py:508
  74.8 136.1 %all-gather.12.cloned.1.call-start = ((), (), s32[]{:S(2)}) async-start(), calls=%async_computation.11 | async-start | bytes 2621440 | tf_op jit(solution)/shard_map/all_gather | solution.py:145
  111.8 118.7 %collective-permute-start.11 = (bf16[2048,1024]{1,0:T(8,128)(2,1)}, bf16[2048,1024]{1,0:T(8,128)(2,1)}, u32[]{:S(2)}, u32[]{:S(2)}) collective-permute-start(bf16[2048,1024]{1,0:T(8,128)(2,1)} %slice_dynamic-update-slice_fusion.refs_0_.refs_4_), channel_id=1, source_target_pairs={{0,2},{2,0},{1,3},{3,1},{4,6},{6,4},{5,7},{7,5},{8,10},{10,8},{9,1... | collective-permute-start | bytes 12582920 | tf_op jit(solution)/shard_map/ppermute | solution.py:1248
  116.9 12.5 %all-to-all-start.1 = ((bf16[4,256,256]{2,1,0:T(8,128)(2,1)}), bf16[4,256,256]{2,1,0:T(8,128)(2,1)S(1)}, u32[]{:S(2)}, u32[]{:S(2)}) async-start(bf16[4,256,256]{2,1,0:T(8,128)(2,1)} %bitcast.101), calls=%async_computation.1 | async-start | bytes 1048576 | tf_op jit(solution)/shard_map/all_to_all | solution.py:508
  120.5 34.3 %collective-permute-start.10 = (bf16[128,1024]{1,0:T(8,128)(2,1)S(1)}, bf16[128,1024]{1,0:T(8,128)(2,1)}, u32[]{:S(2)}, u32[]{:S(2)}) collective-permute-start(bf16[128,1024]{1,0:T(8,128)(2,1)S(1)} %get-tuple-element.494), channel_id=1, source_target_pairs={{0,8},{1,24},{8,0},{9,16},{16,9},{17,25},{24,1},{25,17},{2,10},{3,... | collective-permute-start | bytes 786440 | tf_op jit(solution)/shard_map/ppermute | solution.py:83
  129.4 48.6 %collective-permute-start.6 = (bf16[768,512]{1,0:T(8,128)(2,1)}, bf16[768,512]{1,0:T(8,128)(2,1)S(1)}, u32[]{:S(2)}, u32[]{:S(2)}) collective-permute-start(bf16[768,512]{1,0:T(8,128)(2,1)} %get-tuple-element.224), channel_id=1, source_target_pairs={{0,1},{1,0},{4,5},{5,4},{2,3},{3,2},{6,7},{7,6},{8,9},{9,8},{12,13... | collective-permute-start | bytes 2359304 | tf_op jit(solution)/shard_map/ppermute | solution.py:528
  132.2 45.8 %collective-permute-start.7 = (bf16[768,512]{1,0:T(8,128)(2,1)}, bf16[768,512]{1,0:T(8,128)(2,1)S(1)}, u32[]{:S(2)}, u32[]{:S(2)}) collective-permute-start(bf16[768,512]{1,0:T(8,128)(2,1)} %get-tuple-element.225), channel_id=1, source_target_pairs={{0,4},{1,5},{4,0},{5,1},{2,6},{3,7},{6,2},{7,3},{8,12},{9,13},{12,... | collective-permute-start | bytes 2359304 | tf_op jit(solution)/shard_map/ppermute | solution.py:528
  134.2 43.8 %collective-permute-start.8 = (bf16[768,512]{1,0:T(8,128)(2,1)}, bf16[768,512]{1,0:T(8,128)(2,1)S(1)}, u32[]{:S(2)}, u32[]{:S(2)}) collective-permute-start(bf16[768,512]{1,0:T(8,128)(2,1)} %get-tuple-element.226), channel_id=1, source_target_pairs={{0,5},{1,4},{4,1},{5,0},{2,7},{3,6},{6,3},{7,2},{8,13},{9,12},{12,... | collective-permute-start | bytes 2359304 | tf_op jit(solution)/shard_map/ppermute | solution.py:528
  151.1 23.6 %all-to-all-start.2 = ((bf16[4,256,256]{2,1,0:T(8,128)(2,1)}), bf16[4,256,256]{2,1,0:T(8,128)(2,1)S(1)}, u32[]{:S(2)}, u32[]{:S(2)}) async-start(bf16[4,256,256]{2,1,0:T(8,128)(2,1)} %bitcast.110), calls=%async_computation.2 | async-start | bytes 1048576 | tf_op jit(solution)/shard_map/all_to_all | solution.py:508
  154.8 2.4 collective-permute-start.9
  207.4 12.3 %all-to-all-start.3 = ((bf16[4,256,256]{2,1,0:T(8,128)(2,1)}), bf16[4,256,256]{2,1,0:T(8,128)(2,1)S(1)}, u32[]{:S(2)}, u32[]{:S(2)}) async-start(bf16[4,256,256]{2,1,0:T(8,128)(2,1)} %bitcast.103), calls=%async_computation.3 | async-start | bytes 1048576 | tf_op jit(solution)/shard_map/all_to_all | solution.py:508
  210.9 25.4 %collective-permute-start.12 = (bf16[2048,1024]{1,0:T(8,128)(2,1)}, bf16[2048,1024]{1,0:T(8,128)(2,1)}, u32[]{:S(2)}, u32[]{:S(2)}) collective-permute-start(bf16[2048,1024]{1,0:T(8,128)(2,1)} %slice_dynamic-update-slice_fusion.refs_0_.refs_4_), channel_id=1, source_target_pairs={{0,1},{1,0},{2,3},{3,2},{4,5},{5,4},{6,7},{7,6},{8,9},{9,8},{10,11... | collective-permute-start | bytes 12582920 | tf_op jit(solution)/shard_map/ppermute | solution.py:1268
  230.5 7.5 %collective-permute-start.13 = (bf16[2048,1024]{1,0:T(8,128)(2,1)}, bf16[2048,1024]{1,0:T(8,128)(2,1)}, u32[]{:S(2)}, u32[]{:S(2)}) collective-permute-start(bf16[2048,1024]{1,0:T(8,128)(2,1)} %collective-permute-done.11.refs_2_.refs_6_), channel_id=1, source_target_pairs={{0,1},{1,0},{2,3},{3,2},{4,5},{5,4},{6,7},{7,6},{8,9},{9,8},{10,11... | collective-permute-start | bytes 12582920 | tf_op jit(solution)/shard_map/ppermute | solution.py:1272
  278.4 15.4 %all-to-all-start.4 = ((bf16[4,256,256]{2,1,0:T(8,128)(2,1)}), bf16[4,256,256]{2,1,0:T(8,128)(2,1)S(1)}, u32[]{:S(2)}, u32[]{:S(2)}) async-start(bf16[4,256,256]{2,1,0:T(8,128)(2,1)} %bitcast.111), calls=%async_computation.4 | async-start | bytes 1048576 | tf_op jit(solution)/shard_map/all_to_all | solution.py:508
  281.9 224.0 %reduce-scatter.2.cloned.1.call-start = ((), (), s32[]{:S(2)}) async-start(), calls=%async_computation.12 | async-start | bytes 17825792 | tf_op jit(solution)/shard_map/reduce_scatter | solution.py:859
  295.1 33.0 %collective-permute-start.14 = (bf16[128,1024]{1,0:T(8,128)(2,1)S(1)}, bf16[128,1024]{1,0:T(8,128)(2,1)S(1)}, u32[]{:S(2)}, u32[]{:S(2)}) collective-permute-start(bf16[128,1024]{1,0:T(8,128)(2,1)S(1)} %get-tuple-element.491), channel_id=1, source_target_pairs={{0,0},{16,1},{8,8},{24,9},{1,16},{17,17},{9,24},{25,25},{2,2},{18,... | collective-permute-start | bytes 786440 | tf_op jit(solution)/shard_map/ppermute | solution.py:89
  295.8 32.3 %collective-permute-start.15 = (bf16[128,1024]{1,0:T(8,128)(2,1)S(1)}, bf16[128,1024]{1,0:T(8,128)(2,1)S(1)}, u32[]{:S(2)}, u32[]{:S(2)}) collective-permute-start(bf16[128,1024]{1,0:T(8,128)(2,1)S(1)} %get-tuple-element.492), channel_id=1, source_target_pairs={{8,0},{24,1},{0,8},{16,9},{9,16},{25,17},{1,24},{17,25},{10,2},{26... | collective-permute-start | bytes 786440 | tf_op jit(solution)/shard_map/ppermute | solution.py:89
  331.7 15.5 %all-to-all-start.5 = ((bf16[4,256,256]{2,1,0:T(8,128)(2,1)}), bf16[4,256,256]{2,1,0:T(8,128)(2,1)S(1)}, u32[]{:S(2)}, u32[]{:S(2)}) async-start(bf16[4,256,256]{2,1,0:T(8,128)(2,1)} %bitcast.102), calls=%async_computation.5 | async-start | bytes 1048576 | tf_op jit(solution)/shard_map/all_to_all | solution.py:508
  353.8 12.3 %all-to-all-start.6 = ((bf16[4,256,256]{2,1,0:T(8,128)(2,1)}), bf16[4,256,256]{2,1,0:T(8,128)(2,1)S(1)}, u32[]{:S(2)}, u32[]{:S(2)}) async-start(bf16[4,256,256]{2,1,0:T(8,128)(2,1)} %bitcast.112), calls=%async_computation.6 | async-start | bytes 1048576 | tf_op jit(solution)/shard_map/all_to_all | solution.py:508
  366.1 18.3 %collective-permute-start.16 = (bf16[512,3072]{1,0:T(8,128)(2,1)}, bf16[512,3072]{1,0:T(8,128)(2,1)S(1)}, u32[]{:S(2)}, u32[]{:S(2)}) collective-permute-start(bf16[512,3072]{1,0:T(8,128)(2,1)} %get-tuple-element.299), channel_id=1, source_target_pairs={{0,1},{1,0},{2,3},{3,2},{4,5},{5,4},{6,7},{7,6},{8,9},{9,8},{10,11... | collective-permute-start | bytes 9437192 | tf_op jit(solution)/shard_map/ppermute | solution.py:642
  366.6 24.4 %collective-permute-start.17 = (bf16[768,512]{1,0:T(8,128)(2,1)}, bf16[768,512]{1,0:T(8,128)(2,1)S(1)}, u32[]{:S(2)}, u32[]{:S(2)}) collective-permute-start(bf16[768,512]{1,0:T(8,128)(2,1)} %get-tuple-element.311), channel_id=1, source_target_pairs={{0,1},{1,0},{4,5},{5,4},{2,3},{3,2},{6,7},{7,6},{8,9},{9,8},{12,13... | collective-permute-start | bytes 2359304 | tf_op jit(solution)/shard_map/ppermute | solution.py:528
  367.1 23.9 %collective-permute-start.18 = (bf16[768,512]{1,0:T(8,128)(2,1)}, bf16[768,512]{1,0:T(8,128)(2,1)}, u32[]{:S(2)}, u32[]{:S(2)}) collective-permute-start(bf16[768,512]{1,0:T(8,128)(2,1)} %get-tuple-element.312), channel_id=1, source_target_pairs={{0,4},{1,5},{4,0},{5,1},{2,6},{3,7},{6,2},{7,3},{8,12},{9,13},{12,... | collective-permute-start | bytes 2359304 | tf_op jit(solution)/shard_map/ppermute | solution.py:528
  367.4 35.4 %collective-permute-start.19 = (bf16[768,512]{1,0:T(8,128)(2,1)}, bf16[768,512]{1,0:T(8,128)(2,1)}, u32[]{:S(2)}, u32[]{:S(2)}) collective-permute-start(bf16[768,512]{1,0:T(8,128)(2,1)} %get-tuple-element.313), channel_id=1, source_target_pairs={{0,5},{1,4},{4,1},{5,0},{2,7},{3,6},{6,3},{7,2},{8,13},{9,12},{12,... | collective-permute-start | bytes 2359304 | tf_op jit(solution)/shard_map/ppermute | solution.py:528
  386.9 18.9 %copy-start.36 = (f32[1,4096]{1,0:T(1,128)S(1)}, f32[1,4096]{1,0:T(1,128)}, u32[]{:S(2)}) copy-start(f32[1,4096]{1,0:T(1,128)} %get-tuple-element.334) | copy-start | bytes 49156
  402.8 16.7 %collective-permute-start.20 = (bf16[256,768]{1,0:T(8,128)(2,1)}, bf16[256,768]{1,0:T(8,128)(2,1)S(1)}, u32[]{:S(2)}, u32[]{:S(2)}) collective-permute-start(bf16[256,768]{1,0:T(8,128)(2,1)} %get-tuple-element.325), channel_id=1, source_target_pairs={{0,1},{1,0},{4,5},{5,4},{2,3},{3,2},{6,7},{7,6},{8,9},{9,8},{12,13... | collective-permute-start | bytes 1179656 | tf_op jit(solution)/shard_map/ppermute | solution.py:528
  403.8 15.7 %collective-permute-start.21 = (bf16[256,768]{1,0:T(8,128)(2,1)}, bf16[256,768]{1,0:T(8,128)(2,1)}, u32[]{:S(2)}, u32[]{:S(2)}) collective-permute-start(bf16[256,768]{1,0:T(8,128)(2,1)} %get-tuple-element.326), channel_id=1, source_target_pairs={{0,4},{1,5},{4,0},{5,1},{2,6},{3,7},{6,2},{7,3},{8,12},{9,13},{12,... | collective-permute-start | bytes 1179656 | tf_op jit(solution)/shard_map/ppermute | solution.py:528
  403.9 18.7 %collective-permute-start.22 = (bf16[256,768]{1,0:T(8,128)(2,1)}, bf16[256,768]{1,0:T(8,128)(2,1)}, u32[]{:S(2)}, u32[]{:S(2)}) collective-permute-start(bf16[256,768]{1,0:T(8,128)(2,1)} %get-tuple-element.327), channel_id=1, source_target_pairs={{0,5},{1,4},{4,1},{5,0},{2,7},{3,6},{6,3},{7,2},{8,13},{9,12},{12,... | collective-permute-start | bytes 1179656 | tf_op jit(solution)/shard_map/ppermute | solution.py:528
  430.1 12.3 %collective-permute-start.23 = (bf16[512,1536]{1,0:T(8,128)(2,1)}, bf16[512,1536]{1,0:T(8,128)(2,1)}, u32[]{:S(2)}, u32[]{:S(2)}) collective-permute-start(bf16[512,1536]{1,0:T(8,128)(2,1)} %get-tuple-element.347), channel_id=1, source_target_pairs={{0,1},{1,0},{2,3},{3,2},{4,5},{5,4},{6,7},{7,6},{8,9},{9,8},{10,11... | collective-permute-start | bytes 4718600 | tf_op jit(solution)/shard_map/ppermute | solution.py:642
  431.3 14.2 %collective-permute-start.24 = (bf16[512,1664]{1,0:T(8,128)(2,1)}, bf16[512,1664]{1,0:T(8,128)(2,1)S(1)}, u32[]{:S(2)}, u32[]{:S(2)}) collective-permute-start(bf16[512,1664]{1,0:T(8,128)(2,1)} %get-tuple-element.351), channel_id=1, source_target_pairs={{0,1},{1,0},{2,3},{3,2},{4,5},{5,4},{6,7},{7,6},{8,9},{9,8},{10,11... | collective-permute-start | bytes 5111816 | tf_op jit(solution)/shard_map/ppermute | solution.py:642
  431.3 37.4 %collective-permute-start.26 = (bf16[256,3072]{1,0:T(8,128)(2,1)}, bf16[256,3072]{1,0:T(8,128)(2,1)S(1)}, u32[]{:S(2)}, u32[]{:S(2)}) collective-permute-start(bf16[256,3072]{1,0:T(8,128)(2,1)} %get-tuple-element.457), channel_id=1, source_target_pairs={{0,4},{4,0},{1,5},{5,1},{2,6},{6,2},{3,7},{7,3},{8,12},{12,8},{9,1... | collective-permute-start | bytes 4718600 | tf_op jit(solution)/shard_map/ppermute | solution.py:642
  438.4 9.7 %collective-permute-start.25 = (bf16[512,2048]{1,0:T(8,128)(2,1)}, bf16[512,2048]{1,0:T(8,128)(2,1)S(1)}, u32[]{:S(2)}, u32[]{:S(2)}) collective-permute-start(bf16[512,2048]{1,0:T(8,128)(2,1)} %get-tuple-element.353), channel_id=1, source_target_pairs={{0,1},{1,0},{2,3},{3,2},{4,5},{5,4},{6,7},{7,6},{8,9},{9,8},{10,11... | collective-permute-start | bytes 6291464 | tf_op jit(solution)/shard_map/ppermute | solution.py:642
  438.6 30.8 %collective-permute-start.27 = (bf16[384,1024]{1,0:T(8,128)(2,1)}, bf16[384,1024]{1,0:T(8,128)(2,1)S(1)}, u32[]{:S(2)}, u32[]{:S(2)}) collective-permute-start(bf16[384,1024]{1,0:T(8,128)(2,1)} %get-tuple-element.356), channel_id=1, source_target_pairs={{0,0},{16,1},{8,8},{24,9},{1,16},{17,17},{9,24},{25,25},{2,2},{18,... | collective-permute-start | bytes 2359304 | tf_op jit(solution)/shard_map/ppermute | solution.py:89
  444.4 43.2 %collective-permute-start.29 = (bf16[256,1536]{1,0:T(8,128)(2,1)S(1)}, bf16[256,1536]{1,0:T(8,128)(2,1)S(1)}, u32[]{:S(2)}, u32[]{:S(2)}) collective-permute-start(bf16[256,1536]{1,0:T(8,128)(2,1)S(1)} %get-tuple-element.467), channel_id=1, source_target_pairs={{0,2},{2,0},{1,3},{3,1},{4,6},{6,4},{5,7},{7,5},{8,10},{10,8},{9,1... | collective-permute-start | bytes 2359304 | tf_op jit(solution)/shard_map/ppermute | solution.py:642
  446.3 40.3 %collective-permute-start.28 = (bf16[256,1664]{1,0:T(8,128)(2,1)S(1)}, bf16[256,1664]{1,0:T(8,128)(2,1)S(1)}, u32[]{:S(2)}, u32[]{:S(2)}) collective-permute-start(bf16[256,1664]{1,0:T(8,128)(2,1)S(1)} %get-tuple-element.461), channel_id=1, source_target_pairs={{0,4},{4,0},{1,5},{5,1},{2,6},{6,2},{3,7},{7,3},{8,12},{12,8},{9,1... | collective-permute-start | bytes 2555912 | tf_op jit(solution)/shard_map/ppermute | solution.py:642
  469.5 35.1 %collective-permute-start.30 = (bf16[256,2048]{1,0:T(8,128)(2,1)S(1)}, bf16[256,2048]{1,0:T(8,128)(2,1)S(1)}, u32[]{:S(2)}, u32[]{:S(2)}) collective-permute-start(bf16[256,2048]{1,0:T(8,128)(2,1)S(1)} %get-tuple-element.459), channel_id=1, source_target_pairs={{0,4},{4,0},{1,5},{5,1},{2,6},{6,2},{3,7},{7,3},{8,12},{12,8},{9,1... | collective-permute-start | bytes 3145736 | tf_op jit(solution)/shard_map/ppermute | solution.py:642
  469.8 36.0 %collective-permute-start.31 = (bf16[128,3072]{1,0:T(8,128)(2,1)S(1)}, bf16[128,3072]{1,0:T(8,128)(2,1)}, u32[]{:S(2)}, u32[]{:S(2)}) collective-permute-start(bf16[128,3072]{1,0:T(8,128)(2,1)S(1)} %get-tuple-element.465), channel_id=1, source_target_pairs={{0,2},{2,0},{1,3},{3,1},{4,6},{6,4},{5,7},{7,5},{8,10},{10,8},{9,1... | collective-permute-start | bytes 2359304 | tf_op jit(solution)/shard_map/ppermute | solution.py:642
  470.3 37.0 %collective-permute-start.32 = (bf16[384,1024]{1,0:T(8,128)(2,1)}, bf16[384,1024]{1,0:T(8,128)(2,1)}, u32[]{:S(2)}, u32[]{:S(2)}) collective-permute-start(bf16[384,1024]{1,0:T(8,128)(2,1)} %get-tuple-element.369), channel_id=1, source_target_pairs={{8,0},{24,1},{0,8},{16,9},{9,16},{25,17},{1,24},{17,25},{10,2},{26... | collective-permute-start | bytes 2359304 | tf_op jit(solution)/shard_map/ppermute | solution.py:89
  487.6 19.7 %collective-permute-start.33 = (bf16[128,1664]{1,0:T(8,128)(2,1)}, bf16[128,1664]{1,0:T(8,128)(2,1)}, u32[]{:S(2)}, u32[]{:S(2)}) collective-permute-start(bf16[128,1664]{1,0:T(8,128)(2,1)} %get-tuple-element.477), channel_id=1, source_target_pairs={{0,2},{2,0},{1,3},{3,1},{4,6},{6,4},{5,7},{7,5},{8,10},{10,8},{9,1... | collective-permute-start | bytes 1277960 | tf_op jit(solution)/shard_map/ppermute | solution.py:642
  489.1 24.0 %collective-permute-start.34 = (bf16[128,1536]{1,0:T(8,128)(2,1)}, bf16[128,1536]{1,0:T(8,128)(2,1)}, u32[]{:S(2)}, u32[]{:S(2)}) collective-permute-start(bf16[128,1536]{1,0:T(8,128)(2,1)} %get-tuple-element.481), channel_id=1, source_target_pairs={{0,4},{4,0},{1,5},{5,1},{2,6},{6,2},{3,7},{7,3},{8,12},{12,8},{9,1... | collective-permute-start | bytes 1179656 | tf_op jit(solution)/shard_map/ppermute | solution.py:642
  505.9 15.7 %collective-permute-start.38 = (bf16[128,2048]{1,0:T(8,128)(2,1)}, bf16[128,2048]{1,0:T(8,128)(2,1)S(1)}, u32[]{:S(2)}, u32[]{:S(2)}) collective-permute-start(bf16[128,2048]{1,0:T(8,128)(2,1)} %get-tuple-element.475), channel_id=1, source_target_pairs={{0,2},{2,0},{1,3},{3,1},{4,6},{6,4},{5,7},{7,5},{8,10},{10,8},{9,1... | collective-permute-start | bytes 1572872 | tf_op jit(solution)/shard_map/ppermute | solution.py:642
  513.1 8.3 %collective-permute-start.35 = (bf16[64,3072]{1,0:T(8,128)(2,1)S(1)}, bf16[64,3072]{1,0:T(8,128)(2,1)S(1)}, u32[]{:S(2)}, u32[]{:S(2)}) collective-permute-start(bf16[64,3072]{1,0:T(8,128)(2,1)S(1)} %get-tuple-element.479), channel_id=1, source_target_pairs={{0,8},{8,0},{16,24},{24,16},{1,9},{9,1},{17,25},{25,17},{2,10},{10... | collective-permute-start | bytes 1179656 | tf_op jit(solution)/shard_map/ppermute | solution.py:641
  513.1 8.4 %collective-permute-start.36 = (bf16[128,1024]{1,0:T(8,128)(2,1)S(1)}, bf16[128,1024]{1,0:T(8,128)(2,1)S(1)}, u32[]{:S(2)}, u32[]{:S(2)}) collective-permute-start(bf16[128,1024]{1,0:T(8,128)(2,1)S(1)} %copy-done.28), channel_id=1, source_target_pairs={{0,0},{16,1},{8,8},{24,9},{1,16},{17,17},{9,24},{25,25},{2,2},{18,... | collective-permute-start | bytes 786440 | tf_op jit(solution)/shard_map/ppermute | solution.py:89
  513.8 25.9 %collective-permute-start.39 = (bf16[8,32,1024]{2,1,0:T(8,128)(2,1)S(1)}, bf16[8,32,1024]{2,1,0:T(8,128)(2,1)S(1)}, u32[]{:S(2)}, u32[]{:S(2)}) collective-permute-start(bf16[8,32,1024]{2,1,0:T(8,128)(2,1)S(1)} %dynamic-slice_bitcast_fusion.2), channel_id=1, source_target_pairs={{0,4},{4,0},{1,5},{5,1},{2,6},{6,2},{3,7},{7,3},{8,12},{12,8},{9,1... | collective-permute-start | bytes 1572872 | tf_op jit(solution)/shard_map/ppermute | solution.py:642
  513.9 25.9 %collective-permute-start.40 = (bf16[64,1664]{1,0:T(8,128)(2,1)S(1)}, bf16[64,1664]{1,0:T(8,128)(2,1)S(1)}, u32[]{:S(2)}, u32[]{:S(2)}) collective-permute-start(bf16[64,1664]{1,0:T(8,128)(2,1)S(1)} %get-tuple-element.497), channel_id=1, source_target_pairs={{0,8},{8,0},{16,24},{24,16},{1,9},{9,1},{17,25},{25,17},{2,10},{10... | collective-permute-start | bytes 638984 | tf_op jit(solution)/shard_map/ppermute | solution.py:641
  521.4 18.8 %collective-permute-start.41 = (bf16[64,1536]{1,0:T(8,128)(2,1)S(1)}, bf16[64,1536]{1,0:T(8,128)(2,1)S(1)}, u32[]{:S(2)}, u32[]{:S(2)}) collective-permute-start(bf16[64,1536]{1,0:T(8,128)(2,1)S(1)} %get-tuple-element.504), channel_id=1, source_target_pairs={{0,8},{8,0},{16,24},{24,16},{1,9},{9,1},{17,25},{25,17},{2,10},{10... | collective-permute-start | bytes 589832 | tf_op jit(solution)/shard_map/ppermute | solution.py:641
  521.4 18.4 %copy-start.27 = (bf16[128,1024]{1,0:T(8,128)(2,1)S(1)}, bf16[128,1024]{1,0:T(8,128)(2,1)}, u32[]{:S(2)}) copy-start(bf16[128,1024]{1,0:T(8,128)(2,1)} %get-tuple-element.381) | copy-start | bytes 786436
  521.5 18.6 %copy-start.29 = (bf16[128,1024]{1,0:T(8,128)(2,1)}, bf16[128,1024]{1,0:T(8,128)(2,1)S(1)}, u32[]{:S(2)}) copy-start(bf16[128,1024]{1,0:T(8,128)(2,1)S(1)} %collective-permute-done.36) | copy-start | bytes 786436
  521.7 46.1 %collective-permute-start.42 = (bf16[64,2048]{1,0:T(8,128)(2,1)S(1)}, bf16[64,2048]{1,0:T(8,128)(2,1)S(1)}, u32[]{:S(2)}, u32[]{:S(2)}) collective-permute-start(bf16[64,2048]{1,0:T(8,128)(2,1)S(1)} %get-tuple-element.483), channel_id=1, source_target_pairs={{0,8},{8,0},{16,24},{24,16},{1,9},{9,1},{17,25},{25,17},{2,10},{10... | collective-permute-start | bytes 786440 | tf_op jit(solution)/shard_map/ppermute | solution.py:641
  523.8 26.7 %collective-permute-start.45 = (bf16[32,3072]{1,0:T(8,128)(2,1)S(1)}, bf16[32,3072]{1,0:T(8,128)(2,1)S(1)}, u32[]{:S(2)}, u32[]{:S(2)}) collective-permute-start(bf16[32,3072]{1,0:T(8,128)(2,1)S(1)} %get-tuple-element.502), channel_id=1, source_target_pairs={{0,16},{8,24},{16,0},{24,8},{1,17},{9,25},{17,1},{25,9},{2,18},{10... | collective-permute-start | bytes 589832 | tf_op jit(solution)/shard_map/ppermute | solution.py:641
  539.8 29.0 %collective-permute-start.37 = (bf16[128,1024]{1,0:T(8,128)(2,1)S(1)}, bf16[128,1024]{1,0:T(8,128)(2,1)S(1)}, u32[]{:S(2)}, u32[]{:S(2)}) collective-permute-start(bf16[128,1024]{1,0:T(8,128)(2,1)S(1)} %copy-done.27), channel_id=1, source_target_pairs={{8,0},{24,1},{0,8},{16,9},{9,16},{25,17},{1,24},{17,25},{10,2},{26... | collective-permute-start | bytes 786440 | tf_op jit(solution)/shard_map/ppermute | solution.py:89
  541.9 26.0 %collective-permute-start.43 = (bf16[32,1536]{1,0:T(8,128)(2,1)S(1)}, bf16[32,1536]{1,0:T(8,128)(2,1)S(1)}, u32[]{:S(2)}, u32[]{:S(2)}) collective-permute-start(bf16[32,1536]{1,0:T(8,128)(2,1)S(1)} %get-tuple-element.509), channel_id=1, source_target_pairs={{0,16},{8,24},{16,0},{24,8},{1,17},{9,25},{17,1},{25,9},{2,18},{10... | collective-permute-start | bytes 294920 | tf_op jit(solution)/shard_map/ppermute | solution.py:641
  550.5 15.2 %collective-permute-start.44 = (bf16[32,1664]{1,0:T(8,128)(2,1)S(1)}, bf16[32,1664]{1,0:T(8,128)(2,1)S(1)}, u32[]{:S(2)}, u32[]{:S(2)}) collective-permute-start(bf16[32,1664]{1,0:T(8,128)(2,1)S(1)} %get-tuple-element.507), channel_id=1, source_target_pairs={{0,16},{8,24},{16,0},{24,8},{1,17},{9,25},{17,1},{25,9},{2,18},{10... | collective-permute-start | bytes 319496 | tf_op jit(solution)/shard_map/ppermute | solution.py:641
  550.6 18.2 %copy-start.30 = (bf16[128,1024]{1,0:T(8,128)(2,1)S(1)}, bf16[128,1024]{1,0:T(8,128)(2,1)}, u32[]{:S(2)}) copy-start(bf16[128,1024]{1,0:T(8,128)(2,1)} %copy-done.29) | copy-start | bytes 786436
  567.9 5.9 %collective-permute-start.46 = (bf16[32,2048]{1,0:T(8,128)(2,1)S(1)}, bf16[32,2048]{1,0:T(8,128)(2,1)S(1)}, u32[]{:S(2)}, u32[]{:S(2)}) collective-permute-start(bf16[32,2048]{1,0:T(8,128)(2,1)S(1)} %slice.379), channel_id=1, source_target_pairs={{0,16},{8,24},{16,0},{24,8},{1,17},{9,25},{17,1},{25,9},{2,18},{10... | collective-permute-start | bytes 393224 | tf_op jit(solution)/shard_map/ppermute | solution.py:641
  (38 other events, 281.6 us)
Sparse Core Ops, SparseCore 0:
  9.6 49.0 all-gather.5
  60.3 34.4 all-gather.7
  96.4 49.3 all-gather.9
  147.2 35.6 all-gather.11
  294.0 193.4 reduce-scatter.1

commit v5 on v4

--- a/solution.py
+++ b/solution.py
@@ -1356,11 +1356,10 @@
     last = steps(last, left_sum, right_sum, pair_sum, three_sum)
     last.value, (enc_first, enc_rest) = chain(last.value, (enc_first, enc_rest))
     enc_second = send_back(enc_rest, 1)
-    last = steps(last, right_sum, left_sum, pair_sum)
+    last = steps(last, right_sum, left_sum, three_sum, pair_sum)
     last.value, feed_sum = chain(last.value, feed_sum)
     feed_kept, feed_sent = split_feed(feed_sum)
     feed_arrived = flip(feed_sent, "y")
-    last = steps(last, three_sum)
     last.value, enc_second = chain(last.value, enc_second)
     last = steps(last, right_sum)
     last.value, rows_first = chain(last.value, grad_rows[:half])

time: 586 us -> 580 us (0.990)
  waiting for transfers between devices: 162 us -> 148 us
  starting transfers between devices: 89.2 us -> 98.7 us
    ppermute x13, waiting for transfers between devices: 55.2 us -> 42.8 us  [flip(): return lax.ppermute(block, name, [(i, i ^ 1) for i in range(PAIR)])]
    ppermute x13, starting transfers between devices: 6.35 us -> 14.1 us  [flip(): return lax.ppermute(block, name, [(i, i ^ 1) for i in range(PAIR)])]
    unnamed x92 -> x88, local copies, waits for them, and re-layouts: 13.1 us -> 12.8 us
  transfers between devices with their start and end apart: 59 -> 59, of which waited for: 18 -> 19; matrix products, arithmetic and copies ran while one was open for 11% -> 11% of each run, Pallas kernels for 30% -> 30%
where the time goes in v5:
time: 580 us; the launch traced here: 573 us
  Pallas kernels  215 us (37%)
  waiting for transfers between devices  148 us (26%)
  starting transfers between devices  98.7 us (17%)
  local copies, waits for them, and re-layouts  38.4 us (7%)
  other arithmetic  26.9 us (5%)
  blocking collectives  24.4 us (4%)
  between operations  15.2 us (3%)
  matrix products  6.62 us (1%)
    pallas_call x15, Pallas kernels, small_kernel(): pl.pallas_call(body, in_specs=[pl.BlockSpec(memory_space=pltpu.SMEM)] * l...  61.8 us
    ppermute x13, waiting for transfers between devices, flip(): return lax.ppermute(block, name, [(i, i ^ 1) for i in range(PAIR)])  42.8 us
    all_to_all x7, waiting for transfers between devices, to_members(): return lax.all_to_all(blocks, GROUP, 0, 0, tiled=True)  42.1 us
    pallas_call x2, Pallas kernels, attend_backward(): pl.pallas_call(functools.partial(backward_kernel, chunk), grid_spec=pltpu...  38.7 us
    pallas_call x2, Pallas kernels, attend_forward(): pl.pallas_call(functools.partial(forward_kernel, chunk), grid_spec=pltpu....  29.6 us
    all_to_all x7, starting transfers between devices, to_members(): return lax.all_to_all(blocks, GROUP, 0, 0, tiled=True)  27.9 us
    ppermute x8, starting transfers between devices, flip(): return lax.ppermute(block, 't', [(i, i ^ step) for i in range(T_SIZE)])  26.4 us
    all_gather x1, blocking collectives, on_device(): ids = lax.all_gather(own_ids, GROUP, axis=0, tiled=True)  19.1 us
  transfers between devices with their start and end apart: 59, of which 19 were waited for; matrix products, arithmetic and copies ran while one was open for 11% of the time, Pallas kernels for 30%

profile of v5, /device:TPU:0, one launch (start us, length us, event | category | flops | bytes accessed | tf_op | source)
XLA Modules:
  0.0 573.3 jit_solution(11661397332883255202)
XLA Ops:
  9.8 3.1 collective-permute-start.3
  12.9 6.0 %collective-permute-done.3 = bf16[128,1024]{1,0:T(8,128)(2,1)S(1)} collective-permute-done((bf16[128,1024]{1,0:T(8,128)(2,1)S(1)}, bf16[128,1024]{1,0:T(8,128)(2,1)S(1)}, u32[]{:S(2)}, u32[]{:S(2)}) %collective-permute-start.3) | collective-permute-done | bytes 262176 | tf_op jit(solution)/shard_map/ppermute | solution.py:83
  25.7 2.1 pad_maximum_fusion
  35.4 19.1 %all-gather = s32[4,1,256]{2,1,0:T(1,128)S(1)} all-gather(s32[1,1,256]{2,1,0:T(1,128)S(1)} %bitcast.137), channel_id=1, replica_groups=mesh['t'=4,'s'=1,'y'=2,'x'=2,'core'=2] {'y','core'}, dimensions={0}, use_global_device_ids=true | all-gather | bytes 5120 | tf_op jit(solution)/shard_map/all_gather | solution.py:1169
  56.3 5.2 all_gather.20
  64.7 6.3 %shard_map.264 = bf16[1024,768]{1,0:T(8,128)(2,1)} custom-call(bf16[256,1024]{1,0:T(8,128)(2,1)} %pad_maximum_fusion.1.rows_ref.base_ref, bf16[1024,3072]{1,0:T(8,128)(2,1)} %all-gather.6.cloned.1.call-done.weight_ref, f32[1,3072]{1,0:T(1,128)} %bitcast.129), custom_call_target="tpu_custom_call" | custom-call | tf_op jit(solution)/shard_map/pallas_call | solution.py:134
  71.1 3.7 all-to-all-start
  81.1 3.0 fusion.7.left_ref
  84.1 10.7 %all-to-all-done = bf16[4,256,768]{2,1,0:T(8,128)(2,1)S(1)} async-done(((bf16[4,256,768]{2,1,0:T(8,128)(2,1)}), bf16[4,256,768]{2,1,0:T(8,128)(2,1)S(1)}, u32[]{:S(2)}, u32[]{:S(2)}) %all-to-all-start) | async-done | bytes 1572896 | tf_op jit(solution)/shard_map/all_to_all | solution.py:508
  96.0 4.3 shard_map.265.q_ref.k_ref.v_ref
  100.3 11.4 %shard_map.266 = (bf16[1024,256]{1,0:T(8,128)(2,1)}, f32[1024,256]{1,0:T(8,128)}, f32[8,1024]{1,0:T(8,128)}) custom-call(s32[16]{0:T(128)} %reshape.287.flags_ref, bf16[1024,768]{1,0:T(8,128)(2,1)} %shard_map.265.q_ref.k_ref.v_ref, bf16[1024,768]{1,0:T(8,128)(2,1)} %shard_map.265.q_ref.k_ref.v_ref, bf16[1024,768]{1,0:T(8,128)(2,1)} %shard_map.265.q_ref.k_ref.v_ref, ...), custom_call_target="tpu_custom_call" | custom-call | tf_op jit(solution)/shard_map/pallas_call | solution.py:952
  114.1 2.8 shard_map.267
  116.9 3.5 all-to-all-start.1
  120.4 2.9 collective-permute-start.10
  124.9 7.0 %shard_map.268 = (bf16[768,512]{1,0:T(8,128)(2,1)}, bf16[768,512]{1,0:T(8,128)(2,1)}, bf16[768,512]{1,0:T(8,128)(2,1)}, bf16[768,512]{1,0:T(8,128)(2,1)}) custom-call(s32[1]{0:T(128)} %bitcast.29.me_ref, bf16[768,1024]{1,0:T(8,128)(2,1)} %copy-done.5, bf16[1024,2048]{1,0:T(8,128)(2,1)} %all-gather.8.cloned.1.call-done.weight_ref, f32[1,2048]{1,0:T(1,128)} %bitcast.131), custom_call_target="tpu_custom_call" | custom-call | tf_op jit(solution)/shard_map/pallas_call | solution.py:134
  134.8 11.0 %all-gather.10.cloned.1.call-done.weight_ref = bf16[1024,2048]{1,0:T(8,128)(2,1)} async-done(((bf16[256,2048]{1,0:T(8,128)(2,1)}), bf16[1024,2048]{1,0:T(8,128)(2,1)}) %all-gather.10.cloned.1.call-update) | async-done | bytes 4194320 | tf_op jit(solution)/shard_map/all_gather | solution.py:145
  145.8 5.3 shard_map.269
  151.1 3.7 all-to-all-start.2
  159.0 15.8 %all-to-all-done.2 = bf16[4,256,256]{2,1,0:T(8,128)(2,1)S(1)} async-done(((bf16[4,256,256]{2,1,0:T(8,128)(2,1)}), bf16[4,256,256]{2,1,0:T(8,128)(2,1)S(1)}, u32[]{:S(2)}, u32[]{:S(2)}) %all-to-all-start.2) | async-done | bytes 524320 | tf_op jit(solution)/shard_map/all_to_all | solution.py:508
  175.6 2.6 shard_map.270.q_ref
  180.3 3.7 shard_map.271.k_ref.v_ref
  185.3 18.2 %shard_map.272 = (bf16[1024,256]{1,0:T(8,128)(2,1)}, f32[1024,256]{1,0:T(8,128)}, f32[8,1024]{1,0:T(8,128)}) custom-call(s32[24]{0:T(128)} %reshape.286.flags_ref, bf16[1024,256]{1,0:T(8,128)(2,1)} %shard_map.270.q_ref, bf16[3072,512]{1,0:T(8,128)(2,1)} %shard_map.271.k_ref.v_ref, bf16[3072,512]{1,0:T(8,128)(2,1)} %shard_map.271.k_ref.v_ref, ...), custom_call_target="tpu_custom_call" | custom-call | tf_op jit(solution)/shard_map/pallas_call | solution.py:952
  203.5 2.7 shard_map.273
  206.2 3.5 all-to-all-start.3
  210.2 8.3 %all-to-all-done.3 = bf16[4,256,256]{2,1,0:T(8,128)(2,1)S(1)} async-done(((bf16[4,256,256]{2,1,0:T(8,128)(2,1)}), bf16[4,256,256]{2,1,0:T(8,128)(2,1)S(1)}, u32[]{:S(2)}, u32[]{:S(2)}) %all-to-all-start.3) | async-done | bytes 524320 | tf_op jit(solution)/shard_map/all_to_all | solution.py:508
  218.5 12.0 %collective-permute-done.11.refs_2_.refs_6_ = bf16[2048,1024]{1,0:T(8,128)(2,1)} collective-permute-done((bf16[2048,1024]{1,0:T(8,128)(2,1)}, bf16[2048,1024]{1,0:T(8,128)(2,1)}, u32[]{:S(2)}, u32[]{:S(2)}) %collective-permute-start.11) | collective-permute-done | bytes 4194336 | tf_op jit(solution)/shard_map/ppermute | solution.py:1248
  231.7 4.6 shard_map.274
  238.0 10.2 %shard_map.275 = (f32[256,4096]{1,0:T(8,128)}, bf16[256,4096]{1,0:T(8,128)(2,1)}) custom-call(s32[1]{0:T(128)} %bitcast.me_ref, bf16[256,1024]{1,0:T(8,128)(2,1)} %get-tuple-element.251.rows_ref, bf16[2048,1024]{1,0:T(8,128)(2,1)} %slice_dynamic-update-slice_fusion.refs_0_.refs_4_, bf16[2048,1024]{1,0:T(8,128)(2,1)} %collective-permute-done.12.refs_1_.refs_5_, ...), custom_call_target="tpu_custom_call" | custom-call | tf_op jit(solution)/shard_map/pallas_call | solution.py:297
  248.2 12.0 %shard_map.276 = (bf16[256,1024]{1,0:T(8,128)(2,1)}, f32[256,1024]{1,0:T(8,128)}, bf16[256,1024]{1,0:T(8,128)(2,1)}, f32[8,1024]{1,0:T(8,128)}) custom-call(s32[1]{0:T(128)} %bitcast.me_ref, bf16[256,4096]{1,0:T(8,128)(2,1)} %get-tuple-element.249.hidden_ref, bf16[2048,1024]{1,0:T(8,128)(2,1)} %slice_dynamic-update-slice_fusion.refs_0_.refs_4_, ...), custom_call_target="tpu_custom_call" | custom-call | tf_op jit(solution)/shard_map/pallas_call | solution.py:374
  260.2 18.0 %shard_map.277 = (bf16[256,4096]{1,0:T(8,128)(2,1)}, f32[1,4096]{1,0:T(1,128)}, f32[256,1024]{1,0:T(8,128)}, bf16[256,1024]{1,0:T(8,128)(2,1)}, f32[8,1024]{1,0:T(8,128)}, /*index=5*/bf16[1024,256]{1,0:T(8,128)(2,1)}) custom-call(s32[1]{0:T(128)} %bitcast.me_ref, f32[256,4096]{1,0:T(8,128)} %get-tuple-element.238.slope_ref, ...), custom_call_target="tpu_custom_call" | custom-call | tf_op jit(solution)/shard_map/pallas_call | solution.py:439
  278.3 3.5 all-to-all-start.4
  282.0 11.7 %shard_map.278 = bf16[16,2,8,32,1024]{4,3,2,1,0:T(8,128)(2,1)} custom-call(bf16[256,4096]{1,0:T(8,128)(2,1)} %get-tuple-element.249.hidden_ref, bf16[256,1024]{1,0:T(8,128)(2,1)} %get-tuple-element.250.refs_8_.grads_ref, bf16[256,1024]{1,0:T(8,128)(2,1)} %get-tuple-element.251.rows_ref, bf16[256,4096]{1,0:T(8,128)(2,1)} %get-tuple-element.252.active_grads_ref), custom_call_target="tpu_custom_call" | custom-call | tf_op jit(solution)/shard_map/pallas_call | solution.py:842
  297.2 2.5 shard_map.279.g_ref
  301.0 25.4 %shard_map.280 = (bf16[1024,256]{1,0:T(8,128)(2,1)}, bf16[768,512]{1,0:T(8,128)(2,1)}, bf16[768,512]{1,0:T(8,128)(2,1)}, bf16[768,512]{1,0:T(8,128)(2,1)}, bf16[768,512]{1,0:T(8,128)(2,1)}) custom-call(s32[24]{0:T(128)} %reshape.286.flags_ref, s32[8]{0:T(128)} %stack.62.places_ref, bf16[1024,256]{1,0:T(8,128)(2,1)} %shard_map.270.q_ref, ...), custom_call_target="tpu_custom_call" | custom-call | tf_op jit(solution)/shard_map/pallas_call | solution.py:1092
  327.3 2.7 shard_map.281
  330.1 6.5 %all-to-all-start.5 = ((bf16[4,256,256]{2,1,0:T(8,128)(2,1)}), bf16[4,256,256]{2,1,0:T(8,128)(2,1)S(1)}, u32[]{:S(2)}, u32[]{:S(2)}) async-start(bf16[4,256,256]{2,1,0:T(8,128)(2,1)} %bitcast.102), calls=%async_computation.5 | async-start | bytes 1048576 | tf_op jit(solution)/shard_map/all_to_all | solution.py:508
  336.6 4.7 shard_map.282
  341.3 4.5 all-to-all-done.5
  346.6 5.7 %shard_map.283 = (f32[256,1024]{1,0:T(8,128)}, bf16[256,1024]{1,0:T(8,128)(2,1)}, f32[8,1024]{1,0:T(8,128)}, bf16[1024,256]{1,0:T(8,128)(2,1)}) custom-call(bf16[4,256,256]{2,1,0:T(8,128)(2,1)} %copy-done.4, bf16[1024,2048]{1,0:T(8,128)(2,1)} %all-gather.10.cloned.1.call-done.weight_ref, f32[256,1024]{1,0:T(8,128)} %get-tuple-element.284.resid_ref, ...), custom_call_target="tpu_custom_call" | custom-call | tf_op jit(solution)/shard_map/pallas_call | solution.py:134
  352.3 3.5 all-to-all-start.6
  355.8 6.1 %shard_map.284 = (bf16[512,3072]{1,0:T(8,128)(2,1)}, bf16[512,3072]{1,0:T(8,128)(2,1)}, f32[1,1024]{1,0:T(1,128)}) custom-call(bf16[256,1024]{1,0:T(8,128)(2,1)} %get-tuple-element.280.out_left, bf16[256,1024]{1,0:T(8,128)(2,1)} %get-tuple-element.281.query_left, bf16[256,1024]{1,0:T(8,128)(2,1)} %get-tuple-element.282.cross_left, ...), custom_call_target="tpu_custom_call" | custom-call | tf_op jit(solution)/shard_map/pallas_call | solution.py:704
  361.9 2.7 all-to-all-done.6
  367.1 2.6 shard_map.285.g_ref
  369.6 13.3 %shard_map.286 = (bf16[1024,256]{1,0:T(8,128)(2,1)}, bf16[1024,512]{1,0:T(8,128)(2,1)}) custom-call(s32[16]{0:T(128)} %reshape.287.flags_ref, s32[2]{0:T(128)} %iota_multiply_fusion.places_ref, bf16[1024,768]{1,0:T(8,128)(2,1)} %shard_map.265.q_ref.k_ref.v_ref, bf16[1024,768]{1,0:T(8,128)(2,1)} %shard_map.265.q_ref.k_ref.v_ref, ...), custom_call_target="tpu_custom_call" | custom-call | tf_op jit(solution)/shard_map/pallas_call | solution.py:1092
  385.5 4.2 shard_map.287
  389.7 11.7 %collective-permute-done.19.refs_3_ = bf16[768,512]{1,0:T(8,128)(2,1)} collective-permute-done((bf16[768,512]{1,0:T(8,128)(2,1)}, bf16[768,512]{1,0:T(8,128)(2,1)}, u32[]{:S(2)}, u32[]{:S(2)}) %collective-permute-start.19) | collective-permute-done | bytes 786464 | tf_op jit(solution)/shard_map/ppermute | solution.py:528
  406.3 11.7 %shard_map.288 = (bf16[512,2048]{1,0:T(8,128)(2,1)}, bf16[512,2048]{1,0:T(8,128)(2,1)}, bf16[384,1024]{1,0:T(8,128)(2,1)}, bf16[384,1024]{1,0:T(8,128)(2,1)}, f32[1,1024]{1,0:T(1,128)}) custom-call(s32[1]{0:T(128)} %bitcast.29.me_ref, bf16[768,1024]{1,0:T(8,128)(2,1)} %fusion.7.left_ref, bf16[1024,2048]{1,0:T(8,128)(2,1)} %all-gather.8.cloned.1.call-done.weight_ref, ...), custom_call_target="tpu_custom_call" | custom-call | tf_op jit(solution)/shard_map/pallas_call | solution.py:731
  418.0 3.2 collective-permute-done.22.refs_3_
  421.2 7.5 %shard_map.289 = (bf16[512,1536]{1,0:T(8,128)(2,1)}, bf16[512,1536]{1,0:T(8,128)(2,1)}, bf16[512,1664]{1,0:T(8,128)(2,1)}, bf16[512,1664]{1,0:T(8,128)(2,1)}, bf16[256,3072]{1,0:T(8,128)(2,1)}) custom-call(s32[1]{0:T(128)} %bitcast.29.me_ref, bf16[256,1024]{1,0:T(8,128)(2,1)} %fusion.8.left_ref, bf16[256,1024]{1,0:T(8,128)(2,1)} %fusion.9.right_ref, ...), custom_call_target="tpu_custom_call" | custom-call | tf_op jit(solution)/shard_map/pallas_call | solution.py:776
  430.2 7.3 %shard_map.290 = bf16[256,1024]{1,0:T(8,128)(2,1)} custom-call(bf16[256,3072]{1,0:T(8,128)(2,1)} %get-tuple-element.344.grads_ref, bf16[1024,3072]{1,0:T(8,128)(2,1)} %all-gather.6.cloned.1.call-done.weight_ref, f32[256,1024]{1,0:T(8,128)} %get-tuple-element.345.resid_ref), custom_call_target="tpu_custom_call" | custom-call | tf_op jit(solution)/shard_map/pallas_call | solution.py:492
  448.9 18.4 %collective-permute-done.26 = bf16[256,3072]{1,0:T(8,128)(2,1)S(1)} collective-permute-done((bf16[256,3072]{1,0:T(8,128)(2,1)}, bf16[256,3072]{1,0:T(8,128)(2,1)S(1)}, u32[]{:S(2)}, u32[]{:S(2)}) %collective-permute-start.26) | collective-permute-done | bytes 1572896 | tf_op jit(solution)/shard_map/ppermute | solution.py:642
  470.4 2.2 collective-permute-start.32
  472.5 12.6 %collective-permute-done.28 = bf16[256,1664]{1,0:T(8,128)(2,1)S(1)} collective-permute-done((bf16[256,1664]{1,0:T(8,128)(2,1)S(1)}, bf16[256,1664]{1,0:T(8,128)(2,1)S(1)}, u32[]{:S(2)}, u32[]{:S(2)}) %collective-permute-start.28) | collective-permute-done | bytes 852000 | tf_op jit(solution)/shard_map/ppermute | solution.py:642
  490.4 2.2 collective-permute-start.35
  492.6 8.1 %collective-permute-done.31 = bf16[256,2048]{1,0:T(8,128)(2,1)S(1)} collective-permute-done((bf16[256,2048]{1,0:T(8,128)(2,1)S(1)}, bf16[256,2048]{1,0:T(8,128)(2,1)S(1)}, u32[]{:S(2)}, u32[]{:S(2)}) %collective-permute-start.31) | collective-permute-done | bytes 1048608 | tf_op jit(solution)/shard_map/ppermute | solution.py:642
  502.0 3.3 collective-permute-start.38
  505.5 3.7 collective-permute-done.34
  517.1 12.6 %collective-permute-start.45 = (bf16[32,3072]{1,0:T(8,128)(2,1)S(1)}, bf16[32,3072]{1,0:T(8,128)(2,1)S(1)}, u32[]{:S(2)}, u32[]{:S(2)}) collective-permute-start(bf16[32,3072]{1,0:T(8,128)(2,1)S(1)} %get-tuple-element.502), channel_id=1, source_target_pairs={{0,16},{8,24},{16,0},{24,8},{1,17},{9,25},{17,1},{25,9},{2,18},{10... | collective-permute-start | bytes 589832 | tf_op jit(solution)/shard_map/ppermute | solution.py:641
  529.9 3.7 collective-permute-start.42
  533.7 3.5 collective-permute-done.45
  542.0 2.9 collective-permute-start.46
  545.1 2.8 collective-permute-start.44
  549.8 10.6 %collective-permute-done.43 = bf16[32,1536]{1,0:T(8,128)(2,1)S(1)} collective-permute-done((bf16[32,1536]{1,0:T(8,128)(2,1)S(1)}, bf16[32,1536]{1,0:T(8,128)(2,1)S(1)}, u32[]{:S(2)}, u32[]{:S(2)}) %collective-permute-start.43) | collective-permute-done | bytes 98336 | tf_op jit(solution)/shard_map/ppermute | solution.py:641
  560.4 2.3 collective-permute-done.44
  (295 shorter events, 105.1 us)
Async XLA Ops:
  7.2 57.5 %all-gather.6.cloned.1.call-start = ((), (), s32[]{:S(2)}) async-start(), calls=%async_computation.8 | async-start | bytes 7864320 | tf_op jit(solution)/shard_map/all_gather | solution.py:145
  8.0 116.9 %all-gather.8.cloned.1.call-start = ((), (), s32[]{:S(2)}) async-start(), calls=%async_computation.9 | async-start | bytes 5242880 | tf_op jit(solution)/shard_map/all_gather | solution.py:145
  9.1 3.8 collective-permute-start.2
  9.8 9.1 %collective-permute-start.3 = (bf16[128,1024]{1,0:T(8,128)(2,1)S(1)}, bf16[128,1024]{1,0:T(8,128)(2,1)S(1)}, u32[]{:S(2)}, u32[]{:S(2)}) collective-permute-start(bf16[128,1024]{1,0:T(8,128)(2,1)S(1)} %get-tuple-element.496), channel_id=1, source_target_pairs={{0,8},{1,24},{8,0},{9,16},{16,9},{17,25},{24,1},{25,17},{2,10},{3,... | collective-permute-start | bytes 786440 | tf_op jit(solution)/shard_map/ppermute | solution.py:83
  19.7 126.1 %all-gather.10.cloned.1.call-start = ((), (), s32[]{:S(2)}) async-start(), calls=%async_computation.10 | async-start | bytes 5242880 | tf_op jit(solution)/shard_map/all_gather | solution.py:145
  19.9 5.8 %collective-permute-start = (s32[134]{0:T(256)S(1)}, s32[134]{0:T(256)S(1)}, u32[]{:S(2)}, u32[]{:S(2)}) collective-permute-start(s32[134]{0:T(256)S(1)} %bitcast.142), channel_id=1, source_target_pairs={{0,0},{1,16},{8,8},{9,24},{16,1},{17,17},{24,9},{25,25},{2,2},{3,1... | collective-permute-start | bytes 1616 | tf_op jit(solution)/shard_map/ppermute | solution.py:82
  20.6 14.7 %collective-permute-start.1 = (s32[134]{0:T(256)S(1)}, s32[134]{0:T(256)S(1)}, u32[]{:S(2)}, u32[]{:S(2)}) collective-permute-start(s32[134]{0:T(256)S(1)} %bitcast.141), channel_id=1, source_target_pairs={{0,8},{1,24},{8,0},{9,16},{16,9},{17,25},{24,1},{25,17},{2,10},{3,... | collective-permute-start | bytes 1616 | tf_op jit(solution)/shard_map/ppermute | solution.py:83
  23.3 55.4 %collective-permute-start.4 = (bf16[384,1024]{1,0:T(8,128)(2,1)S(1)}, bf16[384,1024]{1,0:T(8,128)(2,1)}, u32[]{:S(2)}, u32[]{:S(2)}) collective-permute-start(bf16[384,1024]{1,0:T(8,128)(2,1)S(1)} %get-tuple-element.470), channel_id=1, source_target_pairs={{0,0},{1,16},{8,8},{9,24},{16,1},{17,17},{24,9},{25,25},{2,2},{3,1... | collective-permute-start | bytes 2359304 | tf_op jit(solution)/shard_map/ppermute | solution.py:82
  24.9 54.9 %collective-permute-start.5 = (bf16[384,1024]{1,0:T(8,128)(2,1)}, bf16[384,1024]{1,0:T(8,128)(2,1)}, u32[]{:S(2)}, u32[]{:S(2)}) collective-permute-start(bf16[384,1024]{1,0:T(8,128)(2,1)} %get-tuple-element.469), channel_id=1, source_target_pairs={{0,8},{1,24},{8,0},{9,16},{16,9},{17,25},{24,1},{25,17},{2,10},{3,... | collective-permute-start | bytes 2359304 | tf_op jit(solution)/shard_map/ppermute | solution.py:83
  56.2 100.4 %copy-start.32 = (s32[1024]{0:T(1024)}, s32[1024]{0:T(1024)S(1)}, u32[]{:S(2)}) copy-start(s32[1024]{0:T(1024)S(1)} %broadcast_multiply_fusion) | copy-start | bytes 12292
  71.1 23.8 %all-to-all-start = ((bf16[4,256,768]{2,1,0:T(8,128)(2,1)}), bf16[4,256,768]{2,1,0:T(8,128)(2,1)S(1)}, u32[]{:S(2)}, u32[]{:S(2)}) async-start(bf16[4,256,768]{2,1,0:T(8,128)(2,1)} %bitcast.99), calls=%async_computation | async-start | bytes 3145728 | tf_op jit(solution)/shard_map/all_to_all | solution.py:508
  74.8 134.9 %all-gather.12.cloned.1.call-start = ((), (), s32[]{:S(2)}) async-start(), calls=%async_computation.11 | async-start | bytes 2621440 | tf_op jit(solution)/shard_map/all_gather | solution.py:145
  111.8 118.7 %collective-permute-start.11 = (bf16[2048,1024]{1,0:T(8,128)(2,1)}, bf16[2048,1024]{1,0:T(8,128)(2,1)}, u32[]{:S(2)}, u32[]{:S(2)}) collective-permute-start(bf16[2048,1024]{1,0:T(8,128)(2,1)} %slice_dynamic-update-slice_fusion.refs_0_.refs_4_), channel_id=1, source_target_pairs={{0,2},{2,0},{1,3},{3,1},{4,6},{6,4},{5,7},{7,5},{8,10},{10,8},{9,1... | collective-permute-start | bytes 12582920 | tf_op jit(solution)/shard_map/ppermute | solution.py:1248
  116.9 15.0 %all-to-all-start.1 = ((bf16[4,256,256]{2,1,0:T(8,128)(2,1)}), bf16[4,256,256]{2,1,0:T(8,128)(2,1)S(1)}, u32[]{:S(2)}, u32[]{:S(2)}) async-start(bf16[4,256,256]{2,1,0:T(8,128)(2,1)} %bitcast.101), calls=%async_computation.1 | async-start | bytes 1048576 | tf_op jit(solution)/shard_map/all_to_all | solution.py:508
  120.4 34.4 %collective-permute-start.10 = (bf16[128,1024]{1,0:T(8,128)(2,1)S(1)}, bf16[128,1024]{1,0:T(8,128)(2,1)}, u32[]{:S(2)}, u32[]{:S(2)}) collective-permute-start(bf16[128,1024]{1,0:T(8,128)(2,1)S(1)} %get-tuple-element.494), channel_id=1, source_target_pairs={{0,8},{1,24},{8,0},{9,16},{16,9},{17,25},{24,1},{25,17},{2,10},{3,... | collective-permute-start | bytes 786440 | tf_op jit(solution)/shard_map/ppermute | solution.py:83
  131.9 46.3 %collective-permute-start.6 = (bf16[768,512]{1,0:T(8,128)(2,1)}, bf16[768,512]{1,0:T(8,128)(2,1)S(1)}, u32[]{:S(2)}, u32[]{:S(2)}) collective-permute-start(bf16[768,512]{1,0:T(8,128)(2,1)} %get-tuple-element.224), channel_id=1, source_target_pairs={{0,1},{1,0},{4,5},{5,4},{2,3},{3,2},{6,7},{7,6},{8,9},{9,8},{12,13... | collective-permute-start | bytes 2359304 | tf_op jit(solution)/shard_map/ppermute | solution.py:528
  132.2 46.0 %collective-permute-start.7 = (bf16[768,512]{1,0:T(8,128)(2,1)}, bf16[768,512]{1,0:T(8,128)(2,1)S(1)}, u32[]{:S(2)}, u32[]{:S(2)}) collective-permute-start(bf16[768,512]{1,0:T(8,128)(2,1)} %get-tuple-element.225), channel_id=1, source_target_pairs={{0,4},{1,5},{4,0},{5,1},{2,6},{3,7},{6,2},{7,3},{8,12},{9,13},{12,... | collective-permute-start | bytes 2359304 | tf_op jit(solution)/shard_map/ppermute | solution.py:528
  134.2 44.0 %collective-permute-start.8 = (bf16[768,512]{1,0:T(8,128)(2,1)}, bf16[768,512]{1,0:T(8,128)(2,1)S(1)}, u32[]{:S(2)}, u32[]{:S(2)}) collective-permute-start(bf16[768,512]{1,0:T(8,128)(2,1)} %get-tuple-element.226), channel_id=1, source_target_pairs={{0,5},{1,4},{4,1},{5,0},{2,7},{3,6},{6,3},{7,2},{8,13},{9,12},{12,... | collective-permute-start | bytes 2359304 | tf_op jit(solution)/shard_map/ppermute | solution.py:528
  151.1 23.7 %all-to-all-start.2 = ((bf16[4,256,256]{2,1,0:T(8,128)(2,1)}), bf16[4,256,256]{2,1,0:T(8,128)(2,1)S(1)}, u32[]{:S(2)}, u32[]{:S(2)}) async-start(bf16[4,256,256]{2,1,0:T(8,128)(2,1)} %bitcast.110), calls=%async_computation.2 | async-start | bytes 1048576 | tf_op jit(solution)/shard_map/all_to_all | solution.py:508
  154.8 2.4 collective-permute-start.9
  206.2 12.3 %all-to-all-start.3 = ((bf16[4,256,256]{2,1,0:T(8,128)(2,1)}), bf16[4,256,256]{2,1,0:T(8,128)(2,1)S(1)}, u32[]{:S(2)}, u32[]{:S(2)}) async-start(bf16[4,256,256]{2,1,0:T(8,128)(2,1)} %bitcast.103), calls=%async_computation.3 | async-start | bytes 1048576 | tf_op jit(solution)/shard_map/all_to_all | solution.py:508
  209.7 26.5 %collective-permute-start.12 = (bf16[2048,1024]{1,0:T(8,128)(2,1)}, bf16[2048,1024]{1,0:T(8,128)(2,1)}, u32[]{:S(2)}, u32[]{:S(2)}) collective-permute-start(bf16[2048,1024]{1,0:T(8,128)(2,1)} %slice_dynamic-update-slice_fusion.refs_0_.refs_4_), channel_id=1, source_target_pairs={{0,1},{1,0},{2,3},{3,2},{4,5},{5,4},{6,7},{7,6},{8,9},{9,8},{10,11... | collective-permute-start | bytes 12582920 | tf_op jit(solution)/shard_map/ppermute | solution.py:1268
  230.5 7.5 %collective-permute-start.13 = (bf16[2048,1024]{1,0:T(8,128)(2,1)}, bf16[2048,1024]{1,0:T(8,128)(2,1)}, u32[]{:S(2)}, u32[]{:S(2)}) collective-permute-start(bf16[2048,1024]{1,0:T(8,128)(2,1)} %collective-permute-done.11.refs_2_.refs_6_), channel_id=1, source_target_pairs={{0,1},{1,0},{2,3},{3,2},{4,5},{5,4},{6,7},{7,6},{8,9},{9,8},{10,11... | collective-permute-start | bytes 12582920 | tf_op jit(solution)/shard_map/ppermute | solution.py:1272
  278.3 15.4 %all-to-all-start.4 = ((bf16[4,256,256]{2,1,0:T(8,128)(2,1)}), bf16[4,256,256]{2,1,0:T(8,128)(2,1)S(1)}, u32[]{:S(2)}, u32[]{:S(2)}) async-start(bf16[4,256,256]{2,1,0:T(8,128)(2,1)} %bitcast.111), calls=%async_computation.4 | async-start | bytes 1048576 | tf_op jit(solution)/shard_map/all_to_all | solution.py:508
  281.7 223.6 %reduce-scatter.2.cloned.1.call-start = ((), (), s32[]{:S(2)}) async-start(), calls=%async_computation.12 | async-start | bytes 17825792 | tf_op jit(solution)/shard_map/reduce_scatter | solution.py:859
  294.9 31.5 %collective-permute-start.14 = (bf16[128,1024]{1,0:T(8,128)(2,1)S(1)}, bf16[128,1024]{1,0:T(8,128)(2,1)S(1)}, u32[]{:S(2)}, u32[]{:S(2)}) collective-permute-start(bf16[128,1024]{1,0:T(8,128)(2,1)S(1)} %get-tuple-element.491), channel_id=1, source_target_pairs={{0,0},{16,1},{8,8},{24,9},{1,16},{17,17},{9,24},{25,25},{2,2},{18,... | collective-permute-start | bytes 786440 | tf_op jit(solution)/shard_map/ppermute | solution.py:89
  295.6 30.8 %collective-permute-start.15 = (bf16[128,1024]{1,0:T(8,128)(2,1)S(1)}, bf16[128,1024]{1,0:T(8,128)(2,1)S(1)}, u32[]{:S(2)}, u32[]{:S(2)}) collective-permute-start(bf16[128,1024]{1,0:T(8,128)(2,1)S(1)} %get-tuple-element.492), channel_id=1, source_target_pairs={{8,0},{24,1},{0,8},{16,9},{9,16},{25,17},{1,24},{17,25},{10,2},{26... | collective-permute-start | bytes 786440 | tf_op jit(solution)/shard_map/ppermute | solution.py:89
  330.1 15.8 %all-to-all-start.5 = ((bf16[4,256,256]{2,1,0:T(8,128)(2,1)}), bf16[4,256,256]{2,1,0:T(8,128)(2,1)S(1)}, u32[]{:S(2)}, u32[]{:S(2)}) async-start(bf16[4,256,256]{2,1,0:T(8,128)(2,1)} %bitcast.102), calls=%async_computation.5 | async-start | bytes 1048576 | tf_op jit(solution)/shard_map/all_to_all | solution.py:508
  352.3 12.3 %all-to-all-start.6 = ((bf16[4,256,256]{2,1,0:T(8,128)(2,1)}), bf16[4,256,256]{2,1,0:T(8,128)(2,1)S(1)}, u32[]{:S(2)}, u32[]{:S(2)}) async-start(bf16[4,256,256]{2,1,0:T(8,128)(2,1)} %bitcast.112), calls=%async_computation.6 | async-start | bytes 1048576 | tf_op jit(solution)/shard_map/all_to_all | solution.py:508
  364.6 18.3 %collective-permute-start.16 = (bf16[512,3072]{1,0:T(8,128)(2,1)}, bf16[512,3072]{1,0:T(8,128)(2,1)S(1)}, u32[]{:S(2)}, u32[]{:S(2)}) collective-permute-start(bf16[512,3072]{1,0:T(8,128)(2,1)} %get-tuple-element.299), channel_id=1, source_target_pairs={{0,1},{1,0},{2,3},{3,2},{4,5},{5,4},{6,7},{7,6},{8,9},{9,8},{10,11... | collective-permute-start | bytes 9437192 | tf_op jit(solution)/shard_map/ppermute | solution.py:642
  365.2 24.5 %collective-permute-start.17 = (bf16[768,512]{1,0:T(8,128)(2,1)}, bf16[768,512]{1,0:T(8,128)(2,1)S(1)}, u32[]{:S(2)}, u32[]{:S(2)}) collective-permute-start(bf16[768,512]{1,0:T(8,128)(2,1)} %get-tuple-element.311), channel_id=1, source_target_pairs={{0,1},{1,0},{4,5},{5,4},{2,3},{3,2},{6,7},{7,6},{8,9},{9,8},{12,13... | collective-permute-start | bytes 2359304 | tf_op jit(solution)/shard_map/ppermute | solution.py:528
  365.7 24.1 %collective-permute-start.18 = (bf16[768,512]{1,0:T(8,128)(2,1)}, bf16[768,512]{1,0:T(8,128)(2,1)}, u32[]{:S(2)}, u32[]{:S(2)}) collective-permute-start(bf16[768,512]{1,0:T(8,128)(2,1)} %get-tuple-element.312), channel_id=1, source_target_pairs={{0,4},{1,5},{4,0},{5,1},{2,6},{3,7},{6,2},{7,3},{8,12},{9,13},{12,... | collective-permute-start | bytes 2359304 | tf_op jit(solution)/shard_map/ppermute | solution.py:528
  366.0 35.4 %collective-permute-start.19 = (bf16[768,512]{1,0:T(8,128)(2,1)}, bf16[768,512]{1,0:T(8,128)(2,1)}, u32[]{:S(2)}, u32[]{:S(2)}) collective-permute-start(bf16[768,512]{1,0:T(8,128)(2,1)} %get-tuple-element.313), channel_id=1, source_target_pairs={{0,5},{1,4},{4,1},{5,0},{2,7},{3,6},{6,3},{7,2},{8,13},{9,12},{12,... | collective-permute-start | bytes 2359304 | tf_op jit(solution)/shard_map/ppermute | solution.py:528
  385.5 18.8 %copy-start.34 = (f32[1,4096]{1,0:T(1,128)S(1)}, f32[1,4096]{1,0:T(1,128)}, u32[]{:S(2)}) copy-start(f32[1,4096]{1,0:T(1,128)} %get-tuple-element.334) | copy-start | bytes 49156
  389.7 16.6 %copy-start.17 = (bf16[768,512]{1,0:T(8,128)(2,1)}, bf16[768,512]{1,0:T(8,128)(2,1)S(1)}, u32[]{:S(2)}) copy-start(bf16[768,512]{1,0:T(8,128)(2,1)S(1)} %collective-permute-done.17.refs_1_) | copy-start | bytes 2359300
  401.4 16.6 %collective-permute-start.20 = (bf16[256,768]{1,0:T(8,128)(2,1)}, bf16[256,768]{1,0:T(8,128)(2,1)S(1)}, u32[]{:S(2)}, u32[]{:S(2)}) collective-permute-start(bf16[256,768]{1,0:T(8,128)(2,1)} %get-tuple-element.325), channel_id=1, source_target_pairs={{0,1},{1,0},{4,5},{5,4},{2,3},{3,2},{6,7},{7,6},{8,9},{9,8},{12,13... | collective-permute-start | bytes 1179656 | tf_op jit(solution)/shard_map/ppermute | solution.py:528
  402.4 15.6 %collective-permute-start.21 = (bf16[256,768]{1,0:T(8,128)(2,1)}, bf16[256,768]{1,0:T(8,128)(2,1)}, u32[]{:S(2)}, u32[]{:S(2)}) collective-permute-start(bf16[256,768]{1,0:T(8,128)(2,1)} %get-tuple-element.326), channel_id=1, source_target_pairs={{0,4},{1,5},{4,0},{5,1},{2,6},{3,7},{6,2},{7,3},{8,12},{9,13},{12,... | collective-permute-start | bytes 1179656 | tf_op jit(solution)/shard_map/ppermute | solution.py:528
  402.8 18.4 %collective-permute-start.22 = (bf16[256,768]{1,0:T(8,128)(2,1)}, bf16[256,768]{1,0:T(8,128)(2,1)}, u32[]{:S(2)}, u32[]{:S(2)}) collective-permute-start(bf16[256,768]{1,0:T(8,128)(2,1)} %get-tuple-element.327), channel_id=1, source_target_pairs={{0,5},{1,4},{4,1},{5,0},{2,7},{3,6},{6,3},{7,2},{8,13},{9,12},{12,... | collective-permute-start | bytes 1179656 | tf_op jit(solution)/shard_map/ppermute | solution.py:528
  428.7 12.8 %collective-permute-start.23 = (bf16[512,1536]{1,0:T(8,128)(2,1)}, bf16[512,1536]{1,0:T(8,128)(2,1)}, u32[]{:S(2)}, u32[]{:S(2)}) collective-permute-start(bf16[512,1536]{1,0:T(8,128)(2,1)} %get-tuple-element.347), channel_id=1, source_target_pairs={{0,1},{1,0},{2,3},{3,2},{4,5},{5,4},{6,7},{7,6},{8,9},{9,8},{10,11... | collective-permute-start | bytes 4718600 | tf_op jit(solution)/shard_map/ppermute | solution.py:642
  429.9 15.7 %collective-permute-start.24 = (bf16[512,1664]{1,0:T(8,128)(2,1)}, bf16[512,1664]{1,0:T(8,128)(2,1)S(1)}, u32[]{:S(2)}, u32[]{:S(2)}) collective-permute-start(bf16[512,1664]{1,0:T(8,128)(2,1)} %get-tuple-element.351), channel_id=1, source_target_pairs={{0,1},{1,0},{2,3},{3,2},{4,5},{5,4},{6,7},{7,6},{8,9},{9,8},{10,11... | collective-permute-start | bytes 5111816 | tf_op jit(solution)/shard_map/ppermute | solution.py:642
  429.9 37.4 %collective-permute-start.26 = (bf16[256,3072]{1,0:T(8,128)(2,1)}, bf16[256,3072]{1,0:T(8,128)(2,1)S(1)}, u32[]{:S(2)}, u32[]{:S(2)}) collective-permute-start(bf16[256,3072]{1,0:T(8,128)(2,1)} %get-tuple-element.457), channel_id=1, source_target_pairs={{0,4},{4,0},{1,5},{5,1},{2,6},{6,2},{3,7},{7,3},{8,12},{12,8},{9,1... | collective-permute-start | bytes 4718600 | tf_op jit(solution)/shard_map/ppermute | solution.py:642
  437.6 10.3 %collective-permute-start.25 = (bf16[512,2048]{1,0:T(8,128)(2,1)}, bf16[512,2048]{1,0:T(8,128)(2,1)S(1)}, u32[]{:S(2)}, u32[]{:S(2)}) collective-permute-start(bf16[512,2048]{1,0:T(8,128)(2,1)} %get-tuple-element.353), channel_id=1, source_target_pairs={{0,1},{1,0},{2,3},{3,2},{4,5},{5,4},{6,7},{7,6},{8,9},{9,8},{10,11... | collective-permute-start | bytes 6291464 | tf_op jit(solution)/shard_map/ppermute | solution.py:642
  437.6 30.4 %collective-permute-start.27 = (bf16[384,1024]{1,0:T(8,128)(2,1)}, bf16[384,1024]{1,0:T(8,128)(2,1)S(1)}, u32[]{:S(2)}, u32[]{:S(2)}) collective-permute-start(bf16[384,1024]{1,0:T(8,128)(2,1)} %get-tuple-element.356), channel_id=1, source_target_pairs={{0,0},{16,1},{8,8},{24,9},{1,16},{17,17},{9,24},{25,25},{2,2},{18,... | collective-permute-start | bytes 2359304 | tf_op jit(solution)/shard_map/ppermute | solution.py:89
  443.4 42.7 %collective-permute-start.29 = (bf16[256,1536]{1,0:T(8,128)(2,1)S(1)}, bf16[256,1536]{1,0:T(8,128)(2,1)S(1)}, u32[]{:S(2)}, u32[]{:S(2)}) collective-permute-start(bf16[256,1536]{1,0:T(8,128)(2,1)S(1)} %get-tuple-element.467), channel_id=1, source_target_pairs={{0,2},{2,0},{1,3},{3,1},{4,6},{6,4},{5,7},{7,5},{8,10},{10,8},{9,1... | collective-permute-start | bytes 2359304 | tf_op jit(solution)/shard_map/ppermute | solution.py:642
  446.1 39.0 %collective-permute-start.28 = (bf16[256,1664]{1,0:T(8,128)(2,1)S(1)}, bf16[256,1664]{1,0:T(8,128)(2,1)S(1)}, u32[]{:S(2)}, u32[]{:S(2)}) collective-permute-start(bf16[256,1664]{1,0:T(8,128)(2,1)S(1)} %get-tuple-element.461), channel_id=1, source_target_pairs={{0,4},{4,0},{1,5},{5,1},{2,6},{6,2},{3,7},{7,3},{8,12},{12,8},{9,1... | collective-permute-start | bytes 2555912 | tf_op jit(solution)/shard_map/ppermute | solution.py:642
  468.0 18.1 %copy-start.21 = (bf16[384,1024]{1,0:T(8,128)(2,1)}, bf16[384,1024]{1,0:T(8,128)(2,1)S(1)}, u32[]{:S(2)}) copy-start(bf16[384,1024]{1,0:T(8,128)(2,1)S(1)} %collective-permute-done.27) | copy-start | bytes 2359300
  468.0 21.4 %collective-permute-start.30 = (bf16[128,3072]{1,0:T(8,128)(2,1)S(1)}, bf16[128,3072]{1,0:T(8,128)(2,1)S(1)}, u32[]{:S(2)}, u32[]{:S(2)}) collective-permute-start(bf16[128,3072]{1,0:T(8,128)(2,1)S(1)} %get-tuple-element.465), channel_id=1, source_target_pairs={{0,2},{2,0},{1,3},{3,1},{4,6},{6,4},{5,7},{7,5},{8,10},{10,8},{9,1... | collective-permute-start | bytes 2359304 | tf_op jit(solution)/shard_map/ppermute | solution.py:642
  470.1 30.5 %collective-permute-start.31 = (bf16[256,2048]{1,0:T(8,128)(2,1)S(1)}, bf16[256,2048]{1,0:T(8,128)(2,1)S(1)}, u32[]{:S(2)}, u32[]{:S(2)}) collective-permute-start(bf16[256,2048]{1,0:T(8,128)(2,1)S(1)} %get-tuple-element.459), channel_id=1, source_target_pairs={{0,4},{4,0},{1,5},{5,1},{2,6},{6,2},{3,7},{7,3},{8,12},{12,8},{9,1... | collective-permute-start | bytes 3145736 | tf_op jit(solution)/shard_map/ppermute | solution.py:642
  470.4 34.9 %collective-permute-start.32 = (bf16[384,1024]{1,0:T(8,128)(2,1)}, bf16[384,1024]{1,0:T(8,128)(2,1)S(1)}, u32[]{:S(2)}, u32[]{:S(2)}) collective-permute-start(bf16[384,1024]{1,0:T(8,128)(2,1)} %get-tuple-element.372), channel_id=1, source_target_pairs={{8,0},{24,1},{0,8},{16,9},{9,16},{25,17},{1,24},{17,25},{10,2},{26... | collective-permute-start | bytes 2359304 | tf_op jit(solution)/shard_map/ppermute | solution.py:89
  486.2 19.2 %collective-permute-start.33 = (bf16[128,1664]{1,0:T(8,128)(2,1)}, bf16[128,1664]{1,0:T(8,128)(2,1)S(1)}, u32[]{:S(2)}, u32[]{:S(2)}) collective-permute-start(bf16[128,1664]{1,0:T(8,128)(2,1)} %get-tuple-element.477), channel_id=1, source_target_pairs={{0,2},{2,0},{1,3},{3,1},{4,6},{6,4},{5,7},{7,5},{8,10},{10,8},{9,1... | collective-permute-start | bytes 1277960 | tf_op jit(solution)/shard_map/ppermute | solution.py:642
  489.1 20.0 %collective-permute-start.34 = (bf16[128,1536]{1,0:T(8,128)(2,1)}, bf16[128,1536]{1,0:T(8,128)(2,1)}, u32[]{:S(2)}, u32[]{:S(2)}) collective-permute-start(bf16[128,1536]{1,0:T(8,128)(2,1)} %get-tuple-element.481), channel_id=1, source_target_pairs={{0,4},{4,0},{1,5},{5,1},{2,6},{6,2},{3,7},{7,3},{8,12},{12,8},{9,1... | collective-permute-start | bytes 1179656 | tf_op jit(solution)/shard_map/ppermute | solution.py:642
  490.4 19.9 %collective-permute-start.35 = (bf16[64,3072]{1,0:T(8,128)(2,1)}, bf16[64,3072]{1,0:T(8,128)(2,1)}, u32[]{:S(2)}, u32[]{:S(2)}) collective-permute-start(bf16[64,3072]{1,0:T(8,128)(2,1)} %get-tuple-element.479), channel_id=1, source_target_pairs={{0,8},{8,0},{16,24},{24,16},{1,9},{9,1},{17,25},{25,17},{2,10},{10... | collective-permute-start | bytes 1179656 | tf_op jit(solution)/shard_map/ppermute | solution.py:641
  502.0 27.8 %collective-permute-start.38 = (bf16[128,2048]{1,0:T(8,128)(2,1)}, bf16[128,2048]{1,0:T(8,128)(2,1)S(1)}, u32[]{:S(2)}, u32[]{:S(2)}) collective-permute-start(bf16[128,2048]{1,0:T(8,128)(2,1)} %get-tuple-element.475), channel_id=1, source_target_pairs={{0,2},{2,0},{1,3},{3,1},{4,6},{6,4},{5,7},{7,5},{8,10},{10,8},{9,1... | collective-permute-start | bytes 1572872 | tf_op jit(solution)/shard_map/ppermute | solution.py:642
  511.5 5.6 collective-permute-start.36
  512.2 27.8 %collective-permute-start.39 = (bf16[8,32,1024]{2,1,0:T(8,128)(2,1)S(1)}, bf16[8,32,1024]{2,1,0:T(8,128)(2,1)S(1)}, u32[]{:S(2)}, u32[]{:S(2)}) collective-permute-start(bf16[8,32,1024]{2,1,0:T(8,128)(2,1)S(1)} %dynamic-slice_bitcast_fusion.2), channel_id=1, source_target_pairs={{0,4},{4,0},{1,5},{5,1},{2,6},{6,2},{3,7},{7,3},{8,12},{12,8},{9,1... | collective-permute-start | bytes 1572872 | tf_op jit(solution)/shard_map/ppermute | solution.py:642
  513.0 27.0 %collective-permute-start.40 = (bf16[64,1664]{1,0:T(8,128)(2,1)S(1)}, bf16[64,1664]{1,0:T(8,128)(2,1)S(1)}, u32[]{:S(2)}, u32[]{:S(2)}) collective-permute-start(bf16[64,1664]{1,0:T(8,128)(2,1)S(1)} %get-tuple-element.497), channel_id=1, source_target_pairs={{0,8},{8,0},{16,24},{24,16},{1,9},{9,1},{17,25},{25,17},{2,10},{10... | collective-permute-start | bytes 638984 | tf_op jit(solution)/shard_map/ppermute | solution.py:641
  513.2 26.9 %collective-permute-start.41 = (bf16[64,1536]{1,0:T(8,128)(2,1)S(1)}, bf16[64,1536]{1,0:T(8,128)(2,1)S(1)}, u32[]{:S(2)}, u32[]{:S(2)}) collective-permute-start(bf16[64,1536]{1,0:T(8,128)(2,1)S(1)} %get-tuple-element.504), channel_id=1, source_target_pairs={{0,8},{8,0},{16,24},{24,16},{1,9},{9,1},{17,25},{25,17},{2,10},{10... | collective-permute-start | bytes 589832 | tf_op jit(solution)/shard_map/ppermute | solution.py:641
  517.1 20.0 %copy-start.27 = (bf16[128,1024]{1,0:T(8,128)(2,1)S(1)}, bf16[128,1024]{1,0:T(8,128)(2,1)}, u32[]{:S(2)}) copy-start(bf16[128,1024]{1,0:T(8,128)(2,1)} %get-tuple-element.381) | copy-start | bytes 786436
  517.1 20.0 %collective-permute-start.45 = (bf16[32,3072]{1,0:T(8,128)(2,1)S(1)}, bf16[32,3072]{1,0:T(8,128)(2,1)S(1)}, u32[]{:S(2)}, u32[]{:S(2)}) collective-permute-start(bf16[32,3072]{1,0:T(8,128)(2,1)S(1)} %get-tuple-element.502), channel_id=1, source_target_pairs={{0,16},{8,24},{16,0},{24,8},{1,17},{9,25},{17,1},{25,9},{2,18},{10... | collective-permute-start | bytes 589832 | tf_op jit(solution)/shard_map/ppermute | solution.py:641
  529.9 12.0 %collective-permute-start.42 = (bf16[64,2048]{1,0:T(8,128)(2,1)S(1)}, bf16[64,2048]{1,0:T(8,128)(2,1)S(1)}, u32[]{:S(2)}, u32[]{:S(2)}) collective-permute-start(bf16[64,2048]{1,0:T(8,128)(2,1)S(1)} %get-tuple-element.483), channel_id=1, source_target_pairs={{0,8},{8,0},{16,24},{24,16},{1,9},{9,1},{17,25},{25,17},{2,10},{10... | collective-permute-start | bytes 786440 | tf_op jit(solution)/shard_map/ppermute | solution.py:641
  537.1 11.6 %collective-permute-start.37 = (bf16[128,1024]{1,0:T(8,128)(2,1)S(1)}, bf16[128,1024]{1,0:T(8,128)(2,1)S(1)}, u32[]{:S(2)}, u32[]{:S(2)}) collective-permute-start(bf16[128,1024]{1,0:T(8,128)(2,1)S(1)} %copy-done.27), channel_id=1, source_target_pairs={{8,0},{24,1},{0,8},{16,9},{9,16},{25,17},{1,24},{17,25},{10,2},{26... | collective-permute-start | bytes 786440 | tf_op jit(solution)/shard_map/ppermute | solution.py:89
  542.0 23.5 %collective-permute-start.46 = (bf16[32,2048]{1,0:T(8,128)(2,1)S(1)}, bf16[32,2048]{1,0:T(8,128)(2,1)S(1)}, u32[]{:S(2)}, u32[]{:S(2)}) collective-permute-start(bf16[32,2048]{1,0:T(8,128)(2,1)S(1)} %slice.379), channel_id=1, source_target_pairs={{0,16},{8,24},{16,0},{24,8},{1,17},{9,25},{17,1},{25,9},{2,18},{10... | collective-permute-start | bytes 393224 | tf_op jit(solution)/shard_map/ppermute | solution.py:641
  545.0 15.4 %collective-permute-start.43 = (bf16[32,1536]{1,0:T(8,128)(2,1)S(1)}, bf16[32,1536]{1,0:T(8,128)(2,1)S(1)}, u32[]{:S(2)}, u32[]{:S(2)}) collective-permute-start(bf16[32,1536]{1,0:T(8,128)(2,1)S(1)} %get-tuple-element.509), channel_id=1, source_target_pairs={{0,16},{8,24},{16,0},{24,8},{1,17},{9,25},{17,1},{25,9},{2,18},{10... | collective-permute-start | bytes 294920 | tf_op jit(solution)/shard_map/ppermute | solution.py:641
  545.1 17.6 %collective-permute-start.44 = (bf16[32,1664]{1,0:T(8,128)(2,1)S(1)}, bf16[32,1664]{1,0:T(8,128)(2,1)S(1)}, u32[]{:S(2)}, u32[]{:S(2)}) collective-permute-start(bf16[32,1664]{1,0:T(8,128)(2,1)S(1)} %get-tuple-element.507), channel_id=1, source_target_pairs={{0,16},{8,24},{16,0},{24,8},{1,17},{9,25},{17,1},{25,9},{2,18},{10... | collective-permute-start | bytes 319496 | tf_op jit(solution)/shard_map/ppermute | solution.py:641
  (36 other events, 242.0 us)
Sparse Core Ops, SparseCore 0:
  9.6 49.0 all-gather.5
  60.3 34.4 all-gather.7
  96.4 49.3 all-gather.9
  147.2 35.6 all-gather.11
  293.8 196.2 reduce-scatter.1
